TPU v7x, 32 devices: a whole 2x2x4 slice. The times are simulated.
32 devices in a mesh: dp: 4 (over x, core), blk: 8 (over z, y).
Axes of the slice: x: 2, y: 2, z: 4, core: 2. Of those that a mesh axis runs over, the one named last changes fastest.
Arguments:
- queries: bfloat16 [4, 1536, 512], P('dp', 'blk'), may hold values from -6 to 6, as said below
- key_in: bfloat16 [4, 1536, 512], P('dp', 'blk'), may hold values from -6 to 6, as said below
- value_in: bfloat16 [4, 1536, 512], P('dp', 'blk'), may hold values from -6 to 6
- out_weight: bfloat16 [512, 1024], replicated, may hold values from -2 to 2
- conv_kernel: float32 [31, 1024], replicated, may hold values from -1 to 1
- cotangent: bfloat16 [4, 1536, 1024], P('dp', 'blk'), may hold values from -6 to 6
Outputs:
- out_frames: bfloat16 [4, 1536, 1024], P('dp', 'blk')
- query_grad: bfloat16 [4, 1536, 512], P('dp', 'blk')
- key_grad: bfloat16 [4, 1536, 512], P('dp', 'blk')
- value_grad: bfloat16 [4, 1536, 512], P('dp', 'blk')
- weight_grad: float32 [512, 1024], replicated
- kernel_grad: float32 [31, 1024], replicated
Inputs may be any that keep to these rules, and one draw needn't show every extreme that they name: `queries`: independent entries. `key_in`: independent entries.
All inputs are finite; a program needn't handle non-finite values.
Results may differ from a plain program's by a relative error of at most 0.024.
Values may be sent and summed in bfloat16 or wider, within the bound.
No kernel may reach another device: no remote copies, remote signals or barrier semaphores. Data moves between devices by JAX's collectives and lax.ppermute only.
A program may use at most 64 MiB of HBM per device.

v0:
```python
import math

import jax
import jax.numpy as jnp
from jax import lax
from jax.sharding import PartitionSpec as P

ATT_HEADS = 8
HEAD_DIM = 64
CTX_MAX = 3
ATT = 512


NEGATIVE = -1e30


def from_behind(block, axis, distance):
    devices = range(lax.axis_size(axis))
    route = [(i - distance, i) for i in devices if i - distance in devices]
    return lax.ppermute(block, axis, route)


def from_behind_2(x, axis, by):
    size = lax.axis_size(axis)
    return lax.ppermute(x, axis, [(i, (i + by) % size) for i in range(size)])


def split_heads(matrix):
    return matrix.reshape(matrix.shape[0], ATT_HEADS, HEAD_DIM)


def tile_scores(query_heads, tile, query_pos, key_pos, usable, left_span, score_scale):
    key_heads = split_heads(tile[:, :ATT])
    scores = (
        jnp.einsum("qhd,khd->hqk", query_heads, key_heads, preferred_element_type=jnp.float32)
        * score_scale
    )
    distance = query_pos[:, None] - key_pos[None, :]
    visible = ((distance >= 0) & (distance < left_span) & usable)[None]
    return (jnp.where(visible, scores, NEGATIVE), visible)


def attend_tile(
    softmax_state, query_heads, tile, query_pos, key_pos, usable, left_span, score_scale
):
    running_max, running_sum, weighted = softmax_state
    scores, visible = tile_scores(
        query_heads, tile, query_pos, key_pos, usable, left_span, score_scale
    )
    new_max = jnp.maximum(running_max, jnp.max(scores, axis=-1))
    weights = jnp.where(visible, jnp.exp(scores - new_max[..., None]), 0.0)
    fading = jnp.exp(running_max - new_max)
    running_sum = running_sum * fading + jnp.sum(weights, axis=-1)
    value_heads = split_heads(tile[:, ATT:])
    update = jnp.einsum(
        "hqk,khd->qhd",
        weights.astype(jnp.bfloat16),
        value_heads,
        preferred_element_type=jnp.float32,
    )
    weighted = weighted * jnp.transpose(fading)[:, :, None] + update
    return (new_max, running_sum, weighted)


def tile_grads(
    query_heads,
    dout_heads,
    log_sums,
    deltas,
    tile,
    query_pos,
    key_pos,
    usable,
    left_span,
    score_scale,
):
    scores, visible = tile_scores(
        query_heads, tile, query_pos, key_pos, usable, left_span, score_scale
    )
    key_heads = split_heads(tile[:, :ATT])
    value_heads = split_heads(tile[:, ATT:])
    probs = jnp.where(visible, jnp.exp(scores - log_sums[..., None]), 0.0)
    dvalue_heads = jnp.einsum(
        "hqk,qhd->khd", probs.astype(jnp.bfloat16), dout_heads, preferred_element_type=jnp.float32
    )
    dprobs = jnp.einsum("qhd,khd->hqk", dout_heads, value_heads, preferred_element_type=jnp.float32)
    dscores = (probs * (dprobs - deltas[..., None])).astype(jnp.bfloat16)
    dquery = (
        jnp.einsum("hqk,khd->qhd", dscores, key_heads, preferred_element_type=jnp.float32)
        * score_scale
    )
    dkey_heads = (
        jnp.einsum("hqk,qhd->khd", dscores, query_heads, preferred_element_type=jnp.float32)
        * score_scale
    )
    row_count = tile.shape[0]
    return (
        dquery,
        jnp.concatenate(
            [dkey_heads.reshape(row_count, ATT), dvalue_heads.reshape(row_count, ATT)], axis=1
        ),
    )


def depthwise(extended, conv_kernel, row_count, ahead):
    tap_count = conv_kernel.shape[0]

    def add_tap(tap_index, running):
        first_row = tap_index if ahead else tap_count - 1 - tap_index
        return running + conv_kernel[tap_index] * lax.dynamic_slice_in_dim(
            extended, first_row, row_count, 0
        )

    empty = jnp.zeros((row_count, extended.shape[1]), jnp.float32)
    return lax.fori_loop(0, tap_count, add_tap, empty)


def sum_weights(weight_part, kernel_part):
    return lax.psum((weight_part, kernel_part), ("dp", "blk"))


def per_device(queries, key_in, value_in, out_weight, conv_kernel, cotangent):
    cycle_count = lax.axis_size("blk")
    device = lax.axis_index("blk")
    row_count = queries.shape[1]
    context = min(CTX_MAX, cycle_count // 4)
    left_span = context * row_count
    score_scale = 1.0 / math.sqrt(HEAD_DIM)
    edge_rows = conv_kernel.shape[0] - 1
    row_ids = jnp.arange(row_count, dtype=jnp.int32)
    query_heads = split_heads(queries[0])
    own_tile = jnp.concatenate([key_in[0], value_in[0]], axis=1)
    own_pos = device * row_count + row_ids
    always = jnp.array(True)

    def source(offset):
        anchor = device - offset
        return (anchor * row_count + row_ids, anchor >= 0)

    start_state = (
        jnp.full((ATT_HEADS, row_count), NEGATIVE, jnp.float32),
        jnp.zeros((ATT_HEADS, row_count), jnp.float32),
        jnp.zeros((row_count, ATT_HEADS, HEAD_DIM), jnp.float32),
    )
    first_state = attend_tile(
        start_state, query_heads, own_tile, own_pos, own_pos, always, left_span, score_scale
    )

    def forward_step(carry, offset):
        moving, softmax_state = carry
        arrived = from_behind(moving, "blk", 1)
        tile_pos, tile_usable = source(offset)
        softmax_state = attend_tile(
            softmax_state,
            query_heads,
            arrived,
            own_pos,
            tile_pos,
            tile_usable,
            left_span,
            score_scale,
        )
        return ((arrived, softmax_state), arrived)

    offsets = jnp.arange(1, context + 1, dtype=jnp.int32)
    (unused_tile, final_state), kept_tiles = lax.scan(
        forward_step, (own_tile, first_state), offsets
    )
    running_max, running_sum, weighted = final_state
    attended = (weighted / jnp.transpose(running_sum)[:, :, None]).astype(jnp.bfloat16)
    log_sums = running_max + jnp.log(running_sum)
    flat = attended.reshape(row_count, ATT)
    hidden = jnp.dot(flat, out_weight, preferred_element_type=jnp.float32).astype(jnp.bfloat16)
    before = from_behind(hidden[-edge_rows:], "blk", 1)
    extended = jnp.concatenate([before, hidden], axis=0).astype(jnp.float32)
    mixed = depthwise(extended, conv_kernel, row_count, False)
    sigma = jax.nn.sigmoid(mixed)
    out_frames = (mixed * sigma).astype(jnp.bfloat16)[None]
    upstream = cotangent[0].astype(jnp.float32)
    dmixed = upstream * sigma * (1.0 + mixed * (1.0 - sigma))
    after = from_behind(dmixed[:edge_rows].astype(jnp.bfloat16), "blk", -1).astype(jnp.float32)
    dextended = jnp.concatenate([dmixed, after], axis=0)
    dhidden = depthwise(dextended, conv_kernel, row_count, True).astype(jnp.bfloat16)

    def kernel_tap(tap_index):
        window = lax.dynamic_slice_in_dim(extended, edge_rows - tap_index, row_count, 0)
        return jnp.sum(dmixed * window, axis=0)

    kernel_part = lax.map(kernel_tap, jnp.arange(edge_rows + 1, dtype=jnp.int32))
    weight_part = jnp.einsum("ra,rd->ad", flat, dhidden, preferred_element_type=jnp.float32)
    dattended = jnp.einsum(
        "rd,ad->ra", dhidden, out_weight, preferred_element_type=jnp.float32
    ).astype(jnp.bfloat16)
    dout_heads = split_heads(dattended)
    deltas = jnp.einsum("rhe,rhe->hr", dout_heads, attended, preferred_element_type=jnp.float32)
    dquery_own, dkv_own = tile_grads(
        query_heads,
        dout_heads,
        log_sums,
        deltas,
        own_tile,
        own_pos,
        own_pos,
        always,
        left_span,
        score_scale,
    )
    zero_buffer = jnp.zeros((row_count, 2 * ATT), jnp.float32)

    def again_step(carry, offset):
        moving, buffer, dquery_sum = carry
        arrived = from_behind(moving, "blk", 1)
        carried = from_behind_2(buffer.astype(jnp.bfloat16), "blk", 1).astype(buffer.dtype)
        tile_pos, tile_usable = source(offset)
        dquery_part, dkv_part = tile_grads(
            query_heads,
            dout_heads,
            log_sums,
            deltas,
            arrived,
            own_pos,
            tile_pos,
            tile_usable,
            left_span,
            score_scale,
        )
        return ((arrived, carried + dkv_part, dquery_sum + dquery_part), None)

    (unused_moving, buffer, dquery_sum), unused = lax.scan(
        again_step, (own_tile, zero_buffer, dquery_own), offsets
    )
    dkv_total = dkv_own + from_behind_2(buffer.astype(jnp.bfloat16), "blk", -context).astype(
        buffer.dtype
    )
    weight_total, kernel_total = sum_weights(weight_part, kernel_part)
    query_grad = dquery_sum.reshape(row_count, ATT).astype(jnp.bfloat16)[None]
    key_grad = dkv_total[:, :ATT].astype(jnp.bfloat16)[None]
    value_grad = dkv_total[:, ATT:].astype(jnp.bfloat16)[None]
    return (out_frames, query_grad, key_grad, value_grad, weight_total, kernel_total)


def solution(mesh):
    return jax.shard_map(
        per_device,
        mesh=mesh,
        in_specs=(
            P("dp", "blk", None),
            P("dp", "blk", None),
            P("dp", "blk", None),
            P(),
            P(),
            P("dp", "blk", None),
        ),
        out_specs=(
            P("dp", "blk", None),
            P("dp", "blk", None),
            P("dp", "blk", None),
            P("dp", "blk", None),
            P(),
            P(),
        ),
        check_vma=False,
    )
```

profile of v0, /device:TPU:0, one launch (start us, length us, event | category | flops | bytes accessed | tf_op | source)
XLA Modules:
  0.0 446.8 jit_solution(2341774991487903538)
XLA Ops:
  13.3 33.5 %while.75 = (s32[]{:T(128)}, bf16[192,1024]{0,1:T(8,128)(2,1)S(1)}, f32[8,192]{1,0:T(8,128)S(1)}, f32[8,192]{1,0:T(8,128)S(1)}, f32[192,8,64]{0,2,1:T(8,128)S(1)...) while((s32[]{:T(128)}, bf16[192,1024]{0,1:T(8,128)(2,1)S(1)}, ...), condition=%wide.region_5.6_spmd.clone, body=%wide.region_2.5_spmd.clone.sunk | while | flops 78537600 | bytes 8309979 | solution.py:166
  13.3 4.9 %collective-permute-start = (bf16[192,1024]{0,1:T(8,128)(2,1)S(1)}, bf16[192,1024]{0,1:T(8,128)(2,1)S(1)}, u32[]{:S(2)}, u32[]{:S(2)}) collective-permute-start(bf16[192,1024]{0,1:T(8,128)(2,1)S(1)} %get-tuple-element.817), channel_id=1, source_target_pairs={{0,1},{1,2},{2,3},{3,4},{4,5},{5,6},{6,7},{8,9},{9,10},{10,11},{11... | collective-permute-start | bytes 1179656 | tf_op jit(solution)/shard_map/while/body/eval_jaxpr/ppermute | solution.py:20
  19.6 9.8 %collective-permute-done = bf16[192,1024]{0,1:T(8,128)(2,1)S(1)} collective-permute-done((bf16[192,1024]{0,1:T(8,128)(2,1)S(1)}, bf16[192,1024]{0,1:T(8,128)(2,1)S(1)}, u32[]{:S(2)}, u32[]{:S(2)}) %collective-permute-start) | collective-permute-done | bytes 393248 | tf_op jit(solution)/shard_map/while/body/eval_jaxpr/ppermute | solution.py:20
  30.7 4.4 collective-permute-start
  36.5 8.9 %collective-permute-done = bf16[192,1024]{0,1:T(8,128)(2,1)S(1)} collective-permute-done((bf16[192,1024]{0,1:T(8,128)(2,1)S(1)}, bf16[192,1024]{0,1:T(8,128)(2,1)S(1)}, u32[]{:S(2)}, u32[]{:S(2)}) %collective-permute-start) | collective-permute-done | bytes 393248 | tf_op jit(solution)/shard_map/while/body/eval_jaxpr/ppermute | solution.py:20
  47.3 4.4 collective-permute-start.3
  51.8 1.8 collective-permute-done.3
  54.7 36.2 %while.76 = (s32[]{:T(128)}, f32[192,1024]{1,0:T(8,128)S(1)}, f32[31,1024]{1,0:T(8,128)}, f32[222,1024]{1,0:T(8,128)S(1)}, s32[]{:T(128)}, /*index=5*/s32[]{:T(128)}, s32[]{:T(128)}, s32[]{:T(128)}) while((s32[]{:T(128)}, f32[192,1024]{1,0:T(8,128)S(1)}, f32[31,1024]{1,0:T(8,128)}, f32[222,1024]{1,0:T(8,128)S(1)}, s32[]{:T(128)}, ...), condition=%wide.region_7.8_spmd.clone, body=%wide.region_6.7_spmd.clone.sunk | while | flops 589831 | bytes 2371741 | solution.py:115
  91.8 2.3 fusion.34
  95.5 106.3 %while.74 = (s32[]{:T(128)}, f32[31,1024]{1,0:T(8,128)}, s32[31]{0:T(128)S(1)}, f32[222,1024]{1,0:T(8,128)S(1)}, f32[192,1024]{1,0:T(8,128)S(1)}, /*index=5*/s32[]{:T(128)}, s32[1]{0:T(128)}, s32[]{:T(128)}, s32[1]{0:T(128)}) while((s32[]{:T(128)}, f32[31,1024]{1,0:T(8,128)}, s32[31]{0:T(128)S(1)}, f32[222,1024]{1,0:T(8,128)S(1)}, ...), condition=%wide.region_15.16_spmd, body=%wide.region_13.15_spmd.sunk | while | flops 392198 | bytes 1585319 | solution.py:189
  97.5 1.4 dynamic_update_slice.8
  104.4 1.4 dynamic_update_slice.8
  107.8 1.4 dynamic_update_slice.8
  111.2 1.4 dynamic_update_slice.8
  118.1 1.4 dynamic_update_slice.8
  121.5 1.4 dynamic_update_slice.8
  124.9 1.4 dynamic_update_slice.8
  131.8 1.4 dynamic_update_slice.8
  135.2 1.4 dynamic_update_slice.8
  203.2 71.2 %while.77 = (s32[]{:T(128)}, f32[192,1024]{1,0:T(8,128)S(1)}, f32[31,1024]{1,0:T(8,128)}, f32[222,1024]{1,0:T(8,128)}, s32[]{:T(128)}, /*index=5*/s32[]{:T(128)}) while((s32[]{:T(128)}, f32[192,1024]{1,0:T(8,128)S(1)}, f32[31,1024]{1,0:T(8,128)}, f32[222,1024]{1,0:T(8,128)}, s32[]{:T(128)}, /*index=5*/s32[]{:T(128)}) %tuple.173), condition=%wide.region_9.10_spmd.clone, body=%wide.region_8.9_spmd.clone.sunk | while | flops 589827 | bytes 2371679 | solution.py:115
  204.0 1.5 select_add_fusion.5
  206.3 1.5 select_add_fusion.5
  208.6 1.5 select_add_fusion.5
  210.9 1.5 select_add_fusion.5
  213.2 1.5 select_add_fusion.5
  215.5 1.5 select_add_fusion.5
  217.8 1.5 select_add_fusion.5
  220.1 1.5 select_add_fusion.5
  222.4 1.5 select_add_fusion.5
  224.6 1.5 select_add_fusion.5
  226.9 1.5 select_add_fusion.5
  229.2 1.5 select_add_fusion.5
  231.5 1.5 select_add_fusion.5
  233.8 1.5 select_add_fusion.5
  236.1 1.5 select_add_fusion.5
  238.4 1.5 select_add_fusion.5
  240.7 1.5 select_add_fusion.5
  243.0 1.5 select_add_fusion.5
  245.3 1.5 select_add_fusion.5
  247.6 1.5 select_add_fusion.5
  249.9 1.5 select_add_fusion.5
  252.2 1.5 select_add_fusion.5
  254.5 1.5 select_add_fusion.5
  256.8 1.5 select_add_fusion.5
  259.1 1.5 select_add_fusion.5
  261.4 1.5 select_add_fusion.5
  263.7 1.5 select_add_fusion.5
  266.0 1.5 select_add_fusion.5
  268.3 1.5 select_add_fusion.5
  270.6 1.5 select_add_fusion.5
  272.9 1.5 select_add_fusion.5
  276.5 3.0 fusion.43
  284.2 66.7 %while.78 = (s32[]{:T(128)}, bf16[192,1024]{0,1:T(8,128)(2,1)}, bf16[192,1024]{0,1:T(8,128)(2,1)S(1)}, f32[192,8,64]{0,2,1:T(8,128)S(1)}, s32[2]{0:T(128)S(1)}, ...) while((s32[]{:T(128)}, bf16[192,1024]{0,1:T(8,128)(2,1)}, ...), condition=%wide.region_11.12_spmd.clone, body=%wide.region_10.11_spmd.clone.sunk | while | flops 192565632 | bytes 16997680 | solution.py:229
  285.1 3.9 collective-permute-start.2
  289.1 5.2 %collective-permute-start.1 = (bf16[192,1024]{0,1:T(8,128)(2,1)}, bf16[192,1024]{0,1:T(8,128)(2,1)S(1)}, u32[]{:S(2)}, u32[]{:S(2)}) collective-permute-start(bf16[192,1024]{0,1:T(8,128)(2,1)} %get-tuple-element.897), channel_id=1, source_target_pairs={{0,1},{1,2},{2,3},{3,4},{4,5},{5,6},{6,7},{8,9},{9,10},{10,11},{11... | collective-permute-start | bytes 1179656 | tf_op jit(solution)/shard_map/while/body/eval_jaxpr/ppermute | solution.py:20
  295.7 18.0 %collective-permute-done.1 = bf16[192,1024]{0,1:T(8,128)(2,1)S(1)} collective-permute-done((bf16[192,1024]{0,1:T(8,128)(2,1)}, bf16[192,1024]{0,1:T(8,128)(2,1)S(1)}, u32[]{:S(2)}, u32[]{:S(2)}) %collective-permute-start.1) | collective-permute-done | bytes 393248 | tf_op jit(solution)/shard_map/while/body/eval_jaxpr/ppermute | solution.py:20
  319.5 8.9 %collective-permute-start.2 = (bf16[192,1024]{0,1:T(8,128)(2,1)}, bf16[192,1024]{0,1:T(8,128)(2,1)S(1)}, u32[]{:S(2)}, u32[]{:S(2)}) collective-permute-start(bf16[192,1024]{0,1:T(8,128)(2,1)} %select_convert_fusion.2), channel_id=1, source_target_pairs={{0,1},{1,2},{2,3},{3,4},{4,5},{5,6},{6,7},{7,0},{8,9},{9,10},{10,1... | collective-permute-start | bytes 1179656 | tf_op jit(solution)/shard_map/while/body/eval_jaxpr/ppermute | solution.py:25
  328.4 5.2 %collective-permute-start.1 = (bf16[192,1024]{0,1:T(8,128)(2,1)}, bf16[192,1024]{0,1:T(8,128)(2,1)S(1)}, u32[]{:S(2)}, u32[]{:S(2)}) collective-permute-start(bf16[192,1024]{0,1:T(8,128)(2,1)} %get-tuple-element.897), channel_id=1, source_target_pairs={{0,1},{1,2},{2,3},{3,4},{4,5},{5,6},{6,7},{8,9},{9,10},{10,11},{11... | collective-permute-start | bytes 1179656 | tf_op jit(solution)/shard_map/while/body/eval_jaxpr/ppermute | solution.py:20
  335.0 11.1 %collective-permute-done.1 = bf16[192,1024]{0,1:T(8,128)(2,1)S(1)} collective-permute-done((bf16[192,1024]{0,1:T(8,128)(2,1)}, bf16[192,1024]{0,1:T(8,128)(2,1)S(1)}, u32[]{:S(2)}, u32[]{:S(2)}) %collective-permute-start.1) | collective-permute-done | bytes 393248 | tf_op jit(solution)/shard_map/while/body/eval_jaxpr/ppermute | solution.py:20
  351.9 8.8 %collective-permute-start.5 = (bf16[192,1024]{1,0:T(8,128)(2,1)}, bf16[192,1024]{1,0:T(8,128)(2,1)}, u32[]{:S(2)}, u32[]{:S(2)}) collective-permute-start(bf16[192,1024]{1,0:T(8,128)(2,1)} %copy.46), channel_id=1, source_target_pairs={{0,6},{1,7},{2,0},{3,1},{4,2},{5,3},{6,4},{7,5},{8,14},{9,15},{10,... | collective-permute-start | bytes 1179656 | tf_op jit(solution)/shard_map/ppermute | solution.py:25
  360.7 1.8 fusion.30
  364.8 1.4 collective-permute-done.5
  368.1 68.0 %all-reduce.3.cloned.1.call-done = (f32[512,1024]{1,0:T(8,128)}, f32[31,1024]{1,0:T(8,128)}) async-done(((f32[512,1024]{1,0:T(8,128)}, f32[31,1024]{1,0:T(8,128)}), (f32[512,1024]{1,0:T(8,128)}, f32[31,1024]{1,0:T(8,128)})) %all-reduce.3.cloned.1.call-update) | async-done | bytes 2224144 | tf_op jit(solution)/shard_map/psum | solution.py:119
  436.1 3.2 copy.111
  (312 shorter events, 153.1 us)
Async XLA Ops:
  7.2 39.7 %copy-start = (bf16[512,1024]{1,0:T(8,128)(2,1)S(1)}, bf16[512,1024]{1,0:T(8,128)(2,1)}, u32[]{:S(2)}) copy-start(bf16[512,1024]{1,0:T(8,128)(2,1)} %param.19) | copy-start | bytes 3145732
  7.2 428.9 %all-reduce.3.cloned.1.call-start = ((), (), s32[]{:S(2)}) async-start(), calls=%async_computation | async-start | bytes 4456448 | tf_op jit(solution)/shard_map/psum | solution.py:119
  8.5 2.8 copy-start.11
  10.9 0.8 copy-start.15
  11.7 1.1 copy-start.1
  12.0 1.3 copy-start.16
  13.3 16.0 %collective-permute-start = (bf16[192,1024]{0,1:T(8,128)(2,1)S(1)}, bf16[192,1024]{0,1:T(8,128)(2,1)S(1)}, u32[]{:S(2)}, u32[]{:S(2)}) collective-permute-start(bf16[192,1024]{0,1:T(8,128)(2,1)S(1)} %get-tuple-element.817), channel_id=1, source_target_pairs={{0,1},{1,2},{2,3},{3,4},{4,5},{5,6},{6,7},{8,9},{9,10},{10,11},{11... | collective-permute-start | bytes 1179656 | tf_op jit(solution)/shard_map/while/body/eval_jaxpr/ppermute | solution.py:20
  30.7 14.7 %collective-permute-start = (bf16[192,1024]{0,1:T(8,128)(2,1)S(1)}, bf16[192,1024]{0,1:T(8,128)(2,1)S(1)}, u32[]{:S(2)}, u32[]{:S(2)}) collective-permute-start(bf16[192,1024]{0,1:T(8,128)(2,1)S(1)} %get-tuple-element.817), channel_id=1, source_target_pairs={{0,1},{1,2},{2,3},{3,4},{4,5},{5,6},{6,7},{8,9},{9,10},{10,11},{11... | collective-permute-start | bytes 1179656 | tf_op jit(solution)/shard_map/while/body/eval_jaxpr/ppermute | solution.py:20
  46.8 5.0 %copy-start.5 = (f32[192,8,64]{0,2,1:T(8,128)}, f32[192,8,64]{0,2,1:T(8,128)S(1)}, u32[]{:S(2)}) copy-start(f32[192,8,64]{0,2,1:T(8,128)S(1)} %get-tuple-element.377) | copy-start | bytes 1179652
  46.8 4.9 %copy-start.13 = (bf16[192,8,64]{0,2,1:T(8,128)(2,1)}, bf16[192,8,64]{0,2,1:T(8,128)(2,1)S(1)}, u32[]{:S(2)}) copy-start(bf16[192,8,64]{0,2,1:T(8,128)(2,1)S(1)} %divide_convert_fusion) | copy-start | bytes 589828
  47.3 4.5 %copy-start.17 = (bf16[192,1024]{1,0:T(8,128)(2,1)}, bf16[192,1024]{1,0:T(8,128)(2,1)S(1)}, u32[]{:S(2)}) copy-start(bf16[192,1024]{1,0:T(8,128)(2,1)S(1)} %convolution_convert_fusion) | copy-start | bytes 1179652
  47.3 6.3 %collective-permute-start.3 = (bf16[30,1024]{1,0:T(8,128)(2,1)S(1)}, bf16[30,1024]{1,0:T(8,128)(2,1)S(1)}, u32[]{:S(2)}, u32[]{:S(2)}) collective-permute-start(bf16[30,1024]{1,0:T(8,128)(2,1)S(1)} %slice.40), channel_id=1, source_target_pairs={{0,1},{1,2},{2,3},{3,4},{4,5},{5,6},{6,7},{8,9},{9,10},{10,11},{11... | collective-permute-start | bytes 184328 | tf_op jit(solution)/shard_map/ppermute | solution.py:20
  90.9 0.9 copy-start.6
  94.2 107.6 %collective-permute-start.4 = (bf16[30,1024]{1,0:T(8,128)(2,1)S(1)}, bf16[30,1024]{1,0:T(8,128)(2,1)S(1)}, u32[]{:S(2)}, u32[]{:S(2)}) collective-permute-start(bf16[30,1024]{1,0:T(8,128)(2,1)S(1)} %slice.47), channel_id=1, source_target_pairs={{1,0},{2,1},{3,2},{4,3},{5,4},{6,5},{7,6},{9,8},{10,9},{11,10},{12... | collective-permute-start | bytes 184328 | tf_op jit(solution)/shard_map/ppermute | solution.py:20
  201.8 1.5 copy-start.3
  274.4 0.9 copy-start.4
  274.4 2.1 copy-start.14
  276.5 5.2 %copy-start.2 = (f32[8,192,192]{1,2,0:T(8,128)S(1)}, f32[8,192,192]{1,2,0:T(8,128)}, u32[]{:S(2)}) copy-start(f32[8,192,192]{1,2,0:T(8,128)} %copy-done.1) | copy-start | bytes 3538948
  281.7 1.5 copy-start.12
  282.3 0.9 copy-start.9
  283.2 1.0 copy-start.7
  285.1 31.4 %collective-permute-start.2 = (bf16[192,1024]{0,1:T(8,128)(2,1)}, bf16[192,1024]{0,1:T(8,128)(2,1)S(1)}, u32[]{:S(2)}, u32[]{:S(2)}) collective-permute-start(bf16[192,1024]{0,1:T(8,128)(2,1)} %select_convert_fusion.2), channel_id=1, source_target_pairs={{0,1},{1,2},{2,3},{3,4},{4,5},{5,6},{6,7},{7,0},{8,9},{9,10},{10,1... | collective-permute-start | bytes 1179656 | tf_op jit(solution)/shard_map/while/body/eval_jaxpr/ppermute | solution.py:25
  289.1 24.6 %collective-permute-start.1 = (bf16[192,1024]{0,1:T(8,128)(2,1)}, bf16[192,1024]{0,1:T(8,128)(2,1)S(1)}, u32[]{:S(2)}, u32[]{:S(2)}) collective-permute-start(bf16[192,1024]{0,1:T(8,128)(2,1)} %get-tuple-element.897), channel_id=1, source_target_pairs={{0,1},{1,2},{2,3},{3,4},{4,5},{5,6},{6,7},{8,9},{9,10},{10,11},{11... | collective-permute-start | bytes 1179656 | tf_op jit(solution)/shard_map/while/body/eval_jaxpr/ppermute | solution.py:20
  316.5 0.8 copy-start.8
  319.5 29.4 %collective-permute-start.2 = (bf16[192,1024]{0,1:T(8,128)(2,1)}, bf16[192,1024]{0,1:T(8,128)(2,1)S(1)}, u32[]{:S(2)}, u32[]{:S(2)}) collective-permute-start(bf16[192,1024]{0,1:T(8,128)(2,1)} %select_convert_fusion.2), channel_id=1, source_target_pairs={{0,1},{1,2},{2,3},{3,4},{4,5},{5,6},{6,7},{7,0},{8,9},{9,10},{10,1... | collective-permute-start | bytes 1179656 | tf_op jit(solution)/shard_map/while/body/eval_jaxpr/ppermute | solution.py:25
  328.4 17.7 %collective-permute-start.1 = (bf16[192,1024]{0,1:T(8,128)(2,1)}, bf16[192,1024]{0,1:T(8,128)(2,1)S(1)}, u32[]{:S(2)}, u32[]{:S(2)}) collective-permute-start(bf16[192,1024]{0,1:T(8,128)(2,1)} %get-tuple-element.897), channel_id=1, source_target_pairs={{0,1},{1,2},{2,3},{3,4},{4,5},{5,6},{6,7},{8,9},{9,10},{10,11},{11... | collective-permute-start | bytes 1179656 | tf_op jit(solution)/shard_map/while/body/eval_jaxpr/ppermute | solution.py:20
  348.9 0.8 copy-start.8
  351.9 11.6 %copy-start.10 = (bf16[8,192,192]{1,2,0:T(8,128)(2,1)S(1)}, bf16[8,192,192]{1,2,0:T(8,128)(2,1)}, u32[]{:S(2)}) copy-start(bf16[8,192,192]{1,2,0:T(8,128)(2,1)} %copy-done.9) | copy-start | bytes 1769476
  351.9 14.4 %collective-permute-start.5 = (bf16[192,1024]{1,0:T(8,128)(2,1)}, bf16[192,1024]{1,0:T(8,128)(2,1)}, u32[]{:S(2)}, u32[]{:S(2)}) collective-permute-start(bf16[192,1024]{1,0:T(8,128)(2,1)} %copy.46), channel_id=1, source_target_pairs={{0,6},{1,7},{2,0},{3,1},{4,2},{5,3},{6,4},{7,5},{8,14},{9,15},{10,... | collective-permute-start | bytes 1179656 | tf_op jit(solution)/shard_map/ppermute | solution.py:25
  363.8 2.5 copy-start.18
  436.1 3.2 copy-start.19
Sparse Core Ops, SparseCore 0:
  283.6 152.4 all-reduce.2
where the time goes:
time: 456 us; the launch traced here: 447 us
  local copies, waits for them, and re-layouts  132 us (29%)
  waiting for transfers between devices  119 us (26%)
  other arithmetic  75.3 us (17%)
  starting transfers between devices  47.1 us (10%)
  loops' own time  44.8 us (10%)
  between operations  14.5 us (3%)
  matrix products  14.2 us (3%)
    psum x1, waiting for transfers between devices, sum_weights(): return lax.psum((weight_part, kernel_part), ('dp', 'blk'))  68 us
    add x62, other arithmetic, add_tap(): running + conv_kernel[tap_index] * lax.dynamic_slice_in_dim(extended, fir...  58.3 us
    ppermute x6, waiting for transfers between devices, from_behind(): return lax.ppermute(block, axis, route)  49.6 us
    dynamic_slice x62, local copies, waits for them, and re-layouts, add_tap(): conv_kernel[tap_index]  47.7 us
    dynamic_update_slice x31, local copies, waits for them, and re-layouts, per_device(): lax.map(kernel_tap, jnp.arange(edge_rows + 1, dtype=jnp.int32))  43.4 us
    another operation x1, loops' own time, per_device(): lax.map(kernel_tap, jnp.arange(edge_rows + 1, dtype=jnp.int32))  40.4 us
    ppermute x6, starting transfers between devices, from_behind(): return lax.ppermute(block, axis, route)  25.4 us
    ppermute x3, starting transfers between devices, from_behind_2(): return lax.ppermute(x, axis, [(i, (i + by) % size) for i in range(size)])  21.7 us
  transfers between devices with their start and end apart: 10, of which 7 were waited for; matrix products, arithmetic and copies ran while one was open for 19% of the time, Pallas kernels for 0%

commit v1 on v0

v1 whole, which is shorter than its diff:
```python
import functools
import math

import jax
import jax.numpy as jnp
from jax import lax
from jax.experimental import pallas as pl
from jax.experimental.pallas import tpu as pltpu
from jax.sharding import PartitionSpec as P

HEAD_DIM = 64
CTX_MAX = 3
LANES = 128
NEGATIVE = -1e30
VMEM_LIMIT = 40 * 1024 * 1024

NN = (((1,), (0,)), ((), ()))
NT = (((1,), (1,)), ((), ()))
TN = (((0,), (0,)), ((), ()))


def dot(a, b, dims, precision=None):
    return lax.dot_general(a, b, dims, precision=precision, preferred_element_type=jnp.float32)


def shifted(x, by):
    devices = range(lax.axis_size("blk"))
    return lax.ppermute(x, "blk", [(i, i + by) for i in devices if i + by in devices])


def head_masks():
    lane = lax.broadcasted_iota(jnp.int32, (1, LANES), 1)
    first = jnp.where(lane < HEAD_DIM, 1.0, 0.0)
    return first.astype(jnp.bfloat16), (1.0 - first).astype(jnp.bfloat16)


def stack_heads(pair):
    first, second = head_masks()
    return jnp.concatenate([pair * first, pair * second], axis=0)


def merge_heads(stacked):
    rows = stacked.shape[0] // 2
    lane = lax.broadcasted_iota(jnp.int32, (rows, LANES), 1)
    return jnp.where(lane < HEAD_DIM, stacked[:rows], stacked[rows:])


def forward_kernel(context, rows, edge, taps, *refs):
    tiles = context + 1
    device_ref, q_ref, q_tail_ref = refs[:3]
    k_refs = refs[3 : 3 + tiles]
    v_refs = refs[3 + tiles : 3 + 2 * tiles]
    far_ref, near_ref, w_ref, conv_ref, cot_ref = refs[3 + 2 * tiles : 8 + 2 * tiles]
    out_ref, att_ref, lse_ref, dhid_ref, wpart_ref, kpart_ref = refs[8 + 2 * tiles : 14 + 2 * tiles]
    qx, kx, vx, ax, lx, hid, cotx, dm, bias = refs[14 + 2 * tiles :]

    att = q_ref.shape[1]
    width = w_ref.shape[1]
    span = context * rows
    query_rows = rows + 2 * edge
    block = LANES
    keys = span + block
    scale = 1.0 / math.sqrt(HEAD_DIM)
    start = device_ref[0] * rows

    qx[:edge] = q_tail_ref[...] * scale
    qx[edge : edge + rows] = q_ref[...] * scale
    qx[edge + rows :] = near_ref[2 * edge : 3 * edge] * scale
    for ext, own, far_at, near_at in ((kx, k_refs, 0, 0), (vx, v_refs, edge, edge)):
        ext[:edge] = far_ref[far_at : far_at + edge]
        for offset in range(tiles):
            first = edge + (context - offset) * rows
            ext[first : first + rows] = own[offset][...]
        ext[edge + span + rows :] = near_ref[near_at : near_at + edge]
    for chunk in range(width // LANES):
        columns = slice(chunk * LANES, (chunk + 1) * LANES)
        cotx[chunk, :rows] = cot_ref[:, columns].astype(jnp.float32)
        part, lane = divmod(chunk * LANES, att)
        cotx[chunk, rows:] = near_ref[
            (3 + part) * edge : (4 + part) * edge, lane : lane + LANES
        ].astype(jnp.float32)

    lane_id = lax.broadcasted_iota(jnp.int32, (block, LANES), 1)
    for b in range(query_rows // block):
        row_id = lax.broadcasted_iota(jnp.int32, (block, keys), 0)
        key_id = lax.broadcasted_iota(jnp.int32, (block, keys), 1)
        distance = row_id - key_id + span
        key_time = key_id + (start - edge - span + b * block)
        visible = (distance >= 0) & (distance < span) & (key_time >= 0)
        bias[...] = jnp.where(visible, 0.0, NEGATIVE)
        log_sums = jnp.zeros((block, LANES), jnp.float32)
        for pair in range(att // LANES):
            columns = slice(pair * LANES, (pair + 1) * LANES)
            qs = stack_heads(qx[b * block : (b + 1) * block, columns])
            kp = kx[b * block : b * block + keys, columns]
            vp = vx[b * block : b * block + keys, columns]
            scores = dot(qs, kp, NT)
            hidden_pairs = bias[...]
            scores = scores + jnp.concatenate([hidden_pairs, hidden_pairs], axis=0)
            row_max = jnp.max(scores, axis=1, keepdims=True)
            weights = jnp.exp(scores - row_max)
            row_sum = jnp.sum(weights, axis=1, keepdims=True)
            mixed = dot(weights.astype(jnp.bfloat16), vp, NN) / row_sum
            ax[b * block : (b + 1) * block, columns] = merge_heads(mixed).astype(jnp.bfloat16)
            log_sum = row_max + jnp.log(row_sum)
            log_sums = jnp.where(lane_id == 2 * pair, log_sum[:block], log_sums)
            log_sums = jnp.where(lane_id == 2 * pair + 1, log_sum[block:], log_sums)
        lx[b * block : (b + 1) * block] = log_sums
    att_ref[...] = ax[edge : edge + rows]
    lse_ref[...] = jnp.transpose(lx[...])[: lse_ref.shape[0], edge : edge + rows]

    step = 2 * LANES
    for part in range(width // step):
        product = dot(ax[...], w_ref[:, part * step : (part + 1) * step], NN)
        product = product.astype(jnp.bfloat16).astype(jnp.float32)
        time = lax.broadcasted_iota(jnp.int32, product.shape, 0) + (start - edge)
        product = jnp.where(time >= 0, product, 0.0)
        hid[2 * part] = product[:, :LANES]
        hid[2 * part + 1] = product[:, LANES:]

    def convolve(chunk, carry):
        columns = pl.ds(pl.multiple_of(chunk * LANES, LANES), LANES)
        mixed = jnp.zeros((rows + edge, LANES), jnp.float32)
        for tap in range(taps):
            mixed += conv_ref[tap : tap + 1, columns] * hid[chunk, edge - tap : 2 * edge + rows - tap]
        sigma = jax.nn.sigmoid(mixed)
        out_ref[:, columns] = (mixed * sigma)[:rows].astype(jnp.bfloat16)
        dm[...] = cotx[chunk] * sigma * (1.0 + mixed * (1.0 - sigma))
        dhidden = jnp.zeros((rows, LANES), jnp.float32)
        for tap in range(taps):
            dhidden += conv_ref[tap : tap + 1, columns] * dm[tap : tap + rows]
        dhid_ref[:, columns] = dhidden.astype(jnp.bfloat16)
        own = dm[:rows]
        for tap in range(taps):
            product = own * hid[chunk, edge - tap : edge + rows - tap]
            kpart_ref[tap : tap + 1, columns] = jnp.sum(product, axis=0, keepdims=True)
        return carry

    lax.fori_loop(0, width // LANES, convolve, 0)
    own = ax[edge : edge + rows]
    for part in range(width // step):
        columns = slice(part * step, (part + 1) * step)
        wpart_ref[:, columns] = dot(own, dhid_ref[:, columns], TN).astype(wpart_ref.dtype)


def backward_kernel(context, rows, *refs):
    tiles = context + 1
    device_ref, q_ref = refs[:2]
    k_refs = refs[2 : 2 + tiles]
    v_refs = refs[2 + tiles : 2 + 2 * tiles]
    att_ref, lse_ref, dhid_ref, w_ref = refs[2 + 2 * tiles : 6 + 2 * tiles]
    dq_ref, dk_ref, dv_ref = refs[6 + 2 * tiles : 9 + 2 * tiles]
    message_refs = refs[9 + 2 * tiles : 9 + 2 * tiles + context]
    datt, bias = refs[9 + 2 * tiles + context :]

    att = q_ref.shape[1]
    heads = att // HEAD_DIM
    span = context * rows
    scale = 1.0 / math.sqrt(HEAD_DIM)
    start = device_ref[0] * rows

    dattended = dot(dhid_ref[...], w_ref[...], NT).astype(jnp.bfloat16)
    datt[...] = dattended
    product = dattended.astype(jnp.float32) * att_ref[...].astype(jnp.float32)
    head_id = lax.broadcasted_iota(jnp.int32, (heads, att), 0)
    feature_id = lax.broadcasted_iota(jnp.int32, (heads, att), 1)
    ours = (feature_id >= head_id * HEAD_DIM) & (feature_id < (head_id + 1) * HEAD_DIM)
    deltas = dot(jnp.where(ours, 1.0, 0.0), product, NT, lax.Precision.HIGHEST)

    for offset in range(tiles):
        key_id = lax.broadcasted_iota(jnp.int32, (rows, rows), 0)
        row_id = lax.broadcasted_iota(jnp.int32, (rows, rows), 1)
        distance = row_id - key_id + offset * rows
        key_time = key_id + (start - offset * rows)
        visible = (distance >= 0) & (distance < span) & (key_time >= 0)
        bias[offset] = jnp.where(visible, 0.0, NEGATIVE)

    for pair in range(att // LANES):
        columns = slice(pair * LANES, (pair + 1) * LANES)
        qs = stack_heads(q_ref[:, columns] * scale)
        ds = stack_heads(datt[:, columns])
        log_sum = [lse_ref[2 * pair + i : 2 * pair + i + 1] for i in (0, 1)]
        delta = [deltas[2 * pair + i : 2 * pair + i + 1] for i in (0, 1)]
        log_sum = jnp.concatenate(log_sum, axis=1)
        delta = jnp.concatenate(delta, axis=1)
        dquery = jnp.zeros((2 * rows, LANES), jnp.float32)
        for offset in range(tiles):
            kp = k_refs[offset][:, columns]
            vp = v_refs[offset][:, columns]
            hidden_pairs = jnp.concatenate([bias[offset], bias[offset]], axis=1)
            probs = jnp.exp(dot(kp, qs, NT) + hidden_pairs - log_sum)
            dprobs = dot(vp, ds, NT)
            dscores = (probs * (dprobs - delta)).astype(jnp.bfloat16)
            dvalue = dot(probs.astype(jnp.bfloat16), ds, NN)
            dkey = dot(dscores, qs, NN)
            dquery += dot(dscores, kp, TN)
            if offset == 0:
                dk_ref[:, columns] = dkey
                dv_ref[:, columns] = dvalue
            else:
                message_refs[offset - 1][:rows, columns] = dkey.astype(jnp.bfloat16)
                message_refs[offset - 1][rows:, columns] = dvalue.astype(jnp.bfloat16)
        dq_ref[:, columns] = (merge_heads(dquery) * scale).astype(jnp.bfloat16)


def sum_weights(weight_part, kernel_part):
    weight = lax.psum(weight_part, ("dp", "blk"))
    kernel = lax.psum(kernel_part, ("dp", "blk"))
    return weight.astype(jnp.float32), kernel


def per_device(queries, key_in, value_in, out_weight, conv_kernel, cotangent):
    bf16, f32 = jnp.bfloat16, jnp.float32
    query, key, value, cot = queries[0], key_in[0], value_in[0], cotangent[0]
    runs = lax.axis_size("blk")
    device = lax.axis_index("blk").astype(jnp.int32)[None]
    rows, att = query.shape
    width = out_weight.shape[1]
    heads = att // HEAD_DIM
    taps = conv_kernel.shape[0]
    edge = -(-(taps - 1) // 16) * 16
    context = min(CTX_MAX, runs // 4)

    keys = [key] + [shifted(key, o) for o in range(1, context + 1)]
    values = [value] + [shifted(value, o) for o in range(1, context + 1)]
    query_tail = shifted(query[-edge:], 1)
    far = shifted(jnp.concatenate([key[-edge:], value[-edge:]]), context + 1)
    pieces = [key, value, query] + [cot[:, i : i + att] for i in range(0, width, att)]
    near = shifted(jnp.concatenate([piece[:edge] for piece in pieces]), -1)

    query_rows = rows + 2 * edge
    key_rows = query_rows + context * rows
    vmem = pl.BlockSpec(memory_space=pltpu.VMEM)
    smem = pl.BlockSpec(memory_space=pltpu.SMEM)
    params = pltpu.CompilerParams(vmem_limit_bytes=VMEM_LIMIT)
    out_frames, attended, log_sums, dhidden, weight_part, kernel_part = pl.pallas_call(
        functools.partial(forward_kernel, context, rows, edge, taps),
        out_shape=(
            jax.ShapeDtypeStruct((rows, width), bf16),
            jax.ShapeDtypeStruct((rows, att), bf16),
            jax.ShapeDtypeStruct((heads, rows), f32),
            jax.ShapeDtypeStruct((rows, width), bf16),
            jax.ShapeDtypeStruct((att, width), bf16),
            jax.ShapeDtypeStruct((taps, width), f32),
        ),
        in_specs=[smem] + [vmem] * (7 + 2 * (context + 1)),
        out_specs=(vmem,) * 6,
        scratch_shapes=[
            pltpu.VMEM((query_rows, att), bf16),
            pltpu.VMEM((key_rows, att), bf16),
            pltpu.VMEM((key_rows, att), bf16),
            pltpu.VMEM((query_rows, att), bf16),
            pltpu.VMEM((query_rows, LANES), f32),
            pltpu.VMEM((width // LANES, query_rows, LANES), f32),
            pltpu.VMEM((width // LANES, rows + edge, LANES), f32),
            pltpu.VMEM((rows + edge, LANES), f32),
            pltpu.VMEM((LANES, context * rows + LANES), f32),
        ],
        compiler_params=params,
        name="forward",
    )(device, query, query_tail, *keys, *values, far, near, out_weight, conv_kernel, cot)

    weight_total, kernel_total = sum_weights(weight_part, kernel_part)

    outs = pl.pallas_call(
        functools.partial(backward_kernel, context, rows),
        out_shape=(
            jax.ShapeDtypeStruct((rows, att), bf16),
            jax.ShapeDtypeStruct((rows, att), f32),
            jax.ShapeDtypeStruct((rows, att), f32),
        )
        + (jax.ShapeDtypeStruct((2 * rows, att), bf16),) * context,
        in_specs=[smem] + [vmem] * (5 + 2 * (context + 1)),
        out_specs=(vmem,) * (3 + context),
        scratch_shapes=[
            pltpu.VMEM((rows, att), bf16),
            pltpu.VMEM((context + 1, rows, rows), f32),
        ],
        compiler_params=params,
        name="backward",
    )(device, query, *keys, *values, attended, log_sums, dhidden, out_weight)
    query_grad, dkey, dvalue = outs[:3]
    for offset, message in enumerate(outs[3:], 1):
        arrived = shifted(message, -offset).astype(f32)
        dkey = dkey + arrived[:rows]
        dvalue = dvalue + arrived[rows:]
    key_grad = dkey.astype(bf16)
    value_grad = dvalue.astype(bf16)
    return (
        out_frames[None],
        query_grad[None],
        key_grad[None],
        value_grad[None],
        weight_total,
        kernel_total,
    )


def solution(mesh):
    frames = P("dp", "blk", None)
    return jax.shard_map(
        per_device,
        mesh=mesh,
        in_specs=(frames, frames, frames, P(), P(), frames),
        out_specs=(frames, frames, frames, frames, P(), P()),
        check_vma=False,
    )
```

time: 456 us -> 333 us (0.73); the launches traced: 447 us -> 332 us
  waiting for transfers between devices: 119 us -> 258 us
  local copies, waits for them, and re-layouts: 132 us -> 14.3 us
  other arithmetic: 75.3 us -> 3.9 us
  loops' own time: 44.8 us -> 0 us
  starting transfers between devices: 47.1 us -> 25.7 us
  Pallas kernels: 0 us -> 15.8 us
  matrix products: 14.2 us -> 0 us
    psum x1 -> x2, waiting for transfers between devices: 68 us -> 226 us  [the longest x1 126 us: sum_weights(): kernel = lax.psum(kernel_part, ('dp', 'blk'))]
    dynamic_slice x97 -> x0, local copies, waits for them, and re-layouts: 68.1 us -> none  [the longest x62 47.7 us: add_tap(): conv_kernel[tap_index]]
    add x75 -> x0, other arithmetic: 60.7 us -> none  [the longest x62 58.3 us: add_tap(): running + conv_kernel[tap_index] * lax.dynamic_slice_in_dim(extended, fir...]
    another operation x5 -> x0, loops' own time: 44.8 us -> none  [the longest x1 40.4 us: per_device(): lax.map(kernel_tap, jnp.arange(edge_rows + 1, dtype=jnp.int32))]
    dynamic_update_slice x31 -> x0, local copies, waits for them, and re-layouts: 43.4 us -> none  [per_device(): lax.map(kernel_tap, jnp.arange(edge_rows + 1, dtype=jnp.int32))]
    ppermute x9, starting transfers between devices: 47 us -> 25.7 us  [shifted(): lax.ppermute(x, 'blk', [(i, i + by) for i in devices if i + by in devices])]
    ppermute x9, waiting for transfers between devices: 51 us -> 31.5 us  [shifted(): lax.ppermute(x, 'blk', [(i, i + by) for i in devices if i + by in devices])]
    pallas_call x0 -> x2, Pallas kernels: none -> 15.8 us  [the longest x1 10.3 us: per_device(): pl.pallas_call(functools.partial(forward_kernel, context, rows, edge, tap...]
  transfers between devices with their start and end apart: 10 -> 11, of which waited for: 7 -> 6; matrix products, arithmetic and copies ran while one was open for 19% -> 3% of each run, Pallas kernels for 0% -> 2%
where the time goes in v1:
time: 333 us; the launch traced here: 332 us
  waiting for transfers between devices  258 us (77%)
  starting transfers between devices  25.7 us (8%)
  Pallas kernels  15.8 us (5%)
  local copies, waits for them, and re-layouts  14.3 us (4%)
  between operations  14.2 us (4%)
  other arithmetic  3.9 us (1%)
    psum x1, waiting for transfers between devices, sum_weights(): kernel = lax.psum(kernel_part, ('dp', 'blk'))  126 us
    psum x1, waiting for transfers between devices, sum_weights(): weight = lax.psum(weight_part, ('dp', 'blk'))  100 us
    ppermute x9, waiting for transfers between devices, shifted(): lax.ppermute(x, 'blk', [(i, i + by) for i in devices if i + by in devices])  31.5 us
    ppermute x9, starting transfers between devices, shifted(): lax.ppermute(x, 'blk', [(i, i + by) for i in devices if i + by in devices])  25.7 us
    unnamed x29, local copies, waits for them, and re-layouts  11.3 us
    pallas_call x1, Pallas kernels, per_device(): pl.pallas_call(functools.partial(forward_kernel, context, rows, edge, tap...  10.3 us
  transfers between devices with their start and end apart: 11, of which 6 were waited for; matrix products, arithmetic and copies ran while one was open for 3% of the time, Pallas kernels for 2%

profile of v1, /device:TPU:0, one launch (start us, length us, event | category | flops | bytes accessed | tf_op | source)
XLA Modules:
  0.0 331.5 jit_solution(17393253005004971089)
XLA Ops:
  7.2 0.0 all-reduce.3.cloned.1.call-start
  7.2 4.9 %collective-permute-start.2 = (bf16[192,512]{1,0:T(8,128)(2,1)}, bf16[192,512]{1,0:T(8,128)(2,1)S(1)}, u32[]{:S(2)}, u32[]{:S(2)}) collective-permute-start(bf16[192,512]{1,0:T(8,128)(2,1)} %bitcast.25), channel_id=1, source_target_pairs={{0,2},{1,3},{2,4},{3,5},{4,6},{5,7},{8,10},{9,11},{10,12},{11,13},... | collective-permute-start | bytes 589832 | tf_op jit(solution)/shard_map/ppermute | solution.py:28
  12.2 3.4 %collective-permute-start.1 = (bf16[192,512]{1,0:T(8,128)(2,1)}, bf16[192,512]{1,0:T(8,128)(2,1)S(1)}, u32[]{:S(2)}, u32[]{:S(2)}) collective-permute-start(bf16[192,512]{1,0:T(8,128)(2,1)} %bitcast.26), channel_id=1, source_target_pairs={{0,1},{1,2},{2,3},{3,4},{4,5},{5,6},{6,7},{8,9},{9,10},{10,11},{11... | collective-permute-start | bytes 589832 | tf_op jit(solution)/shard_map/ppermute | solution.py:28
  15.6 3.5 %collective-permute-start.4 = (bf16[192,512]{1,0:T(8,128)(2,1)}, bf16[192,512]{1,0:T(8,128)(2,1)S(1)}, u32[]{:S(2)}, u32[]{:S(2)}) collective-permute-start(bf16[192,512]{1,0:T(8,128)(2,1)} %bitcast.29), channel_id=1, source_target_pairs={{0,2},{1,3},{2,4},{3,5},{4,6},{5,7},{8,10},{9,11},{10,12},{11,13},... | collective-permute-start | bytes 589832 | tf_op jit(solution)/shard_map/ppermute | solution.py:28
  19.1 3.4 %collective-permute-start.3 = (bf16[192,512]{1,0:T(8,128)(2,1)}, bf16[192,512]{1,0:T(8,128)(2,1)S(1)}, u32[]{:S(2)}, u32[]{:S(2)}) collective-permute-start(bf16[192,512]{1,0:T(8,128)(2,1)} %bitcast.30), channel_id=1, source_target_pairs={{0,1},{1,2},{2,3},{3,4},{4,5},{5,6},{6,7},{8,9},{9,10},{10,11},{11... | collective-permute-start | bytes 589832 | tf_op jit(solution)/shard_map/ppermute | solution.py:28
  22.5 0.8 slice_bitcast_fusion.2
  23.3 3.4 %collective-permute-start = (bf16[32,512]{1,0:T(8,128)(2,1)S(1)}, bf16[32,512]{1,0:T(8,128)(2,1)S(1)}, u32[]{:S(2)}, u32[]{:S(2)}) collective-permute-start(bf16[32,512]{1,0:T(8,128)(2,1)S(1)} %slice_bitcast_fusion.2), channel_id=1, source_target_pairs={{0,1},{1,2},{2,3},{3,4},{4,5},{5,6},{6,7},{8,9},{9,10},{10,11},{11... | collective-permute-start | bytes 98312 | tf_op jit(solution)/shard_map/ppermute | solution.py:28
  26.7 0.8 slice_bitcast_fusion.1
  27.5 0.8 slice_bitcast_fusion
  28.2 0.8 bitcast_dynamic-update-slice_fusion.2
  29.0 0.8 bitcast_dynamic-update-slice_fusion.1
  29.8 0.8 bitcast_dynamic-update-slice_fusion
  30.5 0.8 slice_dynamic-update-slice_fusion.1
  31.3 0.0 collective-permute-done.refs_2_
  31.3 3.0 collective-permute-start.5
  34.3 0.8 slice_dynamic-update-slice_fusion
  35.0 1.1 collective-permute-done.5.refs_9_
  36.2 1.3 collective-permute-start.6
  37.5 7.3 %collective-permute-done.6.refs_10_ = bf16[160,512]{1,0:T(8,128)(2,1)S(1)} collective-permute-done((bf16[160,512]{1,0:T(8,128)(2,1)S(1)}, bf16[160,512]{1,0:T(8,128)(2,1)S(1)}, u32[]{:S(2)}, u32[]{:S(2)}) %collective-permute-start.6) | collective-permute-done | bytes 163872 | tf_op jit(solution)/shard_map/ppermute | solution.py:28
  44.7 0.0 collective-permute-done.2.refs_5_.refs_4_
  44.7 0.0 collective-permute-done.1.refs_4_.refs_3_
  44.7 0.0 collective-permute-done.4.refs_8_.refs_7_
  44.7 0.0 collective-permute-done.3.refs_7_.refs_6_
  44.8 0.0 copy-start
  44.8 1.2 copy-done
  46.0 0.0 copy-start.2
  46.0 0.9 copy-done.2
  46.9 0.0 copy-start.4
  46.9 0.9 copy-done.4
  47.8 0.0 copy-start.6
  47.8 0.9 copy-done.6
  48.8 0.0 copy-start.8
  48.8 1.0 copy-done.8
  49.8 0.0 copy-start.11
  49.8 0.9 copy-done.11
  50.7 0.0 copy-start.1
  50.7 0.0 copy-start.3
  50.7 0.0 copy-start.5
  50.7 0.0 copy-start.7
  50.7 10.3 %forward.1 = (bf16[192,1024]{1,0:T(8,128)(2,1)}, bf16[192,512]{1,0:T(8,128)(2,1)S(1)}, f32[8,192]{1,0:T(8,128)S(1)}, bf16[192,1024]{1,0:T(8,128)(2,1)S(1)}, bf16...) custom-call(s32[1]{0:T(128)} %bitcast.refs_0_, bf16[192,512]{1,0:T(8,128)(2,1)S(1)} %bitcast.23, ...), custom_call_target="tpu_custom_call" | custom-call | tf_op jit(solution)/shard_map/forward/pallas_call | solution.py:236
  61.0 0.0 all-reduce.3.cloned.1.call-update
  61.0 0.0 all-reduce.5.cloned.1.call-start
  61.1 0.0 copy-done.1
  61.1 0.0 copy-done.3
  61.1 0.0 copy-done.5
  61.1 0.0 copy-done.7
  61.1 5.5 %backward.1 = (bf16[192,512]{1,0:T(8,128)(2,1)}, f32[192,512]{1,0:T(8,128)S(1)}, f32[192,512]{1,0:T(8,128)S(1)}, bf16[384,512]{1,0:T(8,128)(2,1)}, bf16[384,512]{1,0:T(8,128)(2,1)}) custom-call(s32[1]{0:T(128)} %bitcast.refs_0_, bf16[192,512]{1,0:T(8,128)(2,1)S(1)} %bitcast.24, bf16[192,512]{1,0:T(8,128)(2,1)S(1)} %bitcast.28, ...), custom_call_target="tpu_custom_call" | custom-call | tf_op jit(solution)/shard_map/backward/pallas_call | solution.py:265
  66.6 0.0 copy-start.9
  66.6 0.8 copy-done.9
  67.3 0.0 copy-start.10
  67.3 1.4 collective-permute-start.7
  68.8 1.3 collective-permute-start.8
  70.1 0.0 all-reduce.5.cloned.1.call-update
  70.1 10.3 %collective-permute-done.7 = bf16[384,512]{1,0:T(8,128)(2,1)S(1)} collective-permute-done((bf16[384,512]{1,0:T(8,128)(2,1)}, bf16[384,512]{1,0:T(8,128)(2,1)S(1)}, u32[]{:S(2)}, u32[]{:S(2)}) %collective-permute-start.7) | collective-permute-done | bytes 393248 | tf_op jit(solution)/shard_map/ppermute | solution.py:28
  80.4 0.1 convert_element_type.15
  80.5 12.8 %collective-permute-done.8 = bf16[384,512]{1,0:T(8,128)(2,1)S(1)} collective-permute-done((bf16[384,512]{1,0:T(8,128)(2,1)}, bf16[384,512]{1,0:T(8,128)(2,1)S(1)}, u32[]{:S(2)}, u32[]{:S(2)}) %collective-permute-start.8) | collective-permute-done | bytes 393248 | tf_op jit(solution)/shard_map/ppermute | solution.py:28
  93.3 0.1 convert_element_type.16
  93.4 0.0 copy-done.10
  93.4 0.9 fusion.3
  94.4 100.3 %all-reduce.3.cloned.1.call-done = bf16[512,1024]{1,0:T(8,128)(2,1)} async-done(((bf16[512,1024]{1,0:T(8,128)(2,1)}), bf16[512,1024]{1,0:T(8,128)(2,1)}) %all-reduce.3.cloned.1.call-update) | async-done | bytes 1048592 | tf_op jit(solution)/shard_map/psum | solution.py:207
  194.7 2.8 convert_element_type.19
  197.5 125.6 %all-reduce.5.cloned.1.call-done = f32[31,1024]{1,0:T(8,128)} async-done(((f32[31,1024]{1,0:T(8,128)}), f32[31,1024]{1,0:T(8,128)}) %all-reduce.5.cloned.1.call-update) | async-done | bytes 126992 | tf_op jit(solution)/shard_map/psum | solution.py:208
  323.1 1.6 copy.18
  (1 shorter events, 0.0 us)
Async XLA Ops:
  7.2 187.5 %all-reduce.3.cloned.1.call-start = ((), (), s32[]{:S(2)}) async-start(), calls=%async_computation | async-start | bytes 2097152 | tf_op jit(solution)/shard_map/psum | solution.py:207
  7.2 37.5 %collective-permute-start.2 = (bf16[192,512]{1,0:T(8,128)(2,1)}, bf16[192,512]{1,0:T(8,128)(2,1)S(1)}, u32[]{:S(2)}, u32[]{:S(2)}) collective-permute-start(bf16[192,512]{1,0:T(8,128)(2,1)} %bitcast.25), channel_id=1, source_target_pairs={{0,2},{1,3},{2,4},{3,5},{4,6},{5,7},{8,10},{9,11},{10,12},{11,13},... | collective-permute-start | bytes 589832 | tf_op jit(solution)/shard_map/ppermute | solution.py:28
  12.2 32.6 %collective-permute-start.1 = (bf16[192,512]{1,0:T(8,128)(2,1)}, bf16[192,512]{1,0:T(8,128)(2,1)S(1)}, u32[]{:S(2)}, u32[]{:S(2)}) collective-permute-start(bf16[192,512]{1,0:T(8,128)(2,1)} %bitcast.26), channel_id=1, source_target_pairs={{0,1},{1,2},{2,3},{3,4},{4,5},{5,6},{6,7},{8,9},{9,10},{10,11},{11... | collective-permute-start | bytes 589832 | tf_op jit(solution)/shard_map/ppermute | solution.py:28
  15.6 29.1 %collective-permute-start.4 = (bf16[192,512]{1,0:T(8,128)(2,1)}, bf16[192,512]{1,0:T(8,128)(2,1)S(1)}, u32[]{:S(2)}, u32[]{:S(2)}) collective-permute-start(bf16[192,512]{1,0:T(8,128)(2,1)} %bitcast.29), channel_id=1, source_target_pairs={{0,2},{1,3},{2,4},{3,5},{4,6},{5,7},{8,10},{9,11},{10,12},{11,13},... | collective-permute-start | bytes 589832 | tf_op jit(solution)/shard_map/ppermute | solution.py:28
  19.1 25.7 %collective-permute-start.3 = (bf16[192,512]{1,0:T(8,128)(2,1)}, bf16[192,512]{1,0:T(8,128)(2,1)S(1)}, u32[]{:S(2)}, u32[]{:S(2)}) collective-permute-start(bf16[192,512]{1,0:T(8,128)(2,1)} %bitcast.30), channel_id=1, source_target_pairs={{0,1},{1,2},{2,3},{3,4},{4,5},{5,6},{6,7},{8,9},{9,10},{10,11},{11... | collective-permute-start | bytes 589832 | tf_op jit(solution)/shard_map/ppermute | solution.py:28
  23.3 8.0 %collective-permute-start = (bf16[32,512]{1,0:T(8,128)(2,1)S(1)}, bf16[32,512]{1,0:T(8,128)(2,1)S(1)}, u32[]{:S(2)}, u32[]{:S(2)}) collective-permute-start(bf16[32,512]{1,0:T(8,128)(2,1)S(1)} %slice_bitcast_fusion.2), channel_id=1, source_target_pairs={{0,1},{1,2},{2,3},{3,4},{4,5},{5,6},{6,7},{8,9},{9,10},{10,11},{11... | collective-permute-start | bytes 98312 | tf_op jit(solution)/shard_map/ppermute | solution.py:28
  31.3 4.9 %collective-permute-start.5 = (bf16[64,512]{1,0:T(8,128)(2,1)S(1)}, bf16[64,512]{1,0:T(8,128)(2,1)S(1)}, u32[]{:S(2)}, u32[]{:S(2)}) collective-permute-start(bf16[64,512]{1,0:T(8,128)(2,1)S(1)} %pad_maximum_fusion), channel_id=1, source_target_pairs={{0,3},{1,4},{2,5},{3,6},{4,7},{8,11},{9,12},{10,13},{11,14},{12,15... | collective-permute-start | bytes 196616 | tf_op jit(solution)/shard_map/ppermute | solution.py:28
  36.2 8.6 %collective-permute-start.6 = (bf16[160,512]{1,0:T(8,128)(2,1)S(1)}, bf16[160,512]{1,0:T(8,128)(2,1)S(1)}, u32[]{:S(2)}, u32[]{:S(2)}) collective-permute-start(bf16[160,512]{1,0:T(8,128)(2,1)S(1)} %slice_dynamic-update-slice_fusion), channel_id=1, source_target_pairs={{1,0},{2,1},{3,2},{4,3},{5,4},{6,5},{7,6},{9,8},{10,9},{11,10},{12... | collective-permute-start | bytes 491528 | tf_op jit(solution)/shard_map/ppermute | solution.py:28
  44.8 1.2 copy-start
  46.0 0.9 copy-start.2
  46.9 0.9 copy-start.4
  47.8 0.9 copy-start.6
  48.8 1.0 copy-start.8
  49.8 0.9 copy-start.11
  50.7 10.4 %copy-start.1 = (bf16[512,1024]{1,0:T(8,128)(2,1)S(1)}, bf16[512,1024]{1,0:T(8,128)(2,1)}, u32[]{:S(2)}) copy-start(bf16[512,1024]{1,0:T(8,128)(2,1)} %refs_11_.3) | copy-start | bytes 3145732
  50.7 10.4 %copy-start.3 = (bf16[1,192,512]{2,1,0:T(8,128)(2,1)S(1)}, bf16[1,192,512]{2,1,0:T(8,128)(2,1)}, u32[]{:S(2)}) copy-start(bf16[1,192,512]{2,1,0:T(8,128)(2,1)} %param.6) | copy-start | bytes 589828
  50.7 10.4 %copy-start.5 = (bf16[1,192,512]{2,1,0:T(8,128)(2,1)S(1)}, bf16[1,192,512]{2,1,0:T(8,128)(2,1)}, u32[]{:S(2)}) copy-start(bf16[1,192,512]{2,1,0:T(8,128)(2,1)} %param.7) | copy-start | bytes 589828
  50.7 10.4 %copy-start.7 = (bf16[1,192,512]{2,1,0:T(8,128)(2,1)S(1)}, bf16[1,192,512]{2,1,0:T(8,128)(2,1)}, u32[]{:S(2)}) copy-start(bf16[1,192,512]{2,1,0:T(8,128)(2,1)} %param.8) | copy-start | bytes 589828
  61.0 262.1 %all-reduce.5.cloned.1.call-start = ((), (), s32[]{:S(2)}) async-start(), calls=%async_computation.1 | async-start | bytes 262144 | tf_op jit(solution)/shard_map/psum | solution.py:208
  66.6 0.8 copy-start.9
  67.3 26.1 %copy-start.10 = (f32[192,512]{1,0:T(8,128)S(1)}, f32[192,512]{1,0:T(8,128)}, u32[]{:S(2)}) copy-start(f32[192,512]{1,0:T(8,128)} %copy-done.9) | copy-start | bytes 1179652
  67.3 13.0 %collective-permute-start.7 = (bf16[384,512]{1,0:T(8,128)(2,1)}, bf16[384,512]{1,0:T(8,128)(2,1)S(1)}, u32[]{:S(2)}, u32[]{:S(2)}) collective-permute-start(bf16[384,512]{1,0:T(8,128)(2,1)} %get-tuple-element.23), channel_id=1, source_target_pairs={{1,0},{2,1},{3,2},{4,3},{5,4},{6,5},{7,6},{9,8},{10,9},{11,10},{12... | collective-permute-start | bytes 1179656 | tf_op jit(solution)/shard_map/ppermute | solution.py:28
  68.8 24.5 %collective-permute-start.8 = (bf16[384,512]{1,0:T(8,128)(2,1)}, bf16[384,512]{1,0:T(8,128)(2,1)S(1)}, u32[]{:S(2)}, u32[]{:S(2)}) collective-permute-start(bf16[384,512]{1,0:T(8,128)(2,1)} %get-tuple-element.24), channel_id=1, source_target_pairs={{2,0},{3,1},{4,2},{5,3},{6,4},{7,5},{10,8},{11,9},{12,10},{13,11},... | collective-permute-start | bytes 1179656 | tf_op jit(solution)/shard_map/ppermute | solution.py:28
Sparse Core Ops, SparseCore 0:
  61.1 133.5 all-reduce.2
  201.7 121.3 all-reduce.4

commit v2 on v1

--- a/solution.py
+++ b/solution.py
@@ -45,14 +45,38 @@
     return jnp.where(lane < HEAD_DIM, stacked[:rows], stacked[rows:])
 
 
+def pack_kernel(edge, k_ref, v_ref, q_ref, cot_ref, own_ref, far_ref, near_ref, sems):
+    rows, att = k_ref.shape
+    width = cot_ref.shape[1]
+    head, tail = pl.ds(0, edge), pl.ds(rows - edge, edge)
+    moves = [
+        (k_ref, own_ref.at[pl.ds(0, rows)]),
+        (v_ref, own_ref.at[pl.ds(rows, rows)]),
+        (q_ref.at[tail], own_ref.at[pl.ds(2 * rows, edge)]),
+        (k_ref.at[tail], far_ref.at[pl.ds(0, edge)]),
+        (v_ref.at[tail], far_ref.at[pl.ds(edge, edge)]),
+        (k_ref.at[head], near_ref.at[pl.ds(0, edge)]),
+        (v_ref.at[head], near_ref.at[pl.ds(edge, edge)]),
+        (q_ref.at[head], near_ref.at[pl.ds(2 * edge, edge)]),
+    ]
+    for part in range(width // att):
+        piece = cot_ref.at[head, pl.ds(part * att, att)]
+        moves.append((piece, near_ref.at[pl.ds((3 + part) * edge, edge)]))
+    copies = [pltpu.make_async_copy(a, b, sems.at[i]) for i, (a, b) in enumerate(moves)]
+    for copy in copies:
+        copy.start()
+    for copy in copies:
+        copy.wait()
+
+
 def forward_kernel(context, rows, edge, taps, *refs):
     tiles = context + 1
-    device_ref, q_ref, q_tail_ref = refs[:3]
-    k_refs = refs[3 : 3 + tiles]
-    v_refs = refs[3 + tiles : 3 + 2 * tiles]
-    far_ref, near_ref, w_ref, conv_ref, cot_ref = refs[3 + 2 * tiles : 8 + 2 * tiles]
-    out_ref, att_ref, lse_ref, dhid_ref, wpart_ref, kpart_ref = refs[8 + 2 * tiles : 14 + 2 * tiles]
-    qx, kx, vx, ax, lx, hid, cotx, dm, bias = refs[14 + 2 * tiles :]
+    device_ref, q_hbm = refs[:2]
+    own_refs = refs[2 : 2 + tiles]
+    far_ref, near_ref, w_hbm, conv_hbm, cot_hbm = refs[2 + tiles : 7 + tiles]
+    out_ref, att_ref, lse_ref, dhid_ref, part_ref = refs[7 + tiles : 12 + tiles]
+    qx, kx, vx, ax, lx, hid, cotx, dm, bias, kp = refs[12 + tiles : 22 + tiles]
+    q_ref, w_ref, conv_ref, cot_ref, sems = refs[22 + tiles :]
 
     att = q_ref.shape[1]
     width = w_ref.shape[1]
@@ -63,22 +87,25 @@
     scale = 1.0 / math.sqrt(HEAD_DIM)
     start = device_ref[0] * rows
 
-    qx[:edge] = q_tail_ref[...] * scale
-    qx[edge : edge + rows] = q_ref[...] * scale
-    qx[edge + rows :] = near_ref[2 * edge : 3 * edge] * scale
-    for ext, own, far_at, near_at in ((kx, k_refs, 0, 0), (vx, v_refs, edge, edge)):
+    fetches = [
+        pltpu.make_async_copy(source, target, sems.at[i])
+        for i, (source, target) in enumerate(
+            ((q_hbm, q_ref), (w_hbm, w_ref), (cot_hbm, cot_ref), (conv_hbm, conv_ref))
+        )
+    ]
+    for fetch in fetches:
+        fetch.start()
+
+    for ext, own_at, far_at in ((kx, 0, 0), (vx, rows, edge)):
         ext[:edge] = far_ref[far_at : far_at + edge]
         for offset in range(tiles):
             first = edge + (context - offset) * rows
-            ext[first : first + rows] = own[offset][...]
-        ext[edge + span + rows :] = near_ref[near_at : near_at + edge]
-    for chunk in range(width // LANES):
-        columns = slice(chunk * LANES, (chunk + 1) * LANES)
-        cotx[chunk, :rows] = cot_ref[:, columns].astype(jnp.float32)
-        part, lane = divmod(chunk * LANES, att)
-        cotx[chunk, rows:] = near_ref[
-            (3 + part) * edge : (4 + part) * edge, lane : lane + LANES
-        ].astype(jnp.float32)
+            ext[first : first + rows] = own_refs[offset][own_at : own_at + rows]
+        ext[edge + span + rows :] = near_ref[far_at : far_at + edge]
+    qx[:edge] = own_refs[1][2 * rows : 2 * rows + edge] * scale
+    qx[edge + rows :] = near_ref[2 * edge : 3 * edge] * scale
+    fetches[0].wait()
+    qx[edge : edge + rows] = q_ref[...] * scale
 
     lane_id = lax.broadcasted_iota(jnp.int32, (block, LANES), 1)
     for b in range(query_rows // block):
@@ -92,15 +119,15 @@
         for pair in range(att // LANES):
             columns = slice(pair * LANES, (pair + 1) * LANES)
             qs = stack_heads(qx[b * block : (b + 1) * block, columns])
-            kp = kx[b * block : b * block + keys, columns]
-            vp = vx[b * block : b * block + keys, columns]
-            scores = dot(qs, kp, NT)
+            kp_tile = kx[b * block : b * block + keys, columns]
+            vp_tile = vx[b * block : b * block + keys, columns]
+            scores = dot(qs, kp_tile, NT)
             hidden_pairs = bias[...]
             scores = scores + jnp.concatenate([hidden_pairs, hidden_pairs], axis=0)
             row_max = jnp.max(scores, axis=1, keepdims=True)
             weights = jnp.exp(scores - row_max)
             row_sum = jnp.sum(weights, axis=1, keepdims=True)
-            mixed = dot(weights.astype(jnp.bfloat16), vp, NN) / row_sum
+            mixed = dot(weights.astype(jnp.bfloat16), vp_tile, NN) / row_sum
             ax[b * block : (b + 1) * block, columns] = merge_heads(mixed).astype(jnp.bfloat16)
             log_sum = row_max + jnp.log(row_sum)
             log_sums = jnp.where(lane_id == 2 * pair, log_sum[:block], log_sums)
@@ -109,6 +136,7 @@
     att_ref[...] = ax[edge : edge + rows]
     lse_ref[...] = jnp.transpose(lx[...])[: lse_ref.shape[0], edge : edge + rows]
 
+    fetches[1].wait()
     step = 2 * LANES
     for part in range(width // step):
         product = dot(ax[...], w_ref[:, part * step : (part + 1) * step], NN)
@@ -117,6 +145,17 @@
         product = jnp.where(time >= 0, product, 0.0)
         hid[2 * part] = product[:, :LANES]
         hid[2 * part + 1] = product[:, LANES:]
+
+    fetches[2].wait()
+    fetches[3].wait()
+    for chunk in range(width // LANES):
+        columns = slice(chunk * LANES, (chunk + 1) * LANES)
+        cotx[chunk, :rows] = cot_ref[:, columns].astype(jnp.float32)
+        part, lane = divmod(chunk * LANES, att)
+        cotx[chunk, rows:] = near_ref[
+            (3 + part) * edge : (4 + part) * edge, lane : lane + LANES
+        ].astype(jnp.float32)
+    kp[...] = jnp.zeros_like(kp)
 
     def convolve(chunk, carry):
         columns = pl.ds(pl.multiple_of(chunk * LANES, LANES), LANES)
@@ -133,25 +172,59 @@
         own = dm[:rows]
         for tap in range(taps):
             product = own * hid[chunk, edge - tap : edge + rows - tap]
-            kpart_ref[tap : tap + 1, columns] = jnp.sum(product, axis=0, keepdims=True)
+            kp[chunk, tap : tap + 1] = jnp.sum(product, axis=0, keepdims=True)
         return carry
 
     lax.fori_loop(0, width // LANES, convolve, 0)
+
+    pieces, piece_rows, _ = part_ref.shape
+    chunks = width // LANES
+    group = att // pieces
     own = ax[edge : edge + rows]
     for part in range(width // step):
-        columns = slice(part * step, (part + 1) * step)
-        wpart_ref[:, columns] = dot(own, dhid_ref[:, columns], TN).astype(wpart_ref.dtype)
+        product = dot(own, dhid_ref[:, part * step : (part + 1) * step], TN).astype(jnp.bfloat16)
+        for half in range(2):
+            chunk = 2 * part + half
+            tile = product[:, half * LANES : (half + 1) * LANES]
+            for piece in range(pieces):
+                part_ref[piece, chunk * group : (chunk + 1) * group] = tile[
+                    piece * group : (piece + 1) * group
+                ]
+    rest = jnp.zeros((piece_rows - chunks * (group + 1), LANES), jnp.float32)
+    for piece in range(pieces):
+        row = [kp[chunk, piece : piece + 1] for chunk in range(chunks)]
+        part_ref[piece, chunks * group :] = jnp.concatenate(row + [rest], axis=0).astype(
+            jnp.bfloat16
+        )
+
+
+def unpack_kernel(total_ref, weight_ref, kernel_ref):
+    pieces, piece_rows, _ = total_ref.shape
+    att, width = weight_ref.shape
+    taps = kernel_ref.shape[0]
+    chunks = width // LANES
+    group = att // pieces
+    for piece in range(pieces):
+        for chunk in range(chunks):
+            weight_ref[
+                piece * group : (piece + 1) * group, chunk * LANES : (chunk + 1) * LANES
+            ] = total_ref[piece, chunk * group : (chunk + 1) * group].astype(jnp.float32)
+        if piece < taps:
+            rows = total_ref[piece, chunks * group :].astype(jnp.float32)
+            for chunk in range(chunks):
+                kernel_ref[piece : piece + 1, chunk * LANES : (chunk + 1) * LANES] = rows[
+                    chunk : chunk + 1
+                ]
 
 
 def backward_kernel(context, rows, *refs):
     tiles = context + 1
     device_ref, q_ref = refs[:2]
-    k_refs = refs[2 : 2 + tiles]
-    v_refs = refs[2 + tiles : 2 + 2 * tiles]
-    att_ref, lse_ref, dhid_ref, w_ref = refs[2 + 2 * tiles : 6 + 2 * tiles]
-    dq_ref, dk_ref, dv_ref = refs[6 + 2 * tiles : 9 + 2 * tiles]
-    message_refs = refs[9 + 2 * tiles : 9 + 2 * tiles + context]
-    datt, bias = refs[9 + 2 * tiles + context :]
+    own_refs = refs[2 : 2 + tiles]
+    att_ref, lse_ref, dhid_ref, w_ref = refs[2 + tiles : 6 + tiles]
+    dq_ref, dk_ref, dv_ref = refs[6 + tiles : 9 + tiles]
+    message_refs = refs[9 + tiles : 9 + tiles + context]
+    datt, bias = refs[9 + tiles + context :]
 
     att = q_ref.shape[1]
     heads = att // HEAD_DIM
@@ -185,8 +258,8 @@
         delta = jnp.concatenate(delta, axis=1)
         dquery = jnp.zeros((2 * rows, LANES), jnp.float32)
         for offset in range(tiles):
-            kp = k_refs[offset][:, columns]
-            vp = v_refs[offset][:, columns]
+            kp = own_refs[offset][:rows, columns]
+            vp = own_refs[offset][rows : 2 * rows, columns]
             hidden_pairs = jnp.concatenate([bias[offset], bias[offset]], axis=1)
             probs = jnp.exp(dot(kp, qs, NT) + hidden_pairs - log_sum)
             dprobs = dot(vp, ds, NT)
@@ -203,10 +276,25 @@
         dq_ref[:, columns] = (merge_heads(dquery) * scale).astype(jnp.bfloat16)
 
 
-def sum_weights(weight_part, kernel_part):
-    weight = lax.psum(weight_part, ("dp", "blk"))
-    kernel = lax.psum(kernel_part, ("dp", "blk"))
-    return weight.astype(jnp.float32), kernel
+def exchange(x, axis):
+    return lax.all_to_all(x, axis, 0, 0, tiled=True)
+
+
+def summed(x):
+    return jnp.sum(x.astype(jnp.float32), axis=0).astype(x.dtype)
+
+
+def sum_parts(parts):
+    pieces, rows, lanes = parts.shape
+    outer, inner = lax.axis_size("dp"), lax.axis_size("blk")
+    if pieces != outer * inner:
+        return lax.psum(parts, ("dp", "blk"))
+    mine = summed(exchange(parts.reshape(outer, inner * rows, lanes), "dp"))
+    mine = summed(exchange(mine.reshape(inner, rows, lanes), "blk"))
+    mine = exchange(jnp.broadcast_to(mine, (inner, rows, lanes)), "blk")
+    mine = mine.reshape(inner * rows, lanes)
+    mine = exchange(jnp.broadcast_to(mine, (outer, inner * rows, lanes)), "dp")
+    return mine.reshape(pieces, rows, lanes)
 
 
 def per_device(queries, key_in, value_in, out_weight, conv_kernel, cotangent):
@@ -221,46 +309,76 @@
     edge = -(-(taps - 1) // 16) * 16
     context = min(CTX_MAX, runs // 4)
 
-    keys = [key] + [shifted(key, o) for o in range(1, context + 1)]
-    values = [value] + [shifted(value, o) for o in range(1, context + 1)]
-    query_tail = shifted(query[-edge:], 1)
-    far = shifted(jnp.concatenate([key[-edge:], value[-edge:]]), context + 1)
-    pieces = [key, value, query] + [cot[:, i : i + att] for i in range(0, width, att)]
-    near = shifted(jnp.concatenate([piece[:edge] for piece in pieces]), -1)
-
     query_rows = rows + 2 * edge
     key_rows = query_rows + context * rows
+    chunks = width // LANES
     vmem = pl.BlockSpec(memory_space=pltpu.VMEM)
     smem = pl.BlockSpec(memory_space=pltpu.SMEM)
+    hbm = pl.BlockSpec(memory_space=pltpu.HBM)
     params = pltpu.CompilerParams(vmem_limit_bytes=VMEM_LIMIT)
-    out_frames, attended, log_sums, dhidden, weight_part, kernel_part = pl.pallas_call(
+
+    own, far, near = pl.pallas_call(
+        functools.partial(pack_kernel, edge),
+        out_shape=(
+            jax.ShapeDtypeStruct((2 * rows + edge, att), bf16),
+            jax.ShapeDtypeStruct((2 * edge, att), bf16),
+            jax.ShapeDtypeStruct(((3 + width // att) * edge, att), bf16),
+        ),
+        in_specs=[hbm] * 4,
+        out_specs=(vmem,) * 3,
+        scratch_shapes=[pltpu.SemaphoreType.DMA((8 + width // att,))],
+        compiler_params=params,
+        name="pack",
+    )(key, value, query, cot)
+    tiles = [own] + [shifted(own, o) for o in range(1, context + 1)]
+    far = shifted(far, context + 1)
+    near = shifted(near, -1)
+
+    pieces = att // 16
+    piece_rows = -(-(chunks * 16 + chunks) // 16) * 16
+    out_frames, attended, log_sums, dhidden, parts = pl.pallas_call(
         functools.partial(forward_kernel, context, rows, edge, taps),
         out_shape=(
             jax.ShapeDtypeStruct((rows, width), bf16),
             jax.ShapeDtypeStruct((rows, att), bf16),
             jax.ShapeDtypeStruct((heads, rows), f32),
             jax.ShapeDtypeStruct((rows, width), bf16),
-            jax.ShapeDtypeStruct((att, width), bf16),
-            jax.ShapeDtypeStruct((taps, width), f32),
+            jax.ShapeDtypeStruct((pieces, piece_rows, LANES), bf16),
         ),
-        in_specs=[smem] + [vmem] * (7 + 2 * (context + 1)),
-        out_specs=(vmem,) * 6,
+        in_specs=[smem, hbm] + [vmem] * (3 + context) + [hbm] * 3,
+        out_specs=(vmem,) * 5,
         scratch_shapes=[
             pltpu.VMEM((query_rows, att), bf16),
             pltpu.VMEM((key_rows, att), bf16),
             pltpu.VMEM((key_rows, att), bf16),
             pltpu.VMEM((query_rows, att), bf16),
             pltpu.VMEM((query_rows, LANES), f32),
-            pltpu.VMEM((width // LANES, query_rows, LANES), f32),
-            pltpu.VMEM((width // LANES, rows + edge, LANES), f32),
+            pltpu.VMEM((chunks, query_rows, LANES), f32),
+            pltpu.VMEM((chunks, rows + edge, LANES), f32),
             pltpu.VMEM((rows + edge, LANES), f32),
             pltpu.VMEM((LANES, context * rows + LANES), f32),
+            pltpu.VMEM((chunks, pieces, LANES), f32),
+            pltpu.VMEM((rows, att), bf16),
+            pltpu.VMEM((att, width), bf16),
+            pltpu.VMEM((taps, width), f32),
+            pltpu.VMEM((rows, width), bf16),
+            pltpu.SemaphoreType.DMA((4,)),
         ],
         compiler_params=params,
         name="forward",
-    )(device, query, query_tail, *keys, *values, far, near, out_weight, conv_kernel, cot)
-
-    weight_total, kernel_total = sum_weights(weight_part, kernel_part)
+    )(device, query, *tiles, far, near, out_weight, conv_kernel, cot)
+
+    weight_total, kernel_total = pl.pallas_call(
+        unpack_kernel,
+        out_shape=(
+            jax.ShapeDtypeStruct((att, width), f32),
+            jax.ShapeDtypeStruct((taps, width), f32),
+        ),
+        in_specs=[vmem],
+        out_specs=(vmem, vmem),
+        compiler_params=params,
+        name="unpack",
+    )(sum_parts(parts))
 
     outs = pl.pallas_call(
         functools.partial(backward_kernel, context, rows),
@@ -270,7 +388,7 @@
             jax.ShapeDtypeStruct((rows, att), f32),
         )
         + (jax.ShapeDtypeStruct((2 * rows, att), bf16),) * context,
-        in_specs=[smem] + [vmem] * (5 + 2 * (context + 1)),
+        in_specs=[smem] + [vmem] * (6 + context),
         out_specs=(vmem,) * (3 + context),
         scratch_shapes=[
             pltpu.VMEM((rows, att), bf16),
@@ -278,7 +396,7 @@
         ],
         compiler_params=params,
         name="backward",
-    )(device, query, *keys, *values, attended, log_sums, dhidden, out_weight)
+    )(device, query, *tiles, attended, log_sums, dhidden, out_weight)
     query_grad, dkey, dvalue = outs[:3]
     for offset, message in enumerate(outs[3:], 1):
         arrived = shifted(message, -offset).astype(f32)

time: 333 us -> 132 us (0.40)
  waiting for transfers between devices: 258 us -> 24 us
  blocking collectives: 0 us -> 53.3 us
  between operations: 14.2 us -> 0.8 us
  starting transfers between devices: 25.7 us -> 21.4 us
    psum x2 -> x0, waiting for transfers between devices: 226 us -> none  [the longest x1 126 us: sum_weights(): kernel = lax.psum(kernel_part, ('dp', 'blk'))]
    all_to_all x0 -> x3, blocking collectives: none -> 53.3 us  [exchange(): return lax.all_to_all(x, axis, 0, 0, tiled=True)]
    ppermute x9 -> x6, starting transfers between devices: 25.7 us -> 17.8 us  [shifted(): lax.ppermute(x, 'blk', [(i, i + by) for i in devices if i + by in devices])]
    ppermute x9 -> x6, waiting for transfers between devices: 31.5 us -> 24 us  [shifted(): lax.ppermute(x, 'blk', [(i, i + by) for i in devices if i + by in devices])]
    all_to_all x0 -> x1, starting transfers between devices: none -> 3.66 us  [exchange(): return lax.all_to_all(x, axis, 0, 0, tiled=True)]
    unnamed x29 -> x32, local copies, waits for them, and re-layouts: 11.3 us -> 10.6 us
  transfers between devices with their start and end apart: 11 -> 7, of which waited for: 6 -> 4; matrix products, arithmetic and copies ran while one was open for 3% -> 1% of each run, Pallas kernels for 2% -> 4%
where the time goes in v2:
time: 132 us; the launch traced here: 131 us
  blocking collectives  53.3 us (40%)
  waiting for transfers between devices  24 us (18%)
  starting transfers between devices  21.4 us (16%)
  Pallas kernels  18.4 us (14%)
  local copies, waits for them, and re-layouts  11.8 us (9%)
  other arithmetic  1.47 us (1%)
    all_to_all x3, blocking collectives, exchange(): return lax.all_to_all(x, axis, 0, 0, tiled=True)  53.3 us
    ppermute x6, waiting for transfers between devices, shifted(): lax.ppermute(x, 'blk', [(i, i + by) for i in devices if i + by in devices])  24 us
    ppermute x6, starting transfers between devices, shifted(): lax.ppermute(x, 'blk', [(i, i + by) for i in devices if i + by in devices])  17.8 us
    unnamed x32, local copies, waits for them, and re-layouts  10.6 us
    pallas_call x1, Pallas kernels, per_device(): pl.pallas_call(functools.partial(forward_kernel, context, rows, edge, tap...  10.5 us
    pallas_call x1, Pallas kernels, per_device(): pl.pallas_call(functools.partial(backward_kernel, context, rows), out_sha...  5.43 us
    all_to_all x1, starting transfers between devices, exchange(): return lax.all_to_all(x, axis, 0, 0, tiled=True)  3.66 us
  transfers between devices with their start and end apart: 7, of which 4 were waited for; matrix products, arithmetic and copies ran while one was open for 1% of the time, Pallas kernels for 4%

profile of v2, /device:TPU:0, one launch (start us, length us, event | category | flops | bytes accessed | tf_op | source)
XLA Modules:
  0.0 131.2 jit_solution(2406833341850043855)
XLA Ops:
  0.6 0.0 copy-start.2
  0.6 0.9 copy-done.2
  1.6 0.0 copy-start.7
  1.6 1.0 copy-done.7
  2.6 0.0 copy-start.11
  2.6 0.9 copy-done.11
  3.5 0.0 copy-start.12
  3.5 0.9 copy-done.12
  4.4 0.0 copy-start.8
  4.4 0.9 pack.1
  5.3 5.0 %collective-permute-start.1 = (bf16[416,512]{1,0:T(8,128)(2,1)S(1)}, bf16[416,512]{1,0:T(8,128)(2,1)S(1)}, u32[]{:S(2)}, u32[]{:S(2)}) collective-permute-start(bf16[416,512]{1,0:T(8,128)(2,1)S(1)} %get-tuple-element.21.refs_2_), channel_id=1, source_target_pairs={{0,2},{1,3},{2,4},{3,5},{4,6},{5,7},{8,10},{9,11},{10,12},{11,13},... | collective-permute-start | bytes 1277960 | tf_op jit(solution)/shard_map/ppermute | solution.py:28
  10.2 3.5 %collective-permute-start = (bf16[416,512]{1,0:T(8,128)(2,1)S(1)}, bf16[416,512]{1,0:T(8,128)(2,1)S(1)}, u32[]{:S(2)}, u32[]{:S(2)}) collective-permute-start(bf16[416,512]{1,0:T(8,128)(2,1)S(1)} %get-tuple-element.21.refs_2_), channel_id=1, source_target_pairs={{0,1},{1,2},{2,3},{3,4},{4,5},{5,6},{6,7},{8,9},{9,10},{10,11},{11... | collective-permute-start | bytes 1277960 | tf_op jit(solution)/shard_map/ppermute | solution.py:28
  13.7 1.3 collective-permute-start.3
  15.0 5.5 %collective-permute-start.2 = (bf16[64,512]{1,0:T(8,128)(2,1)S(1)}, bf16[64,512]{1,0:T(8,128)(2,1)S(1)}, u32[]{:S(2)}, u32[]{:S(2)}) collective-permute-start(bf16[64,512]{1,0:T(8,128)(2,1)S(1)} %get-tuple-element.22), channel_id=1, source_target_pairs={{0,3},{1,4},{2,5},{3,6},{4,7},{8,11},{9,12},{10,13},{11,14},{12,15... | collective-permute-start | bytes 196616 | tf_op jit(solution)/shard_map/ppermute | solution.py:28
  20.5 1.9 %collective-permute-done.2.refs_5_ = bf16[64,512]{1,0:T(8,128)(2,1)S(1)} collective-permute-done((bf16[64,512]{1,0:T(8,128)(2,1)S(1)}, bf16[64,512]{1,0:T(8,128)(2,1)S(1)}, u32[]{:S(2)}, u32[]{:S(2)}) %collective-permute-start.2) | collective-permute-done | bytes 65568 | tf_op jit(solution)/shard_map/ppermute | solution.py:28
  22.4 0.0 collective-permute-done.3.refs_6_
  22.4 0.0 copy-start.13
  22.4 0.7 copy-done.13
  23.1 0.0 collective-permute-done.1.refs_4_
  23.1 2.9 %collective-permute-done.refs_3_ = bf16[416,512]{1,0:T(8,128)(2,1)S(1)} collective-permute-done((bf16[416,512]{1,0:T(8,128)(2,1)S(1)}, bf16[416,512]{1,0:T(8,128)(2,1)S(1)}, u32[]{:S(2)}, u32[]{:S(2)}) %collective-permute-start) | collective-permute-done | bytes 426016 | tf_op jit(solution)/shard_map/ppermute | solution.py:28
  26.0 0.0 copy-start.5
  26.0 0.0 copy-done.8
  26.0 0.0 copy-start
  26.0 1.4 %copy-done = bf16[512,1024]{1,0:T(8,128)(2,1)S(1)} copy-done((bf16[512,1024]{1,0:T(8,128)(2,1)S(1)}, bf16[512,1024]{1,0:T(8,128)(2,1)}, u32[]{:S(2)}) %copy-start) | copy-done | bytes 1048600
  27.4 0.0 copy-start.3
  27.4 0.9 copy-done.3
  28.3 0.0 copy-start.14
  28.3 0.9 copy-done.14
  29.2 0.0 copy-start.15
  29.2 0.9 copy-done.15
  30.1 10.5 %forward.1 = (bf16[192,1024]{1,0:T(8,128)(2,1)}, bf16[192,512]{1,0:T(8,128)(2,1)S(1)}, f32[8,192]{1,0:T(8,128)S(1)}, bf16[192,1024]{1,0:T(8,128)(2,1)S(1)}, bf16[32,144,128]{2,1,0:T(8,128)(2,1)S(1)}) custom-call(s32[1]{0:T(128)} %bitcast.refs_0_, bf16[192,512]{1,0:T(8,128)(2,1)S(1)} %bitcast.17, bf16[416,512]{1,0:T(8,128)(2,1)S(1)} %get-tuple-element.21.refs_2_, ...), custom_call_target="tpu_custom_call" | custom-call | tf_op jit(solution)/shard_map/forward/pallas_call | solution.py:339
  40.7 0.0 copy-done.5
  40.7 0.0 copy-start.9
  40.7 18.4 %all_to_all.20 = bf16[4,1152,128]{2,1,0:T(8,128)(2,1)S(1)} all-to-all(bf16[4,1152,128]{2,1,0:T(8,128)(2,1)S(1)} %bitcast.21), channel_id=1, replica_groups=mesh['dp'=4,'blk'=8] {'dp'}, dimensions={0} | all-to-all | bytes 2359296 | tf_op jit(solution)/shard_map/all_to_all | solution.py:280
  59.1 0.0 copy-done.9
  59.1 0.3 reduce_sum.24
  59.4 22.4 %all_to_all.21 = bf16[8,144,128]{2,1,0:T(8,128)(2,1)S(1)} all-to-all(bf16[8,144,128]{2,1,0:T(8,128)(2,1)S(1)} %bitcast.24), channel_id=1, replica_groups=mesh['dp'=4,'blk'=8] {'blk'}, dimensions={0} | all-to-all | bytes 589824 | tf_op jit(solution)/shard_map/all_to_all | solution.py:280
  81.9 12.5 %all_to_all.22 = bf16[8,144,128]{2,1,0:T(8,128)(2,1)S(1)} all-to-all(bf16[8,144,128]{2,1,0:T(8,128)(2,1)S(1)} %broadcast_in_dim.26), channel_id=1, replica_groups=mesh['dp'=4,'blk'=8] {'blk'}, dimensions={0} | all-to-all | bytes 589824 | tf_op jit(solution)/shard_map/all_to_all | solution.py:280
  94.4 1.2 broadcast_in_dim.27
  95.6 0.0 copy-start.1
  95.6 0.0 copy-start.4
  95.6 3.7 %all-to-all-start.3 = ((bf16[4,1152,128]{2,1,0:T(8,128)(2,1)}), bf16[4,1152,128]{2,1,0:T(8,128)(2,1)S(1)}, u32[]{:S(2)}, u32[]{:S(2)}) async-start(bf16[4,1152,128]{2,1,0:T(8,128)(2,1)} %broadcast_in_dim.27), calls=%async_computation.3 | async-start | bytes 2359296 | tf_op jit(solution)/shard_map/all_to_all | solution.py:280
  99.2 0.0 copy-done.1
  99.3 0.0 copy-done.4
  99.3 0.0 copy-start.6
  99.3 1.0 copy-done.6
  100.3 0.0 copy-start.10
  100.3 1.0 copy-done.10
  101.3 5.4 %backward.1 = (bf16[192,512]{1,0:T(8,128)(2,1)}, f32[192,512]{1,0:T(8,128)S(1)}, f32[192,512]{1,0:T(8,128)S(1)}, bf16[384,512]{1,0:T(8,128)(2,1)S(1)}, bf16[384,512]{1,0:T(8,128)(2,1)S(1)}) custom-call(s32[1]{0:T(128)} %bitcast.refs_0_, bf16[192,512]{1,0:T(8,128)(2,1)S(1)} %bitcast.18, bf16[416,512]{1,0:T(8,128)(2,1)S(1)} %get-tuple-element.21.refs_2_, ...), custom_call_target="tpu_custom_call" | custom-call | tf_op jit(solution)/shard_map/backward/pallas_call | solution.py:383
  106.7 1.3 collective-permute-start.4
  108.0 1.3 collective-permute-start.5
  109.3 10.8 %collective-permute-done.4 = bf16[384,512]{1,0:T(8,128)(2,1)S(1)} collective-permute-done((bf16[384,512]{1,0:T(8,128)(2,1)S(1)}, bf16[384,512]{1,0:T(8,128)(2,1)S(1)}, u32[]{:S(2)}, u32[]{:S(2)}) %collective-permute-start.4) | collective-permute-done | bytes 393248 | tf_op jit(solution)/shard_map/ppermute | solution.py:28
  120.1 0.1 convert_element_type.16
  120.2 8.5 %collective-permute-done.5 = bf16[384,512]{1,0:T(8,128)(2,1)S(1)} collective-permute-done((bf16[384,512]{1,0:T(8,128)(2,1)S(1)}, bf16[384,512]{1,0:T(8,128)(2,1)S(1)}, u32[]{:S(2)}, u32[]{:S(2)}) %collective-permute-start.5) | collective-permute-done | bytes 393248 | tf_op jit(solution)/shard_map/ppermute | solution.py:28
  128.6 0.1 convert_element_type.17
  128.7 0.9 fusion.3
  129.7 0.0 all-to-all-done.3
  129.7 1.6 %unpack.1 = (f32[512,1024]{1,0:T(8,128)}, f32[31,1024]{1,0:T(8,128)}) custom-call(bf16[32,144,128]{2,1,0:T(8,128)(2,1)S(1)} %bitcast.15), custom_call_target="tpu_custom_call" | custom-call | tf_op jit(solution)/shard_map/unpack/pallas_call | solution.py:371
  (2 shorter events, 0.1 us)
Async XLA Ops:
  0.6 0.9 copy-start.2
  1.6 1.0 copy-start.7
  2.6 0.9 copy-start.11
  3.5 0.9 copy-start.12
  4.4 21.6 %copy-start.8 = (bf16[1,192,1024]{2,1,0:T(8,128)(2,1)S(1)}, bf16[1,192,1024]{2,1,0:T(8,128)(2,1)}, u32[]{:S(2)}) copy-start(bf16[1,192,1024]{2,1,0:T(8,128)(2,1)} %param.11) | copy-start | bytes 1179652
  5.3 17.8 %collective-permute-start.1 = (bf16[416,512]{1,0:T(8,128)(2,1)S(1)}, bf16[416,512]{1,0:T(8,128)(2,1)S(1)}, u32[]{:S(2)}, u32[]{:S(2)}) collective-permute-start(bf16[416,512]{1,0:T(8,128)(2,1)S(1)} %get-tuple-element.21.refs_2_), channel_id=1, source_target_pairs={{0,2},{1,3},{2,4},{3,5},{4,6},{5,7},{8,10},{9,11},{10,12},{11,13},... | collective-permute-start | bytes 1277960 | tf_op jit(solution)/shard_map/ppermute | solution.py:28
  10.2 15.7 %collective-permute-start = (bf16[416,512]{1,0:T(8,128)(2,1)S(1)}, bf16[416,512]{1,0:T(8,128)(2,1)S(1)}, u32[]{:S(2)}, u32[]{:S(2)}) collective-permute-start(bf16[416,512]{1,0:T(8,128)(2,1)S(1)} %get-tuple-element.21.refs_2_), channel_id=1, source_target_pairs={{0,1},{1,2},{2,3},{3,4},{4,5},{5,6},{6,7},{8,9},{9,10},{10,11},{11... | collective-permute-start | bytes 1277960 | tf_op jit(solution)/shard_map/ppermute | solution.py:28
  13.7 8.7 %collective-permute-start.3 = (bf16[160,512]{1,0:T(8,128)(2,1)S(1)}, bf16[160,512]{1,0:T(8,128)(2,1)S(1)}, u32[]{:S(2)}, u32[]{:S(2)}) collective-permute-start(bf16[160,512]{1,0:T(8,128)(2,1)S(1)} %get-tuple-element.23), channel_id=1, source_target_pairs={{1,0},{2,1},{3,2},{4,3},{5,4},{6,5},{7,6},{9,8},{10,9},{11,10},{12... | collective-permute-start | bytes 491528 | tf_op jit(solution)/shard_map/ppermute | solution.py:28
  15.0 7.4 %collective-permute-start.2 = (bf16[64,512]{1,0:T(8,128)(2,1)S(1)}, bf16[64,512]{1,0:T(8,128)(2,1)S(1)}, u32[]{:S(2)}, u32[]{:S(2)}) collective-permute-start(bf16[64,512]{1,0:T(8,128)(2,1)S(1)} %get-tuple-element.22), channel_id=1, source_target_pairs={{0,3},{1,4},{2,5},{3,6},{4,7},{8,11},{9,12},{10,13},{11,14},{12,15... | collective-permute-start | bytes 196616 | tf_op jit(solution)/shard_map/ppermute | solution.py:28
  22.4 0.7 copy-start.13
  26.0 14.7 %copy-start.5 = (bf16[416,512]{1,0:T(8,128)(2,1)}, bf16[416,512]{1,0:T(8,128)(2,1)S(1)}, u32[]{:S(2)}) copy-start(bf16[416,512]{1,0:T(8,128)(2,1)S(1)} %collective-permute-done.refs_3_) | copy-start | bytes 1277956
  26.0 1.4 %copy-start = (bf16[512,1024]{1,0:T(8,128)(2,1)S(1)}, bf16[512,1024]{1,0:T(8,128)(2,1)}, u32[]{:S(2)}) copy-start(bf16[512,1024]{1,0:T(8,128)(2,1)} %refs_8_.3) | copy-start | bytes 3145732
  27.4 0.9 copy-start.3
  28.3 0.9 copy-start.14
  29.2 0.9 copy-start.15
  40.7 18.4 %copy-start.9 = (bf16[192,1024]{1,0:T(8,128)(2,1)}, bf16[192,1024]{1,0:T(8,128)(2,1)S(1)}, u32[]{:S(2)}) copy-start(bf16[192,1024]{1,0:T(8,128)(2,1)S(1)} %get-tuple-element.27.refs_7_) | copy-start | bytes 1179652
  95.6 3.7 %copy-start.1 = (bf16[512,1024]{1,0:T(8,128)(2,1)S(1)}, bf16[512,1024]{1,0:T(8,128)(2,1)}, u32[]{:S(2)}) copy-start(bf16[512,1024]{1,0:T(8,128)(2,1)} %refs_8_.3) | copy-start | bytes 3145732
  95.6 3.7 %copy-start.4 = (bf16[1,192,512]{2,1,0:T(8,128)(2,1)S(1)}, bf16[1,192,512]{2,1,0:T(8,128)(2,1)}, u32[]{:S(2)}) copy-start(bf16[1,192,512]{2,1,0:T(8,128)(2,1)} %param.6) | copy-start | bytes 589828
  95.6 34.1 %all-to-all-start.3 = ((bf16[4,1152,128]{2,1,0:T(8,128)(2,1)}), bf16[4,1152,128]{2,1,0:T(8,128)(2,1)S(1)}, u32[]{:S(2)}, u32[]{:S(2)}) async-start(bf16[4,1152,128]{2,1,0:T(8,128)(2,1)} %broadcast_in_dim.27), calls=%async_computation.3 | async-start | bytes 2359296 | tf_op jit(solution)/shard_map/all_to_all | solution.py:280
  99.3 1.0 copy-start.6
  100.3 1.0 copy-start.10
  106.7 13.4 %collective-permute-start.4 = (bf16[384,512]{1,0:T(8,128)(2,1)S(1)}, bf16[384,512]{1,0:T(8,128)(2,1)S(1)}, u32[]{:S(2)}, u32[]{:S(2)}) collective-permute-start(bf16[384,512]{1,0:T(8,128)(2,1)S(1)} %get-tuple-element.30), channel_id=1, source_target_pairs={{1,0},{2,1},{3,2},{4,3},{5,4},{6,5},{7,6},{9,8},{10,9},{11,10},{12... | collective-permute-start | bytes 1179656 | tf_op jit(solution)/shard_map/ppermute | solution.py:28
  108.0 20.6 %collective-permute-start.5 = (bf16[384,512]{1,0:T(8,128)(2,1)S(1)}, bf16[384,512]{1,0:T(8,128)(2,1)S(1)}, u32[]{:S(2)}, u32[]{:S(2)}) collective-permute-start(bf16[384,512]{1,0:T(8,128)(2,1)S(1)} %get-tuple-element.31), channel_id=1, source_target_pairs={{2,0},{3,1},{4,2},{5,3},{6,4},{7,5},{10,8},{11,9},{12,10},{13,11},... | collective-permute-start | bytes 1179656 | tf_op jit(solution)/shard_map/ppermute | solution.py:28

commit v3 on v2

--- a/solution.py
+++ b/solution.py
@@ -6,12 +6,15 @@
 from jax import lax
 from jax.experimental import pallas as pl
 from jax.experimental.pallas import tpu as pltpu
+from jax.sharding import Mesh
 from jax.sharding import PartitionSpec as P
 
 HEAD_DIM = 64
 CTX_MAX = 3
 LANES = 128
 NEGATIVE = -1e30
+RUN_AXES = ("z", "y")
+CHIP_AXES = ("x", "z", "y")
 VMEM_LIMIT = 40 * 1024 * 1024
 
 NN = (((1,), (0,)), ((), ()))
@@ -24,8 +27,16 @@
 
 
 def shifted(x, by):
-    devices = range(lax.axis_size("blk"))
-    return lax.ppermute(x, "blk", [(i, i + by) for i in devices if i + by in devices])
+    devices = range(lax.axis_size(RUN_AXES))
+    return lax.ppermute(x, RUN_AXES, [(i, i + by) for i in devices if i + by in devices])
+
+
+def in_hbm(x):
+    return pltpu.with_memory_space_constraint(x, pltpu.HBM)
+
+
+def cost(flops, data):
+    return pl.CostEstimate(flops=flops, bytes_accessed=data, transcendentals=0)
 
 
 def head_masks():
@@ -74,9 +85,9 @@
     device_ref, q_hbm = refs[:2]
     own_refs = refs[2 : 2 + tiles]
     far_ref, near_ref, w_hbm, conv_hbm, cot_hbm = refs[2 + tiles : 7 + tiles]
-    out_ref, att_ref, lse_ref, dhid_ref, part_ref = refs[7 + tiles : 12 + tiles]
-    qx, kx, vx, ax, lx, hid, cotx, dm, bias, kp = refs[12 + tiles : 22 + tiles]
-    q_ref, w_ref, conv_ref, cot_ref, sems = refs[22 + tiles :]
+    out_ref, att_ref, lse_ref, dhid_ref, keep_ref, give_ref = refs[7 + tiles : 13 + tiles]
+    qx, kx, vx, ax, lx, hid, cotx, dm, bias, kp, parts = refs[13 + tiles : 24 + tiles]
+    q_ref, w_ref, conv_ref, cot_ref, sems = refs[24 + tiles :]
 
     att = q_ref.shape[1]
     width = w_ref.shape[1]
@@ -177,44 +188,56 @@
 
     lax.fori_loop(0, width // LANES, convolve, 0)
 
-    pieces, piece_rows, _ = part_ref.shape
+    _, pieces, piece_rows, _ = parts.shape
     chunks = width // LANES
-    group = att // pieces
+    group = att // (2 * pieces)
+    core = device_ref[1]
     own = ax[edge : edge + rows]
     for part in range(width // step):
         product = dot(own, dhid_ref[:, part * step : (part + 1) * step], TN).astype(jnp.bfloat16)
-        for half in range(2):
-            chunk = 2 * part + half
-            tile = product[:, half * LANES : (half + 1) * LANES]
-            for piece in range(pieces):
-                part_ref[piece, chunk * group : (chunk + 1) * group] = tile[
-                    piece * group : (piece + 1) * group
-                ]
+        for chunk in (2 * part, 2 * part + 1):
+            tile = product[:, (chunk - 2 * part) * LANES : (chunk - 2 * part + 1) * LANES]
+            for half in range(2):
+                for piece in range(pieces):
+                    first = (half * pieces + piece) * group
+                    parts[half, piece, chunk * group : (chunk + 1) * group] = tile[
+                        first : first + group
+                    ]
     rest = jnp.zeros((piece_rows - chunks * (group + 1), LANES), jnp.float32)
-    for piece in range(pieces):
-        row = [kp[chunk, piece : piece + 1] for chunk in range(chunks)]
-        part_ref[piece, chunks * group :] = jnp.concatenate(row + [rest], axis=0).astype(
-            jnp.bfloat16
-        )
-
-
-def unpack_kernel(total_ref, weight_ref, kernel_ref):
-    pieces, piece_rows, _ = total_ref.shape
+    for half in range(2):
+        for piece in range(pieces):
+            tap = half * pieces + piece
+            row = [kp[chunk, tap : tap + 1] for chunk in range(chunks)]
+            row = jnp.concatenate(row + [rest], axis=0).astype(jnp.bfloat16)
+            parts[half, piece, chunks * group :] = row
+    keep_ref[...] = parts[core]
+    give_ref[...] = parts[1 - core]
+
+
+def unpack_kernel(device_ref, near_ref, far_ref, weight_ref, kernel_ref):
+    pieces, piece_rows, _ = near_ref.shape
     att, width = weight_ref.shape
     taps = kernel_ref.shape[0]
     chunks = width // LANES
-    group = att // pieces
-    for piece in range(pieces):
-        for chunk in range(chunks):
-            weight_ref[
-                piece * group : (piece + 1) * group, chunk * LANES : (chunk + 1) * LANES
-            ] = total_ref[piece, chunk * group : (chunk + 1) * group].astype(jnp.float32)
-        if piece < taps:
-            rows = total_ref[piece, chunks * group :].astype(jnp.float32)
-            for chunk in range(chunks):
-                kernel_ref[piece : piece + 1, chunk * LANES : (chunk + 1) * LANES] = rows[
-                    chunk : chunk + 1
-                ]
+    group = att // (2 * pieces)
+    core = device_ref[1]
+
+    def write(refs):
+        for half, ref in enumerate(refs):
+            for piece in range(pieces):
+                tap = half * pieces + piece
+                for chunk in range(chunks):
+                    columns = slice(chunk * LANES, (chunk + 1) * LANES)
+                    tile = ref[piece, chunk * group : (chunk + 1) * group].astype(jnp.float32)
+                    weight_ref[tap * group : (tap + 1) * group, columns] = tile
+                if tap < taps:
+                    row = ref[piece, chunks * group :].astype(jnp.float32)
+                    for chunk in range(chunks):
+                        columns = slice(chunk * LANES, (chunk + 1) * LANES)
+                        kernel_ref[tap : tap + 1, columns] = row[chunk : chunk + 1]
+
+    pl.when(core == 0)(lambda: write((near_ref, far_ref)))
+    pl.when(core != 0)(lambda: write((far_ref, near_ref)))
 
 
 def backward_kernel(context, rows, *refs):
@@ -276,32 +299,19 @@
         dq_ref[:, columns] = (merge_heads(dquery) * scale).astype(jnp.bfloat16)
 
 
-def exchange(x, axis):
-    return lax.all_to_all(x, axis, 0, 0, tiled=True)
-
-
-def summed(x):
-    return jnp.sum(x.astype(jnp.float32), axis=0).astype(x.dtype)
-
-
-def sum_parts(parts):
-    pieces, rows, lanes = parts.shape
-    outer, inner = lax.axis_size("dp"), lax.axis_size("blk")
-    if pieces != outer * inner:
-        return lax.psum(parts, ("dp", "blk"))
-    mine = summed(exchange(parts.reshape(outer, inner * rows, lanes), "dp"))
-    mine = summed(exchange(mine.reshape(inner, rows, lanes), "blk"))
-    mine = exchange(jnp.broadcast_to(mine, (inner, rows, lanes)), "blk")
-    mine = mine.reshape(inner * rows, lanes)
-    mine = exchange(jnp.broadcast_to(mine, (outer, inner * rows, lanes)), "dp")
-    return mine.reshape(pieces, rows, lanes)
+def exchange(x):
+    return lax.all_to_all(x, CHIP_AXES, 0, 0, tiled=True)
+
+
+def other_core(x):
+    return lax.ppermute(x, "core", [(0, 1), (1, 0)])
 
 
 def per_device(queries, key_in, value_in, out_weight, conv_kernel, cotangent):
     bf16, f32 = jnp.bfloat16, jnp.float32
     query, key, value, cot = queries[0], key_in[0], value_in[0], cotangent[0]
-    runs = lax.axis_size("blk")
-    device = lax.axis_index("blk").astype(jnp.int32)[None]
+    runs = lax.axis_size(RUN_AXES)
+    device = lax.axis_index(RUN_AXES).astype(jnp.int32)
     rows, att = query.shape
     width = out_weight.shape[1]
     heads = att // HEAD_DIM
@@ -329,24 +339,27 @@
         scratch_shapes=[pltpu.SemaphoreType.DMA((8 + width // att,))],
         compiler_params=params,
         name="pack",
-    )(key, value, query, cot)
+    )(in_hbm(key), in_hbm(value), in_hbm(query), in_hbm(cot))
     tiles = [own] + [shifted(own, o) for o in range(1, context + 1)]
     far = shifted(far, context + 1)
     near = shifted(near, -1)
 
-    pieces = att // 16
+    pieces = att // 32
+    split = pieces == lax.axis_size(CHIP_AXES)
+    core = lax.axis_index("core").astype(jnp.int32) if split else jnp.int32(0)
+    place = jnp.stack([device, core])
     piece_rows = -(-(chunks * 16 + chunks) // 16) * 16
-    out_frames, attended, log_sums, dhidden, parts = pl.pallas_call(
+    out_frames, attended, log_sums, dhidden, keep, give = pl.pallas_call(
         functools.partial(forward_kernel, context, rows, edge, taps),
         out_shape=(
             jax.ShapeDtypeStruct((rows, width), bf16),
             jax.ShapeDtypeStruct((rows, att), bf16),
             jax.ShapeDtypeStruct((heads, rows), f32),
             jax.ShapeDtypeStruct((rows, width), bf16),
-            jax.ShapeDtypeStruct((pieces, piece_rows, LANES), bf16),
-        ),
+        )
+        + (jax.ShapeDtypeStruct((pieces, piece_rows, LANES), bf16),) * 2,
         in_specs=[smem, hbm] + [vmem] * (3 + context) + [hbm] * 3,
-        out_specs=(vmem,) * 5,
+        out_specs=(vmem,) * 6,
         scratch_shapes=[
             pltpu.VMEM((query_rows, att), bf16),
             pltpu.VMEM((key_rows, att), bf16),
@@ -357,7 +370,8 @@
             pltpu.VMEM((chunks, rows + edge, LANES), f32),
             pltpu.VMEM((rows + edge, LANES), f32),
             pltpu.VMEM((LANES, context * rows + LANES), f32),
-            pltpu.VMEM((chunks, pieces, LANES), f32),
+            pltpu.VMEM((chunks, 2 * pieces, LANES), f32),
+            pltpu.VMEM((2, pieces, piece_rows, LANES), bf16),
             pltpu.VMEM((rows, att), bf16),
             pltpu.VMEM((att, width), bf16),
             pltpu.VMEM((taps, width), f32),
@@ -365,20 +379,9 @@
             pltpu.SemaphoreType.DMA((4,)),
         ],
         compiler_params=params,
+        cost_estimate=cost(8 * 10**9, 10**7),
         name="forward",
-    )(device, query, *tiles, far, near, out_weight, conv_kernel, cot)
-
-    weight_total, kernel_total = pl.pallas_call(
-        unpack_kernel,
-        out_shape=(
-            jax.ShapeDtypeStruct((att, width), f32),
-            jax.ShapeDtypeStruct((taps, width), f32),
-        ),
-        in_specs=[vmem],
-        out_specs=(vmem, vmem),
-        compiler_params=params,
-        name="unpack",
-    )(sum_parts(parts))
+    )(place, in_hbm(query), *tiles, far, near, in_hbm(out_weight), in_hbm(conv_kernel), in_hbm(cot))
 
     outs = pl.pallas_call(
         functools.partial(backward_kernel, context, rows),
@@ -395,13 +398,34 @@
             pltpu.VMEM((context + 1, rows, rows), f32),
         ],
         compiler_params=params,
+        cost_estimate=cost(5 * 10**9, 10**7),
         name="backward",
-    )(device, query, *tiles, attended, log_sums, dhidden, out_weight)
+    )(place, query, *tiles, attended, log_sums, dhidden, out_weight)
     query_grad, dkey, dvalue = outs[:3]
-    for offset, message in enumerate(outs[3:], 1):
+    messages = outs[3:]
+    if split:
+        mine = (keep.astype(f32) + other_core(give).astype(f32)).astype(bf16)
+        mine, *messages = lax.optimization_barrier((mine, *messages))
+        mine = jnp.sum(exchange(mine).astype(f32), axis=0).astype(bf16)
+        mine = exchange(jnp.broadcast_to(mine, keep.shape))
+        halves = (mine, other_core(mine))
+    else:
+        halves = lax.psum((keep, give), ("x", "core", "z", "y"))
+    for offset, message in enumerate(messages, 1):
         arrived = shifted(message, -offset).astype(f32)
         dkey = dkey + arrived[:rows]
         dvalue = dvalue + arrived[rows:]
+    weight_total, kernel_total = pl.pallas_call(
+        unpack_kernel,
+        out_shape=(
+            jax.ShapeDtypeStruct((att, width), f32),
+            jax.ShapeDtypeStruct((taps, width), f32),
+        ),
+        in_specs=[smem, vmem, vmem],
+        out_specs=(vmem, vmem),
+        compiler_params=params,
+        name="unpack",
+    )(place, *halves)
     key_grad = dkey.astype(bf16)
     value_grad = dvalue.astype(bf16)
     return (
@@ -415,10 +439,12 @@
 
 
 def solution(mesh):
-    frames = P("dp", "blk", None)
+    sizes = (mesh.shape["dp"] // 2, 2, mesh.shape["blk"] // 2, 2)
+    fine = Mesh(mesh.devices.reshape(sizes), ("x", "core", "z", "y"))
+    frames = P(("x", "core"), RUN_AXES, None)
     return jax.shard_map(
         per_device,
-        mesh=mesh,
+        mesh=fine,
         in_specs=(frames, frames, frames, P(), P(), frames),
         out_specs=(frames, frames, frames, frames, P(), P()),
         check_vma=False,

time: 132 us -> 109 us (0.83); the launches traced: 131 us -> 107 us
  blocking collectives: 53.3 us -> 30.8 us
  local copies, waits for them, and re-layouts: 11.8 us -> 0.9 us
  waiting for transfers between devices: 24 us -> 29.6 us
  Pallas kernels: 18.4 us -> 20.6 us
    all_to_all x3 -> x1, blocking collectives: 53.3 us -> 30.8 us  [exchange(): return lax.all_to_all(x, CHIP_AXES, 0, 0, tiled=True)]
    all_to_all x1, waiting for transfers between devices: 0.01 us -> 14 us  [exchange(): return lax.all_to_all(x, CHIP_AXES, 0, 0, tiled=True)]
    unnamed x32 -> x4, local copies, waits for them, and re-layouts: 10.6 us -> 0.01 us
    ppermute x6 -> x8, waiting for transfers between devices: 24 us -> 15.6 us  [the longest x6 15.6 us: shifted(): lax.ppermute(x, RUN_AXES, [(i, i + by) for i in devices if i + by in devi...]
    ppermute x6 -> x8, starting transfers between devices: 17.8 us -> 17.9 us  [the longest x6 17.8 us: shifted(): lax.ppermute(x, RUN_AXES, [(i, i + by) for i in devices if i + by in devi...]
  transfers between devices with their start and end apart: 7 -> 9, of which waited for: 4 -> 5; matrix products, arithmetic and copies ran while one was open for 1% -> 2% of each run, Pallas kernels for 4% -> 6%
where the time goes in v3:
time: 109 us; the launch traced here: 107 us
  blocking collectives  30.8 us (28%)
  waiting for transfers between devices  29.6 us (27%)
  starting transfers between devices  21.5 us (20%)
  Pallas kernels  20.6 us (19%)
  other arithmetic  2.46 us (2%)
    all_to_all x1, blocking collectives, exchange(): return lax.all_to_all(x, CHIP_AXES, 0, 0, tiled=True)  30.8 us
    ppermute x6, starting transfers between devices, shifted(): lax.ppermute(x, RUN_AXES, [(i, i + by) for i in devices if i + by in devi...  17.8 us
    ppermute x6, waiting for transfers between devices, shifted(): lax.ppermute(x, RUN_AXES, [(i, i + by) for i in devices if i + by in devi...  15.6 us
    all_to_all x1, waiting for transfers between devices, exchange(): return lax.all_to_all(x, CHIP_AXES, 0, 0, tiled=True)  14 us
    pallas_call x1, Pallas kernels, per_device(): pl.pallas_call(functools.partial(forward_kernel, context, rows, edge, tap...  11.4 us
    pallas_call x1, Pallas kernels, per_device(): pl.pallas_call(functools.partial(backward_kernel, context, rows), out_sha...  6 us
    all_to_all x1, starting transfers between devices, exchange(): return lax.all_to_all(x, CHIP_AXES, 0, 0, tiled=True)  3.58 us
  transfers between devices with their start and end apart: 9, of which 5 were waited for; matrix products, arithmetic and copies ran while one was open for 2% of the time, Pallas kernels for 6%

profile of v3, /device:TPU:0, one launch (start us, length us, event | category | flops | bytes accessed | tf_op | source)
XLA Modules:
  0.0 106.6 jit_solution(10819980067987527824)
XLA Ops:
  0.6 1.1 %pack.1 = (bf16[416,512]{1,0:T(8,128)(2,1)S(1)}, bf16[64,512]{1,0:T(8,128)(2,1)S(1)}, bf16[160,512]{1,0:T(8,128)(2,1)S(1)}) custom-call(bf16[192,512]{1,0:T(8,128)(2,1)} %bitcast.17, bf16[192,512]{1,0:T(8,128)(2,1)} %bitcast.18, bf16[192,512]{1,0:T(8,128)(2,1)} %bitcast.12, bf16[192,1024]{1,0:T(8,128)(2,1)} %bitcast.15), custom_call_target="tpu_custom_call" | custom-call | tf_op jit(solution)/shard_map/pack/pallas_call | solution.py:330
  1.8 5.0 %collective-permute-start.1 = (bf16[416,512]{1,0:T(8,128)(2,1)S(1)}, bf16[416,512]{1,0:T(8,128)(2,1)S(1)}, u32[]{:S(2)}, u32[]{:S(2)}) collective-permute-start(bf16[416,512]{1,0:T(8,128)(2,1)S(1)} %get-tuple-element.25.refs_2_), channel_id=1, source_target_pairs={{0,2},{1,3},{2,4},{3,5},{4,6},{5,7},{8,10},{9,11},{10,12},{11,13},... | collective-permute-start | bytes 1277960 | tf_op jit(solution)/shard_map/ppermute | solution.py:31
  6.7 3.5 %collective-permute-start = (bf16[416,512]{1,0:T(8,128)(2,1)S(1)}, bf16[416,512]{1,0:T(8,128)(2,1)S(1)}, u32[]{:S(2)}, u32[]{:S(2)}) collective-permute-start(bf16[416,512]{1,0:T(8,128)(2,1)S(1)} %get-tuple-element.25.refs_2_), channel_id=1, source_target_pairs={{0,1},{1,2},{2,3},{3,4},{4,5},{5,6},{6,7},{8,9},{9,10},{10,11},{11... | collective-permute-start | bytes 1277960 | tf_op jit(solution)/shard_map/ppermute | solution.py:31
  10.2 1.3 %collective-permute-start.3 = (bf16[160,512]{1,0:T(8,128)(2,1)S(1)}, bf16[160,512]{1,0:T(8,128)(2,1)S(1)}, u32[]{:S(2)}, u32[]{:S(2)}) collective-permute-start(bf16[160,512]{1,0:T(8,128)(2,1)S(1)} %get-tuple-element.27), channel_id=1, source_target_pairs={{1,0},{2,1},{3,2},{4,3},{5,4},{6,5},{7,6},{9,8},{10,9},{11,10},{12... | collective-permute-start | bytes 491528 | tf_op jit(solution)/shard_map/ppermute | solution.py:31
  11.5 5.5 %collective-permute-start.2 = (bf16[64,512]{1,0:T(8,128)(2,1)S(1)}, bf16[64,512]{1,0:T(8,128)(2,1)S(1)}, u32[]{:S(2)}, u32[]{:S(2)}) collective-permute-start(bf16[64,512]{1,0:T(8,128)(2,1)S(1)} %get-tuple-element.26), channel_id=1, source_target_pairs={{0,3},{1,4},{2,5},{3,6},{4,7},{8,11},{9,12},{10,13},{11,14},{12,15... | collective-permute-start | bytes 196616 | tf_op jit(solution)/shard_map/ppermute | solution.py:31
  17.0 0.1 pad_add_fusion.refs_0_.device_ref
  17.1 0.0 copy-start
  17.1 0.0 copy-start.1
  17.1 1.8 %collective-permute-done.2.refs_5_ = bf16[64,512]{1,0:T(8,128)(2,1)S(1)} collective-permute-done((bf16[64,512]{1,0:T(8,128)(2,1)S(1)}, bf16[64,512]{1,0:T(8,128)(2,1)S(1)}, u32[]{:S(2)}, u32[]{:S(2)}) %collective-permute-start.2) | collective-permute-done | bytes 65568 | tf_op jit(solution)/shard_map/ppermute | solution.py:31
  18.9 0.0 collective-permute-done.3.refs_6_
  18.9 0.0 collective-permute-done.1.refs_4_
  18.9 3.5 %collective-permute-done.refs_3_ = bf16[416,512]{1,0:T(8,128)(2,1)S(1)} collective-permute-done((bf16[416,512]{1,0:T(8,128)(2,1)S(1)}, bf16[416,512]{1,0:T(8,128)(2,1)S(1)}, u32[]{:S(2)}, u32[]{:S(2)}) %collective-permute-start) | collective-permute-done | bytes 426016 | tf_op jit(solution)/shard_map/ppermute | solution.py:31
  22.5 11.4 %forward.1 = (bf16[192,1024]{1,0:T(8,128)(2,1)}, bf16[192,512]{1,0:T(8,128)(2,1)S(1)}, f32[8,192]{1,0:T(8,128)S(1)}, bf16[192,1024]{1,0:T(8,128)(2,1)S(1)}, bf16...) custom-call(s32[2]{0:T(128)S(1)} %pad_add_fusion.refs_0_.device_ref, bf16[192,512]{1,0:T(8,128)(2,1)} %bitcast.13, ...), custom_call_target="tpu_custom_call" | custom-call | flops 8000000000 | bytes 10000000 | tf_op jit(solution)/shard_map/forward/pallas_call | solution.py:352
  33.8 0.1 collective-permute-start.4
  33.9 0.0 copy-done
  33.9 0.0 copy-done.1
  33.9 6.0 %backward.1 = (bf16[192,512]{1,0:T(8,128)(2,1)}, f32[192,512]{1,0:T(8,128)S(1)}, f32[192,512]{1,0:T(8,128)S(1)}, bf16[384,512]{1,0:T(8,128)(2,1)S(1)}, bf16[384,512]{1,0:T(8,128)(2,1)S(1)}) custom-call(s32[2]{0:T(128)S(1)} %pad_add_fusion.refs_0_.device_ref, bf16[192,512]{1,0:T(8,128)(2,1)S(1)} %bitcast.14, bf16[416,512]{1,0:T(8,128)(2,1)S(1)} %get-tuple-element.25.refs_2_, ...), custom_call_target="tpu_custom_call" | custom-call | flops 5000000000 | bytes 10000000 | tf_op jit(solution)/shard_map/backward/pallas_call | solution.py:386
  39.9 0.0 collective-permute-done.4
  39.9 0.2 add_convert_fusion
  40.1 30.8 %all_to_all.10 = bf16[16,144,128]{2,1,0:T(8,128)(2,1)S(1)} all-to-all(bf16[16,144,128]{2,1,0:T(8,128)(2,1)S(1)} %add_convert_fusion), channel_id=1, replica_groups=mesh['x'=2,'core'=2,'z'=4,'y'=2] {'x','z','y'}, dimensions={0} | all-to-all | bytes 1179648 | tf_op jit(solution)/shard_map/all_to_all | solution.py:303
  70.9 0.1 reduce_sum.12
  71.0 0.9 broadcast_in_dim.19
  71.9 3.6 %all-to-all-start.1 = ((bf16[16,144,128]{2,1,0:T(8,128)(2,1)}), bf16[16,144,128]{2,1,0:T(8,128)(2,1)S(1)}, u32[]{:S(2)}, u32[]{:S(2)}) async-start(bf16[16,144,128]{2,1,0:T(8,128)(2,1)} %broadcast_in_dim.19), calls=%async_computation.1 | async-start | bytes 1179648 | tf_op jit(solution)/shard_map/all_to_all | solution.py:303
  75.5 1.3 %collective-permute-start.5 = (bf16[384,512]{1,0:T(8,128)(2,1)S(1)}, bf16[384,512]{1,0:T(8,128)(2,1)}, u32[]{:S(2)}, u32[]{:S(2)}) collective-permute-start(bf16[384,512]{1,0:T(8,128)(2,1)S(1)} %get-tuple-element.38), channel_id=1, source_target_pairs={{1,0},{2,1},{3,2},{4,3},{5,4},{6,5},{7,6},{9,8},{10,9},{11,10},{12... | collective-permute-start | bytes 1179656 | tf_op jit(solution)/shard_map/ppermute | solution.py:31
  76.8 1.3 %collective-permute-start.6 = (bf16[384,512]{1,0:T(8,128)(2,1)S(1)}, bf16[384,512]{1,0:T(8,128)(2,1)S(1)}, u32[]{:S(2)}, u32[]{:S(2)}) collective-permute-start(bf16[384,512]{1,0:T(8,128)(2,1)S(1)} %get-tuple-element.39), channel_id=1, source_target_pairs={{2,0},{3,1},{4,2},{5,3},{6,4},{7,5},{10,8},{11,9},{12,10},{13,11},... | collective-permute-start | bytes 1179656 | tf_op jit(solution)/shard_map/ppermute | solution.py:31
  78.1 14.0 %all-to-all-done.1.near_ref = bf16[16,144,128]{2,1,0:T(8,128)(2,1)S(1)} async-done(((bf16[16,144,128]{2,1,0:T(8,128)(2,1)}), bf16[16,144,128]{2,1,0:T(8,128)(2,1)S(1)}, u32[]{:S(2)}, u32[]{:S(2)}) %all-to-all-start.1) | async-done | bytes 589856 | tf_op jit(solution)/shard_map/all_to_all | solution.py:303
  92.1 0.0 collective-permute-start.7
  92.1 0.9 collective-permute-done.5
  93.0 1.1 %convert_element_type.26 = f32[384,512]{1,0:T(8,128)S(1)} convert(bf16[384,512]{1,0:T(8,128)(2,1)} %collective-permute-done.5) | non-fusion elementwise | flops 196608 | bytes 1179648 | tf_op jit(solution)/shard_map/convert_element_type | solution.py:415
  94.1 9.3 %collective-permute-done.6 = bf16[384,512]{1,0:T(8,128)(2,1)S(1)} collective-permute-done((bf16[384,512]{1,0:T(8,128)(2,1)S(1)}, bf16[384,512]{1,0:T(8,128)(2,1)S(1)}, u32[]{:S(2)}, u32[]{:S(2)}) %collective-permute-start.6) | collective-permute-done | bytes 393248 | tf_op jit(solution)/shard_map/ppermute | solution.py:31
  103.4 0.1 convert_element_type.27
  103.5 1.0 fusion.3
  104.5 0.0 collective-permute-done.7.far_ref
  104.5 2.1 %unpack.1 = (f32[512,1024]{1,0:T(8,128)}, f32[31,1024]{1,0:T(8,128)}) custom-call(s32[2]{0:T(128)S(1)} %pad_add_fusion.refs_0_.device_ref, bf16[16,144,128]{2,1,0:T(8,128)(2,1)S(1)} %all-to-all-done.1.near_ref, bf16[16,144,128]{2,1,0:T(8,128)(2,1)S(1)} %collective-permute-done.7.far_ref), custom_call_target="tpu_custom_call" | custom-call | tf_op jit(solution)/shard_map/unpack/pallas_call | solution.py:418
Async XLA Ops:
  1.8 17.1 %collective-permute-start.1 = (bf16[416,512]{1,0:T(8,128)(2,1)S(1)}, bf16[416,512]{1,0:T(8,128)(2,1)S(1)}, u32[]{:S(2)}, u32[]{:S(2)}) collective-permute-start(bf16[416,512]{1,0:T(8,128)(2,1)S(1)} %get-tuple-element.25.refs_2_), channel_id=1, source_target_pairs={{0,2},{1,3},{2,4},{3,5},{4,6},{5,7},{8,10},{9,11},{10,12},{11,13},... | collective-permute-start | bytes 1277960 | tf_op jit(solution)/shard_map/ppermute | solution.py:31
  6.7 15.7 %collective-permute-start = (bf16[416,512]{1,0:T(8,128)(2,1)S(1)}, bf16[416,512]{1,0:T(8,128)(2,1)S(1)}, u32[]{:S(2)}, u32[]{:S(2)}) collective-permute-start(bf16[416,512]{1,0:T(8,128)(2,1)S(1)} %get-tuple-element.25.refs_2_), channel_id=1, source_target_pairs={{0,1},{1,2},{2,3},{3,4},{4,5},{5,6},{6,7},{8,9},{9,10},{10,11},{11... | collective-permute-start | bytes 1277960 | tf_op jit(solution)/shard_map/ppermute | solution.py:31
  10.2 8.7 %collective-permute-start.3 = (bf16[160,512]{1,0:T(8,128)(2,1)S(1)}, bf16[160,512]{1,0:T(8,128)(2,1)S(1)}, u32[]{:S(2)}, u32[]{:S(2)}) collective-permute-start(bf16[160,512]{1,0:T(8,128)(2,1)S(1)} %get-tuple-element.27), channel_id=1, source_target_pairs={{1,0},{2,1},{3,2},{4,3},{5,4},{6,5},{7,6},{9,8},{10,9},{11,10},{12... | collective-permute-start | bytes 491528 | tf_op jit(solution)/shard_map/ppermute | solution.py:31
  11.5 7.4 %collective-permute-start.2 = (bf16[64,512]{1,0:T(8,128)(2,1)S(1)}, bf16[64,512]{1,0:T(8,128)(2,1)S(1)}, u32[]{:S(2)}, u32[]{:S(2)}) collective-permute-start(bf16[64,512]{1,0:T(8,128)(2,1)S(1)} %get-tuple-element.26), channel_id=1, source_target_pairs={{0,3},{1,4},{2,5},{3,6},{4,7},{8,11},{9,12},{10,13},{11,14},{12,15... | collective-permute-start | bytes 196616 | tf_op jit(solution)/shard_map/ppermute | solution.py:31
  17.1 16.8 %copy-start = (bf16[1,192,512]{2,1,0:T(8,128)(2,1)S(1)}, bf16[1,192,512]{2,1,0:T(8,128)(2,1)}, u32[]{:S(2)}) copy-start(bf16[1,192,512]{2,1,0:T(8,128)(2,1)} %param.6) | copy-start | bytes 589828
  17.1 16.8 %copy-start.1 = (bf16[512,1024]{1,0:T(8,128)(2,1)S(1)}, bf16[512,1024]{1,0:T(8,128)(2,1)}, u32[]{:S(2)}) copy-start(bf16[512,1024]{1,0:T(8,128)(2,1)} %refs_8_.3) | copy-start | bytes 3145732
  33.8 6.1 %collective-permute-start.4 = (bf16[16,144,128]{2,1,0:T(8,128)(2,1)S(1)}, bf16[16,144,128]{2,1,0:T(8,128)(2,1)S(1)}, u32[]{:S(2)}, u32[]{:S(2)}) collective-permute-start(bf16[16,144,128]{2,1,0:T(8,128)(2,1)S(1)} %get-tuple-element.35), channel_id=1, source_target_pairs={{0,8},{8,0},{1,9},{9,1},{2,10},{10,2},{3,11},{11,3},{4,12},{12,4},... | collective-permute-start | bytes 1769480 | tf_op jit(solution)/shard_map/ppermute | solution.py:307
  71.9 20.2 %all-to-all-start.1 = ((bf16[16,144,128]{2,1,0:T(8,128)(2,1)}), bf16[16,144,128]{2,1,0:T(8,128)(2,1)S(1)}, u32[]{:S(2)}, u32[]{:S(2)}) async-start(bf16[16,144,128]{2,1,0:T(8,128)(2,1)} %broadcast_in_dim.19), calls=%async_computation.1 | async-start | bytes 1179648 | tf_op jit(solution)/shard_map/all_to_all | solution.py:303
  75.5 17.5 %collective-permute-start.5 = (bf16[384,512]{1,0:T(8,128)(2,1)S(1)}, bf16[384,512]{1,0:T(8,128)(2,1)}, u32[]{:S(2)}, u32[]{:S(2)}) collective-permute-start(bf16[384,512]{1,0:T(8,128)(2,1)S(1)} %get-tuple-element.38), channel_id=1, source_target_pairs={{1,0},{2,1},{3,2},{4,3},{5,4},{6,5},{7,6},{9,8},{10,9},{11,10},{12... | collective-permute-start | bytes 1179656 | tf_op jit(solution)/shard_map/ppermute | solution.py:31
  76.8 26.6 %collective-permute-start.6 = (bf16[384,512]{1,0:T(8,128)(2,1)S(1)}, bf16[384,512]{1,0:T(8,128)(2,1)S(1)}, u32[]{:S(2)}, u32[]{:S(2)}) collective-permute-start(bf16[384,512]{1,0:T(8,128)(2,1)S(1)} %get-tuple-element.39), channel_id=1, source_target_pairs={{2,0},{3,1},{4,2},{5,3},{6,4},{7,5},{10,8},{11,9},{12,10},{13,11},... | collective-permute-start | bytes 1179656 | tf_op jit(solution)/shard_map/ppermute | solution.py:31
  92.1 12.4 %collective-permute-start.7 = (bf16[16,144,128]{2,1,0:T(8,128)(2,1)S(1)}, bf16[16,144,128]{2,1,0:T(8,128)(2,1)S(1)}, u32[]{:S(2)}, u32[]{:S(2)}) collective-permute-start(bf16[16,144,128]{2,1,0:T(8,128)(2,1)S(1)} %all-to-all-done.1.near_ref), channel_id=1, source_target_pairs={{0,8},{8,0},{1,9},{9,1},{2,10},{10,2},{3,11},{11,3},{4,12},{12,4},... | collective-permute-start | bytes 1769480 | tf_op jit(solution)/shard_map/ppermute | solution.py:307

commit v4 on v3

--- a/solution.py
+++ b/solution.py
@@ -14,7 +14,8 @@
 LANES = 128
 NEGATIVE = -1e30
 RUN_AXES = ("z", "y")
-CHIP_AXES = ("x", "z", "y")
+PLANE_AXES = ("x", "y")
+CHIP_AXES = ("x", "y", "z")
 VMEM_LIMIT = 40 * 1024 * 1024
 
 NN = (((1,), (0,)), ((), ()))
@@ -245,9 +246,9 @@
     device_ref, q_ref = refs[:2]
     own_refs = refs[2 : 2 + tiles]
     att_ref, lse_ref, dhid_ref, w_ref = refs[2 + tiles : 6 + tiles]
-    dq_ref, dk_ref, dv_ref = refs[6 + tiles : 9 + tiles]
-    message_refs = refs[9 + tiles : 9 + tiles + context]
-    datt, bias = refs[9 + tiles + context :]
+    dq_ref, own_ref = refs[6 + tiles : 8 + tiles]
+    message_refs = refs[8 + tiles : 8 + tiles + context]
+    datt, bias = refs[8 + tiles + context :]
 
     att = q_ref.shape[1]
     heads = att // HEAD_DIM
@@ -290,17 +291,31 @@
             dvalue = dot(probs.astype(jnp.bfloat16), ds, NN)
             dkey = dot(dscores, qs, NN)
             dquery += dot(dscores, kp, TN)
-            if offset == 0:
-                dk_ref[:, columns] = dkey
-                dv_ref[:, columns] = dvalue
-            else:
-                message_refs[offset - 1][:rows, columns] = dkey.astype(jnp.bfloat16)
-                message_refs[offset - 1][rows:, columns] = dvalue.astype(jnp.bfloat16)
+            target = message_refs[offset - 1] if offset else own_ref
+            target[:rows, columns] = dkey.astype(target.dtype)
+            target[rows:, columns] = dvalue.astype(target.dtype)
         dq_ref[:, columns] = (merge_heads(dquery) * scale).astype(jnp.bfloat16)
 
 
-def exchange(x):
-    return lax.all_to_all(x, CHIP_AXES, 0, 0, tiled=True)
+def merge_kernel(*refs):
+    own_ref, *message_refs, dk_ref, dv_ref = refs
+    rows = dk_ref.shape[0]
+    total = own_ref[...]
+    for message_ref in message_refs:
+        total += message_ref[...].astype(jnp.float32)
+    total = total.astype(jnp.bfloat16)
+    dk_ref[...] = total[:rows]
+    dv_ref[...] = total[rows:]
+
+
+def exchange(x, axes):
+    return lax.all_to_all(x, axes, 0, 0, tiled=True)
+
+
+def collected(x, axes):
+    parts = lax.axis_size(axes)
+    x = exchange(x.reshape(parts, -1, LANES), axes)
+    return jnp.sum(x.astype(jnp.float32), axis=0).astype(x.dtype)
 
 
 def other_core(x):
@@ -383,38 +398,42 @@
         name="forward",
     )(place, in_hbm(query), *tiles, far, near, in_hbm(out_weight), in_hbm(conv_kernel), in_hbm(cot))
 
-    outs = pl.pallas_call(
+    if split:
+        mine = (keep.astype(f32) + other_core(give).astype(f32)).astype(bf16)
+        mine, dhidden = lax.optimization_barrier((mine, dhidden))
+    query_grad, own_grads, *messages = pl.pallas_call(
         functools.partial(backward_kernel, context, rows),
         out_shape=(
             jax.ShapeDtypeStruct((rows, att), bf16),
-            jax.ShapeDtypeStruct((rows, att), f32),
-            jax.ShapeDtypeStruct((rows, att), f32),
+            jax.ShapeDtypeStruct((2 * rows, att), f32),
         )
         + (jax.ShapeDtypeStruct((2 * rows, att), bf16),) * context,
         in_specs=[smem] + [vmem] * (6 + context),
-        out_specs=(vmem,) * (3 + context),
+        out_specs=(vmem,) * (2 + context),
         scratch_shapes=[
             pltpu.VMEM((rows, att), bf16),
             pltpu.VMEM((context + 1, rows, rows), f32),
         ],
         compiler_params=params,
-        cost_estimate=cost(5 * 10**9, 10**7),
+        cost_estimate=cost(6 * 10**9, 10**7),
         name="backward",
     )(place, query, *tiles, attended, log_sums, dhidden, out_weight)
-    query_grad, dkey, dvalue = outs[:3]
-    messages = outs[3:]
+    messages = [shifted(message, -offset) for offset, message in enumerate(messages, 1)]
     if split:
-        mine = (keep.astype(f32) + other_core(give).astype(f32)).astype(bf16)
+        mine = collected(collected(mine, PLANE_AXES), "z")
         mine, *messages = lax.optimization_barrier((mine, *messages))
-        mine = jnp.sum(exchange(mine).astype(f32), axis=0).astype(bf16)
-        mine = exchange(jnp.broadcast_to(mine, keep.shape))
+        mine = exchange(jnp.broadcast_to(mine, keep.shape), CHIP_AXES)
         halves = (mine, other_core(mine))
     else:
         halves = lax.psum((keep, give), ("x", "core", "z", "y"))
-    for offset, message in enumerate(messages, 1):
-        arrived = shifted(message, -offset).astype(f32)
-        dkey = dkey + arrived[:rows]
-        dvalue = dvalue + arrived[rows:]
+    key_grad, value_grad = pl.pallas_call(
+        merge_kernel,
+        out_shape=(jax.ShapeDtypeStruct((rows, att), bf16),) * 2,
+        in_specs=[vmem] * (1 + context),
+        out_specs=(vmem,) * 2,
+        compiler_params=params,
+        name="merge",
+    )(own_grads, *messages)
     weight_total, kernel_total = pl.pallas_call(
         unpack_kernel,
         out_shape=(
@@ -426,8 +445,6 @@
         compiler_params=params,
         name="unpack",
     )(place, *halves)
-    key_grad = dkey.astype(bf16)
-    value_grad = dvalue.astype(bf16)
     return (
         out_frames[None],
         query_grad[None],

time: 109 us -> 107 us (0.982); the launches traced: 107 us -> 106 us
  waiting for transfers between devices: 29.6 us -> 8.53 us
  blocking collectives: 30.8 us -> 45.7 us
  starting transfers between devices: 21.5 us -> 25.4 us
  Pallas kernels: 20.6 us -> 21.8 us
  local copies, waits for them, and re-layouts: 0.9 us -> 2.02 us
    all_to_all x1 -> x2, blocking collectives: 30.8 us -> 45.7 us  [exchange(): return lax.all_to_all(x, axes, 0, 0, tiled=True)]
    all_to_all x1, waiting for transfers between devices: 14 us -> 0.01 us  [exchange(): return lax.all_to_all(x, axes, 0, 0, tiled=True)]
    ppermute x6, waiting for transfers between devices: 15.6 us -> 5.36 us  [shifted(): lax.ppermute(x, RUN_AXES, [(i, i + by) for i in devices if i + by in devi...]
    all_to_all x1, starting transfers between devices: 3.58 us -> 7.58 us  [exchange(): return lax.all_to_all(x, axes, 0, 0, tiled=True)]
    ppermute x2, waiting for transfers between devices: 0.01 us -> 3.18 us  [other_core(): return lax.ppermute(x, 'core', [(0, 1), (1, 0)])]
    unnamed x4 -> x12, local copies, waits for them, and re-layouts: 0.01 us -> 1.94 us
    convert_element_type x2 -> x0, other arithmetic: 1.16 us -> none  [per_device(): arrived = shifted(message, -offset).astype(f32)]
    reduce_sum x1 -> x2, other arithmetic: 0.09 us -> 1.19 us  [collected(): return jnp.sum(x.astype(jnp.float32), axis=0).astype(x.dtype)]
  transfers between devices with their start and end apart: 9 -> 9, of which waited for: 5 -> 4; matrix products, arithmetic and copies ran while one was open for 2% -> 1% of each run, Pallas kernels for 6% -> 6%
where the time goes in v4:
time: 107 us; the launch traced here: 106 us
  blocking collectives  45.7 us (43%)
  starting transfers between devices  25.4 us (24%)
  Pallas kernels  21.8 us (20%)
  waiting for transfers between devices  8.53 us (8%)
  other arithmetic  2.24 us (2%)
  local copies, waits for them, and re-layouts  2.02 us (2%)
    all_to_all x2, blocking collectives, exchange(): return lax.all_to_all(x, axes, 0, 0, tiled=True)  45.7 us
    ppermute x6, starting transfers between devices, shifted(): lax.ppermute(x, RUN_AXES, [(i, i + by) for i in devices if i + by in devi...  17.8 us
    pallas_call x1, Pallas kernels, per_device(): pl.pallas_call(functools.partial(forward_kernel, context, rows, edge, tap...  11.7 us
    all_to_all x1, starting transfers between devices, exchange(): return lax.all_to_all(x, axes, 0, 0, tiled=True)  7.58 us
    pallas_call x1, Pallas kernels, per_device(): pl.pallas_call(functools.partial(backward_kernel, context, rows), out_sha...  6 us
    ppermute x6, waiting for transfers between devices, shifted(): lax.ppermute(x, RUN_AXES, [(i, i + by) for i in devices if i + by in devi...  5.36 us
    ppermute x2, waiting for transfers between devices, other_core(): return lax.ppermute(x, 'core', [(0, 1), (1, 0)])  3.18 us
  transfers between devices with their start and end apart: 9, of which 4 were waited for; matrix products, arithmetic and copies ran while one was open for 1% of the time, Pallas kernels for 6%

profile of v4, /device:TPU:0, one launch (start us, length us, event | category | flops | bytes accessed | tf_op | source)
XLA Modules:
  0.0 106.5 jit_solution(11975145456141009630)
XLA Ops:
  0.6 1.1 %pack.1 = (bf16[416,512]{1,0:T(8,128)(2,1)S(1)}, bf16[64,512]{1,0:T(8,128)(2,1)S(1)}, bf16[160,512]{1,0:T(8,128)(2,1)S(1)}) custom-call(bf16[192,512]{1,0:T(8,128)(2,1)} %bitcast.18, bf16[192,512]{1,0:T(8,128)(2,1)} %bitcast.19, bf16[192,512]{1,0:T(8,128)(2,1)} %bitcast.12, bf16[192,1024]{1,0:T(8,128)(2,1)} %bitcast.16), custom_call_target="tpu_custom_call" | custom-call | tf_op jit(solution)/shard_map/pack/pallas_call | solution.py:345
  1.8 5.0 %collective-permute-start.1 = (bf16[416,512]{1,0:T(8,128)(2,1)S(1)}, bf16[416,512]{1,0:T(8,128)(2,1)S(1)}, u32[]{:S(2)}, u32[]{:S(2)}) collective-permute-start(bf16[416,512]{1,0:T(8,128)(2,1)S(1)} %get-tuple-element.28.refs_2_), channel_id=1, source_target_pairs={{0,2},{1,3},{2,4},{3,5},{4,6},{5,7},{8,10},{9,11},{10,12},{11,13},... | collective-permute-start | bytes 1277960 | tf_op jit(solution)/shard_map/ppermute | solution.py:32
  6.7 3.5 %collective-permute-start = (bf16[416,512]{1,0:T(8,128)(2,1)S(1)}, bf16[416,512]{1,0:T(8,128)(2,1)S(1)}, u32[]{:S(2)}, u32[]{:S(2)}) collective-permute-start(bf16[416,512]{1,0:T(8,128)(2,1)S(1)} %get-tuple-element.28.refs_2_), channel_id=1, source_target_pairs={{0,1},{1,2},{2,3},{3,4},{4,5},{5,6},{6,7},{8,9},{9,10},{10,11},{11... | collective-permute-start | bytes 1277960 | tf_op jit(solution)/shard_map/ppermute | solution.py:32
  10.2 1.3 %collective-permute-start.3 = (bf16[160,512]{1,0:T(8,128)(2,1)S(1)}, bf16[160,512]{1,0:T(8,128)(2,1)S(1)}, u32[]{:S(2)}, u32[]{:S(2)}) collective-permute-start(bf16[160,512]{1,0:T(8,128)(2,1)S(1)} %get-tuple-element.30), channel_id=1, source_target_pairs={{1,0},{2,1},{3,2},{4,3},{5,4},{6,5},{7,6},{9,8},{10,9},{11,10},{12... | collective-permute-start | bytes 491528 | tf_op jit(solution)/shard_map/ppermute | solution.py:32
  11.5 5.5 %collective-permute-start.2 = (bf16[64,512]{1,0:T(8,128)(2,1)S(1)}, bf16[64,512]{1,0:T(8,128)(2,1)S(1)}, u32[]{:S(2)}, u32[]{:S(2)}) collective-permute-start(bf16[64,512]{1,0:T(8,128)(2,1)S(1)} %get-tuple-element.29), channel_id=1, source_target_pairs={{0,3},{1,4},{2,5},{3,6},{4,7},{8,11},{9,12},{10,13},{11,14},{12,15... | collective-permute-start | bytes 196616 | tf_op jit(solution)/shard_map/ppermute | solution.py:32
  17.0 0.1 pad_add_fusion.refs_0_.device_ref
  17.1 1.8 %collective-permute-done.2.refs_5_ = bf16[64,512]{1,0:T(8,128)(2,1)S(1)} collective-permute-done((bf16[64,512]{1,0:T(8,128)(2,1)S(1)}, bf16[64,512]{1,0:T(8,128)(2,1)S(1)}, u32[]{:S(2)}, u32[]{:S(2)}) %collective-permute-start.2) | collective-permute-done | bytes 65568 | tf_op jit(solution)/shard_map/ppermute | solution.py:32
  18.9 0.0 collective-permute-done.3.refs_6_
  18.9 0.0 collective-permute-done.1.refs_4_
  18.9 3.5 %collective-permute-done.refs_3_ = bf16[416,512]{1,0:T(8,128)(2,1)S(1)} collective-permute-done((bf16[416,512]{1,0:T(8,128)(2,1)S(1)}, bf16[416,512]{1,0:T(8,128)(2,1)S(1)}, u32[]{:S(2)}, u32[]{:S(2)}) %collective-permute-start) | collective-permute-done | bytes 426016 | tf_op jit(solution)/shard_map/ppermute | solution.py:32
  22.5 11.7 %forward.1 = (bf16[192,1024]{1,0:T(8,128)(2,1)}, bf16[192,512]{1,0:T(8,128)(2,1)S(1)}, f32[8,192]{1,0:T(8,128)S(1)}, bf16[192,1024]{1,0:T(8,128)(2,1)S(1)}, bf16...) custom-call(s32[2]{0:T(128)S(1)} %pad_add_fusion.refs_0_.device_ref, bf16[192,512]{1,0:T(8,128)(2,1)} %bitcast.13, ...), custom_call_target="tpu_custom_call" | custom-call | flops 8000000000 | bytes 10000000 | tf_op jit(solution)/shard_map/forward/pallas_call | solution.py:367
  34.2 0.0 copy-start.2
  34.2 0.0 copy-start.4
  34.2 0.1 collective-permute-start.4
  34.3 2.0 %collective-permute-done.4 = bf16[16,144,128]{2,1,0:T(8,128)(2,1)S(1)} collective-permute-done((bf16[16,144,128]{2,1,0:T(8,128)(2,1)S(1)}, bf16[16,144,128]{2,1,0:T(8,128)(2,1)S(1)}, u32[]{:S(2)}, u32[]{:S(2)}) %collective-permute-start.4) | collective-permute-done | bytes 589856 | tf_op jit(solution)/shard_map/ppermute | solution.py:322
  36.3 0.0 copy-start
  36.3 0.0 copy-start.1
  36.3 1.0 add_convert_fusion
  37.3 0.0 copy-done.2
  37.3 0.0 copy-done.4
  37.3 7.6 %all-to-all-start = ((bf16[4,576,128]{2,1,0:T(8,128)(2,1)}), bf16[4,576,128]{2,1,0:T(8,128)(2,1)}, u32[]{:S(2)}, u32[]{:S(2)}) async-start(bf16[4,576,128]{2,1,0:T(8,128)(2,1)} %bitcast.8), calls=%async_computation | async-start | bytes 1179648 | tf_op jit(solution)/shard_map/all_to_all | solution.py:312
  44.9 0.0 copy-done
  44.9 0.0 copy-done.1
  44.9 0.0 copy-start.3
  44.9 1.0 copy-done.3
  45.9 0.0 copy-start.5
  45.9 0.9 copy-done.5
  46.8 6.0 %backward.1 = (bf16[192,512]{1,0:T(8,128)(2,1)}, f32[384,512]{1,0:T(8,128)S(1)}, bf16[384,512]{1,0:T(8,128)(2,1)}, bf16[384,512]{1,0:T(8,128)(2,1)}) custom-call(s32[2]{0:T(128)S(1)} %pad_add_fusion.refs_0_.device_ref, bf16[192,512]{1,0:T(8,128)(2,1)S(1)} %bitcast.14, bf16[416,512]{1,0:T(8,128)(2,1)S(1)} %get-tuple-element.28.refs_2_, ...), custom_call_target="tpu_custom_call" | custom-call | flops 6000000000 | bytes 10000000 | tf_op jit(solution)/shard_map/backward/pallas_call | solution.py:404
  52.8 1.3 %collective-permute-start.5 = (bf16[384,512]{1,0:T(8,128)(2,1)}, bf16[384,512]{1,0:T(8,128)(2,1)S(1)}, u32[]{:S(2)}, u32[]{:S(2)}) collective-permute-start(bf16[384,512]{1,0:T(8,128)(2,1)} %get-tuple-element.41), channel_id=1, source_target_pairs={{1,0},{2,1},{3,2},{4,3},{5,4},{6,5},{7,6},{9,8},{10,9},{11,10},{12... | collective-permute-start | bytes 1179656 | tf_op jit(solution)/shard_map/ppermute | solution.py:32
  54.1 1.3 %collective-permute-start.6 = (bf16[384,512]{1,0:T(8,128)(2,1)}, bf16[384,512]{1,0:T(8,128)(2,1)S(1)}, u32[]{:S(2)}, u32[]{:S(2)}) collective-permute-start(bf16[384,512]{1,0:T(8,128)(2,1)} %get-tuple-element.42), channel_id=1, source_target_pairs={{2,0},{3,1},{4,2},{5,3},{6,4},{7,5},{10,8},{11,9},{12,10},{13,11},... | collective-permute-start | bytes 1179656 | tf_op jit(solution)/shard_map/ppermute | solution.py:32
  55.4 0.0 all-to-all-done
  55.4 1.2 %reduce_sum.24 = bf16[576,128]{1,0:T(8,128)(2,1)S(1)} reduce(bf16[4,576,128]{2,1,0:T(8,128)(2,1)} %all-to-all-done, bf16[]{:T(256)} %constant.16.clone.1), dimensions={0}, to_apply=%region_0.0 | reduce | flops 221184 | bytes 737282 | tf_op jit(solution)/shard_map/reduce_sum | solution.py:318
  56.6 26.3 %all_to_all.15 = bf16[4,144,128]{2,1,0:T(8,128)(2,1)S(1)} all-to-all(bf16[4,144,128]{2,1,0:T(8,128)(2,1)S(1)} %bitcast.15), channel_id=1, replica_groups=mesh['x'=2,'core'=2,'z'=4,'y'=2] {'z'}, dimensions={0} | all-to-all | bytes 294912 | tf_op jit(solution)/shard_map/all_to_all | solution.py:312
  82.9 0.0 collective-permute-done.5.refs_1_
  82.9 0.0 collective-permute-done.6.refs_2_
  82.9 0.1 broadcast_in_dim.19
  83.0 19.4 %all_to_all.16.near_ref = bf16[16,144,128]{2,1,0:T(8,128)(2,1)S(1)} all-to-all(bf16[16,144,128]{2,1,0:T(8,128)(2,1)S(1)} %broadcast_in_dim.19), channel_id=1, replica_groups=mesh['x'=2,'core'=2,'z'=4,'y'=2] {'x','y','z'}, dimensions={0} | all-to-all | bytes 1179648 | tf_op jit(solution)/shard_map/all_to_all | solution.py:312
  102.4 0.0 collective-permute-start.7
  102.4 0.8 merge.1
  103.2 1.2 %collective-permute-done.7.far_ref = bf16[16,144,128]{2,1,0:T(8,128)(2,1)S(1)} collective-permute-done((bf16[16,144,128]{2,1,0:T(8,128)(2,1)S(1)}, bf16[16,144,128]{2,1,0:T(8,128)(2,1)S(1)}, u32[]{:S(2)}, u32[]{:S(2)}) %collective-permute-start.7) | collective-permute-done | bytes 589856 | tf_op jit(solution)/shard_map/ppermute | solution.py:322
  104.4 2.1 %unpack.1 = (f32[512,1024]{1,0:T(8,128)}, f32[31,1024]{1,0:T(8,128)}) custom-call(s32[2]{0:T(128)S(1)} %pad_add_fusion.refs_0_.device_ref, bf16[16,144,128]{2,1,0:T(8,128)(2,1)S(1)} %all_to_all.16.near_ref, bf16[16,144,128]{2,1,0:T(8,128)(2,1)S(1)} %collective-permute-done.7.far_ref), custom_call_target="tpu_custom_call" | custom-call | tf_op jit(solution)/shard_map/unpack/pallas_call | solution.py:437
  (1 shorter events, 0.0 us)
Async XLA Ops:
  1.8 17.1 %collective-permute-start.1 = (bf16[416,512]{1,0:T(8,128)(2,1)S(1)}, bf16[416,512]{1,0:T(8,128)(2,1)S(1)}, u32[]{:S(2)}, u32[]{:S(2)}) collective-permute-start(bf16[416,512]{1,0:T(8,128)(2,1)S(1)} %get-tuple-element.28.refs_2_), channel_id=1, source_target_pairs={{0,2},{1,3},{2,4},{3,5},{4,6},{5,7},{8,10},{9,11},{10,12},{11,13},... | collective-permute-start | bytes 1277960 | tf_op jit(solution)/shard_map/ppermute | solution.py:32
  6.7 15.7 %collective-permute-start = (bf16[416,512]{1,0:T(8,128)(2,1)S(1)}, bf16[416,512]{1,0:T(8,128)(2,1)S(1)}, u32[]{:S(2)}, u32[]{:S(2)}) collective-permute-start(bf16[416,512]{1,0:T(8,128)(2,1)S(1)} %get-tuple-element.28.refs_2_), channel_id=1, source_target_pairs={{0,1},{1,2},{2,3},{3,4},{4,5},{5,6},{6,7},{8,9},{9,10},{10,11},{11... | collective-permute-start | bytes 1277960 | tf_op jit(solution)/shard_map/ppermute | solution.py:32
  10.2 8.7 %collective-permute-start.3 = (bf16[160,512]{1,0:T(8,128)(2,1)S(1)}, bf16[160,512]{1,0:T(8,128)(2,1)S(1)}, u32[]{:S(2)}, u32[]{:S(2)}) collective-permute-start(bf16[160,512]{1,0:T(8,128)(2,1)S(1)} %get-tuple-element.30), channel_id=1, source_target_pairs={{1,0},{2,1},{3,2},{4,3},{5,4},{6,5},{7,6},{9,8},{10,9},{11,10},{12... | collective-permute-start | bytes 491528 | tf_op jit(solution)/shard_map/ppermute | solution.py:32
  11.5 7.4 %collective-permute-start.2 = (bf16[64,512]{1,0:T(8,128)(2,1)S(1)}, bf16[64,512]{1,0:T(8,128)(2,1)S(1)}, u32[]{:S(2)}, u32[]{:S(2)}) collective-permute-start(bf16[64,512]{1,0:T(8,128)(2,1)S(1)} %get-tuple-element.29), channel_id=1, source_target_pairs={{0,3},{1,4},{2,5},{3,6},{4,7},{8,11},{9,12},{10,13},{11,14},{12,15... | collective-permute-start | bytes 196616 | tf_op jit(solution)/shard_map/ppermute | solution.py:32
  34.2 3.1 %copy-start.2 = (bf16[192,1024]{1,0:T(8,128)(2,1)}, bf16[192,1024]{1,0:T(8,128)(2,1)S(1)}, u32[]{:S(2)}) copy-start(bf16[192,1024]{1,0:T(8,128)(2,1)S(1)} %get-tuple-element.37.refs_7_) | copy-start | bytes 1179652
  34.2 3.1 %copy-start.4 = (bf16[192,512]{1,0:T(8,128)(2,1)}, bf16[192,512]{1,0:T(8,128)(2,1)S(1)}, u32[]{:S(2)}) copy-start(bf16[192,512]{1,0:T(8,128)(2,1)S(1)} %get-tuple-element.32.refs_5_) | copy-start | bytes 589828
  34.2 2.1 %collective-permute-start.4 = (bf16[16,144,128]{2,1,0:T(8,128)(2,1)S(1)}, bf16[16,144,128]{2,1,0:T(8,128)(2,1)S(1)}, u32[]{:S(2)}, u32[]{:S(2)}) collective-permute-start(bf16[16,144,128]{2,1,0:T(8,128)(2,1)S(1)} %get-tuple-element.35), channel_id=1, source_target_pairs={{0,8},{8,0},{1,9},{9,1},{2,10},{10,2},{3,11},{11,3},{4,12},{12,4},... | collective-permute-start | bytes 1769480 | tf_op jit(solution)/shard_map/ppermute | solution.py:322
  36.3 8.6 %copy-start = (bf16[1,192,512]{2,1,0:T(8,128)(2,1)S(1)}, bf16[1,192,512]{2,1,0:T(8,128)(2,1)}, u32[]{:S(2)}) copy-start(bf16[1,192,512]{2,1,0:T(8,128)(2,1)} %param.6) | copy-start | bytes 589828
  36.3 8.6 %copy-start.1 = (bf16[512,1024]{1,0:T(8,128)(2,1)S(1)}, bf16[512,1024]{1,0:T(8,128)(2,1)}, u32[]{:S(2)}) copy-start(bf16[512,1024]{1,0:T(8,128)(2,1)} %refs_8_.3) | copy-start | bytes 3145732
  37.3 18.1 %all-to-all-start = ((bf16[4,576,128]{2,1,0:T(8,128)(2,1)}), bf16[4,576,128]{2,1,0:T(8,128)(2,1)}, u32[]{:S(2)}, u32[]{:S(2)}) async-start(bf16[4,576,128]{2,1,0:T(8,128)(2,1)} %bitcast.8), calls=%async_computation | async-start | bytes 1179648 | tf_op jit(solution)/shard_map/all_to_all | solution.py:312
  44.9 1.0 copy-start.3
  45.9 0.9 copy-start.5
  52.8 30.1 %collective-permute-start.5 = (bf16[384,512]{1,0:T(8,128)(2,1)}, bf16[384,512]{1,0:T(8,128)(2,1)S(1)}, u32[]{:S(2)}, u32[]{:S(2)}) collective-permute-start(bf16[384,512]{1,0:T(8,128)(2,1)} %get-tuple-element.41), channel_id=1, source_target_pairs={{1,0},{2,1},{3,2},{4,3},{5,4},{6,5},{7,6},{9,8},{10,9},{11,10},{12... | collective-permute-start | bytes 1179656 | tf_op jit(solution)/shard_map/ppermute | solution.py:32
  54.1 28.9 %collective-permute-start.6 = (bf16[384,512]{1,0:T(8,128)(2,1)}, bf16[384,512]{1,0:T(8,128)(2,1)S(1)}, u32[]{:S(2)}, u32[]{:S(2)}) collective-permute-start(bf16[384,512]{1,0:T(8,128)(2,1)} %get-tuple-element.42), channel_id=1, source_target_pairs={{2,0},{3,1},{4,2},{5,3},{6,4},{7,5},{10,8},{11,9},{12,10},{13,11},... | collective-permute-start | bytes 1179656 | tf_op jit(solution)/shard_map/ppermute | solution.py:32
  102.4 2.0 %collective-permute-start.7 = (bf16[16,144,128]{2,1,0:T(8,128)(2,1)S(1)}, bf16[16,144,128]{2,1,0:T(8,128)(2,1)S(1)}, u32[]{:S(2)}, u32[]{:S(2)}) collective-permute-start(bf16[16,144,128]{2,1,0:T(8,128)(2,1)S(1)} %all_to_all.16.near_ref), channel_id=1, source_target_pairs={{0,8},{8,0},{1,9},{9,1},{2,10},{10,2},{3,11},{11,3},{4,12},{12,4},... | collective-permute-start | bytes 1769480 | tf_op jit(solution)/shard_map/ppermute | solution.py:322

commit v5 on v4

--- a/solution.py
+++ b/solution.py
@@ -12,10 +12,10 @@
 HEAD_DIM = 64
 CTX_MAX = 3
 LANES = 128
+SUBLANES = 8
 NEGATIVE = -1e30
 RUN_AXES = ("z", "y")
 PLANE_AXES = ("x", "y")
-CHIP_AXES = ("x", "y", "z")
 VMEM_LIMIT = 40 * 1024 * 1024
 
 NN = (((1,), (0,)), ((), ()))
@@ -87,8 +87,9 @@
     own_refs = refs[2 : 2 + tiles]
     far_ref, near_ref, w_hbm, conv_hbm, cot_hbm = refs[2 + tiles : 7 + tiles]
     out_ref, att_ref, lse_ref, dhid_ref, keep_ref, give_ref = refs[7 + tiles : 13 + tiles]
-    qx, kx, vx, ax, lx, hid, cotx, dm, bias, kp, parts = refs[13 + tiles : 24 + tiles]
-    q_ref, w_ref, conv_ref, cot_ref, sems = refs[24 + tiles :]
+    q_ref, w_ref = refs[13 + tiles : 15 + tiles]
+    qx, kx, vx, ax, lx, hid, cotx, dm, bias, kp, ks, parts = refs[15 + tiles : 27 + tiles]
+    conv_ref, cot_ref, sems = refs[27 + tiles :]
 
     att = q_ref.shape[1]
     width = w_ref.shape[1]
@@ -168,23 +169,54 @@
             (3 + part) * edge : (4 + part) * edge, lane : lane + LANES
         ].astype(jnp.float32)
     kp[...] = jnp.zeros_like(kp)
+    dm[rows + edge :] = jnp.zeros_like(dm[rows + edge :])
+
+    apart = -(-taps // SUBLANES)
+    reach = (apart - 1) * SUBLANES
+    part_rows = (rows + edge) // 2
 
     def convolve(chunk, carry):
         columns = pl.ds(pl.multiple_of(chunk * LANES, LANES), LANES)
-        mixed = jnp.zeros((rows + edge, LANES), jnp.float32)
-        for tap in range(taps):
-            mixed += conv_ref[tap : tap + 1, columns] * hid[chunk, edge - tap : 2 * edge + rows - tap]
-        sigma = jax.nn.sigmoid(mixed)
-        out_ref[:, columns] = (mixed * sigma)[:rows].astype(jnp.bfloat16)
-        dm[...] = cotx[chunk] * sigma * (1.0 + mixed * (1.0 - sigma))
-        dhidden = jnp.zeros((rows, LANES), jnp.float32)
-        for tap in range(taps):
-            dhidden += conv_ref[tap : tap + 1, columns] * dm[tap : tap + rows]
-        dhid_ref[:, columns] = dhidden.astype(jnp.bfloat16)
-        own = dm[:rows]
-        for tap in range(taps):
-            product = own * hid[chunk, edge - tap : edge + rows - tap]
-            kp[chunk, tap : tap + 1] = jnp.sum(product, axis=0, keepdims=True)
+        for first in range(0, rows + edge, part_rows):
+            mixed = jnp.zeros((part_rows, LANES), jnp.float32)
+            for shift in range(SUBLANES):
+                low = edge + first - shift - reach
+                window = hid[chunk, low : low + part_rows + reach]
+                for tap in range(shift, taps, SUBLANES):
+                    at = reach - (tap - shift)
+                    mixed += conv_ref[tap : tap + 1, columns] * window[at : at + part_rows]
+            sigma = jax.nn.sigmoid(mixed)
+            kept = min(part_rows, rows - first)
+            out_ref[first : first + kept, columns] = (mixed * sigma)[:kept].astype(jnp.bfloat16)
+            dm[first : first + part_rows] = (
+                cotx[chunk, first : first + part_rows] * sigma * (1.0 + mixed * (1.0 - sigma))
+            )
+        part = rows // 2
+        for first in range(0, rows, part):
+            dhidden = jnp.zeros((part, LANES), jnp.float32)
+            for shift in range(SUBLANES):
+                low = first + shift
+                window = dm[low : low + part + reach]
+                for tap in range(shift, taps, SUBLANES):
+                    at = tap - shift
+                    dhidden += conv_ref[tap : tap + 1, columns] * window[at : at + part]
+            dhid_ref[first : first + part, columns] = dhidden.astype(jnp.bfloat16)
+        for shift in range(SUBLANES):
+            sums = [jnp.zeros((SUBLANES, LANES), jnp.float32)] * apart
+            for first in range(0, rows, part):
+                low = edge + first - shift - reach
+                window = hid[chunk, low : low + part + reach]
+                own = dm[first : first + part]
+                for tap in range(shift, taps, SUBLANES):
+                    at = reach - (tap - shift)
+                    product = (own * window[at : at + part]).reshape(-1, SUBLANES, LANES)
+                    sums[tap // SUBLANES] += jnp.sum(product, axis=0)
+            for tap in range(shift, taps, SUBLANES):
+                ks[tap * SUBLANES : (tap + 1) * SUBLANES] = sums[tap // SUBLANES]
+        total = ks[pl.ds(0, taps, SUBLANES)]
+        for row in range(1, SUBLANES):
+            total += ks[pl.ds(row, taps, SUBLANES)]
+        kp[chunk, :taps] = total
         return carry
 
     lax.fori_loop(0, width // LANES, convolve, 0)
@@ -308,14 +340,22 @@
     dv_ref[...] = total[rows:]
 
 
-def exchange(x, axes):
-    return lax.all_to_all(x, axes, 0, 0, tiled=True)
-
-
-def collected(x, axes):
-    parts = lax.axis_size(axes)
-    x = exchange(x.reshape(parts, -1, LANES), axes)
+def exchange(x):
+    return lax.all_to_all(x, PLANE_AXES, 0, 0, tiled=True)
+
+
+def collected(x):
+    x = exchange(x.reshape(lax.axis_size(PLANE_AXES), -1, LANES))
     return jnp.sum(x.astype(jnp.float32), axis=0).astype(x.dtype)
+
+
+def summed_along(x, axis):
+    size, step = lax.axis_size(axis), 1
+    while step < size:
+        other = lax.ppermute(x, axis, [(i, i ^ step) for i in range(size)])
+        x = (x.astype(jnp.float32) + other.astype(jnp.float32)).astype(x.dtype)
+        step *= 2
+    return x
 
 
 def other_core(x):
@@ -360,11 +400,12 @@
     near = shifted(near, -1)
 
     pieces = att // 32
-    split = pieces == lax.axis_size(CHIP_AXES)
+    layers = lax.axis_size("z")
+    split = pieces == layers * lax.axis_size(PLANE_AXES) and layers & (layers - 1) == 0
     core = lax.axis_index("core").astype(jnp.int32) if split else jnp.int32(0)
     place = jnp.stack([device, core])
     piece_rows = -(-(chunks * 16 + chunks) // 16) * 16
-    out_frames, attended, log_sums, dhidden, keep, give = pl.pallas_call(
+    out_frames, attended, log_sums, dhidden, keep, give, query, out_weight = pl.pallas_call(
         functools.partial(forward_kernel, context, rows, edge, taps),
         out_shape=(
             jax.ShapeDtypeStruct((rows, width), bf16),
@@ -372,9 +413,13 @@
             jax.ShapeDtypeStruct((heads, rows), f32),
             jax.ShapeDtypeStruct((rows, width), bf16),
         )
-        + (jax.ShapeDtypeStruct((pieces, piece_rows, LANES), bf16),) * 2,
+        + (jax.ShapeDtypeStruct((pieces, piece_rows, LANES), bf16),) * 2
+        + (
+            jax.ShapeDtypeStruct((rows, att), bf16),
+            jax.ShapeDtypeStruct((att, width), bf16),
+        ),
         in_specs=[smem, hbm] + [vmem] * (3 + context) + [hbm] * 3,
-        out_specs=(vmem,) * 6,
+        out_specs=(vmem,) * 8,
         scratch_shapes=[
             pltpu.VMEM((query_rows, att), bf16),
             pltpu.VMEM((key_rows, att), bf16),
@@ -383,12 +428,11 @@
             pltpu.VMEM((query_rows, LANES), f32),
             pltpu.VMEM((chunks, query_rows, LANES), f32),
             pltpu.VMEM((chunks, rows + edge, LANES), f32),
-            pltpu.VMEM((rows + edge, LANES), f32),
+            pltpu.VMEM((rows + edge + 8, LANES), f32),
             pltpu.VMEM((LANES, context * rows + LANES), f32),
             pltpu.VMEM((chunks, 2 * pieces, LANES), f32),
+            pltpu.VMEM((taps * SUBLANES, LANES), f32),
             pltpu.VMEM((2, pieces, piece_rows, LANES), bf16),
-            pltpu.VMEM((rows, att), bf16),
-            pltpu.VMEM((att, width), bf16),
             pltpu.VMEM((taps, width), f32),
             pltpu.VMEM((rows, width), bf16),
             pltpu.SemaphoreType.DMA((4,)),
@@ -418,11 +462,14 @@
         cost_estimate=cost(6 * 10**9, 10**7),
         name="backward",
     )(place, query, *tiles, attended, log_sums, dhidden, out_weight)
+    if split:
+        mine = summed_along(collected(mine), "z")
+        mine, *messages = lax.optimization_barrier((mine, *messages))
+        mine = exchange(jnp.broadcast_to(mine, (lax.axis_size(PLANE_AXES), *mine.shape)))
+        mine = mine.reshape(keep.shape)
     messages = [shifted(message, -offset) for offset, message in enumerate(messages, 1)]
     if split:
-        mine = collected(collected(mine, PLANE_AXES), "z")
         mine, *messages = lax.optimization_barrier((mine, *messages))
-        mine = exchange(jnp.broadcast_to(mine, keep.shape), CHIP_AXES)
         halves = (mine, other_core(mine))
     else:
         halves = lax.psum((keep, give), ("x", "core", "z", "y"))

time: 107 us -> 103 us (0.963)
  blocking collectives: 45.7 us -> 19.2 us
  waiting for transfers between devices: 8.53 us -> 28.5 us
  starting transfers between devices: 25.4 us -> 28 us
  local copies, waits for them, and re-layouts: 2.02 us -> 4.05 us
  other arithmetic: 2.24 us -> 0.41 us
    all_to_all x2 -> x1, blocking collectives: 45.7 us -> 19.2 us  [exchange(): return lax.all_to_all(x, PLANE_AXES, 0, 0, tiled=True)]
    ppermute x6, waiting for transfers between devices: 5.36 us -> 22.2 us  [shifted(): lax.ppermute(x, RUN_AXES, [(i, i + by) for i in devices if i + by in devi...]
    ppermute x0 -> x2, starting transfers between devices: none -> 6.61 us  [summed_along(): other = lax.ppermute(x, axis, [(i, i ^ step) for i in range(size)])]
    all_to_all x1, starting transfers between devices: 7.58 us -> 3.48 us  [exchange(): return lax.all_to_all(x, PLANE_AXES, 0, 0, tiled=True)]
    ppermute x0 -> x2, waiting for transfers between devices: none -> 3.13 us  [summed_along(): other = lax.ppermute(x, axis, [(i, i ^ step) for i in range(size)])]
    unnamed x12, local copies, waits for them, and re-layouts: 1.94 us -> 3.16 us
    reduce_sum x2 -> x1, other arithmetic: 1.19 us -> 0.1 us  [collected(): return jnp.sum(x.astype(jnp.float32), axis=0).astype(x.dtype)]
  transfers between devices with their start and end apart: 9 -> 11, of which waited for: 4 -> 6; matrix products, arithmetic and copies ran while one was open for 1% -> 0% of each run, Pallas kernels for 6% -> 7%
where the time goes in v5:
time: 103 us; the launch traced here: 102 us
  waiting for transfers between devices  28.5 us (28%)
  starting transfers between devices  28 us (27%)
  Pallas kernels  21.2 us (21%)
  blocking collectives  19.2 us (19%)
  local copies, waits for them, and re-layouts  4.05 us (4%)
    ppermute x6, waiting for transfers between devices, shifted(): lax.ppermute(x, RUN_AXES, [(i, i + by) for i in devices if i + by in devi...  22.2 us
    all_to_all x1, blocking collectives, exchange(): return lax.all_to_all(x, PLANE_AXES, 0, 0, tiled=True)  19.2 us
    ppermute x6, starting transfers between devices, shifted(): lax.ppermute(x, RUN_AXES, [(i, i + by) for i in devices if i + by in devi...  17.8 us
    pallas_call x1, Pallas kernels, per_device(): pl.pallas_call(functools.partial(forward_kernel, context, rows, edge, tap...  11.2 us
    ppermute x2, starting transfers between devices, summed_along(): other = lax.ppermute(x, axis, [(i, i ^ step) for i in range(size)])  6.61 us
    pallas_call x1, Pallas kernels, per_device(): pl.pallas_call(functools.partial(backward_kernel, context, rows), out_sha...  5.99 us
    all_to_all x1, starting transfers between devices, exchange(): return lax.all_to_all(x, PLANE_AXES, 0, 0, tiled=True)  3.48 us
    ppermute x2, waiting for transfers between devices, other_core(): return lax.ppermute(x, 'core', [(0, 1), (1, 0)])  3.19 us
  transfers between devices with their start and end apart: 11, of which 6 were waited for; matrix products, arithmetic and copies ran while one was open for 0% of the time, Pallas kernels for 7%

profile of v5, /device:TPU:0, one launch (start us, length us, event | category | flops | bytes accessed | tf_op | source)
XLA Modules:
  0.0 102.1 jit_solution(9671878511144183284)
XLA Ops:
  0.6 1.1 %pack.1 = (bf16[416,512]{1,0:T(8,128)(2,1)S(1)}, bf16[64,512]{1,0:T(8,128)(2,1)S(1)}, bf16[160,512]{1,0:T(8,128)(2,1)S(1)}) custom-call(bf16[192,512]{1,0:T(8,128)(2,1)} %bitcast.17, bf16[192,512]{1,0:T(8,128)(2,1)} %bitcast.18, bf16[192,512]{1,0:T(8,128)(2,1)} %bitcast.19, bf16[192,1024]{1,0:T(8,128)(2,1)} %bitcast.15), custom_call_target="tpu_custom_call" | custom-call | tf_op jit(solution)/shard_map/pack/pallas_call | solution.py:385
  1.8 4.9 %collective-permute-start = (bf16[416,512]{1,0:T(8,128)(2,1)S(1)}, bf16[416,512]{1,0:T(8,128)(2,1)S(1)}, u32[]{:S(2)}, u32[]{:S(2)}) collective-permute-start(bf16[416,512]{1,0:T(8,128)(2,1)S(1)} %get-tuple-element.33.refs_2_), channel_id=1, source_target_pairs={{0,1},{1,2},{2,3},{3,4},{4,5},{5,6},{6,7},{8,9},{9,10},{10,11},{11... | collective-permute-start | bytes 1277960 | tf_op jit(solution)/shard_map/ppermute | solution.py:32
  6.7 3.5 %collective-permute-start.1 = (bf16[416,512]{1,0:T(8,128)(2,1)S(1)}, bf16[416,512]{1,0:T(8,128)(2,1)S(1)}, u32[]{:S(2)}, u32[]{:S(2)}) collective-permute-start(bf16[416,512]{1,0:T(8,128)(2,1)S(1)} %get-tuple-element.33.refs_2_), channel_id=1, source_target_pairs={{0,2},{1,3},{2,4},{3,5},{4,6},{5,7},{8,10},{9,11},{10,12},{11,13},... | collective-permute-start | bytes 1277960 | tf_op jit(solution)/shard_map/ppermute | solution.py:32
  10.2 1.3 %collective-permute-start.3 = (bf16[160,512]{1,0:T(8,128)(2,1)S(1)}, bf16[160,512]{1,0:T(8,128)(2,1)S(1)}, u32[]{:S(2)}, u32[]{:S(2)}) collective-permute-start(bf16[160,512]{1,0:T(8,128)(2,1)S(1)} %get-tuple-element.35), channel_id=1, source_target_pairs={{1,0},{2,1},{3,2},{4,3},{5,4},{6,5},{7,6},{9,8},{10,9},{11,10},{12... | collective-permute-start | bytes 491528 | tf_op jit(solution)/shard_map/ppermute | solution.py:32
  11.5 5.5 %collective-permute-start.2 = (bf16[64,512]{1,0:T(8,128)(2,1)S(1)}, bf16[64,512]{1,0:T(8,128)(2,1)S(1)}, u32[]{:S(2)}, u32[]{:S(2)}) collective-permute-start(bf16[64,512]{1,0:T(8,128)(2,1)S(1)} %get-tuple-element.34), channel_id=1, source_target_pairs={{0,3},{1,4},{2,5},{3,6},{4,7},{8,11},{9,12},{10,13},{11,14},{12,15... | collective-permute-start | bytes 196616 | tf_op jit(solution)/shard_map/ppermute | solution.py:32
  17.0 0.1 pad_add_fusion.refs_0_.device_ref
  17.1 3.2 %collective-permute-done.2.refs_5_ = bf16[64,512]{1,0:T(8,128)(2,1)S(1)} collective-permute-done((bf16[64,512]{1,0:T(8,128)(2,1)S(1)}, bf16[64,512]{1,0:T(8,128)(2,1)S(1)}, u32[]{:S(2)}, u32[]{:S(2)}) %collective-permute-start.2) | collective-permute-done | bytes 65568 | tf_op jit(solution)/shard_map/ppermute | solution.py:32
  20.3 0.0 collective-permute-done.3.refs_6_
  20.3 0.0 collective-permute-done.refs_3_
  20.3 0.0 collective-permute-done.1.refs_4_
  20.3 11.2 %forward.1 = (bf16[192,1024]{1,0:T(8,128)(2,1)}, bf16[192,512]{1,0:T(8,128)(2,1)S(1)}, f32[8,192]{1,0:T(8,128)S(1)}, bf16[192,1024]{1,0:T(8,128)(2,1)S(1)}, bf16...) custom-call(s32[2]{0:T(128)S(1)} %pad_add_fusion.refs_0_.device_ref,, ...), custom_call_target="tpu_custom_call" | custom-call | flops 8000000000 | bytes 10000000 | tf_op jit(solution)/shard_map/forward/pallas_call | solution.py:408
  31.5 0.0 copy-start
  31.6 0.0 copy-start.2
  31.6 0.0 copy-start.4
  31.6 0.1 collective-permute-start.4
  31.7 2.0 %collective-permute-done.4 = bf16[16,144,128]{2,1,0:T(8,128)(2,1)S(1)} collective-permute-done((bf16[16,144,128]{2,1,0:T(8,128)(2,1)S(1)}, bf16[16,144,128]{2,1,0:T(8,128)(2,1)S(1)}, u32[]{:S(2)}, u32[]{:S(2)}) %collective-permute-start.4) | collective-permute-done | bytes 589856 | tf_op jit(solution)/shard_map/ppermute | solution.py:362
  33.6 0.2 add_convert_fusion
  33.8 0.0 copy-done
  33.8 0.0 copy-done.2
  33.8 0.0 copy-done.4
  33.8 19.2 %all_to_all.10 = bf16[4,576,128]{2,1,0:T(8,128)(2,1)S(1)} all-to-all(bf16[4,576,128]{2,1,0:T(8,128)(2,1)S(1)} %bitcast.14), channel_id=1, replica_groups=mesh['x'=2,'core'=2,'z'=4,'y'=2] {'x','y'}, dimensions={0} | all-to-all | bytes 1179648 | tf_op jit(solution)/shard_map/all_to_all | solution.py:344
  53.0 0.1 reduce_sum.12
  53.1 3.1 %collective-permute-start.5 = (bf16[576,128]{1,0:T(8,128)(2,1)S(1)}, bf16[576,128]{1,0:T(8,128)(2,1)S(1)}, u32[]{:S(2)}, u32[]{:S(2)}) collective-permute-start(bf16[576,128]{1,0:T(8,128)(2,1)S(1)} %reduce_sum.12), channel_id=1, source_target_pairs={{0,2},{2,0},{4,6},{6,4},{1,3},{3,1},{5,7},{7,5},{8,10},{10,8},{12,... | collective-permute-start | bytes 442376 | tf_op jit(solution)/shard_map/ppermute | solution.py:355
  56.2 3.1 %collective-permute-done.5 = bf16[576,128]{1,0:T(8,128)(2,1)S(1)} collective-permute-done((bf16[576,128]{1,0:T(8,128)(2,1)S(1)}, bf16[576,128]{1,0:T(8,128)(2,1)S(1)}, u32[]{:S(2)}, u32[]{:S(2)}) %collective-permute-start.5) | collective-permute-done | bytes 147488 | tf_op jit(solution)/shard_map/ppermute | solution.py:355
  59.3 3.6 %collective-permute-start.6 = (bf16[576,128]{1,0:T(8,128)(2,1)S(1)}, bf16[576,128]{1,0:T(8,128)(2,1)S(1)}, u32[]{:S(2)}, u32[]{:S(2)}) collective-permute-start(bf16[576,128]{1,0:T(8,128)(2,1)S(1)} %add_convert_fusion.2), channel_id=1, source_target_pairs={{0,4},{2,6},{4,0},{6,2},{1,5},{3,7},{5,1},{7,3},{8,12},{10,14},{12... | collective-permute-start | bytes 442376 | tf_op jit(solution)/shard_map/ppermute | solution.py:355
  62.9 0.0 copy-start.1
  62.9 1.2 %copy-done.1 = bf16[512,1024]{1,0:T(8,128)(2,1)S(1)} copy-done((bf16[512,1024]{1,0:T(8,128)(2,1)S(1)}, bf16[512,1024]{1,0:T(8,128)(2,1)}, u32[]{:S(2)}) %copy-start.1) | copy-done | bytes 1048600
  64.1 0.0 copy-start.3
  64.1 1.0 copy-done.3
  65.1 0.0 copy-start.5
  65.1 0.9 copy-done.5
  66.0 6.0 %backward.1 = (bf16[192,512]{1,0:T(8,128)(2,1)}, f32[384,512]{1,0:T(8,128)S(1)}, bf16[384,512]{1,0:T(8,128)(2,1)S(1)}, bf16[384,512]{1,0:T(8,128)(2,1)S(1)}) custom-call(s32[2]{0:T(128)S(1)} %pad_add_fusion.refs_0_.device_ref, bf16[192,512]{1,0:T(8,128)(2,1)S(1)} %copy-done.5, bf16[416,512]{1,0:T(8,128)(2,1)S(1)} %get-tuple-element.33.refs_2_, ...), custom_call_target="tpu_custom_call" | custom-call | flops 6000000000 | bytes 10000000 | tf_op jit(solution)/shard_map/backward/pallas_call | solution.py:448
  72.0 0.0 collective-permute-done.6
  72.1 0.9 broadcast_in_dim.17
  73.0 3.5 %all-to-all-start.1 = ((bf16[4,576,128]{2,1,0:T(8,128)(2,1)}), bf16[4,576,128]{2,1,0:T(8,128)(2,1)S(1)}, u32[]{:S(2)}, u32[]{:S(2)}) async-start(bf16[4,576,128]{2,1,0:T(8,128)(2,1)} %broadcast_in_dim.17), calls=%async_computation.1 | async-start | bytes 1179648 | tf_op jit(solution)/shard_map/all_to_all | solution.py:344
  76.5 1.3 %collective-permute-start.7 = (bf16[384,512]{1,0:T(8,128)(2,1)S(1)}, bf16[384,512]{1,0:T(8,128)(2,1)S(1)}, u32[]{:S(2)}, u32[]{:S(2)}) collective-permute-start(bf16[384,512]{1,0:T(8,128)(2,1)S(1)} %get-tuple-element.51), channel_id=1, source_target_pairs={{1,0},{2,1},{3,2},{4,3},{5,4},{6,5},{7,6},{9,8},{10,9},{11,10},{12... | collective-permute-start | bytes 1179656 | tf_op jit(solution)/shard_map/ppermute | solution.py:32
  77.8 1.3 %collective-permute-start.8 = (bf16[384,512]{1,0:T(8,128)(2,1)S(1)}, bf16[384,512]{1,0:T(8,128)(2,1)S(1)}, u32[]{:S(2)}, u32[]{:S(2)}) collective-permute-start(bf16[384,512]{1,0:T(8,128)(2,1)S(1)} %get-tuple-element.52), channel_id=1, source_target_pairs={{2,0},{3,1},{4,2},{5,3},{6,4},{7,5},{10,8},{11,9},{12,10},{13,11},... | collective-permute-start | bytes 1179656 | tf_op jit(solution)/shard_map/ppermute | solution.py:32
  79.1 12.4 %collective-permute-done.7.refs_1_ = bf16[384,512]{1,0:T(8,128)(2,1)S(1)} collective-permute-done((bf16[384,512]{1,0:T(8,128)(2,1)S(1)}, bf16[384,512]{1,0:T(8,128)(2,1)S(1)}, u32[]{:S(2)}, u32[]{:S(2)}) %collective-permute-start.7) | collective-permute-done | bytes 393248 | tf_op jit(solution)/shard_map/ppermute | solution.py:32
  91.5 6.6 %collective-permute-done.8.refs_2_ = bf16[384,512]{1,0:T(8,128)(2,1)S(1)} collective-permute-done((bf16[384,512]{1,0:T(8,128)(2,1)S(1)}, bf16[384,512]{1,0:T(8,128)(2,1)S(1)}, u32[]{:S(2)}, u32[]{:S(2)}) %collective-permute-start.8) | collective-permute-done | bytes 393248 | tf_op jit(solution)/shard_map/ppermute | solution.py:32
  98.0 0.0 all-to-all-done.1
  98.0 0.0 collective-permute-start.9
  98.0 0.8 merge.1
  98.9 1.2 %collective-permute-done.9.far_ref = bf16[16,144,128]{2,1,0:T(8,128)(2,1)S(1)} collective-permute-done((bf16[16,144,128]{2,1,0:T(8,128)(2,1)S(1)}, bf16[16,144,128]{2,1,0:T(8,128)(2,1)S(1)}, u32[]{:S(2)}, u32[]{:S(2)}) %collective-permute-start.9) | collective-permute-done | bytes 589856 | tf_op jit(solution)/shard_map/ppermute | solution.py:362
  100.0 2.1 %unpack.1 = (f32[512,1024]{1,0:T(8,128)}, f32[31,1024]{1,0:T(8,128)}) custom-call(s32[2]{0:T(128)S(1)} %pad_add_fusion.refs_0_.device_ref, bf16[16,144,128]{2,1,0:T(8,128)(2,1)S(1)} %bitcast.13, bf16[16,144,128]{2,1,0:T(8,128)(2,1)S(1)} %collective-permute-done.9.far_ref), custom_call_target="tpu_custom_call" | custom-call | tf_op jit(solution)/shard_map/unpack/pallas_call | solution.py:484
  (2 shorter events, 0.1 us)
Async XLA Ops:
  1.8 18.6 %collective-permute-start = (bf16[416,512]{1,0:T(8,128)(2,1)S(1)}, bf16[416,512]{1,0:T(8,128)(2,1)S(1)}, u32[]{:S(2)}, u32[]{:S(2)}) collective-permute-start(bf16[416,512]{1,0:T(8,128)(2,1)S(1)} %get-tuple-element.33.refs_2_), channel_id=1, source_target_pairs={{0,1},{1,2},{2,3},{3,4},{4,5},{5,6},{6,7},{8,9},{9,10},{10,11},{11... | collective-permute-start | bytes 1277960 | tf_op jit(solution)/shard_map/ppermute | solution.py:32
  6.7 13.7 %collective-permute-start.1 = (bf16[416,512]{1,0:T(8,128)(2,1)S(1)}, bf16[416,512]{1,0:T(8,128)(2,1)S(1)}, u32[]{:S(2)}, u32[]{:S(2)}) collective-permute-start(bf16[416,512]{1,0:T(8,128)(2,1)S(1)} %get-tuple-element.33.refs_2_), channel_id=1, source_target_pairs={{0,2},{1,3},{2,4},{3,5},{4,6},{5,7},{8,10},{9,11},{10,12},{11,13},... | collective-permute-start | bytes 1277960 | tf_op jit(solution)/shard_map/ppermute | solution.py:32
  10.2 10.2 %collective-permute-start.3 = (bf16[160,512]{1,0:T(8,128)(2,1)S(1)}, bf16[160,512]{1,0:T(8,128)(2,1)S(1)}, u32[]{:S(2)}, u32[]{:S(2)}) collective-permute-start(bf16[160,512]{1,0:T(8,128)(2,1)S(1)} %get-tuple-element.35), channel_id=1, source_target_pairs={{1,0},{2,1},{3,2},{4,3},{5,4},{6,5},{7,6},{9,8},{10,9},{11,10},{12... | collective-permute-start | bytes 491528 | tf_op jit(solution)/shard_map/ppermute | solution.py:32
  11.5 8.9 %collective-permute-start.2 = (bf16[64,512]{1,0:T(8,128)(2,1)S(1)}, bf16[64,512]{1,0:T(8,128)(2,1)S(1)}, u32[]{:S(2)}, u32[]{:S(2)}) collective-permute-start(bf16[64,512]{1,0:T(8,128)(2,1)S(1)} %get-tuple-element.34), channel_id=1, source_target_pairs={{0,3},{1,4},{2,5},{3,6},{4,7},{8,11},{9,12},{10,13},{11,14},{12,15... | collective-permute-start | bytes 196616 | tf_op jit(solution)/shard_map/ppermute | solution.py:32
  31.5 2.3 %copy-start = (bf16[512,1024]{1,0:T(8,128)(2,1)}, bf16[512,1024]{1,0:T(8,128)(2,1)S(1)}, u32[]{:S(2)}) copy-start(bf16[512,1024]{1,0:T(8,128)(2,1)S(1)} %get-tuple-element.44.refs_8_) | copy-start | bytes 3145732
  31.6 2.3 %copy-start.2 = (bf16[192,1024]{1,0:T(8,128)(2,1)}, bf16[192,1024]{1,0:T(8,128)(2,1)S(1)}, u32[]{:S(2)}) copy-start(bf16[192,1024]{1,0:T(8,128)(2,1)S(1)} %get-tuple-element.43.refs_7_) | copy-start | bytes 1179652
  31.6 2.3 %copy-start.4 = (bf16[192,512]{1,0:T(8,128)(2,1)}, bf16[192,512]{1,0:T(8,128)(2,1)S(1)}, u32[]{:S(2)}) copy-start(bf16[192,512]{1,0:T(8,128)(2,1)S(1)} %get-tuple-element.37.refs_1_) | copy-start | bytes 589828
  31.6 2.1 %collective-permute-start.4 = (bf16[16,144,128]{2,1,0:T(8,128)(2,1)S(1)}, bf16[16,144,128]{2,1,0:T(8,128)(2,1)S(1)}, u32[]{:S(2)}, u32[]{:S(2)}) collective-permute-start(bf16[16,144,128]{2,1,0:T(8,128)(2,1)S(1)} %get-tuple-element.41), channel_id=1, source_target_pairs={{0,8},{8,0},{1,9},{9,1},{2,10},{10,2},{3,11},{11,3},{4,12},{12,4},... | collective-permute-start | bytes 1769480 | tf_op jit(solution)/shard_map/ppermute | solution.py:362
  53.1 6.2 %collective-permute-start.5 = (bf16[576,128]{1,0:T(8,128)(2,1)S(1)}, bf16[576,128]{1,0:T(8,128)(2,1)S(1)}, u32[]{:S(2)}, u32[]{:S(2)}) collective-permute-start(bf16[576,128]{1,0:T(8,128)(2,1)S(1)} %reduce_sum.12), channel_id=1, source_target_pairs={{0,2},{2,0},{4,6},{6,4},{1,3},{3,1},{5,7},{7,5},{8,10},{10,8},{12,... | collective-permute-start | bytes 442376 | tf_op jit(solution)/shard_map/ppermute | solution.py:355
  59.3 12.7 %collective-permute-start.6 = (bf16[576,128]{1,0:T(8,128)(2,1)S(1)}, bf16[576,128]{1,0:T(8,128)(2,1)S(1)}, u32[]{:S(2)}, u32[]{:S(2)}) collective-permute-start(bf16[576,128]{1,0:T(8,128)(2,1)S(1)} %add_convert_fusion.2), channel_id=1, source_target_pairs={{0,4},{2,6},{4,0},{6,2},{1,5},{3,7},{5,1},{7,3},{8,12},{10,14},{12... | collective-permute-start | bytes 442376 | tf_op jit(solution)/shard_map/ppermute | solution.py:355
  62.9 1.2 %copy-start.1 = (bf16[512,1024]{1,0:T(8,128)(2,1)S(1)}, bf16[512,1024]{1,0:T(8,128)(2,1)}, u32[]{:S(2)}) copy-start(bf16[512,1024]{1,0:T(8,128)(2,1)} %copy-done) | copy-start | bytes 3145732
  64.1 1.0 copy-start.3
  65.1 0.9 copy-start.5
  73.0 25.1 %all-to-all-start.1 = ((bf16[4,576,128]{2,1,0:T(8,128)(2,1)}), bf16[4,576,128]{2,1,0:T(8,128)(2,1)S(1)}, u32[]{:S(2)}, u32[]{:S(2)}) async-start(bf16[4,576,128]{2,1,0:T(8,128)(2,1)} %broadcast_in_dim.17), calls=%async_computation.1 | async-start | bytes 1179648 | tf_op jit(solution)/shard_map/all_to_all | solution.py:344
  76.5 15.0 %collective-permute-start.7 = (bf16[384,512]{1,0:T(8,128)(2,1)S(1)}, bf16[384,512]{1,0:T(8,128)(2,1)S(1)}, u32[]{:S(2)}, u32[]{:S(2)}) collective-permute-start(bf16[384,512]{1,0:T(8,128)(2,1)S(1)} %get-tuple-element.51), channel_id=1, source_target_pairs={{1,0},{2,1},{3,2},{4,3},{5,4},{6,5},{7,6},{9,8},{10,9},{11,10},{12... | collective-permute-start | bytes 1179656 | tf_op jit(solution)/shard_map/ppermute | solution.py:32
  77.8 20.3 %collective-permute-start.8 = (bf16[384,512]{1,0:T(8,128)(2,1)S(1)}, bf16[384,512]{1,0:T(8,128)(2,1)S(1)}, u32[]{:S(2)}, u32[]{:S(2)}) collective-permute-start(bf16[384,512]{1,0:T(8,128)(2,1)S(1)} %get-tuple-element.52), channel_id=1, source_target_pairs={{2,0},{3,1},{4,2},{5,3},{6,4},{7,5},{10,8},{11,9},{12,10},{13,11},... | collective-permute-start | bytes 1179656 | tf_op jit(solution)/shard_map/ppermute | solution.py:32
  98.0 2.0 %collective-permute-start.9 = (bf16[16,144,128]{2,1,0:T(8,128)(2,1)S(1)}, bf16[16,144,128]{2,1,0:T(8,128)(2,1)S(1)}, u32[]{:S(2)}, u32[]{:S(2)}) collective-permute-start(bf16[16,144,128]{2,1,0:T(8,128)(2,1)S(1)} %bitcast.12), channel_id=1, source_target_pairs={{0,8},{8,0},{1,9},{9,1},{2,10},{10,2},{3,11},{11,3},{4,12},{12,4},... | collective-permute-start | bytes 1769480 | tf_op jit(solution)/shard_map/ppermute | solution.py:362

commit v6 on v5

--- a/solution.py
+++ b/solution.py
@@ -87,9 +87,8 @@
     own_refs = refs[2 : 2 + tiles]
     far_ref, near_ref, w_hbm, conv_hbm, cot_hbm = refs[2 + tiles : 7 + tiles]
     out_ref, att_ref, lse_ref, dhid_ref, keep_ref, give_ref = refs[7 + tiles : 13 + tiles]
-    q_ref, w_ref = refs[13 + tiles : 15 + tiles]
-    qx, kx, vx, ax, lx, hid, cotx, dm, bias, kp, ks, parts = refs[15 + tiles : 27 + tiles]
-    conv_ref, cot_ref, sems = refs[27 + tiles :]
+    qx, kx, vx, ax, lx, hid, cotx, dm, bias, kp, ks, parts = refs[13 + tiles : 25 + tiles]
+    q_ref, w_ref, conv_ref, cot_ref, sems = refs[25 + tiles :]
 
     att = q_ref.shape[1]
     width = w_ref.shape[1]
@@ -275,12 +274,12 @@
 
 def backward_kernel(context, rows, *refs):
     tiles = context + 1
-    device_ref, q_ref = refs[:2]
+    device_ref, q_hbm = refs[:2]
     own_refs = refs[2 : 2 + tiles]
-    att_ref, lse_ref, dhid_ref, w_ref = refs[2 + tiles : 6 + tiles]
+    att_ref, lse_ref, dhid_hbm, w_hbm = refs[2 + tiles : 6 + tiles]
     dq_ref, own_ref = refs[6 + tiles : 8 + tiles]
     message_refs = refs[8 + tiles : 8 + tiles + context]
-    datt, bias = refs[8 + tiles + context :]
+    q_ref, dhid_ref, w_ref, datt, bias, sems = refs[8 + tiles + context :]
 
     att = q_ref.shape[1]
     heads = att // HEAD_DIM
@@ -288,6 +287,24 @@
     scale = 1.0 / math.sqrt(HEAD_DIM)
     start = device_ref[0] * rows
 
+    fetches = [
+        pltpu.make_async_copy(source, target, sems.at[i])
+        for i, (source, target) in enumerate(
+            ((q_hbm, q_ref), (dhid_hbm, dhid_ref), (w_hbm, w_ref))
+        )
+    ]
+    for fetch in fetches:
+        fetch.start()
+    for offset in range(tiles):
+        key_id = lax.broadcasted_iota(jnp.int32, (rows, rows), 0)
+        row_id = lax.broadcasted_iota(jnp.int32, (rows, rows), 1)
+        distance = row_id - key_id + offset * rows
+        key_time = key_id + (start - offset * rows)
+        visible = (distance >= 0) & (distance < span) & (key_time >= 0)
+        bias[offset] = jnp.where(visible, 0.0, NEGATIVE)
+
+    for fetch in fetches:
+        fetch.wait()
     dattended = dot(dhid_ref[...], w_ref[...], NT).astype(jnp.bfloat16)
     datt[...] = dattended
     product = dattended.astype(jnp.float32) * att_ref[...].astype(jnp.float32)
@@ -295,14 +312,6 @@
     feature_id = lax.broadcasted_iota(jnp.int32, (heads, att), 1)
     ours = (feature_id >= head_id * HEAD_DIM) & (feature_id < (head_id + 1) * HEAD_DIM)
     deltas = dot(jnp.where(ours, 1.0, 0.0), product, NT, lax.Precision.HIGHEST)
-
-    for offset in range(tiles):
-        key_id = lax.broadcasted_iota(jnp.int32, (rows, rows), 0)
-        row_id = lax.broadcasted_iota(jnp.int32, (rows, rows), 1)
-        distance = row_id - key_id + offset * rows
-        key_time = key_id + (start - offset * rows)
-        visible = (distance >= 0) & (distance < span) & (key_time >= 0)
-        bias[offset] = jnp.where(visible, 0.0, NEGATIVE)
 
     for pair in range(att // LANES):
         columns = slice(pair * LANES, (pair + 1) * LANES)
@@ -329,6 +338,13 @@
         dq_ref[:, columns] = (merge_heads(dquery) * scale).astype(jnp.bfloat16)
 
 
+def relay_kernel(device_ref, own_ref, swapped_ref, message_ref, own_out, message_out):
+    odd = lax.rem(device_ref[0], 2).astype(jnp.float32)
+    swapped = swapped_ref[...].astype(jnp.float32)
+    own_out[...] = own_ref[...] + swapped * (1.0 - odd)
+    message_out[...] = (message_ref[...].astype(jnp.float32) + swapped * odd).astype(jnp.bfloat16)
+
+
 def merge_kernel(*refs):
     own_ref, *message_refs, dk_ref, dv_ref = refs
     rows = dk_ref.shape[0]
@@ -405,7 +421,7 @@
     core = lax.axis_index("core").astype(jnp.int32) if split else jnp.int32(0)
     place = jnp.stack([device, core])
     piece_rows = -(-(chunks * 16 + chunks) // 16) * 16
-    out_frames, attended, log_sums, dhidden, keep, give, query, out_weight = pl.pallas_call(
+    out_frames, attended, log_sums, dhidden, keep, give = pl.pallas_call(
         functools.partial(forward_kernel, context, rows, edge, taps),
         out_shape=(
             jax.ShapeDtypeStruct((rows, width), bf16),
@@ -413,13 +429,9 @@
             jax.ShapeDtypeStruct((heads, rows), f32),
             jax.ShapeDtypeStruct((rows, width), bf16),
         )
-        + (jax.ShapeDtypeStruct((pieces, piece_rows, LANES), bf16),) * 2
-        + (
-            jax.ShapeDtypeStruct((rows, att), bf16),
-            jax.ShapeDtypeStruct((att, width), bf16),
-        ),
+        + (jax.ShapeDtypeStruct((pieces, piece_rows, LANES), bf16),) * 2,
         in_specs=[smem, hbm] + [vmem] * (3 + context) + [hbm] * 3,
-        out_specs=(vmem,) * 8,
+        out_specs=(vmem,) * 6,
         scratch_shapes=[
             pltpu.VMEM((query_rows, att), bf16),
             pltpu.VMEM((key_rows, att), bf16),
@@ -433,6 +445,8 @@
             pltpu.VMEM((chunks, 2 * pieces, LANES), f32),
             pltpu.VMEM((taps * SUBLANES, LANES), f32),
             pltpu.VMEM((2, pieces, piece_rows, LANES), bf16),
+            pltpu.VMEM((rows, att), bf16),
+            pltpu.VMEM((att, width), bf16),
             pltpu.VMEM((taps, width), f32),
             pltpu.VMEM((rows, width), bf16),
             pltpu.SemaphoreType.DMA((4,)),
@@ -452,22 +466,45 @@
             jax.ShapeDtypeStruct((2 * rows, att), f32),
         )
         + (jax.ShapeDtypeStruct((2 * rows, att), bf16),) * context,
-        in_specs=[smem] + [vmem] * (6 + context),
+        in_specs=[smem, hbm] + [vmem] * (3 + context) + [hbm] * 2,
         out_specs=(vmem,) * (2 + context),
         scratch_shapes=[
             pltpu.VMEM((rows, att), bf16),
+            pltpu.VMEM((rows, width), bf16),
+            pltpu.VMEM((att, width), bf16),
+            pltpu.VMEM((rows, att), bf16),
             pltpu.VMEM((context + 1, rows, rows), f32),
+            pltpu.SemaphoreType.DMA((3,)),
         ],
         compiler_params=params,
         cost_estimate=cost(6 * 10**9, 10**7),
         name="backward",
-    )(place, query, *tiles, attended, log_sums, dhidden, out_weight)
+    )(place, in_hbm(query), *tiles, attended, log_sums, in_hbm(dhidden), in_hbm(out_weight))
     if split:
-        mine = summed_along(collected(mine), "z")
-        mine, *messages = lax.optimization_barrier((mine, *messages))
+        mine, own_grads, *messages = lax.optimization_barrier(
+            (collected(mine), own_grads, *messages)
+        )
+    messages = dict(enumerate(messages, 1))
+    if context > 1:
+        swapped = lax.ppermute(messages.pop(1), "y", [(0, 1), (1, 0)])
+        own_grads, messages[2] = pl.pallas_call(
+            relay_kernel,
+            out_shape=(
+                jax.ShapeDtypeStruct((2 * rows, att), f32),
+                jax.ShapeDtypeStruct((2 * rows, att), bf16),
+            ),
+            in_specs=[smem] + [vmem] * 3,
+            out_specs=(vmem,) * 2,
+            compiler_params=params,
+            cost_estimate=cost(10**9, 3 * 10**6),
+            name="relay",
+        )(place, own_grads, swapped, messages[2])
+    if split:
+        mine = summed_along(mine, "z")
+        mine, messages = lax.optimization_barrier((mine, messages))
         mine = exchange(jnp.broadcast_to(mine, (lax.axis_size(PLANE_AXES), *mine.shape)))
         mine = mine.reshape(keep.shape)
-    messages = [shifted(message, -offset) for offset, message in enumerate(messages, 1)]
+    messages = [shifted(message, -offset) for offset, message in messages.items()]
     if split:
         mine, *messages = lax.optimization_barrier((mine, *messages))
         halves = (mine, other_core(mine))
@@ -476,7 +513,7 @@
     key_grad, value_grad = pl.pallas_call(
         merge_kernel,
         out_shape=(jax.ShapeDtypeStruct((rows, att), bf16),) * 2,
-        in_specs=[vmem] * (1 + context),
+        in_specs=[vmem] * (1 + len(messages)),
         out_specs=(vmem,) * 2,
         compiler_params=params,
         name="merge",

time: 103 us -> 94.2 us (0.915)
  blocking collectives: 19.2 us -> 0 us
  starting transfers between devices: 28 us -> 37.5 us
  local copies, waits for them, and re-layouts: 4.05 us -> 0.9 us
  Pallas kernels: 21.2 us -> 23.4 us
  other arithmetic: 0.41 us -> 2.29 us
    all_to_all x1 -> x0, blocking collectives: 19.2 us -> none  [exchange(): return lax.all_to_all(x, PLANE_AXES, 0, 0, tiled=True)]
    all_to_all x1 -> x2, starting transfers between devices: 3.48 us -> 11.8 us  [exchange(): return lax.all_to_all(x, PLANE_AXES, 0, 0, tiled=True)]
    ppermute x6 -> x5, waiting for transfers between devices: 22.2 us -> 15.8 us  [shifted(): lax.ppermute(x, RUN_AXES, [(i, i + by) for i in devices if i + by in devi...]
    ppermute x2, waiting for transfers between devices: 3.13 us -> 7.71 us  [summed_along(): other = lax.ppermute(x, axis, [(i, i ^ step) for i in range(size)])]
    unnamed x12 -> x2, local copies, waits for them, and re-layouts: 3.16 us -> 0.01 us
    all_to_all x1 -> x2, waiting for transfers between devices: 0.01 us -> 2.13 us  [exchange(): return lax.all_to_all(x, PLANE_AXES, 0, 0, tiled=True)]
    ppermute x0 -> x1, starting transfers between devices: none -> 1.52 us  [per_device(): swapped = lax.ppermute(messages.pop(1), 'y', [(0, 1), (1, 0)])]
    pallas_call x1, Pallas kernels: 5.99 us -> 7.42 us  [per_device(): pl.pallas_call(functools.partial(backward_kernel, context, rows), out_sha...]
  transfers between devices with their start and end apart: 11 -> 12, of which waited for: 6 -> 8; matrix products, arithmetic and copies ran while one was open for 0% -> 0% of each run, Pallas kernels for 7% -> 9%
where the time goes in v6:
time: 94.2 us; the launch traced here: 93.7 us
  starting transfers between devices  37.5 us (40%)
  waiting for transfers between devices  28.9 us (31%)
  Pallas kernels  23.4 us (25%)
  other arithmetic  2.29 us (2%)
    ppermute x5, starting transfers between devices, shifted(): lax.ppermute(x, RUN_AXES, [(i, i + by) for i in devices if i + by in devi...  16.5 us
    ppermute x5, waiting for transfers between devices, shifted(): lax.ppermute(x, RUN_AXES, [(i, i + by) for i in devices if i + by in devi...  15.8 us
    all_to_all x2, starting transfers between devices, exchange(): return lax.all_to_all(x, PLANE_AXES, 0, 0, tiled=True)  11.8 us
    pallas_call x1, Pallas kernels, per_device(): pl.pallas_call(functools.partial(forward_kernel, context, rows, edge, tap...  11.2 us
    ppermute x2, waiting for transfers between devices, summed_along(): other = lax.ppermute(x, axis, [(i, i ^ step) for i in range(size)])  7.71 us
    ppermute x2, starting transfers between devices, summed_along(): other = lax.ppermute(x, axis, [(i, i ^ step) for i in range(size)])  7.65 us
    pallas_call x1, Pallas kernels, per_device(): pl.pallas_call(functools.partial(backward_kernel, context, rows), out_sha...  7.42 us
    ppermute x2, waiting for transfers between devices, other_core(): return lax.ppermute(x, 'core', [(0, 1), (1, 0)])  3.2 us
  transfers between devices with their start and end apart: 12, of which 8 were waited for; matrix products, arithmetic and copies ran while one was open for 0% of the time, Pallas kernels for 9%

profile of v6, /device:TPU:0, one launch (start us, length us, event | category | flops | bytes accessed | tf_op | source)
XLA Modules:
  0.0 93.7 jit_solution(5355497019113161559)
XLA Ops:
  0.6 1.1 %pack.1 = (bf16[416,512]{1,0:T(8,128)(2,1)S(1)}, bf16[64,512]{1,0:T(8,128)(2,1)S(1)}, bf16[160,512]{1,0:T(8,128)(2,1)S(1)}) custom-call(bf16[192,512]{1,0:T(8,128)(2,1)} %bitcast.16, bf16[192,512]{1,0:T(8,128)(2,1)} %bitcast.17, bf16[192,512]{1,0:T(8,128)(2,1)} %bitcast.18, bf16[192,1024]{1,0:T(8,128)(2,1)} %bitcast.14), custom_call_target="tpu_custom_call" | custom-call | tf_op jit(solution)/shard_map/pack/pallas_call | solution.py:401
  1.8 5.0 %collective-permute-start.1 = (bf16[416,512]{1,0:T(8,128)(2,1)S(1)}, bf16[416,512]{1,0:T(8,128)(2,1)S(1)}, u32[]{:S(2)}, u32[]{:S(2)}) collective-permute-start(bf16[416,512]{1,0:T(8,128)(2,1)S(1)} %get-tuple-element.35.refs_2_), channel_id=1, source_target_pairs={{0,2},{1,3},{2,4},{3,5},{4,6},{5,7},{8,10},{9,11},{10,12},{11,13},... | collective-permute-start | bytes 1277960 | tf_op jit(solution)/shard_map/ppermute | solution.py:32
  6.7 3.5 %collective-permute-start = (bf16[416,512]{1,0:T(8,128)(2,1)S(1)}, bf16[416,512]{1,0:T(8,128)(2,1)S(1)}, u32[]{:S(2)}, u32[]{:S(2)}) collective-permute-start(bf16[416,512]{1,0:T(8,128)(2,1)S(1)} %get-tuple-element.35.refs_2_), channel_id=1, source_target_pairs={{0,1},{1,2},{2,3},{3,4},{4,5},{5,6},{6,7},{8,9},{9,10},{10,11},{11... | collective-permute-start | bytes 1277960 | tf_op jit(solution)/shard_map/ppermute | solution.py:32
  10.2 1.3 %collective-permute-start.3 = (bf16[160,512]{1,0:T(8,128)(2,1)S(1)}, bf16[160,512]{1,0:T(8,128)(2,1)S(1)}, u32[]{:S(2)}, u32[]{:S(2)}) collective-permute-start(bf16[160,512]{1,0:T(8,128)(2,1)S(1)} %get-tuple-element.37), channel_id=1, source_target_pairs={{1,0},{2,1},{3,2},{4,3},{5,4},{6,5},{7,6},{9,8},{10,9},{11,10},{12... | collective-permute-start | bytes 491528 | tf_op jit(solution)/shard_map/ppermute | solution.py:32
  11.5 5.5 %collective-permute-start.2 = (bf16[64,512]{1,0:T(8,128)(2,1)S(1)}, bf16[64,512]{1,0:T(8,128)(2,1)S(1)}, u32[]{:S(2)}, u32[]{:S(2)}) collective-permute-start(bf16[64,512]{1,0:T(8,128)(2,1)S(1)} %get-tuple-element.36), channel_id=1, source_target_pairs={{0,3},{1,4},{2,5},{3,6},{4,7},{8,11},{9,12},{10,13},{11,14},{12,15... | collective-permute-start | bytes 196616 | tf_op jit(solution)/shard_map/ppermute | solution.py:32
  17.0 0.1 pad_add_fusion.refs_0_.device_ref
  17.1 1.8 %collective-permute-done.2.refs_5_ = bf16[64,512]{1,0:T(8,128)(2,1)S(1)} collective-permute-done((bf16[64,512]{1,0:T(8,128)(2,1)S(1)}, bf16[64,512]{1,0:T(8,128)(2,1)S(1)}, u32[]{:S(2)}, u32[]{:S(2)}) %collective-permute-start.2) | collective-permute-done | bytes 65568 | tf_op jit(solution)/shard_map/ppermute | solution.py:32
  18.9 0.0 collective-permute-done.3.refs_6_
  18.9 0.0 collective-permute-done.1.refs_4_
  18.9 3.5 %collective-permute-done.refs_3_ = bf16[416,512]{1,0:T(8,128)(2,1)S(1)} collective-permute-done((bf16[416,512]{1,0:T(8,128)(2,1)S(1)}, bf16[416,512]{1,0:T(8,128)(2,1)S(1)}, u32[]{:S(2)}, u32[]{:S(2)}) %collective-permute-start) | collective-permute-done | bytes 426016 | tf_op jit(solution)/shard_map/ppermute | solution.py:32
  22.5 11.2 %forward.1 = (bf16[192,1024]{1,0:T(8,128)(2,1)}, bf16[192,512]{1,0:T(8,128)(2,1)S(1)}, f32[8,192]{1,0:T(8,128)S(1)}, bf16[192,1024]{1,0:T(8,128)(2,1)S(1)}, bf16...) custom-call(s32[2]{0:T(128)S(1)} %pad_add_fusion.refs_0_.device_ref, bf16[192,512]{1,0:T(8,128)(2,1)} %bitcast.19, ...), custom_call_target="tpu_custom_call" | custom-call | flops 8000000000 | bytes 10000000 | tf_op jit(solution)/shard_map/forward/pallas_call | solution.py:424
  33.7 0.0 copy-start
  33.7 0.1 collective-permute-start.4
  33.7 2.0 %collective-permute-done.4 = bf16[16,144,128]{2,1,0:T(8,128)(2,1)S(1)} collective-permute-done((bf16[16,144,128]{2,1,0:T(8,128)(2,1)S(1)}, bf16[16,144,128]{2,1,0:T(8,128)(2,1)S(1)}, u32[]{:S(2)}, u32[]{:S(2)}) %collective-permute-start.4) | collective-permute-done | bytes 589856 | tf_op jit(solution)/shard_map/ppermute | solution.py:378
  35.7 1.0 %add_convert_fusion = bf16[16,144,128]{2,1,0:T(8,128)(2,1)} fusion(bf16[16,144,128]{2,1,0:T(8,128)(2,1)S(1)} %collective-permute-done.4, bf16[16,144,128]{2,1,0:T(8,128)(2,1)S(1)} %get-tuple-element.41), kind=kLoop, calls=%fused_computation | loop fusion | flops 1179648 | bytes 1769472 | tf_op jit(solution)/shard_map/convert_element_type | solution.py:460
  36.7 0.0 copy-done
  36.7 7.6 %all-to-all-start = ((bf16[4,576,128]{2,1,0:T(8,128)(2,1)}), bf16[4,576,128]{2,1,0:T(8,128)(2,1)}, u32[]{:S(2)}, u32[]{:S(2)}) async-start(bf16[4,576,128]{2,1,0:T(8,128)(2,1)} %bitcast.8), calls=%async_computation | async-start | bytes 1179648 | tf_op jit(solution)/shard_map/all_to_all | solution.py:360
  44.3 7.4 %backward.1 = (bf16[192,512]{1,0:T(8,128)(2,1)}, f32[384,512]{1,0:T(8,128)S(1)}, bf16[384,512]{1,0:T(8,128)(2,1)S(1)}, bf16[384,512]{1,0:T(8,128)(2,1)S(1)}) custom-call(s32[2]{0:T(128)S(1)} %pad_add_fusion.refs_0_.device_ref, bf16[192,512]{1,0:T(8,128)(2,1)} %bitcast.20, bf16[416,512]{1,0:T(8,128)(2,1)S(1)} %get-tuple-element.35.refs_2_, ...), custom_call_target="tpu_custom_call" | custom-call | flops 6000000000 | bytes 10000000 | tf_op jit(solution)/shard_map/backward/pallas_call | solution.py:462
  51.7 2.1 %all-to-all-done = bf16[4,576,128]{2,1,0:T(8,128)(2,1)} async-done(((bf16[4,576,128]{2,1,0:T(8,128)(2,1)}), bf16[4,576,128]{2,1,0:T(8,128)(2,1)}, u32[]{:S(2)}, u32[]{:S(2)}) %all-to-all-start) | async-done | bytes 589856 | tf_op jit(solution)/shard_map/all_to_all | solution.py:360
  53.8 1.2 %reduce_sum.12 = bf16[576,128]{1,0:T(8,128)(2,1)S(1)} reduce(bf16[4,576,128]{2,1,0:T(8,128)(2,1)} %all-to-all-done, bf16[]{:T(256)} %constant.15.clone.1), dimensions={0}, to_apply=%region_0.0 | reduce | flops 221184 | bytes 737282 | tf_op jit(solution)/shard_map/reduce_sum | solution.py:365
  55.0 3.0 %collective-permute-start.6 = (bf16[576,128]{1,0:T(8,128)(2,1)S(1)}, bf16[576,128]{1,0:T(8,128)(2,1)S(1)}, u32[]{:S(2)}, u32[]{:S(2)}) collective-permute-start(bf16[576,128]{1,0:T(8,128)(2,1)S(1)} %reduce_sum.12), channel_id=1, source_target_pairs={{0,2},{2,0},{4,6},{6,4},{1,3},{3,1},{5,7},{7,5},{8,10},{10,8},{12,... | collective-permute-start | bytes 442376 | tf_op jit(solution)/shard_map/ppermute | solution.py:371
  58.1 1.5 %collective-permute-start.5 = (bf16[384,512]{1,0:T(8,128)(2,1)S(1)}, bf16[384,512]{1,0:T(8,128)(2,1)S(1)}, u32[]{:S(2)}, u32[]{:S(2)}) collective-permute-start(bf16[384,512]{1,0:T(8,128)(2,1)S(1)} %get-tuple-element.51), channel_id=1, source_target_pairs={{0,1},{1,0},{2,3},{3,2},{4,5},{5,4},{6,7},{7,6},{8,9},{9,8},{10,11... | collective-permute-start | bytes 1179656 | tf_op jit(solution)/shard_map/ppermute | solution.py:489
  59.6 1.9 %collective-permute-done.6 = bf16[576,128]{1,0:T(8,128)(2,1)S(1)} collective-permute-done((bf16[576,128]{1,0:T(8,128)(2,1)S(1)}, bf16[576,128]{1,0:T(8,128)(2,1)S(1)}, u32[]{:S(2)}, u32[]{:S(2)}) %collective-permute-start.6) | collective-permute-done | bytes 147488 | tf_op jit(solution)/shard_map/ppermute | solution.py:371
  61.5 4.6 %collective-permute-start.7 = (bf16[576,128]{1,0:T(8,128)(2,1)S(1)}, bf16[576,128]{1,0:T(8,128)(2,1)S(1)}, u32[]{:S(2)}, u32[]{:S(2)}) collective-permute-start(bf16[576,128]{1,0:T(8,128)(2,1)S(1)} %add_convert_fusion.2), channel_id=1, source_target_pairs={{0,4},{2,6},{4,0},{6,2},{1,5},{3,7},{5,1},{7,3},{8,12},{10,14},{12... | collective-permute-start | bytes 442376 | tf_op jit(solution)/shard_map/ppermute | solution.py:371
  66.1 5.9 %collective-permute-done.7 = bf16[576,128]{1,0:T(8,128)(2,1)S(1)} collective-permute-done((bf16[576,128]{1,0:T(8,128)(2,1)S(1)}, bf16[576,128]{1,0:T(8,128)(2,1)S(1)}, u32[]{:S(2)}, u32[]{:S(2)}) %collective-permute-start.7) | collective-permute-done | bytes 147488 | tf_op jit(solution)/shard_map/ppermute | solution.py:371
  72.0 0.0 collective-permute-done.5.swapped_ref
  72.0 0.7 relay.1
  72.7 0.9 broadcast_in_dim.17
  73.6 4.2 %all-to-all-start.1 = ((bf16[4,576,128]{2,1,0:T(8,128)(2,1)}), bf16[4,576,128]{2,1,0:T(8,128)(2,1)S(1)}, u32[]{:S(2)}, u32[]{:S(2)}) async-start(bf16[4,576,128]{2,1,0:T(8,128)(2,1)} %broadcast_in_dim.17), calls=%async_computation.1 | async-start | bytes 1179648 | tf_op jit(solution)/shard_map/all_to_all | solution.py:360
  77.9 1.3 %collective-permute-start.8 = (bf16[384,512]{1,0:T(8,128)(2,1)S(1)}, bf16[384,512]{1,0:T(8,128)(2,1)S(1)}, u32[]{:S(2)}, u32[]{:S(2)}) collective-permute-start(bf16[384,512]{1,0:T(8,128)(2,1)S(1)} %get-tuple-element.57), channel_id=1, source_target_pairs={{2,0},{3,1},{4,2},{5,3},{6,4},{7,5},{10,8},{11,9},{12,10},{13,11},... | collective-permute-start | bytes 1179656 | tf_op jit(solution)/shard_map/ppermute | solution.py:32
  79.2 10.5 %collective-permute-done.8.refs_1_ = bf16[384,512]{1,0:T(8,128)(2,1)S(1)} collective-permute-done((bf16[384,512]{1,0:T(8,128)(2,1)S(1)}, bf16[384,512]{1,0:T(8,128)(2,1)S(1)}, u32[]{:S(2)}, u32[]{:S(2)}) %collective-permute-start.8) | collective-permute-done | bytes 393248 | tf_op jit(solution)/shard_map/ppermute | solution.py:32
  89.6 0.0 all-to-all-done.1
  89.6 0.0 collective-permute-start.9
  89.6 0.8 merge.1
  90.4 1.2 %collective-permute-done.9.far_ref = bf16[16,144,128]{2,1,0:T(8,128)(2,1)S(1)} collective-permute-done((bf16[16,144,128]{2,1,0:T(8,128)(2,1)S(1)}, bf16[16,144,128]{2,1,0:T(8,128)(2,1)S(1)}, u32[]{:S(2)}, u32[]{:S(2)}) %collective-permute-start.9) | collective-permute-done | bytes 589856 | tf_op jit(solution)/shard_map/ppermute | solution.py:378
  91.6 2.1 %unpack.1 = (f32[512,1024]{1,0:T(8,128)}, f32[31,1024]{1,0:T(8,128)}) custom-call(s32[2]{0:T(128)S(1)} %pad_add_fusion.refs_0_.device_ref, bf16[16,144,128]{2,1,0:T(8,128)(2,1)S(1)} %bitcast.13, bf16[16,144,128]{2,1,0:T(8,128)(2,1)S(1)} %collective-permute-done.9.far_ref), custom_call_target="tpu_custom_call" | custom-call | tf_op jit(solution)/shard_map/unpack/pallas_call | solution.py:521
  (2 shorter events, 0.1 us)
Async XLA Ops:
  1.8 17.1 %collective-permute-start.1 = (bf16[416,512]{1,0:T(8,128)(2,1)S(1)}, bf16[416,512]{1,0:T(8,128)(2,1)S(1)}, u32[]{:S(2)}, u32[]{:S(2)}) collective-permute-start(bf16[416,512]{1,0:T(8,128)(2,1)S(1)} %get-tuple-element.35.refs_2_), channel_id=1, source_target_pairs={{0,2},{1,3},{2,4},{3,5},{4,6},{5,7},{8,10},{9,11},{10,12},{11,13},... | collective-permute-start | bytes 1277960 | tf_op jit(solution)/shard_map/ppermute | solution.py:32
  6.7 15.7 %collective-permute-start = (bf16[416,512]{1,0:T(8,128)(2,1)S(1)}, bf16[416,512]{1,0:T(8,128)(2,1)S(1)}, u32[]{:S(2)}, u32[]{:S(2)}) collective-permute-start(bf16[416,512]{1,0:T(8,128)(2,1)S(1)} %get-tuple-element.35.refs_2_), channel_id=1, source_target_pairs={{0,1},{1,2},{2,3},{3,4},{4,5},{5,6},{6,7},{8,9},{9,10},{10,11},{11... | collective-permute-start | bytes 1277960 | tf_op jit(solution)/shard_map/ppermute | solution.py:32
  10.2 8.7 %collective-permute-start.3 = (bf16[160,512]{1,0:T(8,128)(2,1)S(1)}, bf16[160,512]{1,0:T(8,128)(2,1)S(1)}, u32[]{:S(2)}, u32[]{:S(2)}) collective-permute-start(bf16[160,512]{1,0:T(8,128)(2,1)S(1)} %get-tuple-element.37), channel_id=1, source_target_pairs={{1,0},{2,1},{3,2},{4,3},{5,4},{6,5},{7,6},{9,8},{10,9},{11,10},{12... | collective-permute-start | bytes 491528 | tf_op jit(solution)/shard_map/ppermute | solution.py:32
  11.5 7.4 %collective-permute-start.2 = (bf16[64,512]{1,0:T(8,128)(2,1)S(1)}, bf16[64,512]{1,0:T(8,128)(2,1)S(1)}, u32[]{:S(2)}, u32[]{:S(2)}) collective-permute-start(bf16[64,512]{1,0:T(8,128)(2,1)S(1)} %get-tuple-element.36), channel_id=1, source_target_pairs={{0,3},{1,4},{2,5},{3,6},{4,7},{8,11},{9,12},{10,13},{11,14},{12,15... | collective-permute-start | bytes 196616 | tf_op jit(solution)/shard_map/ppermute | solution.py:32
  33.7 3.1 %copy-start = (bf16[192,1024]{1,0:T(8,128)(2,1)}, bf16[192,1024]{1,0:T(8,128)(2,1)S(1)}, u32[]{:S(2)}) copy-start(bf16[192,1024]{1,0:T(8,128)(2,1)S(1)} %get-tuple-element.44.refs_7_) | copy-start | bytes 1179652
  33.7 2.1 %collective-permute-start.4 = (bf16[16,144,128]{2,1,0:T(8,128)(2,1)S(1)}, bf16[16,144,128]{2,1,0:T(8,128)(2,1)S(1)}, u32[]{:S(2)}, u32[]{:S(2)}) collective-permute-start(bf16[16,144,128]{2,1,0:T(8,128)(2,1)S(1)} %get-tuple-element.42), channel_id=1, source_target_pairs={{0,8},{8,0},{1,9},{9,1},{2,10},{10,2},{3,11},{11,3},{4,12},{12,4},... | collective-permute-start | bytes 1769480 | tf_op jit(solution)/shard_map/ppermute | solution.py:378
  36.7 17.1 %all-to-all-start = ((bf16[4,576,128]{2,1,0:T(8,128)(2,1)}), bf16[4,576,128]{2,1,0:T(8,128)(2,1)}, u32[]{:S(2)}, u32[]{:S(2)}) async-start(bf16[4,576,128]{2,1,0:T(8,128)(2,1)} %bitcast.8), calls=%async_computation | async-start | bytes 1179648 | tf_op jit(solution)/shard_map/all_to_all | solution.py:360
  55.0 6.4 %collective-permute-start.6 = (bf16[576,128]{1,0:T(8,128)(2,1)S(1)}, bf16[576,128]{1,0:T(8,128)(2,1)S(1)}, u32[]{:S(2)}, u32[]{:S(2)}) collective-permute-start(bf16[576,128]{1,0:T(8,128)(2,1)S(1)} %reduce_sum.12), channel_id=1, source_target_pairs={{0,2},{2,0},{4,6},{6,4},{1,3},{3,1},{5,7},{7,5},{8,10},{10,8},{12,... | collective-permute-start | bytes 442376 | tf_op jit(solution)/shard_map/ppermute | solution.py:371
  58.1 13.9 %collective-permute-start.5 = (bf16[384,512]{1,0:T(8,128)(2,1)S(1)}, bf16[384,512]{1,0:T(8,128)(2,1)S(1)}, u32[]{:S(2)}, u32[]{:S(2)}) collective-permute-start(bf16[384,512]{1,0:T(8,128)(2,1)S(1)} %get-tuple-element.51), channel_id=1, source_target_pairs={{0,1},{1,0},{2,3},{3,2},{4,5},{5,4},{6,7},{7,6},{8,9},{9,8},{10,11... | collective-permute-start | bytes 1179656 | tf_op jit(solution)/shard_map/ppermute | solution.py:489
  61.5 10.5 %collective-permute-start.7 = (bf16[576,128]{1,0:T(8,128)(2,1)S(1)}, bf16[576,128]{1,0:T(8,128)(2,1)S(1)}, u32[]{:S(2)}, u32[]{:S(2)}) collective-permute-start(bf16[576,128]{1,0:T(8,128)(2,1)S(1)} %add_convert_fusion.2), channel_id=1, source_target_pairs={{0,4},{2,6},{4,0},{6,2},{1,5},{3,7},{5,1},{7,3},{8,12},{10,14},{12... | collective-permute-start | bytes 442376 | tf_op jit(solution)/shard_map/ppermute | solution.py:371
  73.6 16.0 %all-to-all-start.1 = ((bf16[4,576,128]{2,1,0:T(8,128)(2,1)}), bf16[4,576,128]{2,1,0:T(8,128)(2,1)S(1)}, u32[]{:S(2)}, u32[]{:S(2)}) async-start(bf16[4,576,128]{2,1,0:T(8,128)(2,1)} %broadcast_in_dim.17), calls=%async_computation.1 | async-start | bytes 1179648 | tf_op jit(solution)/shard_map/all_to_all | solution.py:360
  77.9 11.8 %collective-permute-start.8 = (bf16[384,512]{1,0:T(8,128)(2,1)S(1)}, bf16[384,512]{1,0:T(8,128)(2,1)S(1)}, u32[]{:S(2)}, u32[]{:S(2)}) collective-permute-start(bf16[384,512]{1,0:T(8,128)(2,1)S(1)} %get-tuple-element.57), channel_id=1, source_target_pairs={{2,0},{3,1},{4,2},{5,3},{6,4},{7,5},{10,8},{11,9},{12,10},{13,11},... | collective-permute-start | bytes 1179656 | tf_op jit(solution)/shard_map/ppermute | solution.py:32
  89.6 2.0 %collective-permute-start.9 = (bf16[16,144,128]{2,1,0:T(8,128)(2,1)S(1)}, bf16[16,144,128]{2,1,0:T(8,128)(2,1)S(1)}, u32[]{:S(2)}, u32[]{:S(2)}) collective-permute-start(bf16[16,144,128]{2,1,0:T(8,128)(2,1)S(1)} %bitcast.12), channel_id=1, source_target_pairs={{0,8},{8,0},{1,9},{9,1},{2,10},{10,2},{3,11},{11,3},{4,12},{12,4},... | collective-permute-start | bytes 1769480 | tf_op jit(solution)/shard_map/ppermute | solution.py:378

commit v7 on v6

--- a/solution.py
+++ b/solution.py
@@ -16,7 +16,7 @@
 NEGATIVE = -1e30
 RUN_AXES = ("z", "y")
 PLANE_AXES = ("x", "y")
-VMEM_LIMIT = 40 * 1024 * 1024
+VMEM_LIMIT = 28 * 1024 * 1024
 
 NN = (((1,), (0,)), ((), ()))
 NT = (((1,), (1,)), ((), ()))
@@ -57,14 +57,18 @@
     return jnp.where(lane < HEAD_DIM, stacked[:rows], stacked[rows:])
 
 
-def pack_kernel(edge, k_ref, v_ref, q_ref, cot_ref, own_ref, far_ref, near_ref, sems):
+def pack_kernel(
+    edge, k_ref, v_ref, q_ref, cot_ref, own_ref, keys_ref, values_ref, far_ref, near_ref, sems
+):
     rows, att = k_ref.shape
     width = cot_ref.shape[1]
     head, tail = pl.ds(0, edge), pl.ds(rows - edge, edge)
     moves = [
         (k_ref, own_ref.at[pl.ds(0, rows)]),
         (v_ref, own_ref.at[pl.ds(rows, rows)]),
-        (q_ref.at[tail], own_ref.at[pl.ds(2 * rows, edge)]),
+        (k_ref, keys_ref.at[pl.ds(0, rows)]),
+        (q_ref.at[tail], keys_ref.at[pl.ds(rows, edge)]),
+        (v_ref, values_ref),
         (k_ref.at[tail], far_ref.at[pl.ds(0, edge)]),
         (v_ref.at[tail], far_ref.at[pl.ds(edge, edge)]),
         (k_ref.at[head], near_ref.at[pl.ds(0, edge)]),
@@ -81,10 +85,29 @@
         copy.wait()
 
 
+def choose_kernel(device_ref, even_ref, odd_ref, out_ref):
+    odd = lax.rem(device_ref[0], 2)
+    rows = out_ref.shape[0]
+
+    @pl.when(odd == 0)
+    def _():
+        out_ref[...] = even_ref[...]
+
+    @pl.when(odd != 0)
+    def _():
+        out_ref[...] = odd_ref[odd_ref.shape[0] - rows :]
+
+
+def tile_places(rows, own_ref, keys_ref, values_ref, *further_refs):
+    places = [(own_ref, 0, own_ref, rows), (keys_ref, 0, values_ref, 0)]
+    return places + [(ref, 0, ref, rows) for ref in further_refs]
+
+
 def forward_kernel(context, rows, edge, taps, *refs):
-    tiles = context + 1
+    tiles = context + 2
     device_ref, q_hbm = refs[:2]
-    own_refs = refs[2 : 2 + tiles]
+    places = tile_places(rows, *refs[2 : 2 + tiles])
+    keys_ref = refs[3]
     far_ref, near_ref, w_hbm, conv_hbm, cot_hbm = refs[2 + tiles : 7 + tiles]
     out_ref, att_ref, lse_ref, dhid_ref, keep_ref, give_ref = refs[7 + tiles : 13 + tiles]
     qx, kx, vx, ax, lx, hid, cotx, dm, bias, kp, ks, parts = refs[13 + tiles : 25 + tiles]
@@ -108,13 +131,14 @@
     for fetch in fetches:
         fetch.start()
 
-    for ext, own_at, far_at in ((kx, 0, 0), (vx, rows, edge)):
-        ext[:edge] = far_ref[far_at : far_at + edge]
-        for offset in range(tiles):
-            first = edge + (context - offset) * rows
-            ext[first : first + rows] = own_refs[offset][own_at : own_at + rows]
-        ext[edge + span + rows :] = near_ref[far_at : far_at + edge]
-    qx[:edge] = own_refs[1][2 * rows : 2 * rows + edge] * scale
+    for offset, (k_ref, k_at, v_ref, v_at) in enumerate(places):
+        first = edge + (context - offset) * rows
+        kx[first : first + rows] = k_ref[k_at : k_at + rows]
+        vx[first : first + rows] = v_ref[v_at : v_at + rows]
+    for ext, at in ((kx, 0), (vx, edge)):
+        ext[:edge] = far_ref[at : at + edge]
+        ext[edge + span + rows :] = near_ref[at : at + edge]
+    qx[:edge] = keys_ref[rows : rows + edge] * scale
     qx[edge + rows :] = near_ref[2 * edge : 3 * edge] * scale
     fetches[0].wait()
     qx[edge : edge + rows] = q_ref[...] * scale
@@ -273,9 +297,9 @@
 
 
 def backward_kernel(context, rows, *refs):
-    tiles = context + 1
+    tiles = context + 2
     device_ref, q_hbm = refs[:2]
-    own_refs = refs[2 : 2 + tiles]
+    places = tile_places(rows, *refs[2 : 2 + tiles])
     att_ref, lse_ref, dhid_hbm, w_hbm = refs[2 + tiles : 6 + tiles]
     dq_ref, own_ref = refs[6 + tiles : 8 + tiles]
     message_refs = refs[8 + tiles : 8 + tiles + context]
@@ -295,7 +319,7 @@
     ]
     for fetch in fetches:
         fetch.start()
-    for offset in range(tiles):
+    for offset in range(context + 1):
         key_id = lax.broadcasted_iota(jnp.int32, (rows, rows), 0)
         row_id = lax.broadcasted_iota(jnp.int32, (rows, rows), 1)
         distance = row_id - key_id + offset * rows
@@ -322,9 +346,9 @@
         log_sum = jnp.concatenate(log_sum, axis=1)
         delta = jnp.concatenate(delta, axis=1)
         dquery = jnp.zeros((2 * rows, LANES), jnp.float32)
-        for offset in range(tiles):
-            kp = own_refs[offset][:rows, columns]
-            vp = own_refs[offset][rows : 2 * rows, columns]
+        for offset, (k_ref, k_at, v_ref, v_at) in enumerate(places):
+            kp = k_ref[k_at : k_at + rows, columns]
+            vp = v_ref[v_at : v_at + rows, columns]
             hidden_pairs = jnp.concatenate([bias[offset], bias[offset]], axis=1)
             probs = jnp.exp(dot(kp, qs, NT) + hidden_pairs - log_sum)
             dprobs = dot(vp, ds, NT)
@@ -398,22 +422,39 @@
     hbm = pl.BlockSpec(memory_space=pltpu.HBM)
     params = pltpu.CompilerParams(vmem_limit_bytes=VMEM_LIMIT)
 
-    own, far, near = pl.pallas_call(
+    own, keys, values, far, near = pl.pallas_call(
         functools.partial(pack_kernel, edge),
         out_shape=(
-            jax.ShapeDtypeStruct((2 * rows + edge, att), bf16),
+            jax.ShapeDtypeStruct((2 * rows, att), bf16),
+            jax.ShapeDtypeStruct((rows + edge, att), bf16),
+            jax.ShapeDtypeStruct((rows, att), bf16),
             jax.ShapeDtypeStruct((2 * edge, att), bf16),
             jax.ShapeDtypeStruct(((3 + width // att) * edge, att), bf16),
         ),
         in_specs=[hbm] * 4,
-        out_specs=(vmem,) * 3,
-        scratch_shapes=[pltpu.SemaphoreType.DMA((8 + width // att,))],
+        out_specs=(vmem,) * 5,
+        scratch_shapes=[pltpu.SemaphoreType.DMA((10 + width // att,))],
         compiler_params=params,
         name="pack",
     )(in_hbm(key), in_hbm(value), in_hbm(query), in_hbm(cot))
-    tiles = [own] + [shifted(own, o) for o in range(1, context + 1)]
+    further = [shifted(own, offset) for offset in range(2, context + 1)]
+    keys = shifted(keys, 1)
+    near = shifted(near, -1)
+    if further:
+        near, values = lax.optimization_barrier((near, values))
+        values = pl.pallas_call(
+            choose_kernel,
+            out_shape=jax.ShapeDtypeStruct((rows, att), bf16),
+            in_specs=[smem, vmem, vmem],
+            out_specs=vmem,
+            compiler_params=params,
+            name="choose",
+        )(device[None], values, further[0])
+        values = lax.ppermute(values, "y", [(0, 1), (1, 0)])
+    else:
+        values = shifted(values, 1)
+    tiles = [own, keys, values, *further]
     far = shifted(far, context + 1)
-    near = shifted(near, -1)
 
     pieces = att // 32
     layers = lax.axis_size("z")
@@ -430,7 +471,7 @@
             jax.ShapeDtypeStruct((rows, width), bf16),
         )
         + (jax.ShapeDtypeStruct((pieces, piece_rows, LANES), bf16),) * 2,
-        in_specs=[smem, hbm] + [vmem] * (3 + context) + [hbm] * 3,
+        in_specs=[smem, hbm] + [vmem] * (4 + context) + [hbm] * 3,
         out_specs=(vmem,) * 6,
         scratch_shapes=[
             pltpu.VMEM((query_rows, att), bf16),
@@ -466,7 +507,7 @@
             jax.ShapeDtypeStruct((2 * rows, att), f32),
         )
         + (jax.ShapeDtypeStruct((2 * rows, att), bf16),) * context,
-        in_specs=[smem, hbm] + [vmem] * (3 + context) + [hbm] * 2,
+        in_specs=[smem, hbm] + [vmem] * (4 + context) + [hbm] * 2,
         out_specs=(vmem,) * (2 + context),
         scratch_shapes=[
             pltpu.VMEM((rows, att), bf16),

time: 94.2 us -> 91.9 us (0.976)
  waiting for transfers between devices: 28.9 us -> 26.1 us
    ppermute x0 -> x1, starting transfers between devices: none -> 2.73 us  [per_device(): values = lax.ppermute(values, 'y', [(0, 1), (1, 0)])]
    all_to_all x2, starting transfers between devices: 11.8 us -> 9.65 us  [exchange(): return lax.all_to_all(x, PLANE_AXES, 0, 0, tiled=True)]
    ppermute x5, waiting for transfers between devices: 15.8 us -> 14.5 us  [shifted(): lax.ppermute(x, RUN_AXES, [(i, i + by) for i in devices if i + by in devi...]
    all_to_all x2, waiting for transfers between devices: 2.13 us -> 1.19 us  [exchange(): return lax.all_to_all(x, PLANE_AXES, 0, 0, tiled=True)]
  transfers between devices with their start and end apart: 12 -> 13, of which waited for: 8 -> 9; matrix products, arithmetic and copies ran while one was open for 0% -> 0% of each run, Pallas kernels for 9% -> 9%
where the time goes in v7:
time: 91.9 us; the launch traced here: 91.5 us
  starting transfers between devices  36.8 us (40%)
  waiting for transfers between devices  26.1 us (28%)
  Pallas kernels  23.7 us (26%)
  other arithmetic  2.29 us (2%)
  local copies, waits for them, and re-layouts  1.83 us (2%)
    ppermute x5, starting transfers between devices, shifted(): lax.ppermute(x, RUN_AXES, [(i, i + by) for i in devices if i + by in devi...  15.9 us
    ppermute x5, waiting for transfers between devices, shifted(): lax.ppermute(x, RUN_AXES, [(i, i + by) for i in devices if i + by in devi...  14.5 us
    pallas_call x1, Pallas kernels, per_device(): pl.pallas_call(functools.partial(forward_kernel, context, rows, edge, tap...  11.2 us
    all_to_all x2, starting transfers between devices, exchange(): return lax.all_to_all(x, PLANE_AXES, 0, 0, tiled=True)  9.65 us
    pallas_call x1, Pallas kernels, per_device(): pl.pallas_call(functools.partial(backward_kernel, context, rows), out_sha...  7.43 us
    ppermute x2, waiting for transfers between devices, summed_along(): other = lax.ppermute(x, axis, [(i, i ^ step) for i in range(size)])  7.19 us
    ppermute x2, starting transfers between devices, summed_along(): other = lax.ppermute(x, axis, [(i, i ^ step) for i in range(size)])  6.99 us
    ppermute x2, waiting for transfers between devices, other_core(): return lax.ppermute(x, 'core', [(0, 1), (1, 0)])  3.2 us
  transfers between devices with their start and end apart: 13, of which 9 were waited for; matrix products, arithmetic and copies ran while one was open for 0% of the time, Pallas kernels for 9%

profile of v7, /device:TPU:0, one launch (start us, length us, event | category | flops | bytes accessed | tf_op | source)
XLA Modules:
  0.0 91.5 jit_solution(11876249960224438233)
XLA Ops:
  0.6 1.4 %pack.1 = (bf16[384,512]{1,0:T(8,128)(2,1)S(1)}, bf16[224,512]{1,0:T(8,128)(2,1)S(1)}, bf16[192,512]{1,0:T(8,128)(2,1)S(1)}, bf16[64,512]{1,0:T(8,128)(2,1)S(1)}, bf16[160,512]{1,0:T(8,128)(2,1)S(1)}) custom-call(bf16[192,512]{1,0:T(8,128)(2,1)} %bitcast.16, bf16[192,512]{1,0:T(8,128)(2,1)} %bitcast.17, bf16[192,512]{1,0:T(8,128)(2,1)} %bitcast.18, ...), custom_call_target="tpu_custom_call" | custom-call | tf_op jit(solution)/shard_map/pack/pallas_call | solution.py:425
  2.0 5.0 %collective-permute-start.2 = (bf16[384,512]{1,0:T(8,128)(2,1)S(1)}, bf16[384,512]{1,0:T(8,128)(2,1)S(1)}, u32[]{:S(2)}, u32[]{:S(2)}) collective-permute-start(bf16[384,512]{1,0:T(8,128)(2,1)S(1)} %get-tuple-element.39.refs_2_), channel_id=1, source_target_pairs={{0,2},{1,3},{2,4},{3,5},{4,6},{5,7},{8,10},{9,11},{10,12},{11,13},... | collective-permute-start | bytes 1179656 | tf_op jit(solution)/shard_map/ppermute | solution.py:32
  7.0 1.3 %collective-permute-start.1 = (bf16[160,512]{1,0:T(8,128)(2,1)S(1)}, bf16[160,512]{1,0:T(8,128)(2,1)S(1)}, u32[]{:S(2)}, u32[]{:S(2)}) collective-permute-start(bf16[160,512]{1,0:T(8,128)(2,1)S(1)} %get-tuple-element.41), channel_id=1, source_target_pairs={{1,0},{2,1},{3,2},{4,3},{5,4},{6,5},{7,6},{9,8},{10,9},{11,10},{12... | collective-permute-start | bytes 491528 | tf_op jit(solution)/shard_map/ppermute | solution.py:32
  8.3 4.6 %collective-permute-start = (bf16[224,512]{1,0:T(8,128)(2,1)S(1)}, bf16[224,512]{1,0:T(8,128)(2,1)S(1)}, u32[]{:S(2)}, u32[]{:S(2)}) collective-permute-start(bf16[224,512]{1,0:T(8,128)(2,1)S(1)} %get-tuple-element.40), channel_id=1, source_target_pairs={{0,1},{1,2},{2,3},{3,4},{4,5},{5,6},{6,7},{8,9},{9,10},{10,11},{11... | collective-permute-start | bytes 688136 | tf_op jit(solution)/shard_map/ppermute | solution.py:32
  12.9 1.7 %collective-permute-done.1.refs_7_ = bf16[160,512]{1,0:T(8,128)(2,1)S(1)} collective-permute-done((bf16[160,512]{1,0:T(8,128)(2,1)S(1)}, bf16[160,512]{1,0:T(8,128)(2,1)S(1)}, u32[]{:S(2)}, u32[]{:S(2)}) %collective-permute-start.1) | collective-permute-done | bytes 163872 | tf_op jit(solution)/shard_map/ppermute | solution.py:32
  14.6 0.8 collective-permute-done.2.odd_ref.refs_5_
  15.4 2.7 %collective-permute-start.3 = (bf16[192,512]{1,0:T(8,128)(2,1)S(1)}, bf16[192,512]{1,0:T(8,128)(2,1)S(1)}, u32[]{:S(2)}, u32[]{:S(2)}) collective-permute-start(bf16[192,512]{1,0:T(8,128)(2,1)S(1)} %choose.1), channel_id=1, source_target_pairs={{0,1},{1,0},{2,3},{3,2},{4,5},{5,4},{6,7},{7,6},{8,9},{9,8},{10,11... | collective-permute-start | bytes 589832 | tf_op jit(solution)/shard_map/ppermute | solution.py:453
  18.1 3.8 %collective-permute-start.4 = (bf16[64,512]{1,0:T(8,128)(2,1)S(1)}, bf16[64,512]{1,0:T(8,128)(2,1)S(1)}, u32[]{:S(2)}, u32[]{:S(2)}) collective-permute-start(bf16[64,512]{1,0:T(8,128)(2,1)S(1)} %get-tuple-element.44), channel_id=1, source_target_pairs={{0,3},{1,4},{2,5},{3,6},{4,7},{8,11},{9,12},{10,13},{11,14},{12,15... | collective-permute-start | bytes 196616 | tf_op jit(solution)/shard_map/ppermute | solution.py:32
  21.9 0.1 pad_add_fusion.refs_0_.device_ref
  22.0 1.8 %collective-permute-done.4.refs_6_ = bf16[64,512]{1,0:T(8,128)(2,1)S(1)} collective-permute-done((bf16[64,512]{1,0:T(8,128)(2,1)S(1)}, bf16[64,512]{1,0:T(8,128)(2,1)S(1)}, u32[]{:S(2)}, u32[]{:S(2)}) %collective-permute-start.4) | collective-permute-done | bytes 65568 | tf_op jit(solution)/shard_map/ppermute | solution.py:32
  23.8 0.0 collective-permute-done.refs_3_
  23.8 0.0 collective-permute-done.3.refs_4_
  23.8 11.2 %forward.1 = (bf16[192,1024]{1,0:T(8,128)(2,1)}, bf16[192,512]{1,0:T(8,128)(2,1)S(1)}, f32[8,192]{1,0:T(8,128)S(1)}, bf16[192,1024]{1,0:T(8,128)(2,1)S(1)}, bf16...) custom-call(s32[2]{0:T(128)S(1)} %pad_add_fusion.refs_0_.device_ref, bf16[192,512]{1,0:T(8,128)(2,1)} %bitcast.19, ...), custom_call_target="tpu_custom_call" | custom-call | flops 8000000000 | bytes 10000000 | tf_op jit(solution)/shard_map/forward/pallas_call | solution.py:465
  35.0 0.0 copy-start
  35.0 0.0 copy-start.1
  35.0 0.1 collective-permute-start.5
  35.1 2.0 %collective-permute-done.5 = bf16[16,144,128]{2,1,0:T(8,128)(2,1)S(1)} collective-permute-done((bf16[16,144,128]{2,1,0:T(8,128)(2,1)S(1)}, bf16[16,144,128]{2,1,0:T(8,128)(2,1)S(1)}, u32[]{:S(2)}, u32[]{:S(2)}) %collective-permute-start.5) | collective-permute-done | bytes 589856 | tf_op jit(solution)/shard_map/ppermute | solution.py:402
  37.1 1.0 %add_convert_fusion = bf16[16,144,128]{2,1,0:T(8,128)(2,1)} fusion(bf16[16,144,128]{2,1,0:T(8,128)(2,1)S(1)} %collective-permute-done.5, bf16[16,144,128]{2,1,0:T(8,128)(2,1)S(1)} %get-tuple-element.49), kind=kLoop, calls=%fused_computation | loop fusion | flops 1179648 | bytes 1769472 | tf_op jit(solution)/shard_map/convert_element_type | solution.py:501
  38.1 0.0 copy-done
  38.1 0.0 copy-done.1
  38.1 5.2 %all-to-all-start = ((bf16[4,576,128]{2,1,0:T(8,128)(2,1)}), bf16[4,576,128]{2,1,0:T(8,128)(2,1)}, u32[]{:S(2)}, u32[]{:S(2)}) async-start(bf16[4,576,128]{2,1,0:T(8,128)(2,1)} %bitcast.8), calls=%async_computation | async-start | bytes 1179648 | tf_op jit(solution)/shard_map/all_to_all | solution.py:384
  43.3 0.0 copy-start.2
  43.3 0.9 %copy-done.2 = bf16[192,512]{1,0:T(8,128)(2,1)S(1)} copy-done((bf16[192,512]{1,0:T(8,128)(2,1)S(1)}, bf16[192,512]{1,0:T(8,128)(2,1)}, u32[]{:S(2)}) %copy-start.2) | copy-done | bytes 196632
  44.2 7.4 %backward.1 = (bf16[192,512]{1,0:T(8,128)(2,1)}, f32[384,512]{1,0:T(8,128)S(1)}, bf16[384,512]{1,0:T(8,128)(2,1)S(1)}, bf16[384,512]{1,0:T(8,128)(2,1)S(1)}) custom-call(s32[2]{0:T(128)S(1)} %pad_add_fusion.refs_0_.device_ref, bf16[192,512]{1,0:T(8,128)(2,1)} %bitcast.20, bf16[384,512]{1,0:T(8,128)(2,1)S(1)} %get-tuple-element.39.refs_2_, ...), custom_call_target="tpu_custom_call" | custom-call | flops 6000000000 | bytes 10000000 | tf_op jit(solution)/shard_map/backward/pallas_call | solution.py:503
  51.6 1.2 %all-to-all-done = bf16[4,576,128]{2,1,0:T(8,128)(2,1)} async-done(((bf16[4,576,128]{2,1,0:T(8,128)(2,1)}), bf16[4,576,128]{2,1,0:T(8,128)(2,1)}, u32[]{:S(2)}, u32[]{:S(2)}) %all-to-all-start) | async-done | bytes 589856 | tf_op jit(solution)/shard_map/all_to_all | solution.py:384
  52.8 1.2 %reduce_sum.12 = bf16[576,128]{1,0:T(8,128)(2,1)S(1)} reduce(bf16[4,576,128]{2,1,0:T(8,128)(2,1)} %all-to-all-done, bf16[]{:T(256)} %constant.15.clone.1), dimensions={0}, to_apply=%region_0.0 | reduce | flops 221184 | bytes 737282 | tf_op jit(solution)/shard_map/reduce_sum | solution.py:389
  54.0 2.7 %collective-permute-start.7 = (bf16[576,128]{1,0:T(8,128)(2,1)S(1)}, bf16[576,128]{1,0:T(8,128)(2,1)S(1)}, u32[]{:S(2)}, u32[]{:S(2)}) collective-permute-start(bf16[576,128]{1,0:T(8,128)(2,1)S(1)} %reduce_sum.12), channel_id=1, source_target_pairs={{0,2},{2,0},{4,6},{6,4},{1,3},{3,1},{5,7},{7,5},{8,10},{10,8},{12,... | collective-permute-start | bytes 442376 | tf_op jit(solution)/shard_map/ppermute | solution.py:395
  56.7 1.5 %collective-permute-start.6 = (bf16[384,512]{1,0:T(8,128)(2,1)S(1)}, bf16[384,512]{1,0:T(8,128)(2,1)S(1)}, u32[]{:S(2)}, u32[]{:S(2)}) collective-permute-start(bf16[384,512]{1,0:T(8,128)(2,1)S(1)} %get-tuple-element.59), channel_id=1, source_target_pairs={{0,1},{1,0},{2,3},{3,2},{4,5},{5,4},{6,7},{7,6},{8,9},{9,8},{10,11... | collective-permute-start | bytes 1179656 | tf_op jit(solution)/shard_map/ppermute | solution.py:530
  58.1 1.9 %collective-permute-done.7 = bf16[576,128]{1,0:T(8,128)(2,1)S(1)} collective-permute-done((bf16[576,128]{1,0:T(8,128)(2,1)S(1)}, bf16[576,128]{1,0:T(8,128)(2,1)S(1)}, u32[]{:S(2)}, u32[]{:S(2)}) %collective-permute-start.7) | collective-permute-done | bytes 147488 | tf_op jit(solution)/shard_map/ppermute | solution.py:395
  60.0 4.3 %collective-permute-start.8 = (bf16[576,128]{1,0:T(8,128)(2,1)S(1)}, bf16[576,128]{1,0:T(8,128)(2,1)S(1)}, u32[]{:S(2)}, u32[]{:S(2)}) collective-permute-start(bf16[576,128]{1,0:T(8,128)(2,1)S(1)} %add_convert_fusion.2), channel_id=1, source_target_pairs={{0,4},{2,6},{4,0},{6,2},{1,5},{3,7},{5,1},{7,3},{8,12},{10,14},{12... | collective-permute-start | bytes 442376 | tf_op jit(solution)/shard_map/ppermute | solution.py:395
  64.4 5.3 %collective-permute-done.8 = bf16[576,128]{1,0:T(8,128)(2,1)S(1)} collective-permute-done((bf16[576,128]{1,0:T(8,128)(2,1)S(1)}, bf16[576,128]{1,0:T(8,128)(2,1)S(1)}, u32[]{:S(2)}, u32[]{:S(2)}) %collective-permute-start.8) | collective-permute-done | bytes 147488 | tf_op jit(solution)/shard_map/ppermute | solution.py:395
  69.7 0.0 collective-permute-done.6.swapped_ref
  69.7 0.7 relay.1
  70.5 0.9 broadcast_in_dim.18
  71.4 4.4 %all-to-all-start.1 = ((bf16[4,576,128]{2,1,0:T(8,128)(2,1)}), bf16[4,576,128]{2,1,0:T(8,128)(2,1)S(1)}, u32[]{:S(2)}, u32[]{:S(2)}) async-start(bf16[4,576,128]{2,1,0:T(8,128)(2,1)} %broadcast_in_dim.18), calls=%async_computation.1 | async-start | bytes 1179648 | tf_op jit(solution)/shard_map/all_to_all | solution.py:384
  75.8 1.3 %collective-permute-start.9 = (bf16[384,512]{1,0:T(8,128)(2,1)S(1)}, bf16[384,512]{1,0:T(8,128)(2,1)S(1)}, u32[]{:S(2)}, u32[]{:S(2)}) collective-permute-start(bf16[384,512]{1,0:T(8,128)(2,1)S(1)} %get-tuple-element.65), channel_id=1, source_target_pairs={{2,0},{3,1},{4,2},{5,3},{6,4},{7,5},{10,8},{11,9},{12,10},{13,11},... | collective-permute-start | bytes 1179656 | tf_op jit(solution)/shard_map/ppermute | solution.py:32
  77.1 10.2 %collective-permute-done.9.refs_1_ = bf16[384,512]{1,0:T(8,128)(2,1)S(1)} collective-permute-done((bf16[384,512]{1,0:T(8,128)(2,1)S(1)}, bf16[384,512]{1,0:T(8,128)(2,1)S(1)}, u32[]{:S(2)}, u32[]{:S(2)}) %collective-permute-start.9) | collective-permute-done | bytes 393248 | tf_op jit(solution)/shard_map/ppermute | solution.py:32
  87.4 0.0 all-to-all-done.1
  87.4 0.0 collective-permute-start.10
  87.4 0.8 merge.1
  88.2 1.2 %collective-permute-done.10.far_ref = bf16[16,144,128]{2,1,0:T(8,128)(2,1)S(1)} collective-permute-done((bf16[16,144,128]{2,1,0:T(8,128)(2,1)S(1)}, bf16[16,144,128]{2,1,0:T(8,128)(2,1)S(1)}, u32[]{:S(2)}, u32[]{:S(2)}) %collective-permute-start.10) | collective-permute-done | bytes 589856 | tf_op jit(solution)/shard_map/ppermute | solution.py:402
  89.4 2.1 %unpack.1 = (f32[512,1024]{1,0:T(8,128)}, f32[31,1024]{1,0:T(8,128)}) custom-call(s32[2]{0:T(128)S(1)} %pad_add_fusion.refs_0_.device_ref, bf16[16,144,128]{2,1,0:T(8,128)(2,1)S(1)} %bitcast.13, bf16[16,144,128]{2,1,0:T(8,128)(2,1)S(1)} %collective-permute-done.10.far_ref), custom_call_target="tpu_custom_call" | custom-call | tf_op jit(solution)/shard_map/unpack/pallas_call | solution.py:562
  (3 shorter events, 0.1 us)
Async XLA Ops:
  2.0 13.3 %collective-permute-start.2 = (bf16[384,512]{1,0:T(8,128)(2,1)S(1)}, bf16[384,512]{1,0:T(8,128)(2,1)S(1)}, u32[]{:S(2)}, u32[]{:S(2)}) collective-permute-start(bf16[384,512]{1,0:T(8,128)(2,1)S(1)} %get-tuple-element.39.refs_2_), channel_id=1, source_target_pairs={{0,2},{1,3},{2,4},{3,5},{4,6},{5,7},{8,10},{9,11},{10,12},{11,13},... | collective-permute-start | bytes 1179656 | tf_op jit(solution)/shard_map/ppermute | solution.py:32
  7.0 7.6 %collective-permute-start.1 = (bf16[160,512]{1,0:T(8,128)(2,1)S(1)}, bf16[160,512]{1,0:T(8,128)(2,1)S(1)}, u32[]{:S(2)}, u32[]{:S(2)}) collective-permute-start(bf16[160,512]{1,0:T(8,128)(2,1)S(1)} %get-tuple-element.41), channel_id=1, source_target_pairs={{1,0},{2,1},{3,2},{4,3},{5,4},{6,5},{7,6},{9,8},{10,9},{11,10},{12... | collective-permute-start | bytes 491528 | tf_op jit(solution)/shard_map/ppermute | solution.py:32
  8.3 15.5 %collective-permute-start = (bf16[224,512]{1,0:T(8,128)(2,1)S(1)}, bf16[224,512]{1,0:T(8,128)(2,1)S(1)}, u32[]{:S(2)}, u32[]{:S(2)}) collective-permute-start(bf16[224,512]{1,0:T(8,128)(2,1)S(1)} %get-tuple-element.40), channel_id=1, source_target_pairs={{0,1},{1,2},{2,3},{3,4},{4,5},{5,6},{6,7},{8,9},{9,10},{10,11},{11... | collective-permute-start | bytes 688136 | tf_op jit(solution)/shard_map/ppermute | solution.py:32
  15.4 8.5 %collective-permute-start.3 = (bf16[192,512]{1,0:T(8,128)(2,1)S(1)}, bf16[192,512]{1,0:T(8,128)(2,1)S(1)}, u32[]{:S(2)}, u32[]{:S(2)}) collective-permute-start(bf16[192,512]{1,0:T(8,128)(2,1)S(1)} %choose.1), channel_id=1, source_target_pairs={{0,1},{1,0},{2,3},{3,2},{4,5},{5,4},{6,7},{7,6},{8,9},{9,8},{10,11... | collective-permute-start | bytes 589832 | tf_op jit(solution)/shard_map/ppermute | solution.py:453
  18.1 5.7 %collective-permute-start.4 = (bf16[64,512]{1,0:T(8,128)(2,1)S(1)}, bf16[64,512]{1,0:T(8,128)(2,1)S(1)}, u32[]{:S(2)}, u32[]{:S(2)}) collective-permute-start(bf16[64,512]{1,0:T(8,128)(2,1)S(1)} %get-tuple-element.44), channel_id=1, source_target_pairs={{0,3},{1,4},{2,5},{3,6},{4,7},{8,11},{9,12},{10,13},{11,14},{12,15... | collective-permute-start | bytes 196616 | tf_op jit(solution)/shard_map/ppermute | solution.py:32
  35.0 3.1 %copy-start = (bf16[192,1024]{1,0:T(8,128)(2,1)}, bf16[192,1024]{1,0:T(8,128)(2,1)S(1)}, u32[]{:S(2)}) copy-start(bf16[192,1024]{1,0:T(8,128)(2,1)S(1)} %get-tuple-element.52.refs_8_) | copy-start | bytes 1179652
  35.0 3.1 %copy-start.1 = (bf16[192,512]{1,0:T(8,128)(2,1)}, bf16[192,512]{1,0:T(8,128)(2,1)S(1)}, u32[]{:S(2)}) copy-start(bf16[192,512]{1,0:T(8,128)(2,1)S(1)} %get-tuple-element.47.refs_6_) | copy-start | bytes 589828
  35.0 2.1 %collective-permute-start.5 = (bf16[16,144,128]{2,1,0:T(8,128)(2,1)S(1)}, bf16[16,144,128]{2,1,0:T(8,128)(2,1)S(1)}, u32[]{:S(2)}, u32[]{:S(2)}) collective-permute-start(bf16[16,144,128]{2,1,0:T(8,128)(2,1)S(1)} %get-tuple-element.50), channel_id=1, source_target_pairs={{0,8},{8,0},{1,9},{9,1},{2,10},{10,2},{3,11},{11,3},{4,12},{12,4},... | collective-permute-start | bytes 1769480 | tf_op jit(solution)/shard_map/ppermute | solution.py:402
  38.1 14.8 %all-to-all-start = ((bf16[4,576,128]{2,1,0:T(8,128)(2,1)}), bf16[4,576,128]{2,1,0:T(8,128)(2,1)}, u32[]{:S(2)}, u32[]{:S(2)}) async-start(bf16[4,576,128]{2,1,0:T(8,128)(2,1)} %bitcast.8), calls=%async_computation | async-start | bytes 1179648 | tf_op jit(solution)/shard_map/all_to_all | solution.py:384
  43.3 0.9 %copy-start.2 = (bf16[192,512]{1,0:T(8,128)(2,1)S(1)}, bf16[192,512]{1,0:T(8,128)(2,1)}, u32[]{:S(2)}) copy-start(bf16[192,512]{1,0:T(8,128)(2,1)} %copy-done.1) | copy-start | bytes 589828
  54.0 6.0 %collective-permute-start.7 = (bf16[576,128]{1,0:T(8,128)(2,1)S(1)}, bf16[576,128]{1,0:T(8,128)(2,1)S(1)}, u32[]{:S(2)}, u32[]{:S(2)}) collective-permute-start(bf16[576,128]{1,0:T(8,128)(2,1)S(1)} %reduce_sum.12), channel_id=1, source_target_pairs={{0,2},{2,0},{4,6},{6,4},{1,3},{3,1},{5,7},{7,5},{8,10},{10,8},{12,... | collective-permute-start | bytes 442376 | tf_op jit(solution)/shard_map/ppermute | solution.py:395
  56.7 13.1 %collective-permute-start.6 = (bf16[384,512]{1,0:T(8,128)(2,1)S(1)}, bf16[384,512]{1,0:T(8,128)(2,1)S(1)}, u32[]{:S(2)}, u32[]{:S(2)}) collective-permute-start(bf16[384,512]{1,0:T(8,128)(2,1)S(1)} %get-tuple-element.59), channel_id=1, source_target_pairs={{0,1},{1,0},{2,3},{3,2},{4,5},{5,4},{6,7},{7,6},{8,9},{9,8},{10,11... | collective-permute-start | bytes 1179656 | tf_op jit(solution)/shard_map/ppermute | solution.py:530
  60.0 9.6 %collective-permute-start.8 = (bf16[576,128]{1,0:T(8,128)(2,1)S(1)}, bf16[576,128]{1,0:T(8,128)(2,1)S(1)}, u32[]{:S(2)}, u32[]{:S(2)}) collective-permute-start(bf16[576,128]{1,0:T(8,128)(2,1)S(1)} %add_convert_fusion.2), channel_id=1, source_target_pairs={{0,4},{2,6},{4,0},{6,2},{1,5},{3,7},{5,1},{7,3},{8,12},{10,14},{12... | collective-permute-start | bytes 442376 | tf_op jit(solution)/shard_map/ppermute | solution.py:395
  71.4 16.0 %all-to-all-start.1 = ((bf16[4,576,128]{2,1,0:T(8,128)(2,1)}), bf16[4,576,128]{2,1,0:T(8,128)(2,1)S(1)}, u32[]{:S(2)}, u32[]{:S(2)}) async-start(bf16[4,576,128]{2,1,0:T(8,128)(2,1)} %broadcast_in_dim.18), calls=%async_computation.1 | async-start | bytes 1179648 | tf_op jit(solution)/shard_map/all_to_all | solution.py:384
  75.8 11.5 %collective-permute-start.9 = (bf16[384,512]{1,0:T(8,128)(2,1)S(1)}, bf16[384,512]{1,0:T(8,128)(2,1)S(1)}, u32[]{:S(2)}, u32[]{:S(2)}) collective-permute-start(bf16[384,512]{1,0:T(8,128)(2,1)S(1)} %get-tuple-element.65), channel_id=1, source_target_pairs={{2,0},{3,1},{4,2},{5,3},{6,4},{7,5},{10,8},{11,9},{12,10},{13,11},... | collective-permute-start | bytes 1179656 | tf_op jit(solution)/shard_map/ppermute | solution.py:32
  87.4 2.0 %collective-permute-start.10 = (bf16[16,144,128]{2,1,0:T(8,128)(2,1)S(1)}, bf16[16,144,128]{2,1,0:T(8,128)(2,1)S(1)}, u32[]{:S(2)}, u32[]{:S(2)}) collective-permute-start(bf16[16,144,128]{2,1,0:T(8,128)(2,1)S(1)} %bitcast.12), channel_id=1, source_target_pairs={{0,8},{8,0},{1,9},{9,1},{2,10},{10,2},{3,11},{11,3},{4,12},{12,4},... | collective-permute-start | bytes 1769480 | tf_op jit(solution)/shard_map/ppermute | solution.py:402

commit v8 on v7

--- a/solution.py
+++ b/solution.py
@@ -103,48 +103,32 @@
     return places + [(ref, 0, ref, rows) for ref in further_refs]
 
 
-def forward_kernel(context, rows, edge, taps, *refs):
-    tiles = context + 2
-    device_ref, q_hbm = refs[:2]
-    places = tile_places(rows, *refs[2 : 2 + tiles])
-    keys_ref = refs[3]
-    far_ref, near_ref, w_hbm, conv_hbm, cot_hbm = refs[2 + tiles : 7 + tiles]
-    out_ref, att_ref, lse_ref, dhid_ref, keep_ref, give_ref = refs[7 + tiles : 13 + tiles]
-    qx, kx, vx, ax, lx, hid, cotx, dm, bias, kp, ks, parts = refs[13 + tiles : 25 + tiles]
-    q_ref, w_ref, conv_ref, cot_ref, sems = refs[25 + tiles :]
-
+def scores_kernel(context, rows, edge, *refs):
+    device_ref, q_hbm, own_ref, keys_ref = refs[:4]
+    further_refs = refs[4 : 3 + context]
+    far_ref, near_ref, weights_ref, lse_ref, qx, kx, lx, q_ref, bias, sem = refs[3 + context :]
     att = q_ref.shape[1]
-    width = w_ref.shape[1]
+    pairs = att // LANES
     span = context * rows
-    query_rows = rows + 2 * edge
     block = LANES
     keys = span + block
     scale = 1.0 / math.sqrt(HEAD_DIM)
     start = device_ref[0] * rows
 
-    fetches = [
-        pltpu.make_async_copy(source, target, sems.at[i])
-        for i, (source, target) in enumerate(
-            ((q_hbm, q_ref), (w_hbm, w_ref), (cot_hbm, cot_ref), (conv_hbm, conv_ref))
-        )
-    ]
-    for fetch in fetches:
-        fetch.start()
-
-    for offset, (k_ref, k_at, v_ref, v_at) in enumerate(places):
+    fetch = pltpu.make_async_copy(q_hbm, q_ref, sem)
+    fetch.start()
+    kx[:edge] = far_ref[:edge]
+    for offset, ref in enumerate((own_ref, keys_ref, *further_refs)):
         first = edge + (context - offset) * rows
-        kx[first : first + rows] = k_ref[k_at : k_at + rows]
-        vx[first : first + rows] = v_ref[v_at : v_at + rows]
-    for ext, at in ((kx, 0), (vx, edge)):
-        ext[:edge] = far_ref[at : at + edge]
-        ext[edge + span + rows :] = near_ref[at : at + edge]
+        kx[first : first + rows] = ref[:rows]
+    kx[edge + span + rows :] = near_ref[:edge]
     qx[:edge] = keys_ref[rows : rows + edge] * scale
     qx[edge + rows :] = near_ref[2 * edge : 3 * edge] * scale
-    fetches[0].wait()
+    fetch.wait()
     qx[edge : edge + rows] = q_ref[...] * scale
 
     lane_id = lax.broadcasted_iota(jnp.int32, (block, LANES), 1)
-    for b in range(query_rows // block):
+    for b in range(qx.shape[0] // block):
         row_id = lax.broadcasted_iota(jnp.int32, (block, keys), 0)
         key_id = lax.broadcasted_iota(jnp.int32, (block, keys), 1)
         distance = row_id - key_id + span
@@ -152,27 +136,65 @@
         visible = (distance >= 0) & (distance < span) & (key_time >= 0)
         bias[...] = jnp.where(visible, 0.0, NEGATIVE)
         log_sums = jnp.zeros((block, LANES), jnp.float32)
-        for pair in range(att // LANES):
+        for pair in range(pairs):
             columns = slice(pair * LANES, (pair + 1) * LANES)
             qs = stack_heads(qx[b * block : (b + 1) * block, columns])
-            kp_tile = kx[b * block : b * block + keys, columns]
-            vp_tile = vx[b * block : b * block + keys, columns]
-            scores = dot(qs, kp_tile, NT)
+            scores = dot(qs, kx[b * block : b * block + keys, columns], NT)
             hidden_pairs = bias[...]
             scores = scores + jnp.concatenate([hidden_pairs, hidden_pairs], axis=0)
             row_max = jnp.max(scores, axis=1, keepdims=True)
             weights = jnp.exp(scores - row_max)
             row_sum = jnp.sum(weights, axis=1, keepdims=True)
-            mixed = dot(weights.astype(jnp.bfloat16), vp_tile, NN) / row_sum
-            ax[b * block : (b + 1) * block, columns] = merge_heads(mixed).astype(jnp.bfloat16)
+            weights_ref[b * pairs + pair] = (weights * (1.0 / row_sum)).astype(jnp.bfloat16)
             log_sum = row_max + jnp.log(row_sum)
             log_sums = jnp.where(lane_id == 2 * pair, log_sum[:block], log_sums)
             log_sums = jnp.where(lane_id == 2 * pair + 1, log_sum[block:], log_sums)
         lx[b * block : (b + 1) * block] = log_sums
+    lse_ref[...] = jnp.transpose(lx[...])[: lse_ref.shape[0], edge : edge + rows]
+
+
+def forward_kernel(context, rows, edge, taps, *refs):
+    tiles = context + 2
+    device_ref, weights_ref = refs[:2]
+    places = tile_places(rows, *refs[2 : 2 + tiles])
+    far_ref, near_ref, w_hbm, conv_hbm, cot_hbm = refs[2 + tiles : 7 + tiles]
+    out_ref, att_ref, dhid_ref, keep_ref, give_ref = refs[7 + tiles : 12 + tiles]
+    vx, ax, hid, cotx, dm, kp, ks, parts = refs[12 + tiles : 20 + tiles]
+    w_ref, conv_ref, cot_ref, sems = refs[20 + tiles :]
+
+    att = ax.shape[1]
+    width = w_ref.shape[1]
+    span = context * rows
+    query_rows = rows + 2 * edge
+    block = LANES
+    keys = span + block
+    start = device_ref[0] * rows
+
+    fetches = [
+        pltpu.make_async_copy(source, target, sems.at[i])
+        for i, (source, target) in enumerate(
+            ((w_hbm, w_ref), (cot_hbm, cot_ref), (conv_hbm, conv_ref))
+        )
+    ]
+    for fetch in fetches:
+        fetch.start()
+
+    vx[:edge] = far_ref[edge:]
+    for offset, (_, _, ref, at) in enumerate(places):
+        first = edge + (context - offset) * rows
+        vx[first : first + rows] = ref[at : at + rows]
+    vx[edge + span + rows :] = near_ref[edge : 2 * edge]
+
+    pairs = att // LANES
+    for b in range(query_rows // block):
+        for pair in range(pairs):
+            columns = slice(pair * LANES, (pair + 1) * LANES)
+            values = vx[b * block : b * block + keys, columns]
+            mixed = dot(weights_ref[b * pairs + pair], values, NN)
+            ax[b * block : (b + 1) * block, columns] = merge_heads(mixed).astype(jnp.bfloat16)
     att_ref[...] = ax[edge : edge + rows]
-    lse_ref[...] = jnp.transpose(lx[...])[: lse_ref.shape[0], edge : edge + rows]
-
-    fetches[1].wait()
+
+    fetches[0].wait()
     step = 2 * LANES
     for part in range(width // step):
         product = dot(ax[...], w_ref[:, part * step : (part + 1) * step], NN)
@@ -182,8 +204,8 @@
         hid[2 * part] = product[:, :LANES]
         hid[2 * part + 1] = product[:, LANES:]
 
+    fetches[1].wait()
     fetches[2].wait()
-    fetches[3].wait()
     for chunk in range(width // LANES):
         columns = slice(chunk * LANES, (chunk + 1) * LANES)
         cotx[chunk, :rows] = cot_ref[:, columns].astype(jnp.float32)
@@ -300,10 +322,10 @@
     tiles = context + 2
     device_ref, q_hbm = refs[:2]
     places = tile_places(rows, *refs[2 : 2 + tiles])
-    att_ref, lse_ref, dhid_hbm, w_hbm = refs[2 + tiles : 6 + tiles]
+    att_hbm, lse_ref, dhid_hbm, w_hbm = refs[2 + tiles : 6 + tiles]
     dq_ref, own_ref = refs[6 + tiles : 8 + tiles]
     message_refs = refs[8 + tiles : 8 + tiles + context]
-    q_ref, dhid_ref, w_ref, datt, bias, sems = refs[8 + tiles + context :]
+    q_ref, dhid_ref, w_ref, att_ref, datt, bias, sems = refs[8 + tiles + context :]
 
     att = q_ref.shape[1]
     heads = att // HEAD_DIM
@@ -314,7 +336,7 @@
     fetches = [
         pltpu.make_async_copy(source, target, sems.at[i])
         for i, (source, target) in enumerate(
-            ((q_hbm, q_ref), (dhid_hbm, dhid_ref), (w_hbm, w_ref))
+            ((w_hbm, w_ref), (dhid_hbm, dhid_ref), (q_hbm, q_ref), (att_hbm, att_ref))
         )
     ]
     for fetch in fetches:
@@ -462,40 +484,56 @@
     core = lax.axis_index("core").astype(jnp.int32) if split else jnp.int32(0)
     place = jnp.stack([device, core])
     piece_rows = -(-(chunks * 16 + chunks) // 16) * 16
-    out_frames, attended, log_sums, dhidden, keep, give = pl.pallas_call(
+    blocks = query_rows // LANES * (att // LANES)
+    key_span = context * rows + LANES
+    weights, log_sums = pl.pallas_call(
+        functools.partial(scores_kernel, context, rows, edge),
+        out_shape=(
+            jax.ShapeDtypeStruct((blocks, 2 * LANES, key_span), bf16),
+            jax.ShapeDtypeStruct((heads, rows), f32),
+        ),
+        in_specs=[smem, hbm] + [vmem] * (3 + context),
+        out_specs=(vmem,) * 2,
+        scratch_shapes=[
+            pltpu.VMEM((query_rows, att), bf16),
+            pltpu.VMEM((key_rows, att), bf16),
+            pltpu.VMEM((query_rows, LANES), f32),
+            pltpu.VMEM((rows, att), bf16),
+            pltpu.VMEM((LANES, key_span), f32),
+            pltpu.SemaphoreType.DMA,
+        ],
+        compiler_params=params,
+        cost_estimate=cost(8 * 10**9, 10**7),
+        name="scores",
+    )(place, in_hbm(query), own, keys, *further, far, near)
+    out_frames, attended, dhidden, keep, give = pl.pallas_call(
         functools.partial(forward_kernel, context, rows, edge, taps),
         out_shape=(
             jax.ShapeDtypeStruct((rows, width), bf16),
             jax.ShapeDtypeStruct((rows, att), bf16),
-            jax.ShapeDtypeStruct((heads, rows), f32),
             jax.ShapeDtypeStruct((rows, width), bf16),
         )
         + (jax.ShapeDtypeStruct((pieces, piece_rows, LANES), bf16),) * 2,
-        in_specs=[smem, hbm] + [vmem] * (4 + context) + [hbm] * 3,
-        out_specs=(vmem,) * 6,
+        in_specs=[smem] + [vmem] * (5 + context) + [hbm] * 3,
+        out_specs=(vmem,) * 5,
         scratch_shapes=[
-            pltpu.VMEM((query_rows, att), bf16),
-            pltpu.VMEM((key_rows, att), bf16),
             pltpu.VMEM((key_rows, att), bf16),
             pltpu.VMEM((query_rows, att), bf16),
-            pltpu.VMEM((query_rows, LANES), f32),
             pltpu.VMEM((chunks, query_rows, LANES), f32),
             pltpu.VMEM((chunks, rows + edge, LANES), f32),
             pltpu.VMEM((rows + edge + 8, LANES), f32),
-            pltpu.VMEM((LANES, context * rows + LANES), f32),
             pltpu.VMEM((chunks, 2 * pieces, LANES), f32),
             pltpu.VMEM((taps * SUBLANES, LANES), f32),
             pltpu.VMEM((2, pieces, piece_rows, LANES), bf16),
-            pltpu.VMEM((rows, att), bf16),
             pltpu.VMEM((att, width), bf16),
             pltpu.VMEM((taps, width), f32),
             pltpu.VMEM((rows, width), bf16),
-            pltpu.SemaphoreType.DMA((4,)),
+            pltpu.SemaphoreType.DMA((3,)),
         ],
         compiler_params=params,
         cost_estimate=cost(8 * 10**9, 10**7),
         name="forward",
-    )(place, in_hbm(query), *tiles, far, near, in_hbm(out_weight), in_hbm(conv_kernel), in_hbm(cot))
+    )(place, weights, *tiles, far, near, in_hbm(out_weight), in_hbm(conv_kernel), in_hbm(cot))
 
     if split:
         mine = (keep.astype(f32) + other_core(give).astype(f32)).astype(bf16)
@@ -507,20 +545,21 @@
             jax.ShapeDtypeStruct((2 * rows, att), f32),
         )
         + (jax.ShapeDtypeStruct((2 * rows, att), bf16),) * context,
-        in_specs=[smem, hbm] + [vmem] * (4 + context) + [hbm] * 2,
+        in_specs=[smem, hbm] + [vmem] * (2 + context) + [hbm, vmem, hbm, hbm],
         out_specs=(vmem,) * (2 + context),
         scratch_shapes=[
             pltpu.VMEM((rows, att), bf16),
             pltpu.VMEM((rows, width), bf16),
             pltpu.VMEM((att, width), bf16),
             pltpu.VMEM((rows, att), bf16),
+            pltpu.VMEM((rows, att), bf16),
             pltpu.VMEM((context + 1, rows, rows), f32),
-            pltpu.SemaphoreType.DMA((3,)),
+            pltpu.SemaphoreType.DMA((4,)),
         ],
         compiler_params=params,
         cost_estimate=cost(6 * 10**9, 10**7),
         name="backward",
-    )(place, in_hbm(query), *tiles, attended, log_sums, in_hbm(dhidden), in_hbm(out_weight))
+    )(place, in_hbm(query), *tiles, in_hbm(attended), log_sums, in_hbm(dhidden), in_hbm(out_weight))
     if split:
         mine, own_grads, *messages = lax.optimization_barrier(
             (collected(mine), own_grads, *messages)
@@ -537,7 +576,7 @@
             in_specs=[smem] + [vmem] * 3,
             out_specs=(vmem,) * 2,
             compiler_params=params,
-            cost_estimate=cost(10**9, 3 * 10**6),
+            cost_estimate=cost(5 * 10**9, 10**7),
             name="relay",
         )(place, own_grads, swapped, messages[2])
     if split:
@@ -546,19 +585,20 @@
         mine = exchange(jnp.broadcast_to(mine, (lax.axis_size(PLANE_AXES), *mine.shape)))
         mine = mine.reshape(keep.shape)
     messages = [shifted(message, -offset) for offset, message in messages.items()]
-    if split:
-        mine, *messages = lax.optimization_barrier((mine, *messages))
-        halves = (mine, other_core(mine))
-    else:
-        halves = lax.psum((keep, give), ("x", "core", "z", "y"))
     key_grad, value_grad = pl.pallas_call(
         merge_kernel,
         out_shape=(jax.ShapeDtypeStruct((rows, att), bf16),) * 2,
         in_specs=[vmem] * (1 + len(messages)),
         out_specs=(vmem,) * 2,
         compiler_params=params,
+        cost_estimate=cost(8 * 10**9, 10**7),
         name="merge",
     )(own_grads, *messages)
+    if split:
+        mine, key_grad, value_grad = lax.optimization_barrier((mine, key_grad, value_grad))
+        halves = (mine, other_core(mine))
+    else:
+        halves = lax.psum((keep, give), ("x", "core", "z", "y"))
     weight_total, kernel_total = pl.pallas_call(
         unpack_kernel,
         out_shape=(

time: 91.9 us -> 89.6 us (0.975)
  waiting for transfers between devices: 26.1 us -> 21.6 us
  starting transfers between devices: 36.8 us -> 39.5 us
  other arithmetic: 2.29 us -> 1.23 us
    ppermute x5, waiting for transfers between devices: 14.5 us -> 5.78 us  [shifted(): lax.ppermute(x, RUN_AXES, [(i, i + by) for i in devices if i + by in devi...]
    pallas_call x0 -> x1, Pallas kernels: none -> 3.11 us  [per_device(): pl.pallas_call(functools.partial(scores_kernel, context, rows, edge), out...]
    all_to_all x2, waiting for transfers between devices: 1.19 us -> 4.23 us  [exchange(): return lax.all_to_all(x, PLANE_AXES, 0, 0, tiled=True)]
    ppermute x2, starting transfers between devices: 6.99 us -> 9.9 us  [summed_along(): other = lax.ppermute(x, axis, [(i, i ^ step) for i in range(size)])]
    pallas_call x1, Pallas kernels: 11.2 us -> 8.85 us  [per_device(): pl.pallas_call(functools.partial(forward_kernel, context, rows, edge, tap...]
    reduce_sum x1, other arithmetic: 1.17 us -> 0.1 us  [collected(): return jnp.sum(x.astype(jnp.float32), axis=0).astype(x.dtype)]
  transfers between devices with their start and end apart: 13 -> 13, of which waited for: 9 -> 9; matrix products, arithmetic and copies ran while one was open for 0% -> 1% of each run, Pallas kernels for 9% -> 13%
where the time goes in v8:
time: 89.6 us; the launch traced here: 89.2 us
  starting transfers between devices  39.5 us (44%)
  Pallas kernels  24.4 us (27%)
  waiting for transfers between devices  21.6 us (24%)
  local copies, waits for them, and re-layouts  1.65 us (2%)
  other arithmetic  1.23 us (1%)
    ppermute x5, starting transfers between devices, shifted(): lax.ppermute(x, RUN_AXES, [(i, i + by) for i in devices if i + by in devi...  16.5 us
    ppermute x2, starting transfers between devices, summed_along(): other = lax.ppermute(x, axis, [(i, i ^ step) for i in range(size)])  9.9 us
    all_to_all x2, starting transfers between devices, exchange(): return lax.all_to_all(x, PLANE_AXES, 0, 0, tiled=True)  8.95 us
    pallas_call x1, Pallas kernels, per_device(): pl.pallas_call(functools.partial(forward_kernel, context, rows, edge, tap...  8.85 us
    pallas_call x1, Pallas kernels, per_device(): pl.pallas_call(functools.partial(backward_kernel, context, rows), out_sha...  7.41 us
    ppermute x2, waiting for transfers between devices, summed_along(): other = lax.ppermute(x, axis, [(i, i ^ step) for i in range(size)])  7.11 us
    ppermute x5, waiting for transfers between devices, shifted(): lax.ppermute(x, RUN_AXES, [(i, i + by) for i in devices if i + by in devi...  5.78 us
    all_to_all x2, waiting for transfers between devices, exchange(): return lax.all_to_all(x, PLANE_AXES, 0, 0, tiled=True)  4.23 us
  transfers between devices with their start and end apart: 13, of which 9 were waited for; matrix products, arithmetic and copies ran while one was open for 1% of the time, Pallas kernels for 13%

profile of v8, /device:TPU:0, one launch (start us, length us, event | category | flops | bytes accessed | tf_op | source)
XLA Modules:
  0.0 89.2 jit_solution(1894324820853648921)
XLA Ops:
  0.6 1.4 %pack.1 = (bf16[384,512]{1,0:T(8,128)(2,1)S(1)}, bf16[224,512]{1,0:T(8,128)(2,1)S(1)}, bf16[192,512]{1,0:T(8,128)(2,1)S(1)}, bf16[64,512]{1,0:T(8,128)(2,1)S(1)}, bf16[160,512]{1,0:T(8,128)(2,1)S(1)}) custom-call(bf16[192,512]{1,0:T(8,128)(2,1)} %bitcast.16, bf16[192,512]{1,0:T(8,128)(2,1)} %bitcast.17, bf16[192,512]{1,0:T(8,128)(2,1)} %bitcast.18, ...), custom_call_target="tpu_custom_call" | custom-call | tf_op jit(solution)/shard_map/pack/pallas_call | solution.py:447
  2.0 5.0 %collective-permute-start.1 = (bf16[384,512]{1,0:T(8,128)(2,1)S(1)}, bf16[384,512]{1,0:T(8,128)(2,1)S(1)}, u32[]{:S(2)}, u32[]{:S(2)}) collective-permute-start(bf16[384,512]{1,0:T(8,128)(2,1)S(1)} %get-tuple-element.41.refs_2_), channel_id=1, source_target_pairs={{0,2},{1,3},{2,4},{3,5},{4,6},{5,7},{8,10},{9,11},{10,12},{11,13},... | collective-permute-start | bytes 1179656 | tf_op jit(solution)/shard_map/ppermute | solution.py:32
  7.0 3.4 %collective-permute-start = (bf16[224,512]{1,0:T(8,128)(2,1)S(1)}, bf16[224,512]{1,0:T(8,128)(2,1)S(1)}, u32[]{:S(2)}, u32[]{:S(2)}) collective-permute-start(bf16[224,512]{1,0:T(8,128)(2,1)S(1)} %get-tuple-element.42), channel_id=1, source_target_pairs={{0,1},{1,2},{2,3},{3,4},{4,5},{5,6},{6,7},{8,9},{9,10},{10,11},{11... | collective-permute-start | bytes 688136 | tf_op jit(solution)/shard_map/ppermute | solution.py:32
  10.4 1.3 %collective-permute-start.3 = (bf16[160,512]{1,0:T(8,128)(2,1)S(1)}, bf16[160,512]{1,0:T(8,128)(2,1)S(1)}, u32[]{:S(2)}, u32[]{:S(2)}) collective-permute-start(bf16[160,512]{1,0:T(8,128)(2,1)S(1)} %get-tuple-element.44), channel_id=1, source_target_pairs={{1,0},{2,1},{3,2},{4,3},{5,4},{6,5},{7,6},{9,8},{10,9},{11,10},{12... | collective-permute-start | bytes 491528 | tf_op jit(solution)/shard_map/ppermute | solution.py:32
  11.7 5.5 %collective-permute-start.2 = (bf16[64,512]{1,0:T(8,128)(2,1)S(1)}, bf16[64,512]{1,0:T(8,128)(2,1)S(1)}, u32[]{:S(2)}, u32[]{:S(2)}) collective-permute-start(bf16[64,512]{1,0:T(8,128)(2,1)S(1)} %get-tuple-element.43), channel_id=1, source_target_pairs={{0,3},{1,4},{2,5},{3,6},{4,7},{8,11},{9,12},{10,13},{11,14},{12,15... | collective-permute-start | bytes 196616 | tf_op jit(solution)/shard_map/ppermute | solution.py:32
  17.3 0.1 pad_add_fusion.refs_0_.device_ref
  17.4 0.3 collective-permute-done.3.refs_6_.refs_7_
  17.7 0.0 collective-permute-done.1.refs_4_.odd_ref.refs_5_
  17.7 2.6 %collective-permute-start.4 = (bf16[192,512]{1,0:T(8,128)(2,1)S(1)}, bf16[192,512]{1,0:T(8,128)(2,1)S(1)}, u32[]{:S(2)}, u32[]{:S(2)}) collective-permute-start(bf16[192,512]{1,0:T(8,128)(2,1)S(1)} %choose.1), channel_id=1, source_target_pairs={{0,1},{1,0},{2,3},{3,2},{4,5},{5,4},{6,7},{7,6},{8,9},{9,8},{10,11... | collective-permute-start | bytes 589832 | tf_op jit(solution)/shard_map/ppermute | solution.py:475
  20.3 0.0 collective-permute-done.2.refs_5_.refs_6_
  20.3 0.0 collective-permute-done.refs_3_
  20.3 3.1 %scores.1 = (bf16[8,256,512]{2,1,0:T(8,128)(2,1)S(1)}, f32[8,192]{1,0:T(8,128)S(1)}) custom-call(s32[2]{0:T(128)S(1)} %pad_add_fusion.refs_0_.device_ref, bf16[192,512]{1,0:T(8,128)(2,1)} %bitcast.19, bf16[384,512]{1,0:T(8,128)(2,1)S(1)} %get-tuple-element.41.refs_2_, bf16[224,512]{1,0:T(8,128)(2,1)S(1)} %collective-permute-done.refs_3_, ...), custom_call_target="tpu_custom_call" | custom-call | flops 8000000000 | bytes 10000000 | tf_op jit(solution)/shard_map/scores/pallas_call | solution.py:489
  23.4 0.5 collective-permute-done.4.refs_4_
  24.0 8.9 %forward.1 = (bf16[192,1024]{1,0:T(8,128)(2,1)}, bf16[192,512]{1,0:T(8,128)(2,1)S(1)}, bf16[192,1024]{1,0:T(8,128)(2,1)S(1)}, bf16[16,144,128]{2,1,0:T(8,128)(2,1)S(1)}, bf16[16,144,128]{2,1,0:T(8,128)(2,1)S(1)}) custom-call(s32[2]{0:T(128)S(1)} %pad_add_fusion.refs_0_.device_ref, bf16[8,256,512]{2,1,0:T(8,128)(2,1)S(1)} %get-tuple-element.47.refs_1_, ...), custom_call_target="tpu_custom_call" | custom-call | flops 8000000000 | bytes 10000000 | tf_op jit(solution)/shard_map/forward/pallas_call | solution.py:509
  32.8 0.0 copy-start.2
  32.8 0.0 copy-start.3
  32.8 0.1 collective-permute-start.5
  32.9 2.0 %collective-permute-done.5 = bf16[16,144,128]{2,1,0:T(8,128)(2,1)S(1)} collective-permute-done((bf16[16,144,128]{2,1,0:T(8,128)(2,1)S(1)}, bf16[16,144,128]{2,1,0:T(8,128)(2,1)S(1)}, u32[]{:S(2)}, u32[]{:S(2)}) %collective-permute-start.5) | collective-permute-done | bytes 589856 | tf_op jit(solution)/shard_map/ppermute | solution.py:424
  34.9 1.0 %add_convert_fusion = bf16[16,144,128]{2,1,0:T(8,128)(2,1)} fusion(bf16[16,144,128]{2,1,0:T(8,128)(2,1)S(1)} %collective-permute-done.5, bf16[16,144,128]{2,1,0:T(8,128)(2,1)S(1)} %get-tuple-element.52), kind=kLoop, calls=%fused_computation | loop fusion | flops 1179648 | bytes 1769472 | tf_op jit(solution)/shard_map/convert_element_type | solution.py:539
  35.9 0.0 copy-done.2
  35.9 0.0 copy-done.3
  35.9 4.6 %all-to-all-start = ((bf16[4,576,128]{2,1,0:T(8,128)(2,1)}), bf16[4,576,128]{2,1,0:T(8,128)(2,1)S(1)}, u32[]{:S(2)}, u32[]{:S(2)}) async-start(bf16[4,576,128]{2,1,0:T(8,128)(2,1)} %bitcast.8), calls=%async_computation | async-start | bytes 1179648 | tf_op jit(solution)/shard_map/all_to_all | solution.py:406
  40.5 7.4 %backward.1 = (bf16[192,512]{1,0:T(8,128)(2,1)}, f32[384,512]{1,0:T(8,128)S(1)}, bf16[384,512]{1,0:T(8,128)(2,1)S(1)}, bf16[384,512]{1,0:T(8,128)(2,1)S(1)}) custom-call(s32[2]{0:T(128)S(1)} %pad_add_fusion.refs_0_.device_ref, bf16[192,512]{1,0:T(8,128)(2,1)} %bitcast.20, bf16[384,512]{1,0:T(8,128)(2,1)S(1)} %get-tuple-element.41.refs_2_, ...), custom_call_target="tpu_custom_call" | custom-call | flops 6000000000 | bytes 10000000 | tf_op jit(solution)/shard_map/backward/pallas_call | solution.py:541
  47.9 0.0 copy-start
  47.9 0.7 copy-done
  48.6 0.9 all-to-all-done
  49.5 0.0 copy-start.1
  49.5 0.1 reduce_sum.12
  49.6 5.5 %collective-permute-start.6 = (bf16[576,128]{1,0:T(8,128)(2,1)S(1)}, bf16[576,128]{1,0:T(8,128)(2,1)S(1)}, u32[]{:S(2)}, u32[]{:S(2)}) collective-permute-start(bf16[576,128]{1,0:T(8,128)(2,1)S(1)} %reduce_sum.12), channel_id=1, source_target_pairs={{0,2},{2,0},{4,6},{6,4},{1,3},{3,1},{5,7},{7,5},{8,10},{10,8},{12,... | collective-permute-start | bytes 442376 | tf_op jit(solution)/shard_map/ppermute | solution.py:417
  55.1 1.5 %collective-permute-start.8 = (bf16[384,512]{1,0:T(8,128)(2,1)S(1)}, bf16[384,512]{1,0:T(8,128)(2,1)S(1)}, u32[]{:S(2)}, u32[]{:S(2)}) collective-permute-start(bf16[384,512]{1,0:T(8,128)(2,1)S(1)} %get-tuple-element.63), channel_id=1, source_target_pairs={{0,1},{1,0},{2,3},{3,2},{4,5},{5,4},{6,7},{7,6},{8,9},{9,8},{10,11... | collective-permute-start | bytes 1179656 | tf_op jit(solution)/shard_map/ppermute | solution.py:569
  56.6 1.9 %collective-permute-done.6 = bf16[576,128]{1,0:T(8,128)(2,1)S(1)} collective-permute-done((bf16[576,128]{1,0:T(8,128)(2,1)S(1)}, bf16[576,128]{1,0:T(8,128)(2,1)S(1)}, u32[]{:S(2)}, u32[]{:S(2)}) %collective-permute-start.6) | collective-permute-done | bytes 147488 | tf_op jit(solution)/shard_map/ppermute | solution.py:417
  58.5 4.4 %collective-permute-start.7 = (bf16[576,128]{1,0:T(8,128)(2,1)S(1)}, bf16[576,128]{1,0:T(8,128)(2,1)S(1)}, u32[]{:S(2)}, u32[]{:S(2)}) collective-permute-start(bf16[576,128]{1,0:T(8,128)(2,1)S(1)} %add_convert_fusion.2), channel_id=1, source_target_pairs={{0,4},{2,6},{4,0},{6,2},{1,5},{3,7},{5,1},{7,3},{8,12},{10,14},{12... | collective-permute-start | bytes 442376 | tf_op jit(solution)/shard_map/ppermute | solution.py:417
  62.9 5.2 %collective-permute-done.7 = bf16[576,128]{1,0:T(8,128)(2,1)S(1)} collective-permute-done((bf16[576,128]{1,0:T(8,128)(2,1)S(1)}, bf16[576,128]{1,0:T(8,128)(2,1)S(1)}, u32[]{:S(2)}, u32[]{:S(2)}) %collective-permute-start.7) | collective-permute-done | bytes 147488 | tf_op jit(solution)/shard_map/ppermute | solution.py:417
  68.2 0.0 collective-permute-done.8.swapped_ref
  68.2 0.0 copy-done.1
  68.2 0.7 relay.1
  68.9 1.3 %collective-permute-start.9 = (bf16[384,512]{1,0:T(8,128)(2,1)S(1)}, bf16[384,512]{1,0:T(8,128)(2,1)S(1)}, u32[]{:S(2)}, u32[]{:S(2)}) collective-permute-start(bf16[384,512]{1,0:T(8,128)(2,1)S(1)} %get-tuple-element.68), channel_id=1, source_target_pairs={{2,0},{3,1},{4,2},{5,3},{6,4},{7,5},{10,8},{11,9},{12,10},{13,11},... | collective-permute-start | bytes 1179656 | tf_op jit(solution)/shard_map/ppermute | solution.py:32
  70.2 0.9 broadcast_in_dim.18
  71.1 4.4 %all-to-all-start.1 = ((bf16[4,576,128]{2,1,0:T(8,128)(2,1)}), bf16[4,576,128]{2,1,0:T(8,128)(2,1)S(1)}, u32[]{:S(2)}, u32[]{:S(2)}) async-start(bf16[4,576,128]{2,1,0:T(8,128)(2,1)} %broadcast_in_dim.18), calls=%async_computation.1 | async-start | bytes 1179648 | tf_op jit(solution)/shard_map/all_to_all | solution.py:406
  75.5 5.4 %collective-permute-done.9.refs_1_ = bf16[384,512]{1,0:T(8,128)(2,1)S(1)} collective-permute-done((bf16[384,512]{1,0:T(8,128)(2,1)S(1)}, bf16[384,512]{1,0:T(8,128)(2,1)S(1)}, u32[]{:S(2)}, u32[]{:S(2)}) %collective-permute-start.9) | collective-permute-done | bytes 393248 | tf_op jit(solution)/shard_map/ppermute | solution.py:32
  80.9 0.8 merge.1
  81.7 3.4 %all-to-all-done.1 = bf16[4,576,128]{2,1,0:T(8,128)(2,1)S(1)} async-done(((bf16[4,576,128]{2,1,0:T(8,128)(2,1)}), bf16[4,576,128]{2,1,0:T(8,128)(2,1)S(1)}, u32[]{:S(2)}, u32[]{:S(2)}) %all-to-all-start.1) | async-done | bytes 589856 | tf_op jit(solution)/shard_map/all_to_all | solution.py:406
  85.1 0.0 collective-permute-start.10
  85.1 2.0 %collective-permute-done.10.far_ref = bf16[16,144,128]{2,1,0:T(8,128)(2,1)S(1)} collective-permute-done((bf16[16,144,128]{2,1,0:T(8,128)(2,1)S(1)}, bf16[16,144,128]{2,1,0:T(8,128)(2,1)S(1)}, u32[]{:S(2)}, u32[]{:S(2)}) %collective-permute-start.10) | collective-permute-done | bytes 589856 | tf_op jit(solution)/shard_map/ppermute | solution.py:424
  87.1 2.1 %unpack.1 = (f32[512,1024]{1,0:T(8,128)}, f32[31,1024]{1,0:T(8,128)}) custom-call(s32[2]{0:T(128)S(1)} %pad_add_fusion.refs_0_.device_ref, bf16[16,144,128]{2,1,0:T(8,128)(2,1)S(1)} %bitcast.13, bf16[16,144,128]{2,1,0:T(8,128)(2,1)S(1)} %collective-permute-done.10.far_ref), custom_call_target="tpu_custom_call" | custom-call | tf_op jit(solution)/shard_map/unpack/pallas_call | solution.py:602
  (3 shorter events, 0.1 us)
Async XLA Ops:
  2.0 15.7 %collective-permute-start.1 = (bf16[384,512]{1,0:T(8,128)(2,1)S(1)}, bf16[384,512]{1,0:T(8,128)(2,1)S(1)}, u32[]{:S(2)}, u32[]{:S(2)}) collective-permute-start(bf16[384,512]{1,0:T(8,128)(2,1)S(1)} %get-tuple-element.41.refs_2_), channel_id=1, source_target_pairs={{0,2},{1,3},{2,4},{3,5},{4,6},{5,7},{8,10},{9,11},{10,12},{11,13},... | collective-permute-start | bytes 1179656 | tf_op jit(solution)/shard_map/ppermute | solution.py:32
  7.0 13.3 %collective-permute-start = (bf16[224,512]{1,0:T(8,128)(2,1)S(1)}, bf16[224,512]{1,0:T(8,128)(2,1)S(1)}, u32[]{:S(2)}, u32[]{:S(2)}) collective-permute-start(bf16[224,512]{1,0:T(8,128)(2,1)S(1)} %get-tuple-element.42), channel_id=1, source_target_pairs={{0,1},{1,2},{2,3},{3,4},{4,5},{5,6},{6,7},{8,9},{9,10},{10,11},{11... | collective-permute-start | bytes 688136 | tf_op jit(solution)/shard_map/ppermute | solution.py:32
  10.4 7.3 %collective-permute-start.3 = (bf16[160,512]{1,0:T(8,128)(2,1)S(1)}, bf16[160,512]{1,0:T(8,128)(2,1)S(1)}, u32[]{:S(2)}, u32[]{:S(2)}) collective-permute-start(bf16[160,512]{1,0:T(8,128)(2,1)S(1)} %get-tuple-element.44), channel_id=1, source_target_pairs={{1,0},{2,1},{3,2},{4,3},{5,4},{6,5},{7,6},{9,8},{10,9},{11,10},{12... | collective-permute-start | bytes 491528 | tf_op jit(solution)/shard_map/ppermute | solution.py:32
  11.7 8.6 %collective-permute-start.2 = (bf16[64,512]{1,0:T(8,128)(2,1)S(1)}, bf16[64,512]{1,0:T(8,128)(2,1)S(1)}, u32[]{:S(2)}, u32[]{:S(2)}) collective-permute-start(bf16[64,512]{1,0:T(8,128)(2,1)S(1)} %get-tuple-element.43), channel_id=1, source_target_pairs={{0,3},{1,4},{2,5},{3,6},{4,7},{8,11},{9,12},{10,13},{11,14},{12,15... | collective-permute-start | bytes 196616 | tf_op jit(solution)/shard_map/ppermute | solution.py:32
  17.7 6.2 %collective-permute-start.4 = (bf16[192,512]{1,0:T(8,128)(2,1)S(1)}, bf16[192,512]{1,0:T(8,128)(2,1)S(1)}, u32[]{:S(2)}, u32[]{:S(2)}) collective-permute-start(bf16[192,512]{1,0:T(8,128)(2,1)S(1)} %choose.1), channel_id=1, source_target_pairs={{0,1},{1,0},{2,3},{3,2},{4,5},{5,4},{6,7},{7,6},{8,9},{9,8},{10,11... | collective-permute-start | bytes 589832 | tf_op jit(solution)/shard_map/ppermute | solution.py:475
  32.8 3.1 %copy-start.2 = (bf16[192,1024]{1,0:T(8,128)(2,1)}, bf16[192,1024]{1,0:T(8,128)(2,1)S(1)}, u32[]{:S(2)}) copy-start(bf16[192,1024]{1,0:T(8,128)(2,1)S(1)} %get-tuple-element.55.refs_8_) | copy-start | bytes 1179652
  32.8 3.1 %copy-start.3 = (bf16[192,512]{1,0:T(8,128)(2,1)}, bf16[192,512]{1,0:T(8,128)(2,1)S(1)}, u32[]{:S(2)}) copy-start(bf16[192,512]{1,0:T(8,128)(2,1)S(1)} %get-tuple-element.50.refs_6_) | copy-start | bytes 589828
  32.8 2.1 %collective-permute-start.5 = (bf16[16,144,128]{2,1,0:T(8,128)(2,1)S(1)}, bf16[16,144,128]{2,1,0:T(8,128)(2,1)S(1)}, u32[]{:S(2)}, u32[]{:S(2)}) collective-permute-start(bf16[16,144,128]{2,1,0:T(8,128)(2,1)S(1)} %get-tuple-element.53), channel_id=1, source_target_pairs={{0,8},{8,0},{1,9},{9,1},{2,10},{10,2},{3,11},{11,3},{4,12},{12,4},... | collective-permute-start | bytes 1769480 | tf_op jit(solution)/shard_map/ppermute | solution.py:424
  35.9 13.6 %all-to-all-start = ((bf16[4,576,128]{2,1,0:T(8,128)(2,1)}), bf16[4,576,128]{2,1,0:T(8,128)(2,1)S(1)}, u32[]{:S(2)}, u32[]{:S(2)}) async-start(bf16[4,576,128]{2,1,0:T(8,128)(2,1)} %bitcast.8), calls=%async_computation | async-start | bytes 1179648 | tf_op jit(solution)/shard_map/all_to_all | solution.py:406
  47.9 0.7 copy-start
  49.5 18.7 %copy-start.1 = (bf16[384,512]{1,0:T(8,128)(2,1)S(1)}, bf16[384,512]{1,0:T(8,128)(2,1)}, u32[]{:S(2)}) copy-start(bf16[384,512]{1,0:T(8,128)(2,1)} %copy-done) | copy-start | bytes 1179652
  49.6 8.8 %collective-permute-start.6 = (bf16[576,128]{1,0:T(8,128)(2,1)S(1)}, bf16[576,128]{1,0:T(8,128)(2,1)S(1)}, u32[]{:S(2)}, u32[]{:S(2)}) collective-permute-start(bf16[576,128]{1,0:T(8,128)(2,1)S(1)} %reduce_sum.12), channel_id=1, source_target_pairs={{0,2},{2,0},{4,6},{6,4},{1,3},{3,1},{5,7},{7,5},{8,10},{10,8},{12,... | collective-permute-start | bytes 442376 | tf_op jit(solution)/shard_map/ppermute | solution.py:417
  55.1 13.1 %collective-permute-start.8 = (bf16[384,512]{1,0:T(8,128)(2,1)S(1)}, bf16[384,512]{1,0:T(8,128)(2,1)S(1)}, u32[]{:S(2)}, u32[]{:S(2)}) collective-permute-start(bf16[384,512]{1,0:T(8,128)(2,1)S(1)} %get-tuple-element.63), channel_id=1, source_target_pairs={{0,1},{1,0},{2,3},{3,2},{4,5},{5,4},{6,7},{7,6},{8,9},{9,8},{10,11... | collective-permute-start | bytes 1179656 | tf_op jit(solution)/shard_map/ppermute | solution.py:569
  58.5 9.6 %collective-permute-start.7 = (bf16[576,128]{1,0:T(8,128)(2,1)S(1)}, bf16[576,128]{1,0:T(8,128)(2,1)S(1)}, u32[]{:S(2)}, u32[]{:S(2)}) collective-permute-start(bf16[576,128]{1,0:T(8,128)(2,1)S(1)} %add_convert_fusion.2), channel_id=1, source_target_pairs={{0,4},{2,6},{4,0},{6,2},{1,5},{3,7},{5,1},{7,3},{8,12},{10,14},{12... | collective-permute-start | bytes 442376 | tf_op jit(solution)/shard_map/ppermute | solution.py:417
  68.9 12.0 %collective-permute-start.9 = (bf16[384,512]{1,0:T(8,128)(2,1)S(1)}, bf16[384,512]{1,0:T(8,128)(2,1)S(1)}, u32[]{:S(2)}, u32[]{:S(2)}) collective-permute-start(bf16[384,512]{1,0:T(8,128)(2,1)S(1)} %get-tuple-element.68), channel_id=1, source_target_pairs={{2,0},{3,1},{4,2},{5,3},{6,4},{7,5},{10,8},{11,9},{12,10},{13,11},... | collective-permute-start | bytes 1179656 | tf_op jit(solution)/shard_map/ppermute | solution.py:32
  71.1 13.9 %all-to-all-start.1 = ((bf16[4,576,128]{2,1,0:T(8,128)(2,1)}), bf16[4,576,128]{2,1,0:T(8,128)(2,1)S(1)}, u32[]{:S(2)}, u32[]{:S(2)}) async-start(bf16[4,576,128]{2,1,0:T(8,128)(2,1)} %broadcast_in_dim.18), calls=%async_computation.1 | async-start | bytes 1179648 | tf_op jit(solution)/shard_map/all_to_all | solution.py:406
  85.1 2.0 %collective-permute-start.10 = (bf16[16,144,128]{2,1,0:T(8,128)(2,1)S(1)}, bf16[16,144,128]{2,1,0:T(8,128)(2,1)S(1)}, u32[]{:S(2)}, u32[]{:S(2)}) collective-permute-start(bf16[16,144,128]{2,1,0:T(8,128)(2,1)S(1)} %bitcast.12), channel_id=1, source_target_pairs={{0,8},{8,0},{1,9},{9,1},{2,10},{10,2},{3,11},{11,3},{4,12},{12,4},... | collective-permute-start | bytes 1769480 | tf_op jit(solution)/shard_map/ppermute | solution.py:424

commit v9 on v8

--- a/solution.py
+++ b/solution.py
@@ -103,10 +103,10 @@
     return places + [(ref, 0, ref, rows) for ref in further_refs]
 
 
-def scores_kernel(context, rows, edge, *refs):
+def scores_kernel(context, rows, edge, blocks, *refs):
     device_ref, q_hbm, own_ref, keys_ref = refs[:4]
     further_refs = refs[4 : 3 + context]
-    far_ref, near_ref, weights_ref, lse_ref, qx, kx, lx, q_ref, bias, sem = refs[3 + context :]
+    edge_ref, weights_ref, lse_ref, qx, kx, lx, q_ref, bias, sem = refs[3 + context :]
     att = q_ref.shape[1]
     pairs = att // LANES
     span = context * rows
@@ -117,18 +117,20 @@
 
     fetch = pltpu.make_async_copy(q_hbm, q_ref, sem)
     fetch.start()
-    kx[:edge] = far_ref[:edge]
     for offset, ref in enumerate((own_ref, keys_ref, *further_refs)):
         first = edge + (context - offset) * rows
         kx[first : first + rows] = ref[:rows]
-    kx[edge + span + rows :] = near_ref[:edge]
-    qx[:edge] = keys_ref[rows : rows + edge] * scale
-    qx[edge + rows :] = near_ref[2 * edge : 3 * edge] * scale
+    if blocks[0] == 0:
+        kx[:edge] = edge_ref[:edge]
+        qx[:edge] = keys_ref[rows : rows + edge] * scale
+    else:
+        kx[edge + span + rows :] = edge_ref[:edge]
+        qx[edge + rows :] = edge_ref[2 * edge : 3 * edge] * scale
     fetch.wait()
     qx[edge : edge + rows] = q_ref[...] * scale
 
     lane_id = lax.broadcasted_iota(jnp.int32, (block, LANES), 1)
-    for b in range(qx.shape[0] // block):
+    for place, b in enumerate(blocks):
         row_id = lax.broadcasted_iota(jnp.int32, (block, keys), 0)
         key_id = lax.broadcasted_iota(jnp.int32, (block, keys), 1)
         distance = row_id - key_id + span
@@ -145,22 +147,21 @@
             row_max = jnp.max(scores, axis=1, keepdims=True)
             weights = jnp.exp(scores - row_max)
             row_sum = jnp.sum(weights, axis=1, keepdims=True)
-            weights_ref[b * pairs + pair] = (weights * (1.0 / row_sum)).astype(jnp.bfloat16)
+            weights_ref[place * pairs + pair] = (weights * (1.0 / row_sum)).astype(jnp.bfloat16)
             log_sum = row_max + jnp.log(row_sum)
             log_sums = jnp.where(lane_id == 2 * pair, log_sum[:block], log_sums)
             log_sums = jnp.where(lane_id == 2 * pair + 1, log_sum[block:], log_sums)
-        lx[b * block : (b + 1) * block] = log_sums
-    lse_ref[...] = jnp.transpose(lx[...])[: lse_ref.shape[0], edge : edge + rows]
+        lx[place * block : (place + 1) * block] = log_sums
+    lse_ref[...] = jnp.transpose(lx[...])[: lse_ref.shape[0]]
 
 
 def forward_kernel(context, rows, edge, taps, *refs):
     tiles = context + 2
-    device_ref, weights_ref = refs[:2]
-    places = tile_places(rows, *refs[2 : 2 + tiles])
-    far_ref, near_ref, w_hbm, conv_hbm, cot_hbm = refs[2 + tiles : 7 + tiles]
-    out_ref, att_ref, dhid_ref, keep_ref, give_ref = refs[7 + tiles : 12 + tiles]
-    vx, ax, hid, cotx, dm, kp, ks, parts = refs[12 + tiles : 20 + tiles]
-    w_ref, conv_ref, cot_ref, sems = refs[20 + tiles :]
+    device_ref, late_ref, early_ref = refs[:3]
+    places = tile_places(rows, *refs[3 : 3 + tiles])
+    far_ref, near_ref, w_hbm, conv_hbm, cot_hbm = refs[3 + tiles : 8 + tiles]
+    out_hbm, att_hbm, dhid_hbm, keep_ref, give_ref, hid, dm = refs[8 + tiles : 15 + tiles]
+    vx, ax, cotx, parts, w_ref, conv_ref, cot_ref, out_ref, dhid_ref, sems = refs[15 + tiles :]
 
     att = ax.shape[1]
     width = w_ref.shape[1]
@@ -190,9 +191,11 @@
         for pair in range(pairs):
             columns = slice(pair * LANES, (pair + 1) * LANES)
             values = vx[b * block : b * block + keys, columns]
-            mixed = dot(weights_ref[b * pairs + pair], values, NN)
+            weights = early_ref[(b - 1) * pairs + pair] if b else late_ref[pair]
+            mixed = dot(weights, values, NN)
             ax[b * block : (b + 1) * block, columns] = merge_heads(mixed).astype(jnp.bfloat16)
-    att_ref[...] = ax[edge : edge + rows]
+    stores = [pltpu.make_async_copy(ax.at[pl.ds(edge, rows)], att_hbm, sems.at[3])]
+    stores[0].start()
 
     fetches[0].wait()
     step = 2 * LANES
@@ -213,8 +216,7 @@
         cotx[chunk, rows:] = near_ref[
             (3 + part) * edge : (4 + part) * edge, lane : lane + LANES
         ].astype(jnp.float32)
-    kp[...] = jnp.zeros_like(kp)
-    dm[rows + edge :] = jnp.zeros_like(dm[rows + edge :])
+    dm[:, rows + edge :] = jnp.zeros_like(dm[:, rows + edge :])
 
     apart = -(-taps // SUBLANES)
     reach = (apart - 1) * SUBLANES
@@ -233,7 +235,7 @@
             sigma = jax.nn.sigmoid(mixed)
             kept = min(part_rows, rows - first)
             out_ref[first : first + kept, columns] = (mixed * sigma)[:kept].astype(jnp.bfloat16)
-            dm[first : first + part_rows] = (
+            dm[chunk, first : first + part_rows] = (
                 cotx[chunk, first : first + part_rows] * sigma * (1.0 + mixed * (1.0 - sigma))
             )
         part = rows // 2
@@ -241,33 +243,20 @@
             dhidden = jnp.zeros((part, LANES), jnp.float32)
             for shift in range(SUBLANES):
                 low = first + shift
-                window = dm[low : low + part + reach]
+                window = dm[chunk, low : low + part + reach]
                 for tap in range(shift, taps, SUBLANES):
                     at = tap - shift
                     dhidden += conv_ref[tap : tap + 1, columns] * window[at : at + part]
             dhid_ref[first : first + part, columns] = dhidden.astype(jnp.bfloat16)
-        for shift in range(SUBLANES):
-            sums = [jnp.zeros((SUBLANES, LANES), jnp.float32)] * apart
-            for first in range(0, rows, part):
-                low = edge + first - shift - reach
-                window = hid[chunk, low : low + part + reach]
-                own = dm[first : first + part]
-                for tap in range(shift, taps, SUBLANES):
-                    at = reach - (tap - shift)
-                    product = (own * window[at : at + part]).reshape(-1, SUBLANES, LANES)
-                    sums[tap // SUBLANES] += jnp.sum(product, axis=0)
-            for tap in range(shift, taps, SUBLANES):
-                ks[tap * SUBLANES : (tap + 1) * SUBLANES] = sums[tap // SUBLANES]
-        total = ks[pl.ds(0, taps, SUBLANES)]
-        for row in range(1, SUBLANES):
-            total += ks[pl.ds(row, taps, SUBLANES)]
-        kp[chunk, :taps] = total
         return carry
 
     lax.fori_loop(0, width // LANES, convolve, 0)
-
-    _, pieces, piece_rows, _ = parts.shape
-    chunks = width // LANES
+    stores.append(pltpu.make_async_copy(out_ref, out_hbm, sems.at[4]))
+    stores.append(pltpu.make_async_copy(dhid_ref, dhid_hbm, sems.at[5]))
+    for store in stores[1:]:
+        store.start()
+
+    _, pieces, _, _ = parts.shape
     group = att // (2 * pieces)
     core = device_ref[1]
     own = ax[edge : edge + rows]
@@ -281,51 +270,100 @@
                     parts[half, piece, chunk * group : (chunk + 1) * group] = tile[
                         first : first + group
                     ]
-    rest = jnp.zeros((piece_rows - chunks * (group + 1), LANES), jnp.float32)
-    for half in range(2):
-        for piece in range(pieces):
-            tap = half * pieces + piece
-            row = [kp[chunk, tap : tap + 1] for chunk in range(chunks)]
-            row = jnp.concatenate(row + [rest], axis=0).astype(jnp.bfloat16)
-            parts[half, piece, chunks * group :] = row
     keep_ref[...] = parts[core]
     give_ref[...] = parts[1 - core]
-
-
-def unpack_kernel(device_ref, near_ref, far_ref, weight_ref, kernel_ref):
+    for store in stores:
+        store.wait()
+
+
+def kernel_grad_kernel(rows, edge, taps, hid, dm, rows_ref, ks, kp):
+    chunks = hid.shape[0]
+    pieces = rows_ref.shape[0]
+    apart = -(-taps // SUBLANES)
+    reach = (apart - 1) * SUBLANES
+    part = rows // 2
+    kp[...] = jnp.zeros_like(kp)
+
+    def correlate(chunk, carry):
+        for shift in range(SUBLANES):
+            sums = [jnp.zeros((SUBLANES, LANES), jnp.float32)] * apart
+            for first in range(0, rows, part):
+                low = edge + first - shift - reach
+                window = hid[chunk, low : low + part + reach]
+                own = dm[chunk, first : first + part]
+                for tap in range(shift, taps, SUBLANES):
+                    at = reach - (tap - shift)
+                    product = (own * window[at : at + part]).reshape(-1, SUBLANES, LANES)
+                    sums[tap // SUBLANES] += jnp.sum(product, axis=0)
+            for tap in range(shift, taps, SUBLANES):
+                ks[tap * SUBLANES : (tap + 1) * SUBLANES] = sums[tap // SUBLANES]
+        total = ks[pl.ds(0, taps, SUBLANES)]
+        for row in range(1, SUBLANES):
+            total += ks[pl.ds(row, taps, SUBLANES)]
+        kp[chunk, :taps] = total
+        return carry
+
+    lax.fori_loop(0, chunks, correlate, 0)
+    for piece in range(pieces):
+        block = [kp[chunk, tap : tap + 1] for tap in (piece, pieces + piece) for chunk in range(chunks)]
+        rows_ref[piece] = jnp.concatenate(block, axis=0).astype(jnp.bfloat16)
+
+
+def join_kernel(keep_ref, given_ref, rows_ref, mine_ref):
+    split = keep_ref.shape[1]
+    total = keep_ref[...].astype(jnp.float32) + given_ref[...].astype(jnp.float32)
+    mine_ref[:, :split] = total.astype(jnp.bfloat16)
+    mine_ref[:, split:] = rows_ref[...]
+
+
+def write_half(ref, half, scratch, weight_hbm, sem):
+    pieces = ref.shape[0]
+    half_rows, width = scratch.shape
+    group = half_rows // pieces
+    for piece in range(pieces):
+        for chunk in range(width // LANES):
+            tile = ref[piece, chunk * group : (chunk + 1) * group].astype(jnp.float32)
+            scratch[
+                piece * group : (piece + 1) * group, chunk * LANES : (chunk + 1) * LANES
+            ] = tile
+    first = pl.multiple_of(half * half_rows, half_rows)
+    copy = pltpu.make_async_copy(scratch, weight_hbm.at[pl.ds(first, half_rows)], sem)
+    copy.start()
+    return copy
+
+
+def unpack_near_kernel(device_ref, near_ref, weight_hbm, scratch, sem):
+    write_half(near_ref, device_ref[1], scratch, weight_hbm, sem).wait()
+
+
+def unpack_far_kernel(
+    device_ref, near_ref, far_ref, partial_hbm, weight_hbm, kernel_ref, scratch, sem
+):
+    copy = write_half(far_ref, 1 - device_ref[1], scratch, weight_hbm, sem)
     pieces, piece_rows, _ = near_ref.shape
-    att, width = weight_ref.shape
-    taps = kernel_ref.shape[0]
+    taps, width = kernel_ref.shape
     chunks = width // LANES
-    group = att // (2 * pieces)
-    core = device_ref[1]
-
-    def write(refs):
-        for half, ref in enumerate(refs):
-            for piece in range(pieces):
-                tap = half * pieces + piece
+    for piece in range(pieces):
+        total = near_ref[piece, piece_rows - 2 * chunks :].astype(jnp.float32)
+        total += far_ref[piece, piece_rows - 2 * chunks :].astype(jnp.float32)
+        for half in range(2):
+            tap = half * pieces + piece
+            if tap < taps:
                 for chunk in range(chunks):
+                    at = half * chunks + chunk
                     columns = slice(chunk * LANES, (chunk + 1) * LANES)
-                    tile = ref[piece, chunk * group : (chunk + 1) * group].astype(jnp.float32)
-                    weight_ref[tap * group : (tap + 1) * group, columns] = tile
-                if tap < taps:
-                    row = ref[piece, chunks * group :].astype(jnp.float32)
-                    for chunk in range(chunks):
-                        columns = slice(chunk * LANES, (chunk + 1) * LANES)
-                        kernel_ref[tap : tap + 1, columns] = row[chunk : chunk + 1]
-
-    pl.when(core == 0)(lambda: write((near_ref, far_ref)))
-    pl.when(core != 0)(lambda: write((far_ref, near_ref)))
+                    kernel_ref[tap : tap + 1, columns] = total[at : at + 1]
+    copy.wait()
 
 
 def backward_kernel(context, rows, *refs):
     tiles = context + 2
     device_ref, q_hbm = refs[:2]
     places = tile_places(rows, *refs[2 : 2 + tiles])
-    att_hbm, lse_ref, dhid_hbm, w_hbm = refs[2 + tiles : 6 + tiles]
-    dq_ref, own_ref = refs[6 + tiles : 8 + tiles]
-    message_refs = refs[8 + tiles : 8 + tiles + context]
-    q_ref, dhid_ref, w_ref, att_ref, datt, bias, sems = refs[8 + tiles + context :]
+    att_hbm, late_ref, early_ref, dhid_hbm, w_hbm = refs[2 + tiles : 7 + tiles]
+    dq_ref, own_ref = refs[7 + tiles : 9 + tiles]
+    message_refs = refs[9 + tiles : 9 + tiles + context]
+    q_ref, dhid_ref, w_ref, att_ref, datt, bias, lse_ref, sems = refs[9 + tiles + context :]
 
     att = q_ref.shape[1]
     heads = att // HEAD_DIM
@@ -341,6 +379,9 @@
     ]
     for fetch in fetches:
         fetch.start()
+    edge = (late_ref.shape[1] + early_ref.shape[1] - rows) // 2
+    log_sums = jnp.concatenate([late_ref[...], early_ref[...]], axis=1)
+    lse_ref[...] = log_sums[:, edge : edge + rows]
     for offset in range(context + 1):
         key_id = lax.broadcasted_iota(jnp.int32, (rows, rows), 0)
         row_id = lax.broadcasted_iota(jnp.int32, (rows, rows), 1)
@@ -483,60 +524,97 @@
     split = pieces == layers * lax.axis_size(PLANE_AXES) and layers & (layers - 1) == 0
     core = lax.axis_index("core").astype(jnp.int32) if split else jnp.int32(0)
     place = jnp.stack([device, core])
-    piece_rows = -(-(chunks * 16 + chunks) // 16) * 16
-    blocks = query_rows // LANES * (att // LANES)
+    blocks = query_rows // LANES
     key_span = context * rows + LANES
-    weights, log_sums = pl.pallas_call(
-        functools.partial(scores_kernel, context, rows, edge),
-        out_shape=(
-            jax.ShapeDtypeStruct((blocks, 2 * LANES, key_span), bf16),
-            jax.ShapeDtypeStruct((heads, rows), f32),
-        ),
-        in_specs=[smem, hbm] + [vmem] * (3 + context),
-        out_specs=(vmem,) * 2,
-        scratch_shapes=[
-            pltpu.VMEM((query_rows, att), bf16),
-            pltpu.VMEM((key_rows, att), bf16),
-            pltpu.VMEM((query_rows, LANES), f32),
-            pltpu.VMEM((rows, att), bf16),
-            pltpu.VMEM((LANES, key_span), f32),
-            pltpu.SemaphoreType.DMA,
-        ],
-        compiler_params=params,
-        cost_estimate=cost(8 * 10**9, 10**7),
-        name="scores",
-    )(place, in_hbm(query), own, keys, *further, far, near)
-    out_frames, attended, dhidden, keep, give = pl.pallas_call(
+
+    def score(blocks, edge_rows):
+        return pl.pallas_call(
+            functools.partial(scores_kernel, context, rows, edge, blocks),
+            out_shape=(
+                jax.ShapeDtypeStruct((len(blocks) * (att // LANES), 2 * LANES, key_span), bf16),
+                jax.ShapeDtypeStruct((heads, len(blocks) * LANES), f32),
+            ),
+            in_specs=[smem, hbm] + [vmem] * (2 + context),
+            out_specs=(vmem,) * 2,
+            scratch_shapes=[
+                pltpu.VMEM((query_rows, att), bf16),
+                pltpu.VMEM((key_rows, att), bf16),
+                pltpu.VMEM((len(blocks) * LANES, LANES), f32),
+                pltpu.VMEM((rows, att), bf16),
+                pltpu.VMEM((LANES, key_span), f32),
+                pltpu.SemaphoreType.DMA,
+            ],
+            compiler_params=params,
+            cost_estimate=cost(5 * 10**9, 10**7),
+            name="scores",
+        )(place, in_hbm(query), own, keys, *further, edge_rows)
+
+    early, early_sums = score(list(range(1, blocks)), near)
+    late, late_sums = score([0], far)
+    log_sums = (late_sums, early_sums)
+    out_frames, attended, dhidden, keep, give, hidden, dmixed = pl.pallas_call(
         functools.partial(forward_kernel, context, rows, edge, taps),
         out_shape=(
             jax.ShapeDtypeStruct((rows, width), bf16),
             jax.ShapeDtypeStruct((rows, att), bf16),
             jax.ShapeDtypeStruct((rows, width), bf16),
         )
-        + (jax.ShapeDtypeStruct((pieces, piece_rows, LANES), bf16),) * 2,
-        in_specs=[smem] + [vmem] * (5 + context) + [hbm] * 3,
-        out_specs=(vmem,) * 5,
+        + (jax.ShapeDtypeStruct((pieces, chunks * 16, LANES), bf16),) * 2
+        + (
+            jax.ShapeDtypeStruct((chunks, query_rows, LANES), f32),
+            jax.ShapeDtypeStruct((chunks, rows + edge + 8, LANES), f32),
+        ),
+        in_specs=[smem] + [vmem] * (6 + context) + [hbm] * 3,
+        out_specs=(hbm,) * 3 + (vmem,) * 4,
         scratch_shapes=[
             pltpu.VMEM((key_rows, att), bf16),
             pltpu.VMEM((query_rows, att), bf16),
-            pltpu.VMEM((chunks, query_rows, LANES), f32),
             pltpu.VMEM((chunks, rows + edge, LANES), f32),
-            pltpu.VMEM((rows + edge + 8, LANES), f32),
-            pltpu.VMEM((chunks, 2 * pieces, LANES), f32),
-            pltpu.VMEM((taps * SUBLANES, LANES), f32),
-            pltpu.VMEM((2, pieces, piece_rows, LANES), bf16),
+            pltpu.VMEM((2, pieces, chunks * 16, LANES), bf16),
             pltpu.VMEM((att, width), bf16),
             pltpu.VMEM((taps, width), f32),
             pltpu.VMEM((rows, width), bf16),
-            pltpu.SemaphoreType.DMA((3,)),
+            pltpu.VMEM((rows, width), bf16),
+            pltpu.VMEM((rows, width), bf16),
+            pltpu.SemaphoreType.DMA((6,)),
         ],
         compiler_params=params,
         cost_estimate=cost(8 * 10**9, 10**7),
         name="forward",
-    )(place, weights, *tiles, far, near, in_hbm(out_weight), in_hbm(conv_kernel), in_hbm(cot))
+    )(
+        place,
+        late,
+        early,
+        *tiles,
+        far,
+        near,
+        in_hbm(out_weight),
+        in_hbm(conv_kernel),
+        in_hbm(cot),
+    )
+    kernel_rows = pl.pallas_call(
+        functools.partial(kernel_grad_kernel, rows, edge, taps),
+        out_shape=jax.ShapeDtypeStruct((pieces, 2 * chunks, LANES), bf16),
+        in_specs=[vmem, vmem],
+        out_specs=vmem,
+        scratch_shapes=[
+            pltpu.VMEM((taps * SUBLANES, LANES), f32),
+            pltpu.VMEM((chunks, 2 * pieces, LANES), f32),
+        ],
+        compiler_params=params,
+        cost_estimate=cost(2 * 10**9, 3 * 10**6),
+        name="kernel_grad",
+    )(hidden, dmixed)
 
     if split:
-        mine = (keep.astype(f32) + other_core(give).astype(f32)).astype(bf16)
+        mine = pl.pallas_call(
+            join_kernel,
+            out_shape=jax.ShapeDtypeStruct((pieces, 18 * chunks, LANES), bf16),
+            in_specs=[vmem] * 3,
+            out_specs=vmem,
+            compiler_params=params,
+            name="join",
+        )(keep, other_core(give), kernel_rows)
         mine, dhidden = lax.optimization_barrier((mine, dhidden))
     query_grad, own_grads, *messages = pl.pallas_call(
         functools.partial(backward_kernel, context, rows),
@@ -545,7 +623,7 @@
             jax.ShapeDtypeStruct((2 * rows, att), f32),
         )
         + (jax.ShapeDtypeStruct((2 * rows, att), bf16),) * context,
-        in_specs=[smem, hbm] + [vmem] * (2 + context) + [hbm, vmem, hbm, hbm],
+        in_specs=[smem, hbm] + [vmem] * (2 + context) + [hbm, vmem, vmem, hbm, hbm],
         out_specs=(vmem,) * (2 + context),
         scratch_shapes=[
             pltpu.VMEM((rows, att), bf16),
@@ -554,12 +632,13 @@
             pltpu.VMEM((rows, att), bf16),
             pltpu.VMEM((rows, att), bf16),
             pltpu.VMEM((context + 1, rows, rows), f32),
+            pltpu.VMEM((heads, rows), f32),
             pltpu.SemaphoreType.DMA((4,)),
         ],
         compiler_params=params,
         cost_estimate=cost(6 * 10**9, 10**7),
         name="backward",
-    )(place, in_hbm(query), *tiles, in_hbm(attended), log_sums, in_hbm(dhidden), in_hbm(out_weight))
+    )(place, in_hbm(query), *tiles, in_hbm(attended), *log_sums, in_hbm(dhidden), in_hbm(out_weight))
     if split:
         mine, own_grads, *messages = lax.optimization_barrier(
             (collected(mine), own_grads, *messages)
@@ -583,7 +662,7 @@
         mine = summed_along(mine, "z")
         mine, messages = lax.optimization_barrier((mine, messages))
         mine = exchange(jnp.broadcast_to(mine, (lax.axis_size(PLANE_AXES), *mine.shape)))
-        mine = mine.reshape(keep.shape)
+        mine = mine.reshape(pieces, -1, LANES)
     messages = [shifted(message, -offset) for offset, message in messages.items()]
     key_grad, value_grad = pl.pallas_call(
         merge_kernel,
@@ -598,18 +677,34 @@
         mine, key_grad, value_grad = lax.optimization_barrier((mine, key_grad, value_grad))
         halves = (mine, other_core(mine))
     else:
-        halves = lax.psum((keep, give), ("x", "core", "z", "y"))
+        totals = lax.psum((keep, give, kernel_rows), ("x", "core", "z", "y"))
+        halves = [
+            jnp.concatenate([totals[0], totals[2]], axis=1),
+            jnp.concatenate([totals[1], jnp.zeros_like(totals[2])], axis=1),
+        ]
+    scratch = [pltpu.VMEM((att // 2, width), f32), pltpu.SemaphoreType.DMA]
+    weight_total = pl.pallas_call(
+        unpack_near_kernel,
+        out_shape=jax.ShapeDtypeStruct((att, width), f32),
+        in_specs=[smem, vmem],
+        out_specs=hbm,
+        scratch_shapes=scratch,
+        compiler_params=params,
+        name="unpack_near",
+    )(place, halves[0])
     weight_total, kernel_total = pl.pallas_call(
-        unpack_kernel,
+        unpack_far_kernel,
         out_shape=(
             jax.ShapeDtypeStruct((att, width), f32),
             jax.ShapeDtypeStruct((taps, width), f32),
         ),
-        in_specs=[smem, vmem, vmem],
-        out_specs=(vmem, vmem),
+        in_specs=[smem, vmem, vmem, hbm],
+        out_specs=(hbm, vmem),
+        scratch_shapes=scratch,
+        input_output_aliases={3: 0},
         compiler_params=params,
-        name="unpack",
-    )(place, *halves)
+        name="unpack_far",
+    )(place, *halves, weight_total)
     return (
         out_frames[None],
         query_grad[None],

time: 89.6 us -> 89.5 us (level)
  Pallas kernels: 24.4 us -> 28.9 us
  waiting for transfers between devices: 21.6 us -> 18.8 us
  starting transfers between devices: 39.5 us -> 37.5 us
  local copies, waits for them, and re-layouts: 1.65 us -> 2.63 us
  other arithmetic: 1.23 us -> 0.26 us
    pallas_call x2 -> x6, Pallas kernels: 5.2 us -> 11.4 us  [the longest x2 4.71 us: score(): pl.pallas_call(functools.partial(scores_kernel, context, rows, edge, bloc...]
    ppermute x2, waiting for transfers between devices: 3.99 us -> 0.41 us  [other_core(): return lax.ppermute(x, 'core', [(0, 1), (1, 0)])]
    pallas_call x1, Pallas kernels: 8.85 us -> 7.21 us  [per_device(): pl.pallas_call(functools.partial(forward_kernel, context, rows, edge, tap...]
    ppermute x5, waiting for transfers between devices: 5.78 us -> 7.24 us  [shifted(): lax.ppermute(x, RUN_AXES, [(i, i + by) for i in devices if i + by in devi...]
    all_to_all x2, waiting for transfers between devices: 4.23 us -> 2.86 us  [exchange(): return lax.all_to_all(x, PLANE_AXES, 0, 0, tiled=True)]
    ppermute x2, waiting for transfers between devices: 7.11 us -> 8.26 us  [summed_along(): other = lax.ppermute(x, axis, [(i, i ^ step) for i in range(size)])]
    ppermute x2, starting transfers between devices: 9.9 us -> 8.82 us  [summed_along(): other = lax.ppermute(x, axis, [(i, i ^ step) for i in range(size)])]
    unnamed x8, local copies, waits for them, and re-layouts: 0.75 us -> 1.74 us
  transfers between devices with their start and end apart: 13 -> 13, of which waited for: 9 -> 7; matrix products, arithmetic and copies ran while one was open for 1% -> 1% of each run, Pallas kernels for 13% -> 18%
where the time goes in v9:
time: 89.5 us; the launch traced here: 89 us
  starting transfers between devices  37.5 us (42%)
  Pallas kernels  28.9 us (32%)
  waiting for transfers between devices  18.8 us (21%)
  local copies, waits for them, and re-layouts  2.63 us (3%)
    ppermute x5, starting transfers between devices, shifted(): lax.ppermute(x, RUN_AXES, [(i, i + by) for i in devices if i + by in devi...  16.5 us
    ppermute x2, starting transfers between devices, summed_along(): other = lax.ppermute(x, axis, [(i, i ^ step) for i in range(size)])  8.82 us
    ppermute x2, waiting for transfers between devices, summed_along(): other = lax.ppermute(x, axis, [(i, i ^ step) for i in range(size)])  8.26 us
    all_to_all x2, starting transfers between devices, exchange(): return lax.all_to_all(x, PLANE_AXES, 0, 0, tiled=True)  8.13 us
    pallas_call x1, Pallas kernels, per_device(): pl.pallas_call(functools.partial(backward_kernel, context, rows), out_sha...  7.39 us
    ppermute x5, waiting for transfers between devices, shifted(): lax.ppermute(x, RUN_AXES, [(i, i + by) for i in devices if i + by in devi...  7.24 us
    pallas_call x1, Pallas kernels, per_device(): pl.pallas_call(functools.partial(forward_kernel, context, rows, edge, tap...  7.21 us
    pallas_call x2, Pallas kernels, score(): pl.pallas_call(functools.partial(scores_kernel, context, rows, edge, bloc...  4.71 us
  transfers between devices with their start and end apart: 13, of which 7 were waited for; matrix products, arithmetic and copies ran while one was open for 1% of the time, Pallas kernels for 18%

profile of v9, /device:TPU:0, one launch (start us, length us, event | category | flops | bytes accessed | tf_op | source)
XLA Modules:
  0.0 89.0 jit_solution(11708081849528116467)
XLA Ops:
  0.6 1.4 %pack.1 = (bf16[384,512]{1,0:T(8,128)(2,1)S(1)}, bf16[224,512]{1,0:T(8,128)(2,1)S(1)}, bf16[192,512]{1,0:T(8,128)(2,1)S(1)}, bf16[64,512]{1,0:T(8,128)(2,1)S(1)}, bf16[160,512]{1,0:T(8,128)(2,1)S(1)}) custom-call(bf16[192,512]{1,0:T(8,128)(2,1)} %bitcast.17, bf16[192,512]{1,0:T(8,128)(2,1)} %bitcast.18, bf16[192,512]{1,0:T(8,128)(2,1)} %bitcast.19, ...), custom_call_target="tpu_custom_call" | custom-call | tf_op jit(solution)/shard_map/pack/pallas_call | solution.py:488
  2.0 5.0 %collective-permute-start.1 = (bf16[384,512]{1,0:T(8,128)(2,1)S(1)}, bf16[384,512]{1,0:T(8,128)(2,1)S(1)}, u32[]{:S(2)}, u32[]{:S(2)}) collective-permute-start(bf16[384,512]{1,0:T(8,128)(2,1)S(1)} %get-tuple-element.45.refs_2_.refs_3_), channel_id=1, source_target_pairs={{0,2},{1,3},{2,4},{3,5},{4,6},{5,7},{8,10},{9,11},{10,12},{11,13},... | collective-permute-start | bytes 1179656 | tf_op jit(solution)/shard_map/ppermute | solution.py:32
  7.0 3.4 %collective-permute-start = (bf16[224,512]{1,0:T(8,128)(2,1)S(1)}, bf16[224,512]{1,0:T(8,128)(2,1)S(1)}, u32[]{:S(2)}, u32[]{:S(2)}) collective-permute-start(bf16[224,512]{1,0:T(8,128)(2,1)S(1)} %get-tuple-element.46), channel_id=1, source_target_pairs={{0,1},{1,2},{2,3},{3,4},{4,5},{5,6},{6,7},{8,9},{9,10},{10,11},{11... | collective-permute-start | bytes 688136 | tf_op jit(solution)/shard_map/ppermute | solution.py:32
  10.4 1.3 %collective-permute-start.3 = (bf16[160,512]{1,0:T(8,128)(2,1)S(1)}, bf16[160,512]{1,0:T(8,128)(2,1)S(1)}, u32[]{:S(2)}, u32[]{:S(2)}) collective-permute-start(bf16[160,512]{1,0:T(8,128)(2,1)S(1)} %get-tuple-element.49), channel_id=1, source_target_pairs={{1,0},{2,1},{3,2},{4,3},{5,4},{6,5},{7,6},{9,8},{10,9},{11,10},{12... | collective-permute-start | bytes 491528 | tf_op jit(solution)/shard_map/ppermute | solution.py:32
  11.7 5.5 %collective-permute-start.2 = (bf16[64,512]{1,0:T(8,128)(2,1)S(1)}, bf16[64,512]{1,0:T(8,128)(2,1)S(1)}, u32[]{:S(2)}, u32[]{:S(2)}) collective-permute-start(bf16[64,512]{1,0:T(8,128)(2,1)S(1)} %get-tuple-element.47), channel_id=1, source_target_pairs={{0,3},{1,4},{2,5},{3,6},{4,7},{8,11},{9,12},{10,13},{11,14},{12,15... | collective-permute-start | bytes 196616 | tf_op jit(solution)/shard_map/ppermute | solution.py:32
  17.3 0.1 pad_add_fusion.refs_0_.device_ref
  17.4 0.3 collective-permute-done.3.refs_5_.refs_8_
  17.7 0.0 collective-permute-done.1.refs_4_.odd_ref.refs_6_.refs_5_
  17.7 2.6 %collective-permute-start.4 = (bf16[192,512]{1,0:T(8,128)(2,1)S(1)}, bf16[192,512]{1,0:T(8,128)(2,1)S(1)}, u32[]{:S(2)}, u32[]{:S(2)}) collective-permute-start(bf16[192,512]{1,0:T(8,128)(2,1)S(1)} %choose.1), channel_id=1, source_target_pairs={{0,1},{1,0},{2,3},{3,2},{4,5},{5,4},{6,7},{7,6},{8,9},{9,8},{10,11... | collective-permute-start | bytes 589832 | tf_op jit(solution)/shard_map/ppermute | solution.py:516
  20.3 0.0 collective-permute-done.refs_3_.refs_4_
  20.3 2.4 %scores.3 = (bf16[4,256,512]{2,1,0:T(8,128)(2,1)S(1)}, f32[8,128]{1,0:T(8,128)S(1)}) custom-call(s32[2]{0:T(128)S(1)} %pad_add_fusion.refs_0_.device_ref, bf16[192,512]{1,0:T(8,128)(2,1)} %bitcast.20, bf16[384,512]{1,0:T(8,128)(2,1)S(1)} %get-tuple-element.45.refs_2_.refs_3_, bf16[224,512]{1,0:T(8,128)(2,1)S(1)} %collective-permute-done.refs_3_.refs_4_, ...), custom_call_target="tpu_custom_call" | custom-call | flops 5000000000 | bytes 10000000 | tf_op jit(solution)/shard_map/scores/pallas_call | solution.py:531
  22.7 0.0 collective-permute-done.2.refs_5_.refs_7_
  22.7 2.4 %scores.2 = (bf16[4,256,512]{2,1,0:T(8,128)(2,1)S(1)}, f32[8,128]{1,0:T(8,128)S(1)}) custom-call(s32[2]{0:T(128)S(1)} %pad_add_fusion.refs_0_.device_ref, bf16[192,512]{1,0:T(8,128)(2,1)} %bitcast.21, bf16[384,512]{1,0:T(8,128)(2,1)S(1)} %get-tuple-element.45.refs_2_.refs_3_, bf16[224,512]{1,0:T(8,128)(2,1)S(1)} %collective-permute-done.refs_3_.refs_4_, ...), custom_call_target="tpu_custom_call" | custom-call | flops 5000000000 | bytes 10000000 | tf_op jit(solution)/shard_map/scores/pallas_call | solution.py:531
  25.0 0.0 collective-permute-done.4.refs_5_.refs_4_
  25.0 7.2 %forward.1 = (bf16[192,1024]{1,0:T(8,128)(2,1)}, bf16[192,512]{1,0:T(8,128)(2,1)S(1)}, bf16[192,1024]{1,0:T(8,128)(2,1)S(1)}, bf16[16,128,128]{2,1,0:T(8,128)(2,...) custom-call(s32[2]{0:T(128)S(1)} %pad_add_fusion.refs_0_.device_ref, ...), custom_call_target="tpu_custom_call" | custom-call | flops 8000000000 | bytes 10000000 | tf_op jit(solution)/shard_map/forward/pallas_call | solution.py:555
  32.3 0.0 copy-start.2
  32.3 0.0 copy-start.3
  32.3 0.1 collective-permute-start.5
  32.4 1.9 %kernel_grad.1.rows_ref = bf16[16,16,128]{2,1,0:T(8,128)(2,1)S(1)} custom-call(f32[8,256,128]{2,1,0:T(8,128)S(1)} %get-tuple-element.60.hid, f32[8,232,128]{2,1,0:T(8,128)S(1)} %get-tuple-element.61.dm), custom_call_target="tpu_custom_call" | custom-call | flops 2000000000 | bytes 3000000 | tf_op jit(solution)/shard_map/kernel_grad/pallas_call | solution.py:595
  34.3 0.0 copy-done.2
  34.3 0.0 copy-done.3
  34.3 0.0 collective-permute-done.5.given_ref
  34.3 0.9 %join.1 = bf16[16,144,128]{2,1,0:T(8,128)(2,1)} custom-call(bf16[16,128,128]{2,1,0:T(8,128)(2,1)S(1)} %get-tuple-element.58.keep_ref, bf16[16,128,128]{2,1,0:T(8,128)(2,1)S(1)} %collective-permute-done.5.given_ref, bf16[16,16,128]{2,1,0:T(8,128)(2,1)S(1)} %kernel_grad.1.rows_ref), custom_call_target="tpu_custom_call" | custom-call | tf_op jit(solution)/shard_map/join/pallas_call | solution.py:610
  35.2 4.4 %all-to-all-start = ((bf16[4,576,128]{2,1,0:T(8,128)(2,1)}), bf16[4,576,128]{2,1,0:T(8,128)(2,1)S(1)}, u32[]{:S(2)}, u32[]{:S(2)}) async-start(bf16[4,576,128]{2,1,0:T(8,128)(2,1)} %bitcast.8), calls=%async_computation | async-start | bytes 1179648 | tf_op jit(solution)/shard_map/all_to_all | solution.py:447
  39.6 7.4 %backward.1 = (bf16[192,512]{1,0:T(8,128)(2,1)}, f32[384,512]{1,0:T(8,128)S(1)}, bf16[384,512]{1,0:T(8,128)(2,1)S(1)}, bf16[384,512]{1,0:T(8,128)(2,1)S(1)}) custom-call(s32[2]{0:T(128)S(1)} %pad_add_fusion.refs_0_.device_ref, bf16[192,512]{1,0:T(8,128)(2,1)} %bitcast.22, bf16[384,512]{1,0:T(8,128)(2,1)S(1)} %get-tuple-element.45.refs_2_.refs_3_, ...), custom_call_target="tpu_custom_call" | custom-call | flops 6000000000 | bytes 10000000 | tf_op jit(solution)/shard_map/backward/pallas_call | solution.py:619
  47.0 0.0 copy-start
  47.0 0.7 copy-done
  47.8 1.2 %all-to-all-done = bf16[4,576,128]{2,1,0:T(8,128)(2,1)S(1)} async-done(((bf16[4,576,128]{2,1,0:T(8,128)(2,1)}), bf16[4,576,128]{2,1,0:T(8,128)(2,1)S(1)}, u32[]{:S(2)}, u32[]{:S(2)}) %all-to-all-start) | async-done | bytes 589856 | tf_op jit(solution)/shard_map/all_to_all | solution.py:447
  49.0 0.1 reduce_sum.12
  49.1 4.6 %collective-permute-start.6 = (bf16[576,128]{1,0:T(8,128)(2,1)S(1)}, bf16[576,128]{1,0:T(8,128)(2,1)S(1)}, u32[]{:S(2)}, u32[]{:S(2)}) collective-permute-start(bf16[576,128]{1,0:T(8,128)(2,1)S(1)} %reduce_sum.12), channel_id=1, source_target_pairs={{0,2},{2,0},{4,6},{6,4},{1,3},{3,1},{5,7},{7,5},{8,10},{10,8},{12,... | collective-permute-start | bytes 442376 | tf_op jit(solution)/shard_map/ppermute | solution.py:458
  53.7 1.5 %collective-permute-start.8 = (bf16[384,512]{1,0:T(8,128)(2,1)S(1)}, bf16[384,512]{1,0:T(8,128)(2,1)S(1)}, u32[]{:S(2)}, u32[]{:S(2)}) collective-permute-start(bf16[384,512]{1,0:T(8,128)(2,1)S(1)} %get-tuple-element.71), channel_id=1, source_target_pairs={{0,1},{1,0},{2,3},{3,2},{4,5},{5,4},{6,7},{7,6},{8,9},{9,8},{10,11... | collective-permute-start | bytes 1179656 | tf_op jit(solution)/shard_map/ppermute | solution.py:648
  55.2 2.3 %collective-permute-done.6 = bf16[576,128]{1,0:T(8,128)(2,1)S(1)} collective-permute-done((bf16[576,128]{1,0:T(8,128)(2,1)S(1)}, bf16[576,128]{1,0:T(8,128)(2,1)S(1)}, u32[]{:S(2)}, u32[]{:S(2)}) %collective-permute-start.6) | collective-permute-done | bytes 147488 | tf_op jit(solution)/shard_map/ppermute | solution.py:458
  57.5 4.2 %collective-permute-start.7 = (bf16[576,128]{1,0:T(8,128)(2,1)S(1)}, bf16[576,128]{1,0:T(8,128)(2,1)S(1)}, u32[]{:S(2)}, u32[]{:S(2)}) collective-permute-start(bf16[576,128]{1,0:T(8,128)(2,1)S(1)} %add_convert_fusion.1), channel_id=1, source_target_pairs={{0,4},{2,6},{4,0},{6,2},{1,5},{3,7},{5,1},{7,3},{8,12},{10,14},{12... | collective-permute-start | bytes 442376 | tf_op jit(solution)/shard_map/ppermute | solution.py:458
  61.7 6.0 %collective-permute-done.7 = bf16[576,128]{1,0:T(8,128)(2,1)S(1)} collective-permute-done((bf16[576,128]{1,0:T(8,128)(2,1)S(1)}, bf16[576,128]{1,0:T(8,128)(2,1)S(1)}, u32[]{:S(2)}, u32[]{:S(2)}) %collective-permute-start.7) | collective-permute-done | bytes 147488 | tf_op jit(solution)/shard_map/ppermute | solution.py:458
  67.7 0.0 collective-permute-done.8.swapped_ref
  67.8 0.0 copy-start.1
  67.8 1.0 %copy-done.1 = bf16[384,512]{1,0:T(8,128)(2,1)S(1)} copy-done((bf16[384,512]{1,0:T(8,128)(2,1)S(1)}, bf16[384,512]{1,0:T(8,128)(2,1)}, u32[]{:S(2)}) %copy-start.1) | copy-done | bytes 393240
  68.8 0.7 relay.1
  69.5 1.3 %collective-permute-start.9 = (bf16[384,512]{1,0:T(8,128)(2,1)S(1)}, bf16[384,512]{1,0:T(8,128)(2,1)S(1)}, u32[]{:S(2)}, u32[]{:S(2)}) collective-permute-start(bf16[384,512]{1,0:T(8,128)(2,1)S(1)} %get-tuple-element.76), channel_id=1, source_target_pairs={{2,0},{3,1},{4,2},{5,3},{6,4},{7,5},{10,8},{11,9},{12,10},{13,11},... | collective-permute-start | bytes 1179656 | tf_op jit(solution)/shard_map/ppermute | solution.py:32
  70.8 0.9 %broadcast_in_dim.18 = bf16[4,576,128]{2,1,0:T(8,128)(2,1)} broadcast(bf16[576,128]{1,0:T(8,128)(2,1)S(1)} %add_convert_fusion), dimensions={1,2} | broadcast | bytes 737280 | tf_op jit(solution)/shard_map/broadcast_in_dim | solution.py:664
  71.7 3.7 %all-to-all-start.1 = ((bf16[4,576,128]{2,1,0:T(8,128)(2,1)}), bf16[4,576,128]{2,1,0:T(8,128)(2,1)S(1)}, u32[]{:S(2)}, u32[]{:S(2)}) async-start(bf16[4,576,128]{2,1,0:T(8,128)(2,1)} %broadcast_in_dim.18), calls=%async_computation.1 | async-start | bytes 1179648 | tf_op jit(solution)/shard_map/all_to_all | solution.py:447
  75.4 6.9 %collective-permute-done.9.refs_1_ = bf16[384,512]{1,0:T(8,128)(2,1)S(1)} collective-permute-done((bf16[384,512]{1,0:T(8,128)(2,1)S(1)}, bf16[384,512]{1,0:T(8,128)(2,1)S(1)}, u32[]{:S(2)}, u32[]{:S(2)}) %collective-permute-start.9) | collective-permute-done | bytes 393248 | tf_op jit(solution)/shard_map/ppermute | solution.py:32
  82.3 0.8 merge.1
  83.1 1.6 %all-to-all-done.1 = bf16[4,576,128]{2,1,0:T(8,128)(2,1)S(1)} async-done(((bf16[4,576,128]{2,1,0:T(8,128)(2,1)}), bf16[4,576,128]{2,1,0:T(8,128)(2,1)S(1)}, u32[]{:S(2)}, u32[]{:S(2)}) %all-to-all-start.1) | async-done | bytes 589856 | tf_op jit(solution)/shard_map/all_to_all | solution.py:447
  84.7 0.0 collective-permute-start.10
  84.7 1.6 %unpack_near.1.partial_hbm = f32[512,1024]{1,0:T(8,128)} custom-call(s32[2]{0:T(128)S(1)} %pad_add_fusion.refs_0_.device_ref, bf16[16,144,128]{2,1,0:T(8,128)(2,1)S(1)} %bitcast.13), custom_call_target="tpu_custom_call" | custom-call | tf_op jit(solution)/shard_map/unpack_near/pallas_call | solution.py:686
  86.3 0.4 collective-permute-done.10.far_ref
  86.7 2.2 %unpack_far.1 = (f32[512,1024]{1,0:T(8,128)}, f32[31,1024]{1,0:T(8,128)}) custom-call(s32[2]{0:T(128)S(1)} %pad_add_fusion.refs_0_.device_ref, bf16[16,144,128]{2,1,0:T(8,128)(2,1)S(1)} %bitcast.14, bf16[16,144,128]{2,1,0:T(8,128)(2,1)S(1)} %collective-permute-done.10.far_ref, f32[512,1024]{1,0:T(8,128)} %unpack_near.1.partial_hbm), custom_call_target="tpu_custom_call", output_to_operand_aliasing={{0}: (3, {})} | custom-call | tf_op jit(solution)/shard_map/unpack_far/pallas_call | solution.py:695
  (3 shorter events, 0.1 us)
Async XLA Ops:
  2.0 15.7 %collective-permute-start.1 = (bf16[384,512]{1,0:T(8,128)(2,1)S(1)}, bf16[384,512]{1,0:T(8,128)(2,1)S(1)}, u32[]{:S(2)}, u32[]{:S(2)}) collective-permute-start(bf16[384,512]{1,0:T(8,128)(2,1)S(1)} %get-tuple-element.45.refs_2_.refs_3_), channel_id=1, source_target_pairs={{0,2},{1,3},{2,4},{3,5},{4,6},{5,7},{8,10},{9,11},{10,12},{11,13},... | collective-permute-start | bytes 1179656 | tf_op jit(solution)/shard_map/ppermute | solution.py:32
  7.0 13.3 %collective-permute-start = (bf16[224,512]{1,0:T(8,128)(2,1)S(1)}, bf16[224,512]{1,0:T(8,128)(2,1)S(1)}, u32[]{:S(2)}, u32[]{:S(2)}) collective-permute-start(bf16[224,512]{1,0:T(8,128)(2,1)S(1)} %get-tuple-element.46), channel_id=1, source_target_pairs={{0,1},{1,2},{2,3},{3,4},{4,5},{5,6},{6,7},{8,9},{9,10},{10,11},{11... | collective-permute-start | bytes 688136 | tf_op jit(solution)/shard_map/ppermute | solution.py:32
  10.4 7.3 %collective-permute-start.3 = (bf16[160,512]{1,0:T(8,128)(2,1)S(1)}, bf16[160,512]{1,0:T(8,128)(2,1)S(1)}, u32[]{:S(2)}, u32[]{:S(2)}) collective-permute-start(bf16[160,512]{1,0:T(8,128)(2,1)S(1)} %get-tuple-element.49), channel_id=1, source_target_pairs={{1,0},{2,1},{3,2},{4,3},{5,4},{6,5},{7,6},{9,8},{10,9},{11,10},{12... | collective-permute-start | bytes 491528 | tf_op jit(solution)/shard_map/ppermute | solution.py:32
  11.7 10.9 %collective-permute-start.2 = (bf16[64,512]{1,0:T(8,128)(2,1)S(1)}, bf16[64,512]{1,0:T(8,128)(2,1)S(1)}, u32[]{:S(2)}, u32[]{:S(2)}) collective-permute-start(bf16[64,512]{1,0:T(8,128)(2,1)S(1)} %get-tuple-element.47), channel_id=1, source_target_pairs={{0,3},{1,4},{2,5},{3,6},{4,7},{8,11},{9,12},{10,13},{11,14},{12,15... | collective-permute-start | bytes 196616 | tf_op jit(solution)/shard_map/ppermute | solution.py:32
  17.7 7.3 %collective-permute-start.4 = (bf16[192,512]{1,0:T(8,128)(2,1)S(1)}, bf16[192,512]{1,0:T(8,128)(2,1)S(1)}, u32[]{:S(2)}, u32[]{:S(2)}) collective-permute-start(bf16[192,512]{1,0:T(8,128)(2,1)S(1)} %choose.1), channel_id=1, source_target_pairs={{0,1},{1,0},{2,3},{3,2},{4,5},{5,4},{6,7},{7,6},{8,9},{9,8},{10,11... | collective-permute-start | bytes 589832 | tf_op jit(solution)/shard_map/ppermute | solution.py:516
  32.3 2.0 %copy-start.2 = (bf16[192,1024]{1,0:T(8,128)(2,1)}, bf16[192,1024]{1,0:T(8,128)(2,1)S(1)}, u32[]{:S(2)}) copy-start(bf16[192,1024]{1,0:T(8,128)(2,1)S(1)} %get-tuple-element.63.refs_9_) | copy-start | bytes 1179652
  32.3 2.0 %copy-start.3 = (bf16[192,512]{1,0:T(8,128)(2,1)}, bf16[192,512]{1,0:T(8,128)(2,1)S(1)}, u32[]{:S(2)}) copy-start(bf16[192,512]{1,0:T(8,128)(2,1)S(1)} %get-tuple-element.55.refs_6_) | copy-start | bytes 589828
  32.3 2.0 %collective-permute-start.5 = (bf16[16,128,128]{2,1,0:T(8,128)(2,1)S(1)}, bf16[16,128,128]{2,1,0:T(8,128)(2,1)S(1)}, u32[]{:S(2)}, u32[]{:S(2)}) collective-permute-start(bf16[16,128,128]{2,1,0:T(8,128)(2,1)S(1)} %get-tuple-element.59), channel_id=1, source_target_pairs={{0,8},{8,0},{1,9},{9,1},{2,10},{10,2},{3,11},{11,3},{4,12},{12,4},... | collective-permute-start | bytes 1572872 | tf_op jit(solution)/shard_map/ppermute | solution.py:465
  35.2 13.8 %all-to-all-start = ((bf16[4,576,128]{2,1,0:T(8,128)(2,1)}), bf16[4,576,128]{2,1,0:T(8,128)(2,1)S(1)}, u32[]{:S(2)}, u32[]{:S(2)}) async-start(bf16[4,576,128]{2,1,0:T(8,128)(2,1)} %bitcast.8), calls=%async_computation | async-start | bytes 1179648 | tf_op jit(solution)/shard_map/all_to_all | solution.py:447
  47.0 0.8 copy-start
  49.1 8.3 %collective-permute-start.6 = (bf16[576,128]{1,0:T(8,128)(2,1)S(1)}, bf16[576,128]{1,0:T(8,128)(2,1)S(1)}, u32[]{:S(2)}, u32[]{:S(2)}) collective-permute-start(bf16[576,128]{1,0:T(8,128)(2,1)S(1)} %reduce_sum.12), channel_id=1, source_target_pairs={{0,2},{2,0},{4,6},{6,4},{1,3},{3,1},{5,7},{7,5},{8,10},{10,8},{12,... | collective-permute-start | bytes 442376 | tf_op jit(solution)/shard_map/ppermute | solution.py:458
  53.7 14.0 %collective-permute-start.8 = (bf16[384,512]{1,0:T(8,128)(2,1)S(1)}, bf16[384,512]{1,0:T(8,128)(2,1)S(1)}, u32[]{:S(2)}, u32[]{:S(2)}) collective-permute-start(bf16[384,512]{1,0:T(8,128)(2,1)S(1)} %get-tuple-element.71), channel_id=1, source_target_pairs={{0,1},{1,0},{2,3},{3,2},{4,5},{5,4},{6,7},{7,6},{8,9},{9,8},{10,11... | collective-permute-start | bytes 1179656 | tf_op jit(solution)/shard_map/ppermute | solution.py:648
  57.5 10.2 %collective-permute-start.7 = (bf16[576,128]{1,0:T(8,128)(2,1)S(1)}, bf16[576,128]{1,0:T(8,128)(2,1)S(1)}, u32[]{:S(2)}, u32[]{:S(2)}) collective-permute-start(bf16[576,128]{1,0:T(8,128)(2,1)S(1)} %add_convert_fusion.1), channel_id=1, source_target_pairs={{0,4},{2,6},{4,0},{6,2},{1,5},{3,7},{5,1},{7,3},{8,12},{10,14},{12... | collective-permute-start | bytes 442376 | tf_op jit(solution)/shard_map/ppermute | solution.py:458
  67.8 1.0 %copy-start.1 = (bf16[384,512]{1,0:T(8,128)(2,1)S(1)}, bf16[384,512]{1,0:T(8,128)(2,1)}, u32[]{:S(2)}) copy-start(bf16[384,512]{1,0:T(8,128)(2,1)} %copy-done) | copy-start | bytes 1179652
  69.5 12.8 %collective-permute-start.9 = (bf16[384,512]{1,0:T(8,128)(2,1)S(1)}, bf16[384,512]{1,0:T(8,128)(2,1)S(1)}, u32[]{:S(2)}, u32[]{:S(2)}) collective-permute-start(bf16[384,512]{1,0:T(8,128)(2,1)S(1)} %get-tuple-element.76), channel_id=1, source_target_pairs={{2,0},{3,1},{4,2},{5,3},{6,4},{7,5},{10,8},{11,9},{12,10},{13,11},... | collective-permute-start | bytes 1179656 | tf_op jit(solution)/shard_map/ppermute | solution.py:32
  71.7 13.0 %all-to-all-start.1 = ((bf16[4,576,128]{2,1,0:T(8,128)(2,1)}), bf16[4,576,128]{2,1,0:T(8,128)(2,1)S(1)}, u32[]{:S(2)}, u32[]{:S(2)}) async-start(bf16[4,576,128]{2,1,0:T(8,128)(2,1)} %broadcast_in_dim.18), calls=%async_computation.1 | async-start | bytes 1179648 | tf_op jit(solution)/shard_map/all_to_all | solution.py:447
  84.7 2.0 %collective-permute-start.10 = (bf16[16,144,128]{2,1,0:T(8,128)(2,1)S(1)}, bf16[16,144,128]{2,1,0:T(8,128)(2,1)S(1)}, u32[]{:S(2)}, u32[]{:S(2)}) collective-permute-start(bf16[16,144,128]{2,1,0:T(8,128)(2,1)S(1)} %bitcast.12), channel_id=1, source_target_pairs={{0,8},{8,0},{1,9},{9,1},{2,10},{10,2},{3,11},{11,3},{4,12},{12,4},... | collective-permute-start | bytes 1769480 | tf_op jit(solution)/shard_map/ppermute | solution.py:465

commit v10 on v9

--- a/solution.py
+++ b/solution.py
@@ -58,7 +58,18 @@
 
 
 def pack_kernel(
-    edge, k_ref, v_ref, q_ref, cot_ref, own_ref, keys_ref, values_ref, far_ref, near_ref, sems
+    edge,
+    k_ref,
+    v_ref,
+    q_ref,
+    cot_ref,
+    own_ref,
+    keys_ref,
+    values_ref,
+    queries_ref,
+    far_ref,
+    near_ref,
+    sems,
 ):
     rows, att = k_ref.shape
     width = cot_ref.shape[1]
@@ -69,6 +80,7 @@
         (k_ref, keys_ref.at[pl.ds(0, rows)]),
         (q_ref.at[tail], keys_ref.at[pl.ds(rows, edge)]),
         (v_ref, values_ref),
+        (q_ref, queries_ref),
         (k_ref.at[tail], far_ref.at[pl.ds(0, edge)]),
         (v_ref.at[tail], far_ref.at[pl.ds(edge, edge)]),
         (k_ref.at[head], near_ref.at[pl.ds(0, edge)]),
@@ -103,65 +115,62 @@
     return places + [(ref, 0, ref, rows) for ref in further_refs]
 
 
-def scores_kernel(context, rows, edge, blocks, *refs):
-    device_ref, q_hbm, own_ref, keys_ref = refs[:4]
-    further_refs = refs[4 : 3 + context]
-    edge_ref, weights_ref, lse_ref, qx, kx, lx, q_ref, bias, sem = refs[3 + context :]
-    att = q_ref.shape[1]
-    pairs = att // LANES
-    span = context * rows
+def score_block(b, place, start, span, qx, kx, bias, weights_ref):
+    pairs = qx.shape[1] // LANES
     block = LANES
     keys = span + block
+    row_id = lax.broadcasted_iota(jnp.int32, (block, keys), 0)
+    key_id = lax.broadcasted_iota(jnp.int32, (block, keys), 1)
+    distance = row_id - key_id + span
+    key_time = key_id + (start - span + b * block)
+    visible = (distance >= 0) & (distance < span) & (key_time >= 0)
+    bias[...] = jnp.where(visible, 0.0, NEGATIVE)
+    lane_id = lax.broadcasted_iota(jnp.int32, (block, LANES), 1)
+    log_sums = jnp.zeros((block, LANES), jnp.float32)
+    for pair in range(pairs):
+        columns = slice(pair * LANES, (pair + 1) * LANES)
+        qs = stack_heads(qx[b * block : (b + 1) * block, columns])
+        scores = dot(qs, kx[b * block : b * block + keys, columns], NT)
+        hidden_pairs = bias[...]
+        scores = scores + jnp.concatenate([hidden_pairs, hidden_pairs], axis=0)
+        row_max = jnp.max(scores, axis=1, keepdims=True)
+        weights = jnp.exp(scores - row_max)
+        row_sum = jnp.sum(weights, axis=1, keepdims=True)
+        weights_ref[place * pairs + pair] = (weights * (1.0 / row_sum)).astype(jnp.bfloat16)
+        log_sum = row_max + jnp.log(row_sum)
+        log_sums = jnp.where(lane_id == 2 * pair, log_sum[:block], log_sums)
+        log_sums = jnp.where(lane_id == 2 * pair + 1, log_sum[block:], log_sums)
+    return log_sums
+
+
+def scores_kernel(context, rows, edge, device_ref, q_ref, *refs):
+    own_refs = refs[: 1 + context]
+    near_ref, weights_ref, lse_ref, qx, kx, lx, bias = refs[1 + context :]
+    span = context * rows
     scale = 1.0 / math.sqrt(HEAD_DIM)
-    start = device_ref[0] * rows
-
-    fetch = pltpu.make_async_copy(q_hbm, q_ref, sem)
-    fetch.start()
-    for offset, ref in enumerate((own_ref, keys_ref, *further_refs)):
+    start = device_ref[0] * rows - edge
+    for offset, ref in enumerate(own_refs):
         first = edge + (context - offset) * rows
         kx[first : first + rows] = ref[:rows]
-    if blocks[0] == 0:
-        kx[:edge] = edge_ref[:edge]
-        qx[:edge] = keys_ref[rows : rows + edge] * scale
-    else:
-        kx[edge + span + rows :] = edge_ref[:edge]
-        qx[edge + rows :] = edge_ref[2 * edge : 3 * edge] * scale
-    fetch.wait()
+    kx[edge + span + rows :] = near_ref[:edge]
     qx[edge : edge + rows] = q_ref[...] * scale
-
-    lane_id = lax.broadcasted_iota(jnp.int32, (block, LANES), 1)
-    for place, b in enumerate(blocks):
-        row_id = lax.broadcasted_iota(jnp.int32, (block, keys), 0)
-        key_id = lax.broadcasted_iota(jnp.int32, (block, keys), 1)
-        distance = row_id - key_id + span
-        key_time = key_id + (start - edge - span + b * block)
-        visible = (distance >= 0) & (distance < span) & (key_time >= 0)
-        bias[...] = jnp.where(visible, 0.0, NEGATIVE)
-        log_sums = jnp.zeros((block, LANES), jnp.float32)
-        for pair in range(pairs):
-            columns = slice(pair * LANES, (pair + 1) * LANES)
-            qs = stack_heads(qx[b * block : (b + 1) * block, columns])
-            scores = dot(qs, kx[b * block : b * block + keys, columns], NT)
-            hidden_pairs = bias[...]
-            scores = scores + jnp.concatenate([hidden_pairs, hidden_pairs], axis=0)
-            row_max = jnp.max(scores, axis=1, keepdims=True)
-            weights = jnp.exp(scores - row_max)
-            row_sum = jnp.sum(weights, axis=1, keepdims=True)
-            weights_ref[place * pairs + pair] = (weights * (1.0 / row_sum)).astype(jnp.bfloat16)
-            log_sum = row_max + jnp.log(row_sum)
-            log_sums = jnp.where(lane_id == 2 * pair, log_sum[:block], log_sums)
-            log_sums = jnp.where(lane_id == 2 * pair + 1, log_sum[block:], log_sums)
-        lx[place * block : (place + 1) * block] = log_sums
+    qx[edge + rows :] = near_ref[2 * edge : 3 * edge] * scale
+    for place in range(qx.shape[0] // LANES - 1):
+        lx[place * LANES : (place + 1) * LANES] = score_block(
+            place + 1, place, start, span, qx, kx, bias, weights_ref
+        )
     lse_ref[...] = jnp.transpose(lx[...])[: lse_ref.shape[0]]
 
 
 def forward_kernel(context, rows, edge, taps, *refs):
     tiles = context + 2
-    device_ref, late_ref, early_ref = refs[:3]
+    device_ref, q_ref, early_ref = refs[:3]
+    keys_ref = refs[4]
     places = tile_places(rows, *refs[3 : 3 + tiles])
     far_ref, near_ref, w_hbm, conv_hbm, cot_hbm = refs[3 + tiles : 8 + tiles]
-    out_hbm, att_hbm, dhid_hbm, keep_ref, give_ref, hid, dm = refs[8 + tiles : 15 + tiles]
-    vx, ax, cotx, parts, w_ref, conv_ref, cot_ref, out_ref, dhid_ref, sems = refs[15 + tiles :]
+    out_hbm, att_hbm, lse_ref, dhid_hbm, keep_ref, give_ref, hid, dm = refs[8 + tiles : 16 + tiles]
+    qx, kx, vx, ax, late, bias, cotx, parts = refs[16 + tiles : 24 + tiles]
+    w_ref, conv_ref, cot_ref, out_ref, dhid_ref, sems = refs[24 + tiles :]
 
     att = ax.shape[1]
     width = w_ref.shape[1]
@@ -180,18 +189,26 @@
     for fetch in fetches:
         fetch.start()
 
+    scale = 1.0 / math.sqrt(HEAD_DIM)
+    qx[:edge] = keys_ref[rows : rows + edge] * scale
+    qx[edge:] = q_ref[: block - edge] * scale
+    kx[:edge] = far_ref[:edge]
     vx[:edge] = far_ref[edge:]
-    for offset, (_, _, ref, at) in enumerate(places):
+    for offset, (k_ref, k_at, v_ref, v_at) in enumerate(places):
         first = edge + (context - offset) * rows
-        vx[first : first + rows] = ref[at : at + rows]
+        count = min(rows, keys - first)
+        kx[first : first + count] = k_ref[k_at : k_at + count]
+        vx[first : first + rows] = v_ref[v_at : v_at + rows]
     vx[edge + span + rows :] = near_ref[edge : 2 * edge]
+    log_sums = score_block(0, 0, start - edge, span, qx, kx, bias, late)
+    lse_ref[...] = jnp.transpose(log_sums)[: lse_ref.shape[0]]
 
     pairs = att // LANES
     for b in range(query_rows // block):
         for pair in range(pairs):
             columns = slice(pair * LANES, (pair + 1) * LANES)
             values = vx[b * block : b * block + keys, columns]
-            weights = early_ref[(b - 1) * pairs + pair] if b else late_ref[pair]
+            weights = early_ref[(b - 1) * pairs + pair] if b else late[pair]
             mixed = dot(weights, values, NN)
             ax[b * block : (b + 1) * block, columns] = merge_heads(mixed).astype(jnp.bfloat16)
     stores = [pltpu.make_async_copy(ax.at[pl.ds(edge, rows)], att_hbm, sems.at[3])]
@@ -337,23 +354,38 @@
 
 
 def unpack_far_kernel(
-    device_ref, near_ref, far_ref, partial_hbm, weight_hbm, kernel_ref, scratch, sem
+    device_ref,
+    near_ref,
+    far_ref,
+    partial_hbm,
+    weight_hbm,
+    kernel_hbm,
+    scratch,
+    blocks,
+    kernel_ref,
+    sem,
+    kernel_sem,
 ):
     copy = write_half(far_ref, 1 - device_ref[1], scratch, weight_hbm, sem)
     pieces, piece_rows, _ = near_ref.shape
     taps, width = kernel_ref.shape
     chunks = width // LANES
+    size = 2 * chunks
     for piece in range(pieces):
-        total = near_ref[piece, piece_rows - 2 * chunks :].astype(jnp.float32)
-        total += far_ref[piece, piece_rows - 2 * chunks :].astype(jnp.float32)
-        for half in range(2):
-            tap = half * pieces + piece
-            if tap < taps:
-                for chunk in range(chunks):
-                    at = half * chunks + chunk
-                    columns = slice(chunk * LANES, (chunk + 1) * LANES)
-                    kernel_ref[tap : tap + 1, columns] = total[at : at + 1]
+        total = near_ref[piece, piece_rows - size :].astype(jnp.float32)
+        total += far_ref[piece, piece_rows - size :].astype(jnp.float32)
+        blocks[piece * size : (piece + 1) * size] = total
+    for half in range(2):
+        first = half * pieces
+        count = min(pieces, taps - first)
+        for chunk in range(chunks):
+            columns = slice(chunk * LANES, (chunk + 1) * LANES)
+            tap_rows = blocks[pl.ds(half * chunks + chunk, count, size)]
+            kernel_ref[first : first + count, columns] = tap_rows
+    kernel_copy = pltpu.make_async_copy(kernel_ref, kernel_hbm, kernel_sem)
+    kernel_copy.start()
     copy.wait()
+    kernel_copy.wait()
 
 
 def backward_kernel(context, rows, *refs):
@@ -425,20 +457,20 @@
         dq_ref[:, columns] = (merge_heads(dquery) * scale).astype(jnp.bfloat16)
 
 
-def relay_kernel(device_ref, own_ref, swapped_ref, message_ref, own_out, message_out):
+def relay_kernel(device_ref, swapped_ref, message_ref, out_ref):
     odd = lax.rem(device_ref[0], 2).astype(jnp.float32)
-    swapped = swapped_ref[...].astype(jnp.float32)
-    own_out[...] = own_ref[...] + swapped * (1.0 - odd)
-    message_out[...] = (message_ref[...].astype(jnp.float32) + swapped * odd).astype(jnp.bfloat16)
-
-
-def merge_kernel(*refs):
-    own_ref, *message_refs, dk_ref, dv_ref = refs
+    swapped = swapped_ref[...].astype(jnp.float32) * odd
+    out_ref[...] = (message_ref[...].astype(jnp.float32) + swapped).astype(jnp.bfloat16)
+
+
+def merge_kernel(device_ref, *refs):
+    *message_refs, swapped_ref, own_ref, dk_ref, dv_ref = refs
     rows = dk_ref.shape[0]
-    total = own_ref[...]
+    even = 1.0 - lax.rem(device_ref[0], 2).astype(jnp.float32)
+    total = swapped_ref[...].astype(jnp.float32) * even
     for message_ref in message_refs:
         total += message_ref[...].astype(jnp.float32)
-    total = total.astype(jnp.bfloat16)
+    total = (total + own_ref[...]).astype(jnp.bfloat16)
     dk_ref[...] = total[:rows]
     dv_ref[...] = total[rows:]
 
@@ -485,18 +517,19 @@
     hbm = pl.BlockSpec(memory_space=pltpu.HBM)
     params = pltpu.CompilerParams(vmem_limit_bytes=VMEM_LIMIT)
 
-    own, keys, values, far, near = pl.pallas_call(
+    own, keys, values, packed_query, far, near = pl.pallas_call(
         functools.partial(pack_kernel, edge),
         out_shape=(
             jax.ShapeDtypeStruct((2 * rows, att), bf16),
             jax.ShapeDtypeStruct((rows + edge, att), bf16),
             jax.ShapeDtypeStruct((rows, att), bf16),
+            jax.ShapeDtypeStruct((rows, att), bf16),
             jax.ShapeDtypeStruct((2 * edge, att), bf16),
             jax.ShapeDtypeStruct(((3 + width // att) * edge, att), bf16),
         ),
         in_specs=[hbm] * 4,
-        out_specs=(vmem,) * 5,
-        scratch_shapes=[pltpu.SemaphoreType.DMA((10 + width // att,))],
+        out_specs=(vmem,) * 6,
+        scratch_shapes=[pltpu.SemaphoreType.DMA((11 + width // att,))],
         compiler_params=params,
         name="pack",
     )(in_hbm(key), in_hbm(value), in_hbm(query), in_hbm(cot))
@@ -525,38 +558,32 @@
     core = lax.axis_index("core").astype(jnp.int32) if split else jnp.int32(0)
     place = jnp.stack([device, core])
     blocks = query_rows // LANES
+    pairs = att // LANES
     key_span = context * rows + LANES
-
-    def score(blocks, edge_rows):
-        return pl.pallas_call(
-            functools.partial(scores_kernel, context, rows, edge, blocks),
-            out_shape=(
-                jax.ShapeDtypeStruct((len(blocks) * (att // LANES), 2 * LANES, key_span), bf16),
-                jax.ShapeDtypeStruct((heads, len(blocks) * LANES), f32),
-            ),
-            in_specs=[smem, hbm] + [vmem] * (2 + context),
-            out_specs=(vmem,) * 2,
-            scratch_shapes=[
-                pltpu.VMEM((query_rows, att), bf16),
-                pltpu.VMEM((key_rows, att), bf16),
-                pltpu.VMEM((len(blocks) * LANES, LANES), f32),
-                pltpu.VMEM((rows, att), bf16),
-                pltpu.VMEM((LANES, key_span), f32),
-                pltpu.SemaphoreType.DMA,
-            ],
-            compiler_params=params,
-            cost_estimate=cost(5 * 10**9, 10**7),
-            name="scores",
-        )(place, in_hbm(query), own, keys, *further, edge_rows)
-
-    early, early_sums = score(list(range(1, blocks)), near)
-    late, late_sums = score([0], far)
-    log_sums = (late_sums, early_sums)
-    out_frames, attended, dhidden, keep, give, hidden, dmixed = pl.pallas_call(
+    early, early_sums = pl.pallas_call(
+        functools.partial(scores_kernel, context, rows, edge),
+        out_shape=(
+            jax.ShapeDtypeStruct(((blocks - 1) * pairs, 2 * LANES, key_span), bf16),
+            jax.ShapeDtypeStruct((heads, (blocks - 1) * LANES), f32),
+        ),
+        in_specs=[smem] + [vmem] * (3 + context),
+        out_specs=(vmem,) * 2,
+        scratch_shapes=[
+            pltpu.VMEM((query_rows, att), bf16),
+            pltpu.VMEM((key_rows, att), bf16),
+            pltpu.VMEM(((blocks - 1) * LANES, LANES), f32),
+            pltpu.VMEM((LANES, key_span), f32),
+        ],
+        compiler_params=params,
+        cost_estimate=cost(5 * 10**9, 10**7),
+        name="scores",
+    )(place, packed_query, own, keys, *further, near)
+    out_frames, attended, late_sums, dhidden, keep, give, hidden, dmixed = pl.pallas_call(
         functools.partial(forward_kernel, context, rows, edge, taps),
         out_shape=(
             jax.ShapeDtypeStruct((rows, width), bf16),
             jax.ShapeDtypeStruct((rows, att), bf16),
+            jax.ShapeDtypeStruct((heads, LANES), f32),
             jax.ShapeDtypeStruct((rows, width), bf16),
         )
         + (jax.ShapeDtypeStruct((pieces, chunks * 16, LANES), bf16),) * 2
@@ -565,10 +592,14 @@
             jax.ShapeDtypeStruct((chunks, rows + edge + 8, LANES), f32),
         ),
         in_specs=[smem] + [vmem] * (6 + context) + [hbm] * 3,
-        out_specs=(hbm,) * 3 + (vmem,) * 4,
+        out_specs=(hbm, hbm, vmem, hbm) + (vmem,) * 4,
         scratch_shapes=[
+            pltpu.VMEM((LANES, att), bf16),
+            pltpu.VMEM((key_span, att), bf16),
             pltpu.VMEM((key_rows, att), bf16),
             pltpu.VMEM((query_rows, att), bf16),
+            pltpu.VMEM((pairs, 2 * LANES, key_span), bf16),
+            pltpu.VMEM((LANES, key_span), f32),
             pltpu.VMEM((chunks, rows + edge, LANES), f32),
             pltpu.VMEM((2, pieces, chunks * 16, LANES), bf16),
             pltpu.VMEM((att, width), bf16),
@@ -583,7 +614,7 @@
         name="forward",
     )(
         place,
-        late,
+        packed_query,
         early,
         *tiles,
         far,
@@ -638,26 +669,23 @@
         compiler_params=params,
         cost_estimate=cost(6 * 10**9, 10**7),
         name="backward",
-    )(place, in_hbm(query), *tiles, in_hbm(attended), *log_sums, in_hbm(dhidden), in_hbm(out_weight))
+    )(place, in_hbm(query), *tiles, in_hbm(attended), late_sums, early_sums, in_hbm(dhidden), in_hbm(out_weight))
     if split:
-        mine, own_grads, *messages = lax.optimization_barrier(
-            (collected(mine), own_grads, *messages)
-        )
+        mine, *messages = lax.optimization_barrier((collected(mine), *messages))
     messages = dict(enumerate(messages, 1))
     if context > 1:
         swapped = lax.ppermute(messages.pop(1), "y", [(0, 1), (1, 0)])
-        own_grads, messages[2] = pl.pallas_call(
+        messages[2] = pl.pallas_call(
             relay_kernel,
-            out_shape=(
-                jax.ShapeDtypeStruct((2 * rows, att), f32),
-                jax.ShapeDtypeStruct((2 * rows, att), bf16),
-            ),
-            in_specs=[smem] + [vmem] * 3,
-            out_specs=(vmem,) * 2,
+            out_shape=jax.ShapeDtypeStruct((2 * rows, att), bf16),
+            in_specs=[smem] + [vmem] * 2,
+            out_specs=vmem,
             compiler_params=params,
-            cost_estimate=cost(5 * 10**9, 10**7),
+            cost_estimate=cost(25 * 10**9, 10**7),
             name="relay",
-        )(place, own_grads, swapped, messages[2])
+        )(place, swapped, messages[2])
+    else:
+        swapped = jnp.zeros((2 * rows, att), bf16)
     if split:
         mine = summed_along(mine, "z")
         mine, messages = lax.optimization_barrier((mine, messages))
@@ -667,12 +695,12 @@
     key_grad, value_grad = pl.pallas_call(
         merge_kernel,
         out_shape=(jax.ShapeDtypeStruct((rows, att), bf16),) * 2,
-        in_specs=[vmem] * (1 + len(messages)),
+        in_specs=[smem] + [vmem] * (2 + len(messages)),
         out_specs=(vmem,) * 2,
         compiler_params=params,
         cost_estimate=cost(8 * 10**9, 10**7),
         name="merge",
-    )(own_grads, *messages)
+    )(place, *messages, swapped, own_grads)
     if split:
         mine, key_grad, value_grad = lax.optimization_barrier((mine, key_grad, value_grad))
         halves = (mine, other_core(mine))
@@ -699,8 +727,14 @@
             jax.ShapeDtypeStruct((taps, width), f32),
         ),
         in_specs=[smem, vmem, vmem, hbm],
-        out_specs=(hbm, vmem),
-        scratch_shapes=scratch,
+        out_specs=(hbm, hbm),
+        scratch_shapes=[
+            scratch[0],
+            pltpu.VMEM((pieces * 2 * chunks, LANES), f32),
+            pltpu.VMEM((taps, width), f32),
+            scratch[1],
+            scratch[1],
+        ],
         input_output_aliases={3: 0},
         compiler_params=params,
         name="unpack_far",

time: 89.5 us -> 88.7 us (level)
  waiting for transfers between devices: 18.8 us -> 21.4 us
  Pallas kernels: 28.9 us -> 26.6 us
  local copies, waits for them, and re-layouts: 2.63 us -> 0.9 us
  starting transfers between devices: 37.5 us -> 38.4 us
    pallas_call x3 -> x2, Pallas kernels: 5.45 us -> 2.09 us  [the longest x1 1.43 us: per_device(): pl.pallas_call(functools.partial(scores_kernel, context, rows, edge), out...]
    ppermute x1, waiting for transfers between devices: 0.01 us -> 2.22 us  [per_device(): values = lax.ppermute(values, 'y', [(0, 1), (1, 0)])]
    unnamed x8 -> x4, local copies, waits for them, and re-layouts: 1.74 us -> 0.01 us
    ppermute x2, starting transfers between devices: 8.82 us -> 10.1 us  [summed_along(): other = lax.ppermute(x, axis, [(i, i ^ step) for i in range(size)])]
    pallas_call x1, Pallas kernels: 7.21 us -> 8.2 us  [per_device(): pl.pallas_call(functools.partial(forward_kernel, context, rows, edge, tap...]
  transfers between devices with their start and end apart: 13 -> 13, of which waited for: 7 -> 8; matrix products, arithmetic and copies ran while one was open for 1% -> 1% of each run, Pallas kernels for 18% -> 15%
where the time goes in v10:
time: 88.7 us; the launch traced here: 88.3 us
  starting transfers between devices  38.4 us (43%)
  Pallas kernels  26.6 us (30%)
  waiting for transfers between devices  21.4 us (24%)
  local copies, waits for them, and re-layouts  0.9 us (1%)
    ppermute x5, starting transfers between devices, shifted(): lax.ppermute(x, RUN_AXES, [(i, i + by) for i in devices if i + by in devi...  16.5 us
    ppermute x2, starting transfers between devices, summed_along(): other = lax.ppermute(x, axis, [(i, i ^ step) for i in range(size)])  10.1 us
    ppermute x2, waiting for transfers between devices, summed_along(): other = lax.ppermute(x, axis, [(i, i ^ step) for i in range(size)])  8.26 us
    pallas_call x1, Pallas kernels, per_device(): pl.pallas_call(functools.partial(forward_kernel, context, rows, edge, tap...  8.2 us
    all_to_all x2, starting transfers between devices, exchange(): return lax.all_to_all(x, PLANE_AXES, 0, 0, tiled=True)  7.7 us
    ppermute x5, waiting for transfers between devices, shifted(): lax.ppermute(x, RUN_AXES, [(i, i + by) for i in devices if i + by in devi...  7.5 us
    pallas_call x1, Pallas kernels, per_device(): pl.pallas_call(functools.partial(backward_kernel, context, rows), out_sha...  7.4 us
    all_to_all x2, waiting for transfers between devices, exchange(): return lax.all_to_all(x, PLANE_AXES, 0, 0, tiled=True)  3.02 us
  transfers between devices with their start and end apart: 13, of which 8 were waited for; matrix products, arithmetic and copies ran while one was open for 1% of the time, Pallas kernels for 15%

profile of v10, /device:TPU:0, one launch (start us, length us, event | category | flops | bytes accessed | tf_op | source)
XLA Modules:
  0.0 88.3 jit_solution(4668473867391310709)
XLA Ops:
  0.6 1.4 %pack.1 = (bf16[384,512]{1,0:T(8,128)(2,1)S(1)}, bf16[224,512]{1,0:T(8,128)(2,1)S(1)}, bf16[192,512]{1,0:T(8,128)(2,1)S(1)}, bf16[192,512]{1,0:T(8,128)(2,1)S(1)...) custom-call(bf16[192,512]{1,0:T(8,128)(2,1)} %bitcast.17, bf16[192,512]{1,0:T(8,128)(2,1)} %bitcast.18, ...), custom_call_target="tpu_custom_call" | custom-call | tf_op jit(solution)/shard_map/pack/pallas_call | solution.py:520
  2.1 5.0 %collective-permute-start.1 = (bf16[384,512]{1,0:T(8,128)(2,1)S(1)}, bf16[384,512]{1,0:T(8,128)(2,1)S(1)}, u32[]{:S(2)}, u32[]{:S(2)}) collective-permute-start(bf16[384,512]{1,0:T(8,128)(2,1)S(1)} %get-tuple-element.43.refs_0_.refs_3_.refs_2_), channel_id=1, source_target_pairs={{0,2},{1,3},{2,4},{3,5},{4,6},{5,7},{8,10},{9,11},{10,12},{11,13},... | collective-permute-start | bytes 1179656 | tf_op jit(solution)/shard_map/ppermute | solution.py:32
  7.0 3.4 %collective-permute-start = (bf16[224,512]{1,0:T(8,128)(2,1)S(1)}, bf16[224,512]{1,0:T(8,128)(2,1)S(1)}, u32[]{:S(2)}, u32[]{:S(2)}) collective-permute-start(bf16[224,512]{1,0:T(8,128)(2,1)S(1)} %get-tuple-element.44), channel_id=1, source_target_pairs={{0,1},{1,2},{2,3},{3,4},{4,5},{5,6},{6,7},{8,9},{9,10},{10,11},{11... | collective-permute-start | bytes 688136 | tf_op jit(solution)/shard_map/ppermute | solution.py:32
  10.5 1.3 %collective-permute-start.2 = (bf16[160,512]{1,0:T(8,128)(2,1)S(1)}, bf16[160,512]{1,0:T(8,128)(2,1)S(1)}, u32[]{:S(2)}, u32[]{:S(2)}) collective-permute-start(bf16[160,512]{1,0:T(8,128)(2,1)S(1)} %get-tuple-element.45), channel_id=1, source_target_pairs={{1,0},{2,1},{3,2},{4,3},{5,4},{6,5},{7,6},{9,8},{10,9},{11,10},{12... | collective-permute-start | bytes 491528 | tf_op jit(solution)/shard_map/ppermute | solution.py:32
  11.8 5.5 %collective-permute-start.4 = (bf16[64,512]{1,0:T(8,128)(2,1)S(1)}, bf16[64,512]{1,0:T(8,128)(2,1)S(1)}, u32[]{:S(2)}, u32[]{:S(2)}) collective-permute-start(bf16[64,512]{1,0:T(8,128)(2,1)S(1)} %get-tuple-element.50), channel_id=1, source_target_pairs={{0,3},{1,4},{2,5},{3,6},{4,7},{8,11},{9,12},{10,13},{11,14},{12,15... | collective-permute-start | bytes 196616 | tf_op jit(solution)/shard_map/ppermute | solution.py:32
  17.3 0.1 pad_add_fusion.device_ref.refs_0_
  17.4 0.3 collective-permute-done.2.refs_3_.refs_8_
  17.8 0.0 collective-permute-done.1.refs_2_.odd_ref.refs_6_.refs_5_
  17.8 2.6 %collective-permute-start.3 = (bf16[192,512]{1,0:T(8,128)(2,1)S(1)}, bf16[192,512]{1,0:T(8,128)(2,1)S(1)}, u32[]{:S(2)}, u32[]{:S(2)}) collective-permute-start(bf16[192,512]{1,0:T(8,128)(2,1)S(1)} %choose.1), channel_id=1, source_target_pairs={{0,1},{1,0},{2,3},{3,2},{4,5},{5,4},{6,7},{7,6},{8,9},{9,8},{10,11... | collective-permute-start | bytes 589832 | tf_op jit(solution)/shard_map/ppermute | solution.py:549
  20.4 0.0 collective-permute-done.refs_1_.refs_4_.refs_3_
  20.4 1.4 %scores.1 = (bf16[4,256,512]{2,1,0:T(8,128)(2,1)S(1)}, f32[8,128]{1,0:T(8,128)S(1)}) custom-call(s32[2]{0:T(128)S(1)} %pad_add_fusion.device_ref.refs_0_, bf16[192,512]{1,0:T(8,128)(2,1)S(1)} %get-tuple-element.42.q_ref.refs_1_, bf16[384,512]{1,0:T(8,128)(2,1)S(1)} %get-tuple-element.43.refs_0_.refs_3_.refs_2_, ...), custom_call_target="tpu_custom_call" | custom-call | flops 5000000000 | bytes 10000000 | tf_op jit(solution)/shard_map/scores/pallas_call | solution.py:563
  21.8 0.0 collective-permute-done.4.refs_7_
  21.8 2.2 %collective-permute-done.3.refs_5_.refs_4_ = bf16[192,512]{1,0:T(8,128)(2,1)S(1)} collective-permute-done((bf16[192,512]{1,0:T(8,128)(2,1)S(1)}, bf16[192,512]{1,0:T(8,128)(2,1)S(1)}, u32[]{:S(2)}, u32[]{:S(2)}) %collective-permute-start.3) | collective-permute-done | bytes 196640 | tf_op jit(solution)/shard_map/ppermute | solution.py:549
  24.0 8.2 %forward.1 = (bf16[192,1024]{1,0:T(8,128)(2,1)}, bf16[192,512]{1,0:T(8,128)(2,1)S(1)}, f32[8,128]{1,0:T(8,128)S(1)}, bf16[192,1024]{1,0:T(8,128)(2,1)S(1)}, bf16...) custom-call(s32[2]{0:T(128)S(1)} %pad_add_fusion.device_ref.refs_0_,, ...), custom_call_target="tpu_custom_call" | custom-call | flops 8000000000 | bytes 10000000 | tf_op jit(solution)/shard_map/forward/pallas_call | solution.py:581
  32.2 0.0 copy-start
  32.2 0.0 copy-start.1
  32.2 0.1 collective-permute-start.5
  32.3 1.9 %kernel_grad.1.rows_ref = bf16[16,16,128]{2,1,0:T(8,128)(2,1)S(1)} custom-call(f32[8,256,128]{2,1,0:T(8,128)S(1)} %get-tuple-element.57.hid, f32[8,232,128]{2,1,0:T(8,128)S(1)} %get-tuple-element.58.dm), custom_call_target="tpu_custom_call" | custom-call | flops 2000000000 | bytes 3000000 | tf_op jit(solution)/shard_map/kernel_grad/pallas_call | solution.py:626
  34.2 0.0 copy-done
  34.2 0.0 copy-done.1
  34.2 0.0 collective-permute-done.5.given_ref
  34.2 0.9 %join.1 = bf16[16,144,128]{2,1,0:T(8,128)(2,1)} custom-call(bf16[16,128,128]{2,1,0:T(8,128)(2,1)S(1)} %get-tuple-element.55.keep_ref, bf16[16,128,128]{2,1,0:T(8,128)(2,1)S(1)} %collective-permute-done.5.given_ref, bf16[16,16,128]{2,1,0:T(8,128)(2,1)S(1)} %kernel_grad.1.rows_ref), custom_call_target="tpu_custom_call" | custom-call | tf_op jit(solution)/shard_map/join/pallas_call | solution.py:641
  35.2 4.2 %all-to-all-start = ((bf16[4,576,128]{2,1,0:T(8,128)(2,1)}), bf16[4,576,128]{2,1,0:T(8,128)(2,1)S(1)}, u32[]{:S(2)}, u32[]{:S(2)}) async-start(bf16[4,576,128]{2,1,0:T(8,128)(2,1)} %bitcast.8), calls=%async_computation | async-start | bytes 1179648 | tf_op jit(solution)/shard_map/all_to_all | solution.py:479
  39.4 7.4 %backward.1 = (bf16[192,512]{1,0:T(8,128)(2,1)}, f32[384,512]{1,0:T(8,128)S(1)}, bf16[384,512]{1,0:T(8,128)(2,1)S(1)}, bf16[384,512]{1,0:T(8,128)(2,1)S(1)}) custom-call(s32[2]{0:T(128)S(1)} %pad_add_fusion.device_ref.refs_0_, bf16[192,512]{1,0:T(8,128)(2,1)} %bitcast.20, bf16[384,512]{1,0:T(8,128)(2,1)S(1)} %get-tuple-element.43.refs_0_.refs_3_.refs_2_, ...), custom_call_target="tpu_custom_call" | custom-call | flops 6000000000 | bytes 10000000 | tf_op jit(solution)/shard_map/backward/pallas_call | solution.py:650
  46.8 2.0 %all-to-all-done = bf16[4,576,128]{2,1,0:T(8,128)(2,1)S(1)} async-done(((bf16[4,576,128]{2,1,0:T(8,128)(2,1)}), bf16[4,576,128]{2,1,0:T(8,128)(2,1)S(1)}, u32[]{:S(2)}, u32[]{:S(2)}) %all-to-all-start) | async-done | bytes 589856 | tf_op jit(solution)/shard_map/all_to_all | solution.py:479
  48.8 0.1 reduce_sum.12
  48.9 5.9 %collective-permute-start.6 = (bf16[576,128]{1,0:T(8,128)(2,1)S(1)}, bf16[576,128]{1,0:T(8,128)(2,1)S(1)}, u32[]{:S(2)}, u32[]{:S(2)}) collective-permute-start(bf16[576,128]{1,0:T(8,128)(2,1)S(1)} %reduce_sum.12), channel_id=1, source_target_pairs={{0,2},{2,0},{4,6},{6,4},{1,3},{3,1},{5,7},{7,5},{8,10},{10,8},{12,... | collective-permute-start | bytes 442376 | tf_op jit(solution)/shard_map/ppermute | solution.py:490
  54.8 1.5 %collective-permute-start.8 = (bf16[384,512]{1,0:T(8,128)(2,1)S(1)}, bf16[384,512]{1,0:T(8,128)(2,1)S(1)}, u32[]{:S(2)}, u32[]{:S(2)}) collective-permute-start(bf16[384,512]{1,0:T(8,128)(2,1)S(1)} %get-tuple-element.66), channel_id=1, source_target_pairs={{0,1},{1,0},{2,3},{3,2},{4,5},{5,4},{6,7},{7,6},{8,9},{9,8},{10,11... | collective-permute-start | bytes 1179656 | tf_op jit(solution)/shard_map/ppermute | solution.py:677
  56.2 2.3 %collective-permute-done.6 = bf16[576,128]{1,0:T(8,128)(2,1)S(1)} collective-permute-done((bf16[576,128]{1,0:T(8,128)(2,1)S(1)}, bf16[576,128]{1,0:T(8,128)(2,1)S(1)}, u32[]{:S(2)}, u32[]{:S(2)}) %collective-permute-start.6) | collective-permute-done | bytes 147488 | tf_op jit(solution)/shard_map/ppermute | solution.py:490
  58.5 4.2 %collective-permute-start.7 = (bf16[576,128]{1,0:T(8,128)(2,1)S(1)}, bf16[576,128]{1,0:T(8,128)(2,1)S(1)}, u32[]{:S(2)}, u32[]{:S(2)}) collective-permute-start(bf16[576,128]{1,0:T(8,128)(2,1)S(1)} %add_convert_fusion.1), channel_id=1, source_target_pairs={{0,4},{2,6},{4,0},{6,2},{1,5},{3,7},{5,1},{7,3},{8,12},{10,14},{12... | collective-permute-start | bytes 442376 | tf_op jit(solution)/shard_map/ppermute | solution.py:490
  62.8 6.0 %collective-permute-done.7 = bf16[576,128]{1,0:T(8,128)(2,1)S(1)} collective-permute-done((bf16[576,128]{1,0:T(8,128)(2,1)S(1)}, bf16[576,128]{1,0:T(8,128)(2,1)S(1)}, u32[]{:S(2)}, u32[]{:S(2)}) %collective-permute-start.7) | collective-permute-done | bytes 147488 | tf_op jit(solution)/shard_map/ppermute | solution.py:490
  68.8 0.0 collective-permute-done.8.swapped_ref.refs_1_
  68.8 0.7 relay.1
  69.5 1.3 %collective-permute-start.9 = (bf16[384,512]{1,0:T(8,128)(2,1)S(1)}, bf16[384,512]{1,0:T(8,128)(2,1)S(1)}, u32[]{:S(2)}, u32[]{:S(2)}) collective-permute-start(bf16[384,512]{1,0:T(8,128)(2,1)S(1)} %relay.1), channel_id=1, source_target_pairs={{2,0},{3,1},{4,2},{5,3},{6,4},{7,5},{10,8},{11,9},{12,10},{13,11},... | collective-permute-start | bytes 1179656 | tf_op jit(solution)/shard_map/ppermute | solution.py:32
  70.8 0.9 %broadcast_in_dim.18 = bf16[4,576,128]{2,1,0:T(8,128)(2,1)} broadcast(bf16[576,128]{1,0:T(8,128)(2,1)S(1)} %add_convert_fusion), dimensions={1,2} | broadcast | bytes 737280 | tf_op jit(solution)/shard_map/broadcast_in_dim | solution.py:692
  71.7 3.5 %all-to-all-start.1 = ((bf16[4,576,128]{2,1,0:T(8,128)(2,1)}), bf16[4,576,128]{2,1,0:T(8,128)(2,1)S(1)}, u32[]{:S(2)}, u32[]{:S(2)}) async-start(bf16[4,576,128]{2,1,0:T(8,128)(2,1)} %broadcast_in_dim.18), calls=%async_computation.1 | async-start | bytes 1179648 | tf_op jit(solution)/shard_map/all_to_all | solution.py:479
  75.2 7.1 %collective-permute-done.9.refs_0_ = bf16[384,512]{1,0:T(8,128)(2,1)S(1)} collective-permute-done((bf16[384,512]{1,0:T(8,128)(2,1)S(1)}, bf16[384,512]{1,0:T(8,128)(2,1)S(1)}, u32[]{:S(2)}, u32[]{:S(2)}) %collective-permute-start.9) | collective-permute-done | bytes 393248 | tf_op jit(solution)/shard_map/ppermute | solution.py:32
  82.3 1.4 %merge.1 = (bf16[192,512]{1,0:T(8,128)(2,1)}, bf16[192,512]{1,0:T(8,128)(2,1)}) custom-call(s32[2]{0:T(128)S(1)} %pad_add_fusion.device_ref.refs_0_, bf16[384,512]{1,0:T(8,128)(2,1)S(1)} %collective-permute-done.9.refs_0_, bf16[384,512]{1,0:T(8,128)(2,1)S(1)} %collective-permute-done.8.swapped_ref.refs_1_, f32[384,512]{1,0:T(8,128)S(1)} %get-tuple-element.70.refs_2_), custom_call_target="tpu_custom_call" | custom-call | flops 8000000000 | bytes 10000000 | tf_op jit(solution)/shard_map/merge/pallas_call | solution.py:695
  83.7 1.0 %all-to-all-done.1 = bf16[4,576,128]{2,1,0:T(8,128)(2,1)S(1)} async-done(((bf16[4,576,128]{2,1,0:T(8,128)(2,1)}), bf16[4,576,128]{2,1,0:T(8,128)(2,1)S(1)}, u32[]{:S(2)}, u32[]{:S(2)}) %all-to-all-start.1) | async-done | bytes 589856 | tf_op jit(solution)/shard_map/all_to_all | solution.py:479
  84.7 0.0 collective-permute-start.10
  84.7 1.6 %unpack_near.1.partial_hbm = f32[512,1024]{1,0:T(8,128)} custom-call(s32[2]{0:T(128)S(1)} %pad_add_fusion.device_ref.refs_0_, bf16[16,144,128]{2,1,0:T(8,128)(2,1)S(1)} %bitcast.13), custom_call_target="tpu_custom_call" | custom-call | tf_op jit(solution)/shard_map/unpack_near/pallas_call | solution.py:714
  86.3 0.4 collective-permute-done.10.far_ref
  86.7 1.6 %unpack_far.1 = (f32[512,1024]{1,0:T(8,128)}, f32[31,1024]{1,0:T(8,128)}) custom-call(s32[2]{0:T(128)S(1)} %pad_add_fusion.device_ref.refs_0_, bf16[16,144,128]{2,1,0:T(8,128)(2,1)S(1)} %bitcast.14, bf16[16,144,128]{2,1,0:T(8,128)(2,1)S(1)} %collective-permute-done.10.far_ref, f32[512,1024]{1,0:T(8,128)} %unpack_near.1.partial_hbm), custom_call_target="tpu_custom_call", output_to_operand_aliasing={{0}: (3, {})} | custom-call | tf_op jit(solution)/shard_map/unpack_far/pallas_call | solution.py:723
  (3 shorter events, 0.1 us)
Async XLA Ops:
  2.1 15.7 %collective-permute-start.1 = (bf16[384,512]{1,0:T(8,128)(2,1)S(1)}, bf16[384,512]{1,0:T(8,128)(2,1)S(1)}, u32[]{:S(2)}, u32[]{:S(2)}) collective-permute-start(bf16[384,512]{1,0:T(8,128)(2,1)S(1)} %get-tuple-element.43.refs_0_.refs_3_.refs_2_), channel_id=1, source_target_pairs={{0,2},{1,3},{2,4},{3,5},{4,6},{5,7},{8,10},{9,11},{10,12},{11,13},... | collective-permute-start | bytes 1179656 | tf_op jit(solution)/shard_map/ppermute | solution.py:32
  7.0 13.3 %collective-permute-start = (bf16[224,512]{1,0:T(8,128)(2,1)S(1)}, bf16[224,512]{1,0:T(8,128)(2,1)S(1)}, u32[]{:S(2)}, u32[]{:S(2)}) collective-permute-start(bf16[224,512]{1,0:T(8,128)(2,1)S(1)} %get-tuple-element.44), channel_id=1, source_target_pairs={{0,1},{1,2},{2,3},{3,4},{4,5},{5,6},{6,7},{8,9},{9,10},{10,11},{11... | collective-permute-start | bytes 688136 | tf_op jit(solution)/shard_map/ppermute | solution.py:32
  10.5 7.3 %collective-permute-start.2 = (bf16[160,512]{1,0:T(8,128)(2,1)S(1)}, bf16[160,512]{1,0:T(8,128)(2,1)S(1)}, u32[]{:S(2)}, u32[]{:S(2)}) collective-permute-start(bf16[160,512]{1,0:T(8,128)(2,1)S(1)} %get-tuple-element.45), channel_id=1, source_target_pairs={{1,0},{2,1},{3,2},{4,3},{5,4},{6,5},{7,6},{9,8},{10,9},{11,10},{12... | collective-permute-start | bytes 491528 | tf_op jit(solution)/shard_map/ppermute | solution.py:32
  11.8 10.0 %collective-permute-start.4 = (bf16[64,512]{1,0:T(8,128)(2,1)S(1)}, bf16[64,512]{1,0:T(8,128)(2,1)S(1)}, u32[]{:S(2)}, u32[]{:S(2)}) collective-permute-start(bf16[64,512]{1,0:T(8,128)(2,1)S(1)} %get-tuple-element.50), channel_id=1, source_target_pairs={{0,3},{1,4},{2,5},{3,6},{4,7},{8,11},{9,12},{10,13},{11,14},{12,15... | collective-permute-start | bytes 196616 | tf_op jit(solution)/shard_map/ppermute | solution.py:32
  17.8 6.2 %collective-permute-start.3 = (bf16[192,512]{1,0:T(8,128)(2,1)S(1)}, bf16[192,512]{1,0:T(8,128)(2,1)S(1)}, u32[]{:S(2)}, u32[]{:S(2)}) collective-permute-start(bf16[192,512]{1,0:T(8,128)(2,1)S(1)} %choose.1), channel_id=1, source_target_pairs={{0,1},{1,0},{2,3},{3,2},{4,5},{5,4},{6,7},{7,6},{8,9},{9,8},{10,11... | collective-permute-start | bytes 589832 | tf_op jit(solution)/shard_map/ppermute | solution.py:549
  32.2 2.0 %copy-start = (bf16[192,1024]{1,0:T(8,128)(2,1)}, bf16[192,1024]{1,0:T(8,128)(2,1)S(1)}, u32[]{:S(2)}) copy-start(bf16[192,1024]{1,0:T(8,128)(2,1)S(1)} %get-tuple-element.60.refs_9_) | copy-start | bytes 1179652
  32.2 2.0 %copy-start.1 = (bf16[192,512]{1,0:T(8,128)(2,1)}, bf16[192,512]{1,0:T(8,128)(2,1)S(1)}, u32[]{:S(2)}) copy-start(bf16[192,512]{1,0:T(8,128)(2,1)S(1)} %get-tuple-element.52.refs_6_) | copy-start | bytes 589828
  32.2 2.0 %collective-permute-start.5 = (bf16[16,128,128]{2,1,0:T(8,128)(2,1)S(1)}, bf16[16,128,128]{2,1,0:T(8,128)(2,1)S(1)}, u32[]{:S(2)}, u32[]{:S(2)}) collective-permute-start(bf16[16,128,128]{2,1,0:T(8,128)(2,1)S(1)} %get-tuple-element.56), channel_id=1, source_target_pairs={{0,8},{8,0},{1,9},{9,1},{2,10},{10,2},{3,11},{11,3},{4,12},{12,4},... | collective-permute-start | bytes 1572872 | tf_op jit(solution)/shard_map/ppermute | solution.py:497
  35.2 13.6 %all-to-all-start = ((bf16[4,576,128]{2,1,0:T(8,128)(2,1)}), bf16[4,576,128]{2,1,0:T(8,128)(2,1)S(1)}, u32[]{:S(2)}, u32[]{:S(2)}) async-start(bf16[4,576,128]{2,1,0:T(8,128)(2,1)} %bitcast.8), calls=%async_computation | async-start | bytes 1179648 | tf_op jit(solution)/shard_map/all_to_all | solution.py:479
  48.9 9.6 %collective-permute-start.6 = (bf16[576,128]{1,0:T(8,128)(2,1)S(1)}, bf16[576,128]{1,0:T(8,128)(2,1)S(1)}, u32[]{:S(2)}, u32[]{:S(2)}) collective-permute-start(bf16[576,128]{1,0:T(8,128)(2,1)S(1)} %reduce_sum.12), channel_id=1, source_target_pairs={{0,2},{2,0},{4,6},{6,4},{1,3},{3,1},{5,7},{7,5},{8,10},{10,8},{12,... | collective-permute-start | bytes 442376 | tf_op jit(solution)/shard_map/ppermute | solution.py:490
  54.8 14.1 %collective-permute-start.8 = (bf16[384,512]{1,0:T(8,128)(2,1)S(1)}, bf16[384,512]{1,0:T(8,128)(2,1)S(1)}, u32[]{:S(2)}, u32[]{:S(2)}) collective-permute-start(bf16[384,512]{1,0:T(8,128)(2,1)S(1)} %get-tuple-element.66), channel_id=1, source_target_pairs={{0,1},{1,0},{2,3},{3,2},{4,5},{5,4},{6,7},{7,6},{8,9},{9,8},{10,11... | collective-permute-start | bytes 1179656 | tf_op jit(solution)/shard_map/ppermute | solution.py:677
  58.5 10.2 %collective-permute-start.7 = (bf16[576,128]{1,0:T(8,128)(2,1)S(1)}, bf16[576,128]{1,0:T(8,128)(2,1)S(1)}, u32[]{:S(2)}, u32[]{:S(2)}) collective-permute-start(bf16[576,128]{1,0:T(8,128)(2,1)S(1)} %add_convert_fusion.1), channel_id=1, source_target_pairs={{0,4},{2,6},{4,0},{6,2},{1,5},{3,7},{5,1},{7,3},{8,12},{10,14},{12... | collective-permute-start | bytes 442376 | tf_op jit(solution)/shard_map/ppermute | solution.py:490
  69.5 12.8 %collective-permute-start.9 = (bf16[384,512]{1,0:T(8,128)(2,1)S(1)}, bf16[384,512]{1,0:T(8,128)(2,1)S(1)}, u32[]{:S(2)}, u32[]{:S(2)}) collective-permute-start(bf16[384,512]{1,0:T(8,128)(2,1)S(1)} %relay.1), channel_id=1, source_target_pairs={{2,0},{3,1},{4,2},{5,3},{6,4},{7,5},{10,8},{11,9},{12,10},{13,11},... | collective-permute-start | bytes 1179656 | tf_op jit(solution)/shard_map/ppermute | solution.py:32
  71.7 13.0 %all-to-all-start.1 = ((bf16[4,576,128]{2,1,0:T(8,128)(2,1)}), bf16[4,576,128]{2,1,0:T(8,128)(2,1)S(1)}, u32[]{:S(2)}, u32[]{:S(2)}) async-start(bf16[4,576,128]{2,1,0:T(8,128)(2,1)} %broadcast_in_dim.18), calls=%async_computation.1 | async-start | bytes 1179648 | tf_op jit(solution)/shard_map/all_to_all | solution.py:479
  84.7 2.0 %collective-permute-start.10 = (bf16[16,144,128]{2,1,0:T(8,128)(2,1)S(1)}, bf16[16,144,128]{2,1,0:T(8,128)(2,1)S(1)}, u32[]{:S(2)}, u32[]{:S(2)}) collective-permute-start(bf16[16,144,128]{2,1,0:T(8,128)(2,1)S(1)} %bitcast.12), channel_id=1, source_target_pairs={{0,8},{8,0},{1,9},{9,1},{2,10},{10,2},{3,11},{11,3},{4,12},{12,4},... | collective-permute-start | bytes 1769480 | tf_op jit(solution)/shard_map/ppermute | solution.py:497

commit v11 on v10

--- a/solution.py
+++ b/solution.py
@@ -143,34 +143,37 @@
     return log_sums
 
 
-def scores_kernel(context, rows, edge, device_ref, q_ref, *refs):
+def scores_kernel(context, rows, edge, blocks, device_ref, q_ref, *refs):
     own_refs = refs[: 1 + context]
-    near_ref, weights_ref, lse_ref, qx, kx, lx, bias = refs[1 + context :]
+    keys_ref = own_refs[1]
+    edge_ref, weights_ref, lse_ref, qx, kx, lx, bias = refs[1 + context :]
     span = context * rows
     scale = 1.0 / math.sqrt(HEAD_DIM)
     start = device_ref[0] * rows - edge
     for offset, ref in enumerate(own_refs):
         first = edge + (context - offset) * rows
         kx[first : first + rows] = ref[:rows]
-    kx[edge + span + rows :] = near_ref[:edge]
     qx[edge : edge + rows] = q_ref[...] * scale
-    qx[edge + rows :] = near_ref[2 * edge : 3 * edge] * scale
-    for place in range(qx.shape[0] // LANES - 1):
+    if blocks[0] == 0:
+        kx[:edge] = edge_ref[:edge]
+        qx[:edge] = keys_ref[rows : rows + edge] * scale
+    else:
+        kx[edge + span + rows :] = edge_ref[:edge]
+        qx[edge + rows :] = edge_ref[2 * edge : 3 * edge] * scale
+    for place, b in enumerate(blocks):
         lx[place * LANES : (place + 1) * LANES] = score_block(
-            place + 1, place, start, span, qx, kx, bias, weights_ref
+            b, place, start, span, qx, kx, bias, weights_ref
         )
     lse_ref[...] = jnp.transpose(lx[...])[: lse_ref.shape[0]]
 
 
 def forward_kernel(context, rows, edge, taps, *refs):
     tiles = context + 2
-    device_ref, q_ref, early_ref = refs[:3]
-    keys_ref = refs[4]
+    device_ref, late_ref, early_ref = refs[:3]
     places = tile_places(rows, *refs[3 : 3 + tiles])
     far_ref, near_ref, w_hbm, conv_hbm, cot_hbm = refs[3 + tiles : 8 + tiles]
-    out_hbm, att_hbm, lse_ref, dhid_hbm, keep_ref, give_ref, hid, dm = refs[8 + tiles : 16 + tiles]
-    qx, kx, vx, ax, late, bias, cotx, parts = refs[16 + tiles : 24 + tiles]
-    w_ref, conv_ref, cot_ref, out_ref, dhid_ref, sems = refs[24 + tiles :]
+    out_hbm, att_hbm, dhid_hbm, keep_ref, give_ref, hid, dm = refs[8 + tiles : 15 + tiles]
+    vx, ax, cotx, parts, w_ref, conv_ref, cot_ref, out_ref, dhid_ref, sems = refs[15 + tiles :]
 
     att = ax.shape[1]
     width = w_ref.shape[1]
@@ -189,26 +192,18 @@
     for fetch in fetches:
         fetch.start()
 
-    scale = 1.0 / math.sqrt(HEAD_DIM)
-    qx[:edge] = keys_ref[rows : rows + edge] * scale
-    qx[edge:] = q_ref[: block - edge] * scale
-    kx[:edge] = far_ref[:edge]
     vx[:edge] = far_ref[edge:]
-    for offset, (k_ref, k_at, v_ref, v_at) in enumerate(places):
+    for offset, (_, _, ref, at) in enumerate(places):
         first = edge + (context - offset) * rows
-        count = min(rows, keys - first)
-        kx[first : first + count] = k_ref[k_at : k_at + count]
-        vx[first : first + rows] = v_ref[v_at : v_at + rows]
+        vx[first : first + rows] = ref[at : at + rows]
     vx[edge + span + rows :] = near_ref[edge : 2 * edge]
-    log_sums = score_block(0, 0, start - edge, span, qx, kx, bias, late)
-    lse_ref[...] = jnp.transpose(log_sums)[: lse_ref.shape[0]]
 
     pairs = att // LANES
     for b in range(query_rows // block):
         for pair in range(pairs):
             columns = slice(pair * LANES, (pair + 1) * LANES)
             values = vx[b * block : b * block + keys, columns]
-            weights = early_ref[(b - 1) * pairs + pair] if b else late[pair]
+            weights = early_ref[(b - 1) * pairs + pair] if b else late_ref[pair]
             mixed = dot(weights, values, NN)
             ax[b * block : (b + 1) * block, columns] = merge_heads(mixed).astype(jnp.bfloat16)
     stores = [pltpu.make_async_copy(ax.at[pl.ds(edge, rows)], att_hbm, sems.at[3])]
@@ -333,59 +328,58 @@
     mine_ref[:, split:] = rows_ref[...]
 
 
-def write_half(ref, half, scratch, weight_hbm, sem):
-    pieces = ref.shape[0]
-    half_rows, width = scratch.shape
-    group = half_rows // pieces
-    for piece in range(pieces):
-        for chunk in range(width // LANES):
-            tile = ref[piece, chunk * group : (chunk + 1) * group].astype(jnp.float32)
-            scratch[
-                piece * group : (piece + 1) * group, chunk * LANES : (chunk + 1) * LANES
-            ] = tile
-    first = pl.multiple_of(half * half_rows, half_rows)
-    copy = pltpu.make_async_copy(scratch, weight_hbm.at[pl.ds(first, half_rows)], sem)
-    copy.start()
-    return copy
-
-
-def unpack_near_kernel(device_ref, near_ref, weight_hbm, scratch, sem):
-    write_half(near_ref, device_ref[1], scratch, weight_hbm, sem).wait()
-
-
-def unpack_far_kernel(
-    device_ref,
-    near_ref,
-    far_ref,
-    partial_hbm,
-    weight_hbm,
-    kernel_hbm,
-    scratch,
-    blocks,
-    kernel_ref,
-    sem,
-    kernel_sem,
-):
-    copy = write_half(far_ref, 1 - device_ref[1], scratch, weight_hbm, sem)
-    pieces, piece_rows, _ = near_ref.shape
+def write_half(refs, half, me, scratch, weight_hbm, sems):
+    slabs, slab_rows, width = scratch.shape
+    pieces = refs[0].shape[0]
+    group = slab_rows // pieces
+    copies = []
+    for slab, ref in enumerate(refs):
+        for piece in range(pieces):
+            for chunk in range(width // LANES):
+                tile = ref[piece, chunk * group : (chunk + 1) * group].astype(jnp.float32)
+                scratch[
+                    slab, piece * group : (piece + 1) * group, chunk * LANES : (chunk + 1) * LANES
+                ] = tile
+        first = pl.multiple_of((half * slabs + (me ^ slab)) * slab_rows, slab_rows)
+        target = weight_hbm.at[pl.ds(first, slab_rows)]
+        copies.append(pltpu.make_async_copy(scratch.at[slab], target, sems.at[slab]))
+        copies[-1].start()
+    return copies
+
+
+def unpack_near_kernel(device_ref, *refs):
+    *near_refs, weight_hbm, scratch, sems = refs
+    for copy in write_half(near_refs, device_ref[1], device_ref[2], scratch, weight_hbm, sems):
+        copy.wait()
+
+
+def unpack_far_kernel(device_ref, *refs):
+    *refs, _, weight_hbm, kernel_hbm, scratch, blocks, kernel_ref, sems, kernel_sem = refs
+    slabs = len(refs) // 2
+    near_refs, far_refs = refs[:slabs], refs[slabs:]
+    me = device_ref[2]
+    copies = write_half(far_refs, 1 - device_ref[1], me, scratch, weight_hbm, sems)
+    pieces, piece_rows, _ = near_refs[0].shape
     taps, width = kernel_ref.shape
     chunks = width // LANES
     size = 2 * chunks
-    for piece in range(pieces):
-        total = near_ref[piece, piece_rows - size :].astype(jnp.float32)
-        total += far_ref[piece, piece_rows - size :].astype(jnp.float32)
-        blocks[piece * size : (piece + 1) * size] = total
+    for slab in range(slabs):
+        for piece in range(pieces):
+            total = near_refs[slab][piece, piece_rows - size :].astype(jnp.float32)
+            total += far_refs[slab][piece, piece_rows - size :].astype(jnp.float32)
+            first = pl.multiple_of(((me ^ slab) * pieces + piece) * size, size)
+            blocks[pl.ds(first, size)] = total
     for half in range(2):
-        first = half * pieces
-        count = min(pieces, taps - first)
+        first = half * slabs * pieces
+        count = min(slabs * pieces, taps - first)
         for chunk in range(chunks):
             columns = slice(chunk * LANES, (chunk + 1) * LANES)
             tap_rows = blocks[pl.ds(half * chunks + chunk, count, size)]
             kernel_ref[first : first + count, columns] = tap_rows
-    kernel_copy = pltpu.make_async_copy(kernel_ref, kernel_hbm, kernel_sem)
-    kernel_copy.start()
-    copy.wait()
-    kernel_copy.wait()
+    copies.append(pltpu.make_async_copy(kernel_ref, kernel_hbm, kernel_sem))
+    copies[-1].start()
+    for copy in copies:
+        copy.wait()
 
 
 def backward_kernel(context, rows, *refs):
@@ -556,34 +550,40 @@
     layers = lax.axis_size("z")
     split = pieces == layers * lax.axis_size(PLANE_AXES) and layers & (layers - 1) == 0
     core = lax.axis_index("core").astype(jnp.int32) if split else jnp.int32(0)
-    place = jnp.stack([device, core])
+    plane = lax.axis_size(PLANE_AXES)
+    spot = lax.axis_index(PLANE_AXES).astype(jnp.int32) if split else jnp.int32(0)
+    place = jnp.stack([device, core, spot])
     blocks = query_rows // LANES
     pairs = att // LANES
     key_span = context * rows + LANES
-    early, early_sums = pl.pallas_call(
-        functools.partial(scores_kernel, context, rows, edge),
-        out_shape=(
-            jax.ShapeDtypeStruct(((blocks - 1) * pairs, 2 * LANES, key_span), bf16),
-            jax.ShapeDtypeStruct((heads, (blocks - 1) * LANES), f32),
-        ),
-        in_specs=[smem] + [vmem] * (3 + context),
-        out_specs=(vmem,) * 2,
-        scratch_shapes=[
-            pltpu.VMEM((query_rows, att), bf16),
-            pltpu.VMEM((key_rows, att), bf16),
-            pltpu.VMEM(((blocks - 1) * LANES, LANES), f32),
-            pltpu.VMEM((LANES, key_span), f32),
-        ],
-        compiler_params=params,
-        cost_estimate=cost(5 * 10**9, 10**7),
-        name="scores",
-    )(place, packed_query, own, keys, *further, near)
-    out_frames, attended, late_sums, dhidden, keep, give, hidden, dmixed = pl.pallas_call(
+
+    def score(blocks, edge_rows):
+        return pl.pallas_call(
+            functools.partial(scores_kernel, context, rows, edge, blocks),
+            out_shape=(
+                jax.ShapeDtypeStruct((len(blocks) * pairs, 2 * LANES, key_span), bf16),
+                jax.ShapeDtypeStruct((heads, len(blocks) * LANES), f32),
+            ),
+            in_specs=[smem] + [vmem] * (3 + context),
+            out_specs=(vmem,) * 2,
+            scratch_shapes=[
+                pltpu.VMEM((query_rows, att), bf16),
+                pltpu.VMEM((key_rows, att), bf16),
+                pltpu.VMEM((len(blocks) * LANES, LANES), f32),
+                pltpu.VMEM((LANES, key_span), f32),
+            ],
+            compiler_params=params,
+            cost_estimate=cost(5 * 10**9, 10**7),
+            name="scores",
+        )(place, packed_query, own, keys, *further, edge_rows)
+
+    early, early_sums = score(list(range(1, blocks)), near)
+    late, late_sums = score([0], far)
+    out_frames, attended, dhidden, keep, give, hidden, dmixed = pl.pallas_call(
         functools.partial(forward_kernel, context, rows, edge, taps),
         out_shape=(
             jax.ShapeDtypeStruct((rows, width), bf16),
             jax.ShapeDtypeStruct((rows, att), bf16),
-            jax.ShapeDtypeStruct((heads, LANES), f32),
             jax.ShapeDtypeStruct((rows, width), bf16),
         )
         + (jax.ShapeDtypeStruct((pieces, chunks * 16, LANES), bf16),) * 2
@@ -592,14 +592,10 @@
             jax.ShapeDtypeStruct((chunks, rows + edge + 8, LANES), f32),
         ),
         in_specs=[smem] + [vmem] * (6 + context) + [hbm] * 3,
-        out_specs=(hbm, hbm, vmem, hbm) + (vmem,) * 4,
+        out_specs=(hbm,) * 3 + (vmem,) * 4,
         scratch_shapes=[
-            pltpu.VMEM((LANES, att), bf16),
-            pltpu.VMEM((key_span, att), bf16),
             pltpu.VMEM((key_rows, att), bf16),
             pltpu.VMEM((query_rows, att), bf16),
-            pltpu.VMEM((pairs, 2 * LANES, key_span), bf16),
-            pltpu.VMEM((LANES, key_span), f32),
             pltpu.VMEM((chunks, rows + edge, LANES), f32),
             pltpu.VMEM((2, pieces, chunks * 16, LANES), bf16),
             pltpu.VMEM((att, width), bf16),
@@ -614,7 +610,7 @@
         name="forward",
     )(
         place,
-        packed_query,
+        late,
         early,
         *tiles,
         far,
@@ -689,9 +685,13 @@
     if split:
         mine = summed_along(mine, "z")
         mine, messages = lax.optimization_barrier((mine, messages))
-        mine = exchange(jnp.broadcast_to(mine, (lax.axis_size(PLANE_AXES), *mine.shape)))
-        mine = mine.reshape(pieces, -1, LANES)
+        mine = mine.reshape(layers, -1, LANES)
     messages = [shifted(message, -offset) for offset, message in messages.items()]
+    if split:
+        near_slabs = [mine] + [
+            lax.ppermute(mine, PLANE_AXES, [(i, i ^ mask) for i in range(plane)])
+            for mask in range(1, plane)
+        ]
     key_grad, value_grad = pl.pallas_call(
         merge_kernel,
         out_shape=(jax.ShapeDtypeStruct((rows, att), bf16),) * 2,
@@ -702,43 +702,47 @@
         name="merge",
     )(place, *messages, swapped, own_grads)
     if split:
-        mine, key_grad, value_grad = lax.optimization_barrier((mine, key_grad, value_grad))
-        halves = (mine, other_core(mine))
+        near_slabs[-1], key_grad, value_grad = lax.optimization_barrier(
+            (near_slabs[-1], key_grad, value_grad)
+        )
+        far_slabs = [other_core(slab) for slab in near_slabs]
     else:
         totals = lax.psum((keep, give, kernel_rows), ("x", "core", "z", "y"))
-        halves = [
-            jnp.concatenate([totals[0], totals[2]], axis=1),
-            jnp.concatenate([totals[1], jnp.zeros_like(totals[2])], axis=1),
-        ]
-    scratch = [pltpu.VMEM((att // 2, width), f32), pltpu.SemaphoreType.DMA]
+        near_slabs = jnp.concatenate([totals[0], totals[2]], axis=1)
+        far_slabs = jnp.concatenate([totals[1], jnp.zeros_like(totals[2])], axis=1)
+        near_slabs = jnp.split(near_slabs, plane)
+        far_slabs = jnp.split(far_slabs, plane)
+    slab_scratch = pltpu.VMEM((plane, att // 2 // plane, width), f32)
+    slab_sems = pltpu.SemaphoreType.DMA((plane,))
     weight_total = pl.pallas_call(
         unpack_near_kernel,
         out_shape=jax.ShapeDtypeStruct((att, width), f32),
-        in_specs=[smem, vmem],
+        in_specs=[smem] + [vmem] * plane,
         out_specs=hbm,
-        scratch_shapes=scratch,
+        scratch_shapes=[slab_scratch, slab_sems],
         compiler_params=params,
+        cost_estimate=cost(10**9, 3 * 10**6),
         name="unpack_near",
-    )(place, halves[0])
+    )(place, *near_slabs)
     weight_total, kernel_total = pl.pallas_call(
         unpack_far_kernel,
         out_shape=(
             jax.ShapeDtypeStruct((att, width), f32),
             jax.ShapeDtypeStruct((taps, width), f32),
         ),
-        in_specs=[smem, vmem, vmem, hbm],
+        in_specs=[smem] + [vmem] * (2 * plane) + [hbm],
         out_specs=(hbm, hbm),
         scratch_shapes=[
-            scratch[0],
+            slab_scratch,
             pltpu.VMEM((pieces * 2 * chunks, LANES), f32),
             pltpu.VMEM((taps, width), f32),
-            scratch[1],
-            scratch[1],
+            slab_sems,
+            pltpu.SemaphoreType.DMA,
         ],
-        input_output_aliases={3: 0},
+        input_output_aliases={1 + 2 * plane: 0},
         compiler_params=params,
         name="unpack_far",
-    )(place, *halves, weight_total)
+    )(place, *near_slabs, *far_slabs, weight_total)
     return (
         out_frames[None],
         query_grad[None],

time: 88.7 us -> 86.3 us (0.973)
  waiting for transfers between devices: 21.4 us -> 19.1 us
  local copies, waits for them, and re-layouts: 0.9 us -> 0.01 us
    ppermute x0 -> x3, waiting for transfers between devices: none -> 7.06 us  [per_device(): lax.ppermute(mine, PLANE_AXES, [(i, i ^ mask) for i in range(plane)])]
    ppermute x5, waiting for transfers between devices: 7.5 us -> 1.01 us  [shifted(): lax.ppermute(x, RUN_AXES, [(i, i + by) for i in devices if i + by in devi...]
    ppermute x0 -> x3, starting transfers between devices: none -> 3.78 us  [per_device(): lax.ppermute(mine, PLANE_AXES, [(i, i ^ mask) for i in range(plane)])]
    all_to_all x2 -> x1, starting transfers between devices: 7.7 us -> 4.22 us  [exchange(): return lax.all_to_all(x, PLANE_AXES, 0, 0, tiled=True)]
    ppermute x1, waiting for transfers between devices: 2.22 us -> 0.79 us  [per_device(): values = lax.ppermute(values, 'y', [(0, 1), (1, 0)])]
    pallas_call x1 -> x2, Pallas kernels: 1.43 us -> 2.85 us  [score(): pl.pallas_call(functools.partial(scores_kernel, context, rows, edge, bloc...]
    all_to_all x2 -> x1, waiting for transfers between devices: 3.02 us -> 1.98 us  [exchange(): return lax.all_to_all(x, PLANE_AXES, 0, 0, tiled=True)]
    pallas_call x1, Pallas kernels: 8.2 us -> 7.2 us  [per_device(): pl.pallas_call(functools.partial(forward_kernel, context, rows, edge, tap...]
  transfers between devices with their start and end apart: 13 -> 18, of which waited for: 8 -> 8; matrix products, arithmetic and copies ran while one was open for 1% -> 0% of each run, Pallas kernels for 15% -> 18%
where the time goes in v11:
time: 86.3 us; the launch traced here: 85.9 us
  starting transfers between devices  38.7 us (45%)
  Pallas kernels  26.9 us (31%)
  waiting for transfers between devices  19.1 us (22%)
    ppermute x5, starting transfers between devices, shifted(): lax.ppermute(x, RUN_AXES, [(i, i + by) for i in devices if i + by in devi...  16.5 us
    ppermute x2, starting transfers between devices, summed_along(): other = lax.ppermute(x, axis, [(i, i ^ step) for i in range(size)])  10.1 us
    ppermute x2, waiting for transfers between devices, summed_along(): other = lax.ppermute(x, axis, [(i, i ^ step) for i in range(size)])  8.26 us
    pallas_call x1, Pallas kernels, per_device(): pl.pallas_call(functools.partial(backward_kernel, context, rows), out_sha...  7.39 us
    pallas_call x1, Pallas kernels, per_device(): pl.pallas_call(functools.partial(forward_kernel, context, rows, edge, tap...  7.2 us
    ppermute x3, waiting for transfers between devices, per_device(): lax.ppermute(mine, PLANE_AXES, [(i, i ^ mask) for i in range(plane)])  7.06 us
    all_to_all x1, starting transfers between devices, exchange(): return lax.all_to_all(x, PLANE_AXES, 0, 0, tiled=True)  4.22 us
    ppermute x3, starting transfers between devices, per_device(): lax.ppermute(mine, PLANE_AXES, [(i, i ^ mask) for i in range(plane)])  3.78 us
  transfers between devices with their start and end apart: 18, of which 8 were waited for; matrix products, arithmetic and copies ran while one was open for 0% of the time, Pallas kernels for 18%

profile of v11, /device:TPU:0, one launch (start us, length us, event | category | flops | bytes accessed | tf_op | source)
XLA Modules:
  0.0 85.9 jit_solution(3686108736460807899)
XLA Ops:
  0.6 1.4 %pack.1 = (bf16[384,512]{1,0:T(8,128)(2,1)S(1)}, bf16[224,512]{1,0:T(8,128)(2,1)S(1)}, bf16[192,512]{1,0:T(8,128)(2,1)S(1)}, bf16[192,512]{1,0:T(8,128)(2,1)S(1)...) custom-call(bf16[192,512]{1,0:T(8,128)(2,1)} %bitcast.21, bf16[192,512]{1,0:T(8,128)(2,1)} %bitcast.22, ...), custom_call_target="tpu_custom_call" | custom-call | tf_op jit(solution)/shard_map/pack/pallas_call | solution.py:514
  2.1 5.0 %collective-permute-start.1 = (bf16[384,512]{1,0:T(8,128)(2,1)S(1)}, bf16[384,512]{1,0:T(8,128)(2,1)S(1)}, u32[]{:S(2)}, u32[]{:S(2)}) collective-permute-start(bf16[384,512]{1,0:T(8,128)(2,1)S(1)} %get-tuple-element.44.refs_0_.refs_3_.refs_2_), channel_id=1, source_target_pairs={{0,2},{1,3},{2,4},{3,5},{4,6},{5,7},{8,10},{9,11},{10,12},{11,13},... | collective-permute-start | bytes 1179656 | tf_op jit(solution)/shard_map/ppermute | solution.py:32
  7.0 3.4 %collective-permute-start = (bf16[224,512]{1,0:T(8,128)(2,1)S(1)}, bf16[224,512]{1,0:T(8,128)(2,1)S(1)}, u32[]{:S(2)}, u32[]{:S(2)}) collective-permute-start(bf16[224,512]{1,0:T(8,128)(2,1)S(1)} %get-tuple-element.45), channel_id=1, source_target_pairs={{0,1},{1,2},{2,3},{3,4},{4,5},{5,6},{6,7},{8,9},{9,10},{10,11},{11... | collective-permute-start | bytes 688136 | tf_op jit(solution)/shard_map/ppermute | solution.py:32
  10.5 1.3 %collective-permute-start.3 = (bf16[160,512]{1,0:T(8,128)(2,1)S(1)}, bf16[160,512]{1,0:T(8,128)(2,1)S(1)}, u32[]{:S(2)}, u32[]{:S(2)}) collective-permute-start(bf16[160,512]{1,0:T(8,128)(2,1)S(1)} %get-tuple-element.48), channel_id=1, source_target_pairs={{1,0},{2,1},{3,2},{4,3},{5,4},{6,5},{7,6},{9,8},{10,9},{11,10},{12... | collective-permute-start | bytes 491528 | tf_op jit(solution)/shard_map/ppermute | solution.py:32
  11.8 5.5 %collective-permute-start.2 = (bf16[64,512]{1,0:T(8,128)(2,1)S(1)}, bf16[64,512]{1,0:T(8,128)(2,1)S(1)}, u32[]{:S(2)}, u32[]{:S(2)}) collective-permute-start(bf16[64,512]{1,0:T(8,128)(2,1)S(1)} %get-tuple-element.46), channel_id=1, source_target_pairs={{0,3},{1,4},{2,5},{3,6},{4,7},{8,11},{9,12},{10,13},{11,14},{12,15... | collective-permute-start | bytes 196616 | tf_op jit(solution)/shard_map/ppermute | solution.py:32
  17.3 0.1 pad_add_fusion.device_ref.refs_0_
  17.4 0.3 collective-permute-done.3.refs_3_.refs_8_
  17.8 0.0 collective-permute-done.1.refs_2_.odd_ref.refs_6_.refs_5_
  17.8 2.6 %collective-permute-start.4 = (bf16[192,512]{1,0:T(8,128)(2,1)S(1)}, bf16[192,512]{1,0:T(8,128)(2,1)S(1)}, u32[]{:S(2)}, u32[]{:S(2)}) collective-permute-start(bf16[192,512]{1,0:T(8,128)(2,1)S(1)} %choose.1), channel_id=1, source_target_pairs={{0,1},{1,0},{2,3},{3,2},{4,5},{5,4},{6,7},{7,6},{8,9},{9,8},{10,11... | collective-permute-start | bytes 589832 | tf_op jit(solution)/shard_map/ppermute | solution.py:543
  20.4 0.0 collective-permute-done.refs_1_.refs_4_.refs_3_
  20.4 1.4 %scores.3 = (bf16[4,256,512]{2,1,0:T(8,128)(2,1)S(1)}, f32[8,128]{1,0:T(8,128)S(1)}) custom-call(s32[3]{0:T(128)S(1)} %pad_add_fusion.device_ref.refs_0_, bf16[192,512]{1,0:T(8,128)(2,1)S(1)} %get-tuple-element.43.q_ref, bf16[384,512]{1,0:T(8,128)(2,1)S(1)} %get-tuple-element.44.refs_0_.refs_3_.refs_2_, ...), custom_call_target="tpu_custom_call" | custom-call | flops 5000000000 | bytes 10000000 | tf_op jit(solution)/shard_map/scores/pallas_call | solution.py:561
  21.8 0.0 collective-permute-done.2.refs_3_.refs_7_
  21.8 1.4 %scores.2 = (bf16[4,256,512]{2,1,0:T(8,128)(2,1)S(1)}, f32[8,128]{1,0:T(8,128)S(1)}) custom-call(s32[3]{0:T(128)S(1)} %pad_add_fusion.device_ref.refs_0_, bf16[192,512]{1,0:T(8,128)(2,1)S(1)} %get-tuple-element.43.q_ref, bf16[384,512]{1,0:T(8,128)(2,1)S(1)} %get-tuple-element.44.refs_0_.refs_3_.refs_2_, ...), custom_call_target="tpu_custom_call" | custom-call | flops 5000000000 | bytes 10000000 | tf_op jit(solution)/shard_map/scores/pallas_call | solution.py:561
  23.2 0.8 collective-permute-done.4.refs_5_.refs_4_
  24.0 7.2 %forward.1 = (bf16[192,1024]{1,0:T(8,128)(2,1)}, bf16[192,512]{1,0:T(8,128)(2,1)S(1)}, bf16[192,1024]{1,0:T(8,128)(2,1)S(1)}, bf16[16,128,128]{2,1,0:T(8,128)(2,...) custom-call(s32[3]{0:T(128)S(1)} %pad_add_fusion.device_ref.refs_0_, ...), custom_call_target="tpu_custom_call" | custom-call | flops 8000000000 | bytes 10000000 | tf_op jit(solution)/shard_map/forward/pallas_call | solution.py:582
  31.2 0.0 copy-start
  31.2 0.0 copy-start.1
  31.2 0.1 collective-permute-start.5
  31.3 1.9 %kernel_grad.1.rows_ref = bf16[16,16,128]{2,1,0:T(8,128)(2,1)S(1)} custom-call(f32[8,256,128]{2,1,0:T(8,128)S(1)} %get-tuple-element.59.hid, f32[8,232,128]{2,1,0:T(8,128)S(1)} %get-tuple-element.60.dm), custom_call_target="tpu_custom_call" | custom-call | flops 2000000000 | bytes 3000000 | tf_op jit(solution)/shard_map/kernel_grad/pallas_call | solution.py:622
  33.2 0.0 copy-done
  33.2 0.0 copy-done.1
  33.2 0.0 collective-permute-done.5.given_ref
  33.2 0.9 %join.1 = bf16[16,144,128]{2,1,0:T(8,128)(2,1)} custom-call(bf16[16,128,128]{2,1,0:T(8,128)(2,1)S(1)} %get-tuple-element.57.keep_ref, bf16[16,128,128]{2,1,0:T(8,128)(2,1)S(1)} %collective-permute-done.5.given_ref, bf16[16,16,128]{2,1,0:T(8,128)(2,1)S(1)} %kernel_grad.1.rows_ref), custom_call_target="tpu_custom_call" | custom-call | tf_op jit(solution)/shard_map/join/pallas_call | solution.py:637
  34.2 4.2 %all-to-all-start = ((bf16[4,576,128]{2,1,0:T(8,128)(2,1)}), bf16[4,576,128]{2,1,0:T(8,128)(2,1)S(1)}, u32[]{:S(2)}, u32[]{:S(2)}) async-start(bf16[4,576,128]{2,1,0:T(8,128)(2,1)} %bitcast.9), calls=%async_computation | async-start | bytes 1179648 | tf_op jit(solution)/shard_map/all_to_all | solution.py:473
  38.4 7.4 %backward.1 = (bf16[192,512]{1,0:T(8,128)(2,1)}, f32[384,512]{1,0:T(8,128)S(1)}, bf16[384,512]{1,0:T(8,128)(2,1)S(1)}, bf16[384,512]{1,0:T(8,128)(2,1)S(1)}) custom-call(s32[3]{0:T(128)S(1)} %pad_add_fusion.device_ref.refs_0_, bf16[192,512]{1,0:T(8,128)(2,1)} %bitcast.24, bf16[384,512]{1,0:T(8,128)(2,1)S(1)} %get-tuple-element.44.refs_0_.refs_3_.refs_2_, ...), custom_call_target="tpu_custom_call" | custom-call | flops 6000000000 | bytes 10000000 | tf_op jit(solution)/shard_map/backward/pallas_call | solution.py:646
  45.8 2.0 %all-to-all-done = bf16[4,576,128]{2,1,0:T(8,128)(2,1)S(1)} async-done(((bf16[4,576,128]{2,1,0:T(8,128)(2,1)}), bf16[4,576,128]{2,1,0:T(8,128)(2,1)S(1)}, u32[]{:S(2)}, u32[]{:S(2)}) %all-to-all-start) | async-done | bytes 589856 | tf_op jit(solution)/shard_map/all_to_all | solution.py:473
  47.8 0.1 reduce_sum.12
  47.9 5.9 %collective-permute-start.6 = (bf16[576,128]{1,0:T(8,128)(2,1)S(1)}, bf16[576,128]{1,0:T(8,128)(2,1)S(1)}, u32[]{:S(2)}, u32[]{:S(2)}) collective-permute-start(bf16[576,128]{1,0:T(8,128)(2,1)S(1)} %reduce_sum.12), channel_id=1, source_target_pairs={{0,2},{2,0},{4,6},{6,4},{1,3},{3,1},{5,7},{7,5},{8,10},{10,8},{12,... | collective-permute-start | bytes 442376 | tf_op jit(solution)/shard_map/ppermute | solution.py:484
  53.8 1.5 %collective-permute-start.8 = (bf16[384,512]{1,0:T(8,128)(2,1)S(1)}, bf16[384,512]{1,0:T(8,128)(2,1)S(1)}, u32[]{:S(2)}, u32[]{:S(2)}) collective-permute-start(bf16[384,512]{1,0:T(8,128)(2,1)S(1)} %get-tuple-element.68), channel_id=1, source_target_pairs={{0,1},{1,0},{2,3},{3,2},{4,5},{5,4},{6,7},{7,6},{8,9},{9,8},{10,11... | collective-permute-start | bytes 1179656 | tf_op jit(solution)/shard_map/ppermute | solution.py:673
  55.2 2.3 %collective-permute-done.6 = bf16[576,128]{1,0:T(8,128)(2,1)S(1)} collective-permute-done((bf16[576,128]{1,0:T(8,128)(2,1)S(1)}, bf16[576,128]{1,0:T(8,128)(2,1)S(1)}, u32[]{:S(2)}, u32[]{:S(2)}) %collective-permute-start.6) | collective-permute-done | bytes 147488 | tf_op jit(solution)/shard_map/ppermute | solution.py:484
  57.5 4.2 %collective-permute-start.7 = (bf16[576,128]{1,0:T(8,128)(2,1)S(1)}, bf16[576,128]{1,0:T(8,128)(2,1)S(1)}, u32[]{:S(2)}, u32[]{:S(2)}) collective-permute-start(bf16[576,128]{1,0:T(8,128)(2,1)S(1)} %add_convert_fusion.1), channel_id=1, source_target_pairs={{0,4},{2,6},{4,0},{6,2},{1,5},{3,7},{5,1},{7,3},{8,12},{10,14},{12... | collective-permute-start | bytes 442376 | tf_op jit(solution)/shard_map/ppermute | solution.py:484
  61.8 6.0 %collective-permute-done.7 = bf16[576,128]{1,0:T(8,128)(2,1)S(1)} collective-permute-done((bf16[576,128]{1,0:T(8,128)(2,1)S(1)}, bf16[576,128]{1,0:T(8,128)(2,1)S(1)}, u32[]{:S(2)}, u32[]{:S(2)}) %collective-permute-start.7) | collective-permute-done | bytes 147488 | tf_op jit(solution)/shard_map/ppermute | solution.py:484
  67.8 0.0 collective-permute-done.8.swapped_ref.refs_1_
  67.8 0.7 relay.1
  68.5 1.3 %collective-permute-start.10 = (bf16[384,512]{1,0:T(8,128)(2,1)S(1)}, bf16[384,512]{1,0:T(8,128)(2,1)S(1)}, u32[]{:S(2)}, u32[]{:S(2)}) collective-permute-start(bf16[384,512]{1,0:T(8,128)(2,1)S(1)} %relay.1), channel_id=1, source_target_pairs={{2,0},{3,1},{4,2},{5,3},{6,4},{7,5},{10,8},{11,9},{12,10},{13,11},... | collective-permute-start | bytes 1179656 | tf_op jit(solution)/shard_map/ppermute | solution.py:32
  69.8 2.2 %collective-permute-start.12 = (bf16[4,144,128]{2,1,0:T(8,128)(2,1)S(1)}, bf16[4,144,128]{2,1,0:T(8,128)(2,1)S(1)}, u32[]{:S(2)}, u32[]{:S(2)}) collective-permute-start(bf16[4,144,128]{2,1,0:T(8,128)(2,1)S(1)} %bitcast.13), channel_id=1, source_target_pairs={{0,16},{1,17},{16,0},{17,1},{2,18},{3,19},{18,2},{19,3},{4,20},{5,... | collective-permute-start | bytes 442376 | tf_op jit(solution)/shard_map/ppermute | solution.py:692
  72.0 0.0 collective-permute-start.11
  72.0 0.0 collective-permute-start.13
  72.0 1.5 %collective-permute-start.9 = (bf16[4,144,128]{2,1,0:T(8,128)(2,1)S(1)}, bf16[4,144,128]{2,1,0:T(8,128)(2,1)S(1)}, u32[]{:S(2)}, u32[]{:S(2)}) collective-permute-start(bf16[4,144,128]{2,1,0:T(8,128)(2,1)S(1)} %bitcast.16), channel_id=1, source_target_pairs={{0,17},{1,16},{16,1},{17,0},{2,19},{3,18},{18,3},{19,2},{4,21},{5,... | collective-permute-start | bytes 442376 | tf_op jit(solution)/shard_map/ppermute | solution.py:692
  73.6 2.7 %collective-permute-done.12.refs_2_ = bf16[4,144,128]{2,1,0:T(8,128)(2,1)S(1)} collective-permute-done((bf16[4,144,128]{2,1,0:T(8,128)(2,1)S(1)}, bf16[4,144,128]{2,1,0:T(8,128)(2,1)S(1)}, u32[]{:S(2)}, u32[]{:S(2)}) %collective-permute-start.12) | collective-permute-done | bytes 147488 | tf_op jit(solution)/shard_map/ppermute | solution.py:692
  76.3 0.0 collective-permute-start.15
  76.3 4.4 %collective-permute-done.11.refs_1_ = bf16[4,144,128]{2,1,0:T(8,128)(2,1)S(1)} collective-permute-done((bf16[4,144,128]{2,1,0:T(8,128)(2,1)S(1)}, bf16[4,144,128]{2,1,0:T(8,128)(2,1)S(1)}, u32[]{:S(2)}, u32[]{:S(2)}) %collective-permute-start.11) | collective-permute-done | bytes 147488 | tf_op jit(solution)/shard_map/ppermute | solution.py:692
  80.6 0.0 collective-permute-start.14
  80.6 0.7 collective-permute-done.10.refs_0_
  81.3 1.4 %merge.1 = (bf16[192,512]{1,0:T(8,128)(2,1)}, bf16[192,512]{1,0:T(8,128)(2,1)}) custom-call(s32[3]{0:T(128)S(1)} %pad_add_fusion.device_ref.refs_0_, bf16[384,512]{1,0:T(8,128)(2,1)S(1)} %collective-permute-done.10.refs_0_, bf16[384,512]{1,0:T(8,128)(2,1)S(1)} %collective-permute-done.8.swapped_ref.refs_1_, f32[384,512]{1,0:T(8,128)S(1)} %get-tuple-element.72.refs_2_), custom_call_target="tpu_custom_call" | custom-call | flops 8000000000 | bytes 10000000 | tf_op jit(solution)/shard_map/merge/pallas_call | solution.py:695
  82.6 0.0 collective-permute-done.9.refs_3_
  82.6 0.0 collective-permute-start.16
  82.7 1.6 %unpack_near.1.refs_8_ = f32[512,1024]{1,0:T(8,128)} custom-call(s32[3]{0:T(128)S(1)} %pad_add_fusion.device_ref.refs_0_, bf16[4,144,128]{2,1,0:T(8,128)(2,1)S(1)} %bitcast.17, bf16[4,144,128]{2,1,0:T(8,128)(2,1)S(1)} %collective-permute-done.11.refs_1_, bf16[4,144,128]{2,1,0:T(8,128)(2,1)S(1)} %collective-permute-done.12.refs_2_, ...), custom_call_target="tpu_custom_call" | custom-call | flops 1000000000 | bytes 3000000 | tf_op jit(solution)/shard_map/unpack_near/pallas_call | solution.py:717
  84.2 0.0 collective-permute-done.13.refs_4_
  84.2 0.0 collective-permute-done.15.refs_6_
  84.2 0.0 collective-permute-done.14.refs_5_
  84.2 0.0 collective-permute-done.16.refs_7_
  84.3 1.6 %unpack_far.1 = (f32[512,1024]{1,0:T(8,128)}, f32[31,1024]{1,0:T(8,128)}) custom-call(s32[3]{0:T(128)S(1)} %pad_add_fusion.device_ref.refs_0_, bf16[4,144,128]{2,1,0:T(8,128)(2,1)S(1)} %bitcast.18, bf16[4,144,128]{2,1,0:T(8,128)(2,1)S(1)} %collective-permute-done.11.refs_1_, ...), custom_call_target="tpu_custom_call", output_to_operand_aliasing={{0}: (9, {})} | custom-call | tf_op jit(solution)/shard_map/unpack_far/pallas_call | solution.py:727
  (3 shorter events, 0.1 us)
Async XLA Ops:
  2.1 15.7 %collective-permute-start.1 = (bf16[384,512]{1,0:T(8,128)(2,1)S(1)}, bf16[384,512]{1,0:T(8,128)(2,1)S(1)}, u32[]{:S(2)}, u32[]{:S(2)}) collective-permute-start(bf16[384,512]{1,0:T(8,128)(2,1)S(1)} %get-tuple-element.44.refs_0_.refs_3_.refs_2_), channel_id=1, source_target_pairs={{0,2},{1,3},{2,4},{3,5},{4,6},{5,7},{8,10},{9,11},{10,12},{11,13},... | collective-permute-start | bytes 1179656 | tf_op jit(solution)/shard_map/ppermute | solution.py:32
  7.0 13.3 %collective-permute-start = (bf16[224,512]{1,0:T(8,128)(2,1)S(1)}, bf16[224,512]{1,0:T(8,128)(2,1)S(1)}, u32[]{:S(2)}, u32[]{:S(2)}) collective-permute-start(bf16[224,512]{1,0:T(8,128)(2,1)S(1)} %get-tuple-element.45), channel_id=1, source_target_pairs={{0,1},{1,2},{2,3},{3,4},{4,5},{5,6},{6,7},{8,9},{9,10},{10,11},{11... | collective-permute-start | bytes 688136 | tf_op jit(solution)/shard_map/ppermute | solution.py:32
  10.5 7.3 %collective-permute-start.3 = (bf16[160,512]{1,0:T(8,128)(2,1)S(1)}, bf16[160,512]{1,0:T(8,128)(2,1)S(1)}, u32[]{:S(2)}, u32[]{:S(2)}) collective-permute-start(bf16[160,512]{1,0:T(8,128)(2,1)S(1)} %get-tuple-element.48), channel_id=1, source_target_pairs={{1,0},{2,1},{3,2},{4,3},{5,4},{6,5},{7,6},{9,8},{10,9},{11,10},{12... | collective-permute-start | bytes 491528 | tf_op jit(solution)/shard_map/ppermute | solution.py:32
  11.8 10.0 %collective-permute-start.2 = (bf16[64,512]{1,0:T(8,128)(2,1)S(1)}, bf16[64,512]{1,0:T(8,128)(2,1)S(1)}, u32[]{:S(2)}, u32[]{:S(2)}) collective-permute-start(bf16[64,512]{1,0:T(8,128)(2,1)S(1)} %get-tuple-element.46), channel_id=1, source_target_pairs={{0,3},{1,4},{2,5},{3,6},{4,7},{8,11},{9,12},{10,13},{11,14},{12,15... | collective-permute-start | bytes 196616 | tf_op jit(solution)/shard_map/ppermute | solution.py:32
  17.8 6.2 %collective-permute-start.4 = (bf16[192,512]{1,0:T(8,128)(2,1)S(1)}, bf16[192,512]{1,0:T(8,128)(2,1)S(1)}, u32[]{:S(2)}, u32[]{:S(2)}) collective-permute-start(bf16[192,512]{1,0:T(8,128)(2,1)S(1)} %choose.1), channel_id=1, source_target_pairs={{0,1},{1,0},{2,3},{3,2},{4,5},{5,4},{6,7},{7,6},{8,9},{9,8},{10,11... | collective-permute-start | bytes 589832 | tf_op jit(solution)/shard_map/ppermute | solution.py:543
  31.2 2.0 %copy-start = (bf16[192,1024]{1,0:T(8,128)(2,1)}, bf16[192,1024]{1,0:T(8,128)(2,1)S(1)}, u32[]{:S(2)}) copy-start(bf16[192,1024]{1,0:T(8,128)(2,1)S(1)} %get-tuple-element.62.refs_9_) | copy-start | bytes 1179652
  31.2 2.0 %copy-start.1 = (bf16[192,512]{1,0:T(8,128)(2,1)}, bf16[192,512]{1,0:T(8,128)(2,1)S(1)}, u32[]{:S(2)}) copy-start(bf16[192,512]{1,0:T(8,128)(2,1)S(1)} %get-tuple-element.54.refs_6_) | copy-start | bytes 589828
  31.2 2.0 %collective-permute-start.5 = (bf16[16,128,128]{2,1,0:T(8,128)(2,1)S(1)}, bf16[16,128,128]{2,1,0:T(8,128)(2,1)S(1)}, u32[]{:S(2)}, u32[]{:S(2)}) collective-permute-start(bf16[16,128,128]{2,1,0:T(8,128)(2,1)S(1)} %get-tuple-element.58), channel_id=1, source_target_pairs={{0,8},{8,0},{1,9},{9,1},{2,10},{10,2},{3,11},{11,3},{4,12},{12,4},... | collective-permute-start | bytes 1572872 | tf_op jit(solution)/shard_map/ppermute | solution.py:491
  34.2 13.6 %all-to-all-start = ((bf16[4,576,128]{2,1,0:T(8,128)(2,1)}), bf16[4,576,128]{2,1,0:T(8,128)(2,1)S(1)}, u32[]{:S(2)}, u32[]{:S(2)}) async-start(bf16[4,576,128]{2,1,0:T(8,128)(2,1)} %bitcast.9), calls=%async_computation | async-start | bytes 1179648 | tf_op jit(solution)/shard_map/all_to_all | solution.py:473
  47.9 9.6 %collective-permute-start.6 = (bf16[576,128]{1,0:T(8,128)(2,1)S(1)}, bf16[576,128]{1,0:T(8,128)(2,1)S(1)}, u32[]{:S(2)}, u32[]{:S(2)}) collective-permute-start(bf16[576,128]{1,0:T(8,128)(2,1)S(1)} %reduce_sum.12), channel_id=1, source_target_pairs={{0,2},{2,0},{4,6},{6,4},{1,3},{3,1},{5,7},{7,5},{8,10},{10,8},{12,... | collective-permute-start | bytes 442376 | tf_op jit(solution)/shard_map/ppermute | solution.py:484
  53.8 14.0 %collective-permute-start.8 = (bf16[384,512]{1,0:T(8,128)(2,1)S(1)}, bf16[384,512]{1,0:T(8,128)(2,1)S(1)}, u32[]{:S(2)}, u32[]{:S(2)}) collective-permute-start(bf16[384,512]{1,0:T(8,128)(2,1)S(1)} %get-tuple-element.68), channel_id=1, source_target_pairs={{0,1},{1,0},{2,3},{3,2},{4,5},{5,4},{6,7},{7,6},{8,9},{9,8},{10,11... | collective-permute-start | bytes 1179656 | tf_op jit(solution)/shard_map/ppermute | solution.py:673
  57.5 10.2 %collective-permute-start.7 = (bf16[576,128]{1,0:T(8,128)(2,1)S(1)}, bf16[576,128]{1,0:T(8,128)(2,1)S(1)}, u32[]{:S(2)}, u32[]{:S(2)}) collective-permute-start(bf16[576,128]{1,0:T(8,128)(2,1)S(1)} %add_convert_fusion.1), channel_id=1, source_target_pairs={{0,4},{2,6},{4,0},{6,2},{1,5},{3,7},{5,1},{7,3},{8,12},{10,14},{12... | collective-permute-start | bytes 442376 | tf_op jit(solution)/shard_map/ppermute | solution.py:484
  68.5 12.8 %collective-permute-start.10 = (bf16[384,512]{1,0:T(8,128)(2,1)S(1)}, bf16[384,512]{1,0:T(8,128)(2,1)S(1)}, u32[]{:S(2)}, u32[]{:S(2)}) collective-permute-start(bf16[384,512]{1,0:T(8,128)(2,1)S(1)} %relay.1), channel_id=1, source_target_pairs={{2,0},{3,1},{4,2},{5,3},{6,4},{7,5},{10,8},{11,9},{12,10},{13,11},... | collective-permute-start | bytes 1179656 | tf_op jit(solution)/shard_map/ppermute | solution.py:32
  69.8 6.5 %collective-permute-start.12 = (bf16[4,144,128]{2,1,0:T(8,128)(2,1)S(1)}, bf16[4,144,128]{2,1,0:T(8,128)(2,1)S(1)}, u32[]{:S(2)}, u32[]{:S(2)}) collective-permute-start(bf16[4,144,128]{2,1,0:T(8,128)(2,1)S(1)} %bitcast.13), channel_id=1, source_target_pairs={{0,16},{1,17},{16,0},{17,1},{2,18},{3,19},{18,2},{19,3},{4,20},{5,... | collective-permute-start | bytes 442376 | tf_op jit(solution)/shard_map/ppermute | solution.py:692
  72.0 8.6 %collective-permute-start.11 = (bf16[4,144,128]{2,1,0:T(8,128)(2,1)S(1)}, bf16[4,144,128]{2,1,0:T(8,128)(2,1)S(1)}, u32[]{:S(2)}, u32[]{:S(2)}) collective-permute-start(bf16[4,144,128]{2,1,0:T(8,128)(2,1)S(1)} %bitcast.14), channel_id=1, source_target_pairs={{0,1},{1,0},{16,17},{17,16},{2,3},{3,2},{18,19},{19,18},{4,5},{5,4... | collective-permute-start | bytes 442376 | tf_op jit(solution)/shard_map/ppermute | solution.py:692
  72.0 12.2 %collective-permute-start.13 = (bf16[4,144,128]{2,1,0:T(8,128)(2,1)S(1)}, bf16[4,144,128]{2,1,0:T(8,128)(2,1)S(1)}, u32[]{:S(2)}, u32[]{:S(2)}) collective-permute-start(bf16[4,144,128]{2,1,0:T(8,128)(2,1)S(1)} %bitcast.15), channel_id=1, source_target_pairs={{0,8},{8,0},{1,9},{9,1},{2,10},{10,2},{3,11},{11,3},{4,12},{12,4},... | collective-permute-start | bytes 442376 | tf_op jit(solution)/shard_map/ppermute | solution.py:491
  72.0 10.6 %collective-permute-start.9 = (bf16[4,144,128]{2,1,0:T(8,128)(2,1)S(1)}, bf16[4,144,128]{2,1,0:T(8,128)(2,1)S(1)}, u32[]{:S(2)}, u32[]{:S(2)}) collective-permute-start(bf16[4,144,128]{2,1,0:T(8,128)(2,1)S(1)} %bitcast.16), channel_id=1, source_target_pairs={{0,17},{1,16},{16,1},{17,0},{2,19},{3,18},{18,3},{19,2},{4,21},{5,... | collective-permute-start | bytes 442376 | tf_op jit(solution)/shard_map/ppermute | solution.py:692
  76.3 8.0 %collective-permute-start.15 = (bf16[4,144,128]{2,1,0:T(8,128)(2,1)S(1)}, bf16[4,144,128]{2,1,0:T(8,128)(2,1)S(1)}, u32[]{:S(2)}, u32[]{:S(2)}) collective-permute-start(bf16[4,144,128]{2,1,0:T(8,128)(2,1)S(1)} %collective-permute-done.12.refs_2_), channel_id=1, source_target_pairs={{0,8},{8,0},{1,9},{9,1},{2,10},{10,2},{3,11},{11,3},{4,12},{12,4},... | collective-permute-start | bytes 442376 | tf_op jit(solution)/shard_map/ppermute | solution.py:491
  80.6 3.6 %collective-permute-start.14 = (bf16[4,144,128]{2,1,0:T(8,128)(2,1)S(1)}, bf16[4,144,128]{2,1,0:T(8,128)(2,1)S(1)}, u32[]{:S(2)}, u32[]{:S(2)}) collective-permute-start(bf16[4,144,128]{2,1,0:T(8,128)(2,1)S(1)} %collective-permute-done.11.refs_1_), channel_id=1, source_target_pairs={{0,8},{8,0},{1,9},{9,1},{2,10},{10,2},{3,11},{11,3},{4,12},{12,4},... | collective-permute-start | bytes 442376 | tf_op jit(solution)/shard_map/ppermute | solution.py:491
  82.6 1.6 %collective-permute-start.16 = (bf16[4,144,128]{2,1,0:T(8,128)(2,1)S(1)}, bf16[4,144,128]{2,1,0:T(8,128)(2,1)S(1)}, u32[]{:S(2)}, u32[]{:S(2)}) collective-permute-start(bf16[4,144,128]{2,1,0:T(8,128)(2,1)S(1)} %collective-permute-done.9.refs_3_), channel_id=1, source_target_pairs={{0,8},{8,0},{1,9},{9,1},{2,10},{10,2},{3,11},{11,3},{4,12},{12,4},... | collective-permute-start | bytes 442376 | tf_op jit(solution)/shard_map/ppermute | solution.py:491

commit v12 on v11

--- a/solution.py
+++ b/solution.py
@@ -16,6 +16,8 @@
 NEGATIVE = -1e30
 RUN_AXES = ("z", "y")
 PLANE_AXES = ("x", "y")
+EARLY_SLABS = (0, 2)
+LATE_SLABS = (1, 3)
 VMEM_LIMIT = 28 * 1024 * 1024
 
 NN = (((1,), (0,)), ((), ()))
@@ -172,8 +174,8 @@
     device_ref, late_ref, early_ref = refs[:3]
     places = tile_places(rows, *refs[3 : 3 + tiles])
     far_ref, near_ref, w_hbm, conv_hbm, cot_hbm = refs[3 + tiles : 8 + tiles]
-    out_hbm, att_hbm, dhid_hbm, keep_ref, give_ref, hid, dm = refs[8 + tiles : 15 + tiles]
-    vx, ax, cotx, parts, w_ref, conv_ref, cot_ref, out_ref, dhid_ref, sems = refs[15 + tiles :]
+    out_hbm, att_ref, dhid_ref, keep_ref, give_ref, hid, dm, w_ref = refs[8 + tiles : 16 + tiles]
+    vx, ax, cotx, parts, conv_ref, cot_ref, out_ref, sems = refs[16 + tiles :]
 
     att = ax.shape[1]
     width = w_ref.shape[1]
@@ -206,8 +208,7 @@
             weights = early_ref[(b - 1) * pairs + pair] if b else late_ref[pair]
             mixed = dot(weights, values, NN)
             ax[b * block : (b + 1) * block, columns] = merge_heads(mixed).astype(jnp.bfloat16)
-    stores = [pltpu.make_async_copy(ax.at[pl.ds(edge, rows)], att_hbm, sems.at[3])]
-    stores[0].start()
+    att_ref[...] = ax[edge : edge + rows]
 
     fetches[0].wait()
     step = 2 * LANES
@@ -263,10 +264,8 @@
         return carry
 
     lax.fori_loop(0, width // LANES, convolve, 0)
-    stores.append(pltpu.make_async_copy(out_ref, out_hbm, sems.at[4]))
-    stores.append(pltpu.make_async_copy(dhid_ref, dhid_hbm, sems.at[5]))
-    for store in stores[1:]:
-        store.start()
+    store = pltpu.make_async_copy(out_ref, out_hbm, sems.at[3])
+    store.start()
 
     _, pieces, _, _ = parts.shape
     group = att // (2 * pieces)
@@ -284,8 +283,7 @@
                     ]
     keep_ref[...] = parts[core]
     give_ref[...] = parts[1 - core]
-    for store in stores:
-        store.wait()
+    store.wait()
 
 
 def kernel_grad_kernel(rows, edge, taps, hid, dm, rows_ref, ks, kp):
@@ -321,44 +319,55 @@
         rows_ref[piece] = jnp.concatenate(block, axis=0).astype(jnp.bfloat16)
 
 
-def join_kernel(keep_ref, given_ref, rows_ref, mine_ref):
+def join_kernel(device_ref, keep_ref, given_ref, rows_ref, *slab_refs):
     split = keep_ref.shape[1]
-    total = keep_ref[...].astype(jnp.float32) + given_ref[...].astype(jnp.float32)
-    mine_ref[:, :split] = total.astype(jnp.bfloat16)
-    mine_ref[:, split:] = rows_ref[...]
-
-
-def write_half(refs, half, me, scratch, weight_hbm, sems):
-    slabs, slab_rows, width = scratch.shape
-    pieces = refs[0].shape[0]
-    group = slab_rows // pieces
+    pieces = slab_refs[0].shape[0]
+    for slab, ref in enumerate(slab_refs):
+        first = (device_ref[2] ^ slab) * pieces
+        for piece in range(pieces):
+            total = keep_ref[first + piece].astype(jnp.float32)
+            total += given_ref[first + piece].astype(jnp.float32)
+            ref[piece, :split] = total.astype(jnp.bfloat16)
+            ref[piece, split:] = rows_ref[first + piece]
+
+
+def write_slabs(slabs, half, me, scratch, weight_hbm, sems):
+    count, slab_rows, width = scratch.shape
     copies = []
-    for slab, ref in enumerate(refs):
+    for place, (slab, ref) in enumerate(slabs):
+        pieces = ref.shape[0]
+        group = slab_rows // pieces
         for piece in range(pieces):
             for chunk in range(width // LANES):
                 tile = ref[piece, chunk * group : (chunk + 1) * group].astype(jnp.float32)
                 scratch[
-                    slab, piece * group : (piece + 1) * group, chunk * LANES : (chunk + 1) * LANES
+                    place, piece * group : (piece + 1) * group, chunk * LANES : (chunk + 1) * LANES
                 ] = tile
-        first = pl.multiple_of((half * slabs + (me ^ slab)) * slab_rows, slab_rows)
+        plane = EARLY_SLABS + LATE_SLABS
+        first = pl.multiple_of((half * len(plane) + (me ^ slab)) * slab_rows, slab_rows)
         target = weight_hbm.at[pl.ds(first, slab_rows)]
-        copies.append(pltpu.make_async_copy(scratch.at[slab], target, sems.at[slab]))
+        copies.append(pltpu.make_async_copy(scratch.at[place], target, sems.at[place]))
         copies[-1].start()
     return copies
 
 
-def unpack_near_kernel(device_ref, *refs):
+def unpack_early_kernel(device_ref, *refs):
     *near_refs, weight_hbm, scratch, sems = refs
-    for copy in write_half(near_refs, device_ref[1], device_ref[2], scratch, weight_hbm, sems):
+    slabs = list(zip(EARLY_SLABS, near_refs))
+    for copy in write_slabs(slabs, device_ref[1], device_ref[2], scratch, weight_hbm, sems):
         copy.wait()
 
 
-def unpack_far_kernel(device_ref, *refs):
-    *refs, _, weight_hbm, kernel_hbm, scratch, blocks, kernel_ref, sems, kernel_sem = refs
-    slabs = len(refs) // 2
-    near_refs, far_refs = refs[:slabs], refs[slabs:]
-    me = device_ref[2]
-    copies = write_half(far_refs, 1 - device_ref[1], me, scratch, weight_hbm, sems)
+def unpack_late_kernel(device_ref, *refs):
+    slabs = len(EARLY_SLABS) + len(LATE_SLABS)
+    near_refs, far_refs = refs[:slabs], refs[slabs : 2 * slabs]
+    weight_hbm, kernel_hbm, scratch, far_scratch, blocks, kernel_ref = refs[2 * slabs + 1 : -3]
+    sems, far_sems, kernel_sem = refs[-3:]
+    core, me = device_ref[1], device_ref[2]
+    late = [(slab, near_refs[slab]) for slab in LATE_SLABS]
+    copies = write_slabs(late, core, me, scratch, weight_hbm, sems)
+    far = list(enumerate(far_refs))
+    copies += write_slabs(far, 1 - core, me, far_scratch, weight_hbm, far_sems)
     pieces, piece_rows, _ = near_refs[0].shape
     taps, width = kernel_ref.shape
     chunks = width // LANES
@@ -384,12 +393,12 @@
 
 def backward_kernel(context, rows, *refs):
     tiles = context + 2
-    device_ref, q_hbm = refs[:2]
+    device_ref, q_ref = refs[:2]
     places = tile_places(rows, *refs[2 : 2 + tiles])
-    att_hbm, late_ref, early_ref, dhid_hbm, w_hbm = refs[2 + tiles : 7 + tiles]
+    att_ref, late_ref, early_ref, dhid_ref, w_ref = refs[2 + tiles : 7 + tiles]
     dq_ref, own_ref = refs[7 + tiles : 9 + tiles]
     message_refs = refs[9 + tiles : 9 + tiles + context]
-    q_ref, dhid_ref, w_ref, att_ref, datt, bias, lse_ref, sems = refs[9 + tiles + context :]
+    datt, bias, lse_ref = refs[9 + tiles + context :]
 
     att = q_ref.shape[1]
     heads = att // HEAD_DIM
@@ -397,14 +406,6 @@
     scale = 1.0 / math.sqrt(HEAD_DIM)
     start = device_ref[0] * rows
 
-    fetches = [
-        pltpu.make_async_copy(source, target, sems.at[i])
-        for i, (source, target) in enumerate(
-            ((w_hbm, w_ref), (dhid_hbm, dhid_ref), (q_hbm, q_ref), (att_hbm, att_ref))
-        )
-    ]
-    for fetch in fetches:
-        fetch.start()
     edge = (late_ref.shape[1] + early_ref.shape[1] - rows) // 2
     log_sums = jnp.concatenate([late_ref[...], early_ref[...]], axis=1)
     lse_ref[...] = log_sums[:, edge : edge + rows]
@@ -416,8 +417,6 @@
         visible = (distance >= 0) & (distance < span) & (key_time >= 0)
         bias[offset] = jnp.where(visible, 0.0, NEGATIVE)
 
-    for fetch in fetches:
-        fetch.wait()
     dattended = dot(dhid_ref[...], w_ref[...], NT).astype(jnp.bfloat16)
     datt[...] = dattended
     product = dattended.astype(jnp.float32) * att_ref[...].astype(jnp.float32)
@@ -469,13 +468,9 @@
     dv_ref[...] = total[rows:]
 
 
-def exchange(x):
-    return lax.all_to_all(x, PLANE_AXES, 0, 0, tiled=True)
-
-
-def collected(x):
-    x = exchange(x.reshape(lax.axis_size(PLANE_AXES), -1, LANES))
-    return jnp.sum(x.astype(jnp.float32), axis=0).astype(x.dtype)
+def from_peer(x, mask):
+    devices = range(lax.axis_size(PLANE_AXES))
+    return lax.ppermute(x, PLANE_AXES, [(i, i ^ mask) for i in devices])
 
 
 def summed_along(x, axis):
@@ -579,7 +574,7 @@
 
     early, early_sums = score(list(range(1, blocks)), near)
     late, late_sums = score([0], far)
-    out_frames, attended, dhidden, keep, give, hidden, dmixed = pl.pallas_call(
+    out_frames, attended, dhidden, keep, give, hidden, dmixed, held_weight = pl.pallas_call(
         functools.partial(forward_kernel, context, rows, edge, taps),
         out_shape=(
             jax.ShapeDtypeStruct((rows, width), bf16),
@@ -590,20 +585,19 @@
         + (
             jax.ShapeDtypeStruct((chunks, query_rows, LANES), f32),
             jax.ShapeDtypeStruct((chunks, rows + edge + 8, LANES), f32),
+            jax.ShapeDtypeStruct((att, width), bf16),
         ),
         in_specs=[smem] + [vmem] * (6 + context) + [hbm] * 3,
-        out_specs=(hbm,) * 3 + (vmem,) * 4,
+        out_specs=(hbm,) + (vmem,) * 7,
         scratch_shapes=[
             pltpu.VMEM((key_rows, att), bf16),
             pltpu.VMEM((query_rows, att), bf16),
             pltpu.VMEM((chunks, rows + edge, LANES), f32),
             pltpu.VMEM((2, pieces, chunks * 16, LANES), bf16),
-            pltpu.VMEM((att, width), bf16),
             pltpu.VMEM((taps, width), f32),
             pltpu.VMEM((rows, width), bf16),
             pltpu.VMEM((rows, width), bf16),
-            pltpu.VMEM((rows, width), bf16),
-            pltpu.SemaphoreType.DMA((6,)),
+            pltpu.SemaphoreType.DMA((4,)),
         ],
         compiler_params=params,
         cost_estimate=cost(8 * 10**9, 10**7),
@@ -634,15 +628,16 @@
     )(hidden, dmixed)
 
     if split:
-        mine = pl.pallas_call(
+        slabs = pl.pallas_call(
             join_kernel,
-            out_shape=jax.ShapeDtypeStruct((pieces, 18 * chunks, LANES), bf16),
-            in_specs=[vmem] * 3,
-            out_specs=vmem,
+            out_shape=(jax.ShapeDtypeStruct((layers, 18 * chunks, LANES), bf16),) * plane,
+            in_specs=[smem] + [vmem] * 3,
+            out_specs=(vmem,) * plane,
             compiler_params=params,
             name="join",
-        )(keep, other_core(give), kernel_rows)
-        mine, dhidden = lax.optimization_barrier((mine, dhidden))
+        )(place, keep, other_core(give), kernel_rows)
+        *slabs, dhidden = lax.optimization_barrier((*slabs, dhidden))
+        slabs = [slabs[0]] + [from_peer(slabs[mask], mask) for mask in range(1, plane)]
     query_grad, own_grads, *messages = pl.pallas_call(
         functools.partial(backward_kernel, context, rows),
         out_shape=(
@@ -650,24 +645,20 @@
             jax.ShapeDtypeStruct((2 * rows, att), f32),
         )
         + (jax.ShapeDtypeStruct((2 * rows, att), bf16),) * context,
-        in_specs=[smem, hbm] + [vmem] * (2 + context) + [hbm, vmem, vmem, hbm, hbm],
+        in_specs=[smem] + [vmem] * (8 + context),
         out_specs=(vmem,) * (2 + context),
         scratch_shapes=[
             pltpu.VMEM((rows, att), bf16),
-            pltpu.VMEM((rows, width), bf16),
-            pltpu.VMEM((att, width), bf16),
-            pltpu.VMEM((rows, att), bf16),
-            pltpu.VMEM((rows, att), bf16),
             pltpu.VMEM((context + 1, rows, rows), f32),
             pltpu.VMEM((heads, rows), f32),
-            pltpu.SemaphoreType.DMA((4,)),
         ],
         compiler_params=params,
         cost_estimate=cost(6 * 10**9, 10**7),
         name="backward",
-    )(place, in_hbm(query), *tiles, in_hbm(attended), late_sums, early_sums, in_hbm(dhidden), in_hbm(out_weight))
+    )(place, packed_query, *tiles, attended, late_sums, early_sums, dhidden, held_weight)
     if split:
-        mine, *messages = lax.optimization_barrier((collected(mine), *messages))
+        mine = sum(slab.astype(f32) for slab in slabs).astype(bf16)
+        mine, *messages = lax.optimization_barrier((mine, *messages))
     messages = dict(enumerate(messages, 1))
     if context > 1:
         swapped = lax.ppermute(messages.pop(1), "y", [(0, 1), (1, 0)])
@@ -685,13 +676,9 @@
     if split:
         mine = summed_along(mine, "z")
         mine, messages = lax.optimization_barrier((mine, messages))
-        mine = mine.reshape(layers, -1, LANES)
     messages = [shifted(message, -offset) for offset, message in messages.items()]
     if split:
-        near_slabs = [mine] + [
-            lax.ppermute(mine, PLANE_AXES, [(i, i ^ mask) for i in range(plane)])
-            for mask in range(1, plane)
-        ]
+        near_slabs = [mine] + [from_peer(mine, mask) for mask in range(1, plane)]
     key_grad, value_grad = pl.pallas_call(
         merge_kernel,
         out_shape=(jax.ShapeDtypeStruct((rows, att), bf16),) * 2,
@@ -702,30 +689,34 @@
         name="merge",
     )(place, *messages, swapped, own_grads)
     if split:
-        near_slabs[-1], key_grad, value_grad = lax.optimization_barrier(
-            (near_slabs[-1], key_grad, value_grad)
+        far_slabs = [other_core(slab) for slab in near_slabs]
+        far_slabs, key_grad, value_grad = lax.optimization_barrier(
+            (far_slabs, key_grad, value_grad)
         )
-        far_slabs = [other_core(slab) for slab in near_slabs]
     else:
         totals = lax.psum((keep, give, kernel_rows), ("x", "core", "z", "y"))
         near_slabs = jnp.concatenate([totals[0], totals[2]], axis=1)
         far_slabs = jnp.concatenate([totals[1], jnp.zeros_like(totals[2])], axis=1)
         near_slabs = jnp.split(near_slabs, plane)
         far_slabs = jnp.split(far_slabs, plane)
-    slab_scratch = pltpu.VMEM((plane, att // 2 // plane, width), f32)
-    slab_sems = pltpu.SemaphoreType.DMA((plane,))
+    def slab_scratch(count):
+        return pltpu.VMEM((count, att // 2 // plane, width), f32)
+
     weight_total = pl.pallas_call(
-        unpack_near_kernel,
+        unpack_early_kernel,
         out_shape=jax.ShapeDtypeStruct((att, width), f32),
-        in_specs=[smem] + [vmem] * plane,
+        in_specs=[smem] + [vmem] * len(EARLY_SLABS),
         out_specs=hbm,
-        scratch_shapes=[slab_scratch, slab_sems],
+        scratch_shapes=[
+            slab_scratch(len(EARLY_SLABS)),
+            pltpu.SemaphoreType.DMA((len(EARLY_SLABS),)),
+        ],
         compiler_params=params,
         cost_estimate=cost(10**9, 3 * 10**6),
-        name="unpack_near",
-    )(place, *near_slabs)
+        name="unpack_early",
+    )(place, *[near_slabs[slab] for slab in EARLY_SLABS])
     weight_total, kernel_total = pl.pallas_call(
-        unpack_far_kernel,
+        unpack_late_kernel,
         out_shape=(
             jax.ShapeDtypeStruct((att, width), f32),
             jax.ShapeDtypeStruct((taps, width), f32),
@@ -733,15 +724,17 @@
         in_specs=[smem] + [vmem] * (2 * plane) + [hbm],
         out_specs=(hbm, hbm),
         scratch_shapes=[
-            slab_scratch,
+            slab_scratch(len(LATE_SLABS)),
+            slab_scratch(plane),
             pltpu.VMEM((pieces * 2 * chunks, LANES), f32),
             pltpu.VMEM((taps, width), f32),
-            slab_sems,
+            pltpu.SemaphoreType.DMA((len(LATE_SLABS),)),
+            pltpu.SemaphoreType.DMA((plane,)),
             pltpu.SemaphoreType.DMA,
         ],
         input_output_aliases={1 + 2 * plane: 0},
         compiler_params=params,
-        name="unpack_far",
+        name="unpack_late",
     )(place, *near_slabs, *far_slabs, weight_total)
     return (
         out_frames[None],

time: 86.3 us -> 80.7 us (0.935)
  Pallas kernels: 26.9 us -> 24.9 us
  waiting for transfers between devices: 19.1 us -> 17.1 us
  starting transfers between devices: 38.7 us -> 37.4 us
    all_to_all x1 -> x0, starting transfers between devices: 4.22 us -> none  [exchange(): return lax.all_to_all(x, PLANE_AXES, 0, 0, tiled=True)]
    ppermute x3 -> x6, starting transfers between devices: 3.78 us -> 7.18 us  [from_peer(): return lax.ppermute(x, PLANE_AXES, [(i, i ^ mask) for i in devices])]
    all_to_all x1 -> x0, waiting for transfers between devices: 1.98 us -> none  [exchange(): return lax.all_to_all(x, PLANE_AXES, 0, 0, tiled=True)]
    pallas_call x1, Pallas kernels: 7.39 us -> 5.98 us  [per_device(): pl.pallas_call(functools.partial(backward_kernel, context, rows), out_sha...]
    ppermute x1, starting transfers between devices: 1.46 us -> 0.36 us  [per_device(): swapped = lax.ppermute(messages.pop(1), 'y', [(0, 1), (1, 0)])]
    ppermute x3 -> x6, waiting for transfers between devices: 7.06 us -> 7.43 us  [from_peer(): return lax.ppermute(x, PLANE_AXES, [(i, i ^ mask) for i in devices])]
  transfers between devices with their start and end apart: 18 -> 20, of which waited for: 8 -> 7; matrix products, arithmetic and copies ran while one was open for 0% -> 0% of each run, Pallas kernels for 18% -> 17%
where the time goes in v12:
time: 80.7 us; the launch traced here: 80.4 us
  starting transfers between devices  37.4 us (46%)
  Pallas kernels  24.9 us (31%)
  waiting for transfers between devices  17.1 us (21%)
    ppermute x5, starting transfers between devices, shifted(): lax.ppermute(x, RUN_AXES, [(i, i + by) for i in devices if i + by in devi...  16.5 us
    ppermute x2, starting transfers between devices, summed_along(): other = lax.ppermute(x, axis, [(i, i ^ step) for i in range(size)])  10.3 us
    ppermute x2, waiting for transfers between devices, summed_along(): other = lax.ppermute(x, axis, [(i, i ^ step) for i in range(size)])  8.46 us
    ppermute x6, waiting for transfers between devices, from_peer(): return lax.ppermute(x, PLANE_AXES, [(i, i ^ mask) for i in devices])  7.43 us
    ppermute x6, starting transfers between devices, from_peer(): return lax.ppermute(x, PLANE_AXES, [(i, i ^ mask) for i in devices])  7.18 us
    pallas_call x1, Pallas kernels, per_device(): pl.pallas_call(functools.partial(forward_kernel, context, rows, edge, tap...  6.9 us
    pallas_call x1, Pallas kernels, per_device(): pl.pallas_call(functools.partial(backward_kernel, context, rows), out_sha...  5.98 us
    pallas_call x2, Pallas kernels, score(): pl.pallas_call(functools.partial(scores_kernel, context, rows, edge, bloc...  2.85 us
  transfers between devices with their start and end apart: 20, of which 7 were waited for; matrix products, arithmetic and copies ran while one was open for 0% of the time, Pallas kernels for 17%

profile of v12, /device:TPU:0, one launch (start us, length us, event | category | flops | bytes accessed | tf_op | source)
XLA Modules:
  0.0 80.4 jit_solution(226961708520898054)
XLA Ops:
  0.6 1.4 %pack.1 = (bf16[384,512]{1,0:T(8,128)(2,1)S(1)}, bf16[224,512]{1,0:T(8,128)(2,1)S(1)}, bf16[192,512]{1,0:T(8,128)(2,1)S(1)}, bf16[192,512]{1,0:T(8,128)(2,1)S(1)...) custom-call(bf16[192,512]{1,0:T(8,128)(2,1)} %bitcast.13, bf16[192,512]{1,0:T(8,128)(2,1)} %bitcast.14, ...), custom_call_target="tpu_custom_call" | custom-call | tf_op jit(solution)/shard_map/pack/pallas_call | solution.py:509
  2.1 5.0 %collective-permute-start.1 = (bf16[384,512]{1,0:T(8,128)(2,1)S(1)}, bf16[384,512]{1,0:T(8,128)(2,1)S(1)}, u32[]{:S(2)}, u32[]{:S(2)}) collective-permute-start(bf16[384,512]{1,0:T(8,128)(2,1)S(1)} %get-tuple-element.55.refs_0_.refs_3_.refs_2_), channel_id=1, source_target_pairs={{0,2},{1,3},{2,4},{3,5},{4,6},{5,7},{8,10},{9,11},{10,12},{11,13},... | collective-permute-start | bytes 1179656 | tf_op jit(solution)/shard_map/ppermute | solution.py:34
  7.0 3.4 %collective-permute-start = (bf16[224,512]{1,0:T(8,128)(2,1)S(1)}, bf16[224,512]{1,0:T(8,128)(2,1)S(1)}, u32[]{:S(2)}, u32[]{:S(2)}) collective-permute-start(bf16[224,512]{1,0:T(8,128)(2,1)S(1)} %get-tuple-element.56), channel_id=1, source_target_pairs={{0,1},{1,2},{2,3},{3,4},{4,5},{5,6},{6,7},{8,9},{9,10},{10,11},{11... | collective-permute-start | bytes 688136 | tf_op jit(solution)/shard_map/ppermute | solution.py:34
  10.5 1.3 %collective-permute-start.3 = (bf16[160,512]{1,0:T(8,128)(2,1)S(1)}, bf16[160,512]{1,0:T(8,128)(2,1)S(1)}, u32[]{:S(2)}, u32[]{:S(2)}) collective-permute-start(bf16[160,512]{1,0:T(8,128)(2,1)S(1)} %get-tuple-element.59), channel_id=1, source_target_pairs={{1,0},{2,1},{3,2},{4,3},{5,4},{6,5},{7,6},{9,8},{10,9},{11,10},{12... | collective-permute-start | bytes 491528 | tf_op jit(solution)/shard_map/ppermute | solution.py:34
  11.8 5.5 %collective-permute-start.2 = (bf16[64,512]{1,0:T(8,128)(2,1)S(1)}, bf16[64,512]{1,0:T(8,128)(2,1)S(1)}, u32[]{:S(2)}, u32[]{:S(2)}) collective-permute-start(bf16[64,512]{1,0:T(8,128)(2,1)S(1)} %get-tuple-element.57), channel_id=1, source_target_pairs={{0,3},{1,4},{2,5},{3,6},{4,7},{8,11},{9,12},{10,13},{11,14},{12,15... | collective-permute-start | bytes 196616 | tf_op jit(solution)/shard_map/ppermute | solution.py:34
  17.3 0.1 pad_add_fusion.device_ref.refs_0_
  17.4 0.3 collective-permute-done.3.refs_3_.refs_8_
  17.7 0.0 collective-permute-done.1.refs_2_.odd_ref.refs_6_.refs_5_
  17.8 2.6 %collective-permute-start.4 = (bf16[192,512]{1,0:T(8,128)(2,1)S(1)}, bf16[192,512]{1,0:T(8,128)(2,1)S(1)}, u32[]{:S(2)}, u32[]{:S(2)}) collective-permute-start(bf16[192,512]{1,0:T(8,128)(2,1)S(1)} %choose.1), channel_id=1, source_target_pairs={{0,1},{1,0},{2,3},{3,2},{4,5},{5,4},{6,7},{7,6},{8,9},{9,8},{10,11... | collective-permute-start | bytes 589832 | tf_op jit(solution)/shard_map/ppermute | solution.py:538
  20.3 0.0 collective-permute-done.refs_1_.refs_4_.refs_3_
  20.3 1.4 %scores.3 = (bf16[4,256,512]{2,1,0:T(8,128)(2,1)S(1)}, f32[8,128]{1,0:T(8,128)S(1)}) custom-call(s32[3]{0:T(128)S(1)} %pad_add_fusion.device_ref.refs_0_, bf16[192,512]{1,0:T(8,128)(2,1)S(1)} %get-tuple-element.54.q_ref.refs_1_, bf16[384,512]{1,0:T(8,128)(2,1)S(1)} %get-tuple-element.55.refs_0_.refs_3_.refs_2_, ...), custom_call_target="tpu_custom_call" | custom-call | flops 5000000000 | bytes 10000000 | tf_op jit(solution)/shard_map/scores/pallas_call | solution.py:556
  21.8 0.0 collective-permute-done.2.refs_3_.refs_7_
  21.8 1.4 %scores.2 = (bf16[4,256,512]{2,1,0:T(8,128)(2,1)S(1)}, f32[8,128]{1,0:T(8,128)S(1)}) custom-call(s32[3]{0:T(128)S(1)} %pad_add_fusion.device_ref.refs_0_, bf16[192,512]{1,0:T(8,128)(2,1)S(1)} %get-tuple-element.54.q_ref.refs_1_, bf16[384,512]{1,0:T(8,128)(2,1)S(1)} %get-tuple-element.55.refs_0_.refs_3_.refs_2_, ...), custom_call_target="tpu_custom_call" | custom-call | flops 5000000000 | bytes 10000000 | tf_op jit(solution)/shard_map/scores/pallas_call | solution.py:556
  23.2 0.8 collective-permute-done.4.refs_5_.refs_4_
  24.0 6.9 %forward.1 = (bf16[192,1024]{1,0:T(8,128)(2,1)}, bf16[192,512]{1,0:T(8,128)(2,1)S(1)}, bf16[192,1024]{1,0:T(8,128)(2,1)S(1)}, bf16[16,128,128]{2,1,0:T(8,128)(2,...) custom-call(s32[3]{0:T(128)S(1)} %pad_add_fusion.device_ref.refs_0_,, ...), custom_call_target="tpu_custom_call" | custom-call | flops 8000000000 | bytes 10000000 | tf_op jit(solution)/shard_map/forward/pallas_call | solution.py:577
  30.9 0.1 collective-permute-start.5
  31.0 1.9 %kernel_grad.1.rows_ref = bf16[16,16,128]{2,1,0:T(8,128)(2,1)S(1)} custom-call(f32[8,256,128]{2,1,0:T(8,128)S(1)} %get-tuple-element.70.hid, f32[8,232,128]{2,1,0:T(8,128)S(1)} %get-tuple-element.71.dm), custom_call_target="tpu_custom_call" | custom-call | flops 2000000000 | bytes 3000000 | tf_op jit(solution)/shard_map/kernel_grad/pallas_call | solution.py:616
  32.8 0.0 collective-permute-done.5.given_ref
  32.9 0.7 join.1
  33.5 2.1 %collective-permute-start.6 = (bf16[4,144,128]{2,1,0:T(8,128)(2,1)S(1)}, bf16[4,144,128]{2,1,0:T(8,128)(2,1)S(1)}, u32[]{:S(2)}, u32[]{:S(2)}) collective-permute-start(bf16[4,144,128]{2,1,0:T(8,128)(2,1)S(1)} %get-tuple-element.81), channel_id=1, source_target_pairs={{0,1},{1,0},{16,17},{17,16},{2,3},{3,2},{18,19},{19,18},{4,5},{5,4... | collective-permute-start | bytes 442376 | tf_op jit(solution)/shard_map/ppermute | solution.py:473
  35.6 1.5 %collective-permute-start.7 = (bf16[4,144,128]{2,1,0:T(8,128)(2,1)S(1)}, bf16[4,144,128]{2,1,0:T(8,128)(2,1)S(1)}, u32[]{:S(2)}, u32[]{:S(2)}) collective-permute-start(bf16[4,144,128]{2,1,0:T(8,128)(2,1)S(1)} %get-tuple-element.82), channel_id=1, source_target_pairs={{0,16},{1,17},{16,0},{17,1},{2,18},{3,19},{18,2},{19,3},{4,20},{5,... | collective-permute-start | bytes 442376 | tf_op jit(solution)/shard_map/ppermute | solution.py:473
  37.1 0.1 collective-permute-start.8
  37.2 6.0 %backward.1 = (bf16[192,512]{1,0:T(8,128)(2,1)}, f32[384,512]{1,0:T(8,128)S(1)}, bf16[384,512]{1,0:T(8,128)(2,1)S(1)}, bf16[384,512]{1,0:T(8,128)(2,1)S(1)}) custom-call(s32[3]{0:T(128)S(1)} %pad_add_fusion.device_ref.refs_0_, bf16[192,512]{1,0:T(8,128)(2,1)S(1)} %get-tuple-element.54.q_ref.refs_1_, ...), custom_call_target="tpu_custom_call" | custom-call | flops 6000000000 | bytes 10000000 | tf_op jit(solution)/shard_map/backward/pallas_call | solution.py:641
  43.1 0.0 collective-permute-done.6
  43.1 0.0 collective-permute-done.7
  43.1 1.4 %collective-permute-done.8 = bf16[4,144,128]{2,1,0:T(8,128)(2,1)S(1)} collective-permute-done((bf16[4,144,128]{2,1,0:T(8,128)(2,1)S(1)}, bf16[4,144,128]{2,1,0:T(8,128)(2,1)S(1)}, u32[]{:S(2)}, u32[]{:S(2)}) %collective-permute-start.8) | collective-permute-done | bytes 147488 | tf_op jit(solution)/shard_map/ppermute | solution.py:473
  44.5 0.1 add_convert_fusion.2
  44.6 6.0 %collective-permute-start.9 = (bf16[4,144,128]{2,1,0:T(8,128)(2,1)S(1)}, bf16[4,144,128]{2,1,0:T(8,128)(2,1)S(1)}, u32[]{:S(2)}, u32[]{:S(2)}) collective-permute-start(bf16[4,144,128]{2,1,0:T(8,128)(2,1)S(1)} %add_convert_fusion.2), channel_id=1, source_target_pairs={{0,2},{2,0},{4,6},{6,4},{1,3},{3,1},{5,7},{7,5},{8,10},{10,8},{12,... | collective-permute-start | bytes 442376 | tf_op jit(solution)/shard_map/ppermute | solution.py:479
  50.7 0.4 collective-permute-start.11
  51.0 3.1 %collective-permute-done.9 = bf16[4,144,128]{2,1,0:T(8,128)(2,1)S(1)} collective-permute-done((bf16[4,144,128]{2,1,0:T(8,128)(2,1)S(1)}, bf16[4,144,128]{2,1,0:T(8,128)(2,1)S(1)}, u32[]{:S(2)}, u32[]{:S(2)}) %collective-permute-start.9) | collective-permute-done | bytes 147488 | tf_op jit(solution)/shard_map/ppermute | solution.py:479
  54.1 4.2 %collective-permute-start.10 = (bf16[4,144,128]{2,1,0:T(8,128)(2,1)S(1)}, bf16[4,144,128]{2,1,0:T(8,128)(2,1)S(1)}, u32[]{:S(2)}, u32[]{:S(2)}) collective-permute-start(bf16[4,144,128]{2,1,0:T(8,128)(2,1)S(1)} %add_convert_fusion.1), channel_id=1, source_target_pairs={{0,4},{2,6},{4,0},{6,2},{1,5},{3,7},{5,1},{7,3},{8,12},{10,14},{12... | collective-permute-start | bytes 442376 | tf_op jit(solution)/shard_map/ppermute | solution.py:479
  58.3 5.4 %collective-permute-done.10 = bf16[4,144,128]{2,1,0:T(8,128)(2,1)S(1)} collective-permute-done((bf16[4,144,128]{2,1,0:T(8,128)(2,1)S(1)}, bf16[4,144,128]{2,1,0:T(8,128)(2,1)S(1)}, u32[]{:S(2)}, u32[]{:S(2)}) %collective-permute-start.10) | collective-permute-done | bytes 147488 | tf_op jit(solution)/shard_map/ppermute | solution.py:479
  63.8 0.0 collective-permute-done.11.swapped_ref.refs_1_
  63.8 0.7 relay.1
  64.5 1.3 %collective-permute-start.19 = (bf16[384,512]{1,0:T(8,128)(2,1)S(1)}, bf16[384,512]{1,0:T(8,128)(2,1)S(1)}, u32[]{:S(2)}, u32[]{:S(2)}) collective-permute-start(bf16[384,512]{1,0:T(8,128)(2,1)S(1)} %relay.1), channel_id=1, source_target_pairs={{2,0},{3,1},{4,2},{5,3},{6,4},{7,5},{10,8},{11,9},{12,10},{13,11},... | collective-permute-start | bytes 1179656 | tf_op jit(solution)/shard_map/ppermute | solution.py:34
  65.8 2.3 %collective-permute-start.17 = (bf16[4,144,128]{2,1,0:T(8,128)(2,1)S(1)}, bf16[4,144,128]{2,1,0:T(8,128)(2,1)S(1)}, u32[]{:S(2)}, u32[]{:S(2)}) collective-permute-start(bf16[4,144,128]{2,1,0:T(8,128)(2,1)S(1)} %add_convert_fusion.refs_0_), channel_id=1, source_target_pairs={{0,17},{1,16},{16,1},{17,0},{2,19},{3,18},{18,3},{19,2},{4,21},{5,... | collective-permute-start | bytes 442376 | tf_op jit(solution)/shard_map/ppermute | solution.py:473
  68.0 0.5 collective-permute-start.15
  68.6 0.8 collective-permute-start.13
  69.3 0.0 collective-permute-start.12
  69.3 4.3 %collective-permute-done.17.refs_3_ = bf16[4,144,128]{2,1,0:T(8,128)(2,1)S(1)} collective-permute-done((bf16[4,144,128]{2,1,0:T(8,128)(2,1)S(1)}, bf16[4,144,128]{2,1,0:T(8,128)(2,1)S(1)}, u32[]{:S(2)}, u32[]{:S(2)}) %collective-permute-start.17) | collective-permute-done | bytes 147488 | tf_op jit(solution)/shard_map/ppermute | solution.py:473
  73.6 0.0 collective-permute-start.18
  73.6 1.7 %collective-permute-done.15.refs_1_.refs_2_ = bf16[4,144,128]{2,1,0:T(8,128)(2,1)S(1)} collective-permute-done((bf16[4,144,128]{2,1,0:T(8,128)(2,1)S(1)}, bf16[4,144,128]{2,1,0:T(8,128)(2,1)S(1)}, u32[]{:S(2)}, u32[]{:S(2)}) %collective-permute-start.15) | collective-permute-done | bytes 147488 | tf_op jit(solution)/shard_map/ppermute | solution.py:473
  75.4 0.0 collective-permute-start.16
  75.4 0.0 collective-permute-done.13.refs_1_
  75.4 0.5 collective-permute-start.14
  75.9 1.4 %unpack_early.1.refs_8_ = f32[512,1024]{1,0:T(8,128)} custom-call(s32[3]{0:T(128)S(1)} %pad_add_fusion.device_ref.refs_0_, bf16[4,144,128]{2,1,0:T(8,128)(2,1)S(1)} %add_convert_fusion.refs_0_, bf16[4,144,128]{2,1,0:T(8,128)(2,1)S(1)} %collective-permute-done.15.refs_1_.refs_2_), custom_call_target="tpu_custom_call" | custom-call | flops 1000000000 | bytes 3000000 | tf_op jit(solution)/shard_map/unpack_early/pallas_call | solution.py:705
  77.3 0.0 collective-permute-done.19.refs_0_
  77.3 1.4 %merge.1 = (bf16[192,512]{1,0:T(8,128)(2,1)}, bf16[192,512]{1,0:T(8,128)(2,1)}) custom-call(s32[3]{0:T(128)S(1)} %pad_add_fusion.device_ref.refs_0_, bf16[384,512]{1,0:T(8,128)(2,1)S(1)} %collective-permute-done.19.refs_0_, bf16[384,512]{1,0:T(8,128)(2,1)S(1)} %collective-permute-done.11.swapped_ref.refs_1_, f32[384,512]{1,0:T(8,128)S(1)} %get-tuple-element.91.refs_2_), custom_call_target="tpu_custom_call" | custom-call | flops 8000000000 | bytes 10000000 | tf_op jit(solution)/shard_map/merge/pallas_call | solution.py:682
  78.6 0.0 collective-permute-done.12.refs_4_
  78.6 0.0 collective-permute-done.18.refs_7_
  78.6 0.0 collective-permute-done.16.refs_6_
  78.6 0.0 collective-permute-done.14.refs_5_
  78.7 1.8 %unpack_late.1 = (f32[512,1024]{1,0:T(8,128)}, f32[31,1024]{1,0:T(8,128)}) custom-call(s32[3]{0:T(128)S(1)} %pad_add_fusion.device_ref.refs_0_, bf16[4,144,128]{2,1,0:T(8,128)(2,1)S(1)} %add_convert_fusion.refs_0_, bf16[4,144,128]{2,1,0:T(8,128)(2,1)S(1)} %collective-permute-done.13.refs_1_, ...), custom_call_target="tpu_custom_call", output_to_operand_aliasing={{0}: (9, {})} | custom-call | tf_op jit(solution)/shard_map/unpack_late/pallas_call | solution.py:718
  (3 shorter events, 0.1 us)
Async XLA Ops:
  2.1 15.7 %collective-permute-start.1 = (bf16[384,512]{1,0:T(8,128)(2,1)S(1)}, bf16[384,512]{1,0:T(8,128)(2,1)S(1)}, u32[]{:S(2)}, u32[]{:S(2)}) collective-permute-start(bf16[384,512]{1,0:T(8,128)(2,1)S(1)} %get-tuple-element.55.refs_0_.refs_3_.refs_2_), channel_id=1, source_target_pairs={{0,2},{1,3},{2,4},{3,5},{4,6},{5,7},{8,10},{9,11},{10,12},{11,13},... | collective-permute-start | bytes 1179656 | tf_op jit(solution)/shard_map/ppermute | solution.py:34
  7.0 13.3 %collective-permute-start = (bf16[224,512]{1,0:T(8,128)(2,1)S(1)}, bf16[224,512]{1,0:T(8,128)(2,1)S(1)}, u32[]{:S(2)}, u32[]{:S(2)}) collective-permute-start(bf16[224,512]{1,0:T(8,128)(2,1)S(1)} %get-tuple-element.56), channel_id=1, source_target_pairs={{0,1},{1,2},{2,3},{3,4},{4,5},{5,6},{6,7},{8,9},{9,10},{10,11},{11... | collective-permute-start | bytes 688136 | tf_op jit(solution)/shard_map/ppermute | solution.py:34
  10.5 7.3 %collective-permute-start.3 = (bf16[160,512]{1,0:T(8,128)(2,1)S(1)}, bf16[160,512]{1,0:T(8,128)(2,1)S(1)}, u32[]{:S(2)}, u32[]{:S(2)}) collective-permute-start(bf16[160,512]{1,0:T(8,128)(2,1)S(1)} %get-tuple-element.59), channel_id=1, source_target_pairs={{1,0},{2,1},{3,2},{4,3},{5,4},{6,5},{7,6},{9,8},{10,9},{11,10},{12... | collective-permute-start | bytes 491528 | tf_op jit(solution)/shard_map/ppermute | solution.py:34
  11.8 10.0 %collective-permute-start.2 = (bf16[64,512]{1,0:T(8,128)(2,1)S(1)}, bf16[64,512]{1,0:T(8,128)(2,1)S(1)}, u32[]{:S(2)}, u32[]{:S(2)}) collective-permute-start(bf16[64,512]{1,0:T(8,128)(2,1)S(1)} %get-tuple-element.57), channel_id=1, source_target_pairs={{0,3},{1,4},{2,5},{3,6},{4,7},{8,11},{9,12},{10,13},{11,14},{12,15... | collective-permute-start | bytes 196616 | tf_op jit(solution)/shard_map/ppermute | solution.py:34
  17.8 6.2 %collective-permute-start.4 = (bf16[192,512]{1,0:T(8,128)(2,1)S(1)}, bf16[192,512]{1,0:T(8,128)(2,1)S(1)}, u32[]{:S(2)}, u32[]{:S(2)}) collective-permute-start(bf16[192,512]{1,0:T(8,128)(2,1)S(1)} %choose.1), channel_id=1, source_target_pairs={{0,1},{1,0},{2,3},{3,2},{4,5},{5,4},{6,7},{7,6},{8,9},{9,8},{10,11... | collective-permute-start | bytes 589832 | tf_op jit(solution)/shard_map/ppermute | solution.py:538
  30.9 2.0 %collective-permute-start.5 = (bf16[16,128,128]{2,1,0:T(8,128)(2,1)S(1)}, bf16[16,128,128]{2,1,0:T(8,128)(2,1)S(1)}, u32[]{:S(2)}, u32[]{:S(2)}) collective-permute-start(bf16[16,128,128]{2,1,0:T(8,128)(2,1)S(1)} %get-tuple-element.69), channel_id=1, source_target_pairs={{0,8},{8,0},{1,9},{9,1},{2,10},{10,2},{3,11},{11,3},{4,12},{12,4},... | collective-permute-start | bytes 1572872 | tf_op jit(solution)/shard_map/ppermute | solution.py:486
  33.5 9.6 %collective-permute-start.6 = (bf16[4,144,128]{2,1,0:T(8,128)(2,1)S(1)}, bf16[4,144,128]{2,1,0:T(8,128)(2,1)S(1)}, u32[]{:S(2)}, u32[]{:S(2)}) collective-permute-start(bf16[4,144,128]{2,1,0:T(8,128)(2,1)S(1)} %get-tuple-element.81), channel_id=1, source_target_pairs={{0,1},{1,0},{16,17},{17,16},{2,3},{3,2},{18,19},{19,18},{4,5},{5,4... | collective-permute-start | bytes 442376 | tf_op jit(solution)/shard_map/ppermute | solution.py:473
  35.6 7.5 %collective-permute-start.7 = (bf16[4,144,128]{2,1,0:T(8,128)(2,1)S(1)}, bf16[4,144,128]{2,1,0:T(8,128)(2,1)S(1)}, u32[]{:S(2)}, u32[]{:S(2)}) collective-permute-start(bf16[4,144,128]{2,1,0:T(8,128)(2,1)S(1)} %get-tuple-element.82), channel_id=1, source_target_pairs={{0,16},{1,17},{16,0},{17,1},{2,18},{3,19},{18,2},{19,3},{4,20},{5,... | collective-permute-start | bytes 442376 | tf_op jit(solution)/shard_map/ppermute | solution.py:473
  37.1 7.4 %collective-permute-start.8 = (bf16[4,144,128]{2,1,0:T(8,128)(2,1)S(1)}, bf16[4,144,128]{2,1,0:T(8,128)(2,1)S(1)}, u32[]{:S(2)}, u32[]{:S(2)}) collective-permute-start(bf16[4,144,128]{2,1,0:T(8,128)(2,1)S(1)} %get-tuple-element.83), channel_id=1, source_target_pairs={{0,17},{1,16},{16,1},{17,0},{2,19},{3,18},{18,3},{19,2},{4,21},{5,... | collective-permute-start | bytes 442376 | tf_op jit(solution)/shard_map/ppermute | solution.py:473
  44.6 9.4 %collective-permute-start.9 = (bf16[4,144,128]{2,1,0:T(8,128)(2,1)S(1)}, bf16[4,144,128]{2,1,0:T(8,128)(2,1)S(1)}, u32[]{:S(2)}, u32[]{:S(2)}) collective-permute-start(bf16[4,144,128]{2,1,0:T(8,128)(2,1)S(1)} %add_convert_fusion.2), channel_id=1, source_target_pairs={{0,2},{2,0},{4,6},{6,4},{1,3},{3,1},{5,7},{7,5},{8,10},{10,8},{12,... | collective-permute-start | bytes 442376 | tf_op jit(solution)/shard_map/ppermute | solution.py:479
  50.7 13.1 %collective-permute-start.11 = (bf16[384,512]{1,0:T(8,128)(2,1)S(1)}, bf16[384,512]{1,0:T(8,128)(2,1)S(1)}, u32[]{:S(2)}, u32[]{:S(2)}) collective-permute-start(bf16[384,512]{1,0:T(8,128)(2,1)S(1)} %get-tuple-element.87), channel_id=1, source_target_pairs={{0,1},{1,0},{2,3},{3,2},{4,5},{5,4},{6,7},{7,6},{8,9},{9,8},{10,11... | collective-permute-start | bytes 1179656 | tf_op jit(solution)/shard_map/ppermute | solution.py:664
  54.1 9.6 %collective-permute-start.10 = (bf16[4,144,128]{2,1,0:T(8,128)(2,1)S(1)}, bf16[4,144,128]{2,1,0:T(8,128)(2,1)S(1)}, u32[]{:S(2)}, u32[]{:S(2)}) collective-permute-start(bf16[4,144,128]{2,1,0:T(8,128)(2,1)S(1)} %add_convert_fusion.1), channel_id=1, source_target_pairs={{0,4},{2,6},{4,0},{6,2},{1,5},{3,7},{5,1},{7,3},{8,12},{10,14},{12... | collective-permute-start | bytes 442376 | tf_op jit(solution)/shard_map/ppermute | solution.py:479
  64.5 12.8 %collective-permute-start.19 = (bf16[384,512]{1,0:T(8,128)(2,1)S(1)}, bf16[384,512]{1,0:T(8,128)(2,1)S(1)}, u32[]{:S(2)}, u32[]{:S(2)}) collective-permute-start(bf16[384,512]{1,0:T(8,128)(2,1)S(1)} %relay.1), channel_id=1, source_target_pairs={{2,0},{3,1},{4,2},{5,3},{6,4},{7,5},{10,8},{11,9},{12,10},{13,11},... | collective-permute-start | bytes 1179656 | tf_op jit(solution)/shard_map/ppermute | solution.py:34
  65.8 7.8 %collective-permute-start.17 = (bf16[4,144,128]{2,1,0:T(8,128)(2,1)S(1)}, bf16[4,144,128]{2,1,0:T(8,128)(2,1)S(1)}, u32[]{:S(2)}, u32[]{:S(2)}) collective-permute-start(bf16[4,144,128]{2,1,0:T(8,128)(2,1)S(1)} %add_convert_fusion.refs_0_), channel_id=1, source_target_pairs={{0,17},{1,16},{16,1},{17,0},{2,19},{3,18},{18,3},{19,2},{4,21},{5,... | collective-permute-start | bytes 442376 | tf_op jit(solution)/shard_map/ppermute | solution.py:473
  68.0 7.3 %collective-permute-start.15 = (bf16[4,144,128]{2,1,0:T(8,128)(2,1)S(1)}, bf16[4,144,128]{2,1,0:T(8,128)(2,1)S(1)}, u32[]{:S(2)}, u32[]{:S(2)}) collective-permute-start(bf16[4,144,128]{2,1,0:T(8,128)(2,1)S(1)} %add_convert_fusion.refs_0_), channel_id=1, source_target_pairs={{0,16},{1,17},{16,0},{17,1},{2,18},{3,19},{18,2},{19,3},{4,20},{5,... | collective-permute-start | bytes 442376 | tf_op jit(solution)/shard_map/ppermute | solution.py:473
  68.6 6.8 %collective-permute-start.13 = (bf16[4,144,128]{2,1,0:T(8,128)(2,1)S(1)}, bf16[4,144,128]{2,1,0:T(8,128)(2,1)S(1)}, u32[]{:S(2)}, u32[]{:S(2)}) collective-permute-start(bf16[4,144,128]{2,1,0:T(8,128)(2,1)S(1)} %add_convert_fusion.refs_0_), channel_id=1, source_target_pairs={{0,1},{1,0},{16,17},{17,16},{2,3},{3,2},{18,19},{19,18},{4,5},{5,4... | collective-permute-start | bytes 442376 | tf_op jit(solution)/shard_map/ppermute | solution.py:473
  69.3 9.3 %collective-permute-start.12 = (bf16[4,144,128]{2,1,0:T(8,128)(2,1)S(1)}, bf16[4,144,128]{2,1,0:T(8,128)(2,1)S(1)}, u32[]{:S(2)}, u32[]{:S(2)}) collective-permute-start(bf16[4,144,128]{2,1,0:T(8,128)(2,1)S(1)} %add_convert_fusion.refs_0_), channel_id=1, source_target_pairs={{0,8},{8,0},{1,9},{9,1},{2,10},{10,2},{3,11},{11,3},{4,12},{12,4},... | collective-permute-start | bytes 442376 | tf_op jit(solution)/shard_map/ppermute | solution.py:486
  73.6 5.0 %collective-permute-start.18 = (bf16[4,144,128]{2,1,0:T(8,128)(2,1)S(1)}, bf16[4,144,128]{2,1,0:T(8,128)(2,1)S(1)}, u32[]{:S(2)}, u32[]{:S(2)}) collective-permute-start(bf16[4,144,128]{2,1,0:T(8,128)(2,1)S(1)} %collective-permute-done.17.refs_3_), channel_id=1, source_target_pairs={{0,8},{8,0},{1,9},{9,1},{2,10},{10,2},{3,11},{11,3},{4,12},{12,4},... | collective-permute-start | bytes 442376 | tf_op jit(solution)/shard_map/ppermute | solution.py:486
  75.4 3.3 %collective-permute-start.16 = (bf16[4,144,128]{2,1,0:T(8,128)(2,1)S(1)}, bf16[4,144,128]{2,1,0:T(8,128)(2,1)S(1)}, u32[]{:S(2)}, u32[]{:S(2)}) collective-permute-start(bf16[4,144,128]{2,1,0:T(8,128)(2,1)S(1)} %collective-permute-done.15.refs_1_.refs_2_), channel_id=1, source_target_pairs={{0,8},{8,0},{1,9},{9,1},{2,10},{10,2},{3,11},{11,3},{4,12},{12,4},... | collective-permute-start | bytes 442376 | tf_op jit(solution)/shard_map/ppermute | solution.py:486
  75.4 3.3 %collective-permute-start.14 = (bf16[4,144,128]{2,1,0:T(8,128)(2,1)S(1)}, bf16[4,144,128]{2,1,0:T(8,128)(2,1)S(1)}, u32[]{:S(2)}, u32[]{:S(2)}) collective-permute-start(bf16[4,144,128]{2,1,0:T(8,128)(2,1)S(1)} %collective-permute-done.13.refs_1_), channel_id=1, source_target_pairs={{0,8},{8,0},{1,9},{9,1},{2,10},{10,2},{3,11},{11,3},{4,12},{12,4},... | collective-permute-start | bytes 442376 | tf_op jit(solution)/shard_map/ppermute | solution.py:486

commit v13 on v12

--- a/solution.py
+++ b/solution.py
@@ -16,8 +16,8 @@
 NEGATIVE = -1e30
 RUN_AXES = ("z", "y")
 PLANE_AXES = ("x", "y")
-EARLY_SLABS = (0, 2)
-LATE_SLABS = (1, 3)
+EARLY_SLABS = (0,)
+LATE_SLABS = (1, 2, 3)
 VMEM_LIMIT = 28 * 1024 * 1024
 
 NN = (((1,), (0,)), ((), ()))
@@ -526,7 +526,6 @@
     keys = shifted(keys, 1)
     near = shifted(near, -1)
     if further:
-        near, values = lax.optimization_barrier((near, values))
         values = pl.pallas_call(
             choose_kernel,
             out_shape=jax.ShapeDtypeStruct((rows, att), bf16),
@@ -685,7 +684,7 @@
         in_specs=[smem] + [vmem] * (2 + len(messages)),
         out_specs=(vmem,) * 2,
         compiler_params=params,
-        cost_estimate=cost(8 * 10**9, 10**7),
+        cost_estimate=cost(16 * 10**9, 10**7),
         name="merge",
     )(place, *messages, swapped, own_grads)
     if split:

time: 80.7 us -> 78.2 us (0.969)
  starting transfers between devices: 37.4 us -> 35.8 us
  waiting for transfers between devices: 17.1 us -> 16.2 us
    ppermute x6, waiting for transfers between devices: 7.43 us -> 5.84 us  [from_peer(): return lax.ppermute(x, PLANE_AXES, [(i, i ^ mask) for i in devices])]
    ppermute x2, starting transfers between devices: 10.3 us -> 8.8 us  [summed_along(): other = lax.ppermute(x, axis, [(i, i ^ step) for i in range(size)])]
where the time goes in v13:
time: 78.2 us; the launch traced here: 78 us
  starting transfers between devices  35.8 us (46%)
  Pallas kernels  24.9 us (32%)
  waiting for transfers between devices  16.2 us (21%)
  between operations  0.79 us (1%)
    ppermute x5, starting transfers between devices, shifted(): lax.ppermute(x, RUN_AXES, [(i, i + by) for i in devices if i + by in devi...  16.5 us
    ppermute x2, starting transfers between devices, summed_along(): other = lax.ppermute(x, axis, [(i, i ^ step) for i in range(size)])  8.8 us
    ppermute x2, waiting for transfers between devices, summed_along(): other = lax.ppermute(x, axis, [(i, i ^ step) for i in range(size)])  8.46 us
    ppermute x6, starting transfers between devices, from_peer(): return lax.ppermute(x, PLANE_AXES, [(i, i ^ mask) for i in devices])  7.11 us
    pallas_call x1, Pallas kernels, per_device(): pl.pallas_call(functools.partial(forward_kernel, context, rows, edge, tap...  6.9 us
    pallas_call x1, Pallas kernels, per_device(): pl.pallas_call(functools.partial(backward_kernel, context, rows), out_sha...  5.98 us
    ppermute x6, waiting for transfers between devices, from_peer(): return lax.ppermute(x, PLANE_AXES, [(i, i ^ mask) for i in devices])  5.84 us
    pallas_call x2, Pallas kernels, score(): pl.pallas_call(functools.partial(scores_kernel, context, rows, edge, bloc...  2.85 us
  transfers between devices with their start and end apart: 20, of which 7 were waited for; matrix products, arithmetic and copies ran while one was open for 0% of the time, Pallas kernels for 17%

profile of v13, /device:TPU:0, one launch (start us, length us, event | category | flops | bytes accessed | tf_op | source)
XLA Modules:
  0.0 78.0 jit_solution(6356057533828142340)
XLA Ops:
  0.6 1.4 %pack.1 = (bf16[384,512]{1,0:T(8,128)(2,1)S(1)}, bf16[224,512]{1,0:T(8,128)(2,1)S(1)}, bf16[192,512]{1,0:T(8,128)(2,1)S(1)}, bf16[192,512]{1,0:T(8,128)(2,1)S(1)...) custom-call(bf16[192,512]{1,0:T(8,128)(2,1)} %bitcast.13, bf16[192,512]{1,0:T(8,128)(2,1)} %bitcast.14, ...), custom_call_target="tpu_custom_call" | custom-call | tf_op jit(solution)/shard_map/pack/pallas_call | solution.py:509
  2.1 5.0 %collective-permute-start.1 = (bf16[384,512]{1,0:T(8,128)(2,1)S(1)}, bf16[384,512]{1,0:T(8,128)(2,1)S(1)}, u32[]{:S(2)}, u32[]{:S(2)}) collective-permute-start(bf16[384,512]{1,0:T(8,128)(2,1)S(1)} %get-tuple-element.53.refs_0_.refs_3_.refs_2_), channel_id=1, source_target_pairs={{0,2},{1,3},{2,4},{3,5},{4,6},{5,7},{8,10},{9,11},{10,12},{11,13},... | collective-permute-start | bytes 1179656 | tf_op jit(solution)/shard_map/ppermute | solution.py:34
  7.0 3.4 %collective-permute-start = (bf16[224,512]{1,0:T(8,128)(2,1)S(1)}, bf16[224,512]{1,0:T(8,128)(2,1)S(1)}, u32[]{:S(2)}, u32[]{:S(2)}) collective-permute-start(bf16[224,512]{1,0:T(8,128)(2,1)S(1)} %get-tuple-element.54), channel_id=1, source_target_pairs={{0,1},{1,2},{2,3},{3,4},{4,5},{5,6},{6,7},{8,9},{9,10},{10,11},{11... | collective-permute-start | bytes 688136 | tf_op jit(solution)/shard_map/ppermute | solution.py:34
  10.5 1.3 %collective-permute-start.3 = (bf16[160,512]{1,0:T(8,128)(2,1)S(1)}, bf16[160,512]{1,0:T(8,128)(2,1)S(1)}, u32[]{:S(2)}, u32[]{:S(2)}) collective-permute-start(bf16[160,512]{1,0:T(8,128)(2,1)S(1)} %get-tuple-element.57), channel_id=1, source_target_pairs={{1,0},{2,1},{3,2},{4,3},{5,4},{6,5},{7,6},{9,8},{10,9},{11,10},{12... | collective-permute-start | bytes 491528 | tf_op jit(solution)/shard_map/ppermute | solution.py:34
  11.8 5.5 %collective-permute-start.2 = (bf16[64,512]{1,0:T(8,128)(2,1)S(1)}, bf16[64,512]{1,0:T(8,128)(2,1)S(1)}, u32[]{:S(2)}, u32[]{:S(2)}) collective-permute-start(bf16[64,512]{1,0:T(8,128)(2,1)S(1)} %get-tuple-element.55), channel_id=1, source_target_pairs={{0,3},{1,4},{2,5},{3,6},{4,7},{8,11},{9,12},{10,13},{11,14},{12,15... | collective-permute-start | bytes 196616 | tf_op jit(solution)/shard_map/ppermute | solution.py:34
  17.3 0.1 pad_add_fusion.device_ref.refs_0_
  17.4 0.0 collective-permute-done.1.refs_2_.odd_ref.refs_6_.refs_5_
  17.4 2.5 %collective-permute-start.4 = (bf16[192,512]{1,0:T(8,128)(2,1)S(1)}, bf16[192,512]{1,0:T(8,128)(2,1)S(1)}, u32[]{:S(2)}, u32[]{:S(2)}) collective-permute-start(bf16[192,512]{1,0:T(8,128)(2,1)S(1)} %choose.1), channel_id=1, source_target_pairs={{0,1},{1,0},{2,3},{3,2},{4,5},{5,4},{6,7},{7,6},{8,9},{9,8},{10,11... | collective-permute-start | bytes 589832 | tf_op jit(solution)/shard_map/ppermute | solution.py:537
  19.9 0.0 collective-permute-done.3.refs_3_.refs_8_
  19.9 0.0 collective-permute-done.refs_1_.refs_4_.refs_3_
  19.9 1.4 %scores.3 = (bf16[4,256,512]{2,1,0:T(8,128)(2,1)S(1)}, f32[8,128]{1,0:T(8,128)S(1)}) custom-call(s32[3]{0:T(128)S(1)} %pad_add_fusion.device_ref.refs_0_, bf16[192,512]{1,0:T(8,128)(2,1)S(1)} %get-tuple-element.52.q_ref.refs_1_, bf16[384,512]{1,0:T(8,128)(2,1)S(1)} %get-tuple-element.53.refs_0_.refs_3_.refs_2_, ...), custom_call_target="tpu_custom_call" | custom-call | flops 5000000000 | bytes 10000000 | tf_op jit(solution)/shard_map/scores/pallas_call | solution.py:555
  21.3 0.0 collective-permute-done.2.refs_3_.refs_7_
  21.3 1.4 %scores.2 = (bf16[4,256,512]{2,1,0:T(8,128)(2,1)S(1)}, f32[8,128]{1,0:T(8,128)S(1)}) custom-call(s32[3]{0:T(128)S(1)} %pad_add_fusion.device_ref.refs_0_, bf16[192,512]{1,0:T(8,128)(2,1)S(1)} %get-tuple-element.52.q_ref.refs_1_, bf16[384,512]{1,0:T(8,128)(2,1)S(1)} %get-tuple-element.53.refs_0_.refs_3_.refs_2_, ...), custom_call_target="tpu_custom_call" | custom-call | flops 5000000000 | bytes 10000000 | tf_op jit(solution)/shard_map/scores/pallas_call | solution.py:555
  22.8 0.9 %collective-permute-done.4.refs_5_.refs_4_ = bf16[192,512]{1,0:T(8,128)(2,1)S(1)} collective-permute-done((bf16[192,512]{1,0:T(8,128)(2,1)S(1)}, bf16[192,512]{1,0:T(8,128)(2,1)S(1)}, u32[]{:S(2)}, u32[]{:S(2)}) %collective-permute-start.4) | collective-permute-done | bytes 196640 | tf_op jit(solution)/shard_map/ppermute | solution.py:537
  23.7 6.9 %forward.1 = (bf16[192,1024]{1,0:T(8,128)(2,1)}, bf16[192,512]{1,0:T(8,128)(2,1)S(1)}, bf16[192,1024]{1,0:T(8,128)(2,1)S(1)}, bf16[16,128,128]{2,1,0:T(8,128)(2,...) custom-call(s32[3]{0:T(128)S(1)} %pad_add_fusion.device_ref.refs_0_,, ...), custom_call_target="tpu_custom_call" | custom-call | flops 8000000000 | bytes 10000000 | tf_op jit(solution)/shard_map/forward/pallas_call | solution.py:576
  30.6 0.1 collective-permute-start.5
  30.7 1.9 %kernel_grad.1.rows_ref = bf16[16,16,128]{2,1,0:T(8,128)(2,1)S(1)} custom-call(f32[8,256,128]{2,1,0:T(8,128)S(1)} %get-tuple-element.66.hid, f32[8,232,128]{2,1,0:T(8,128)S(1)} %get-tuple-element.67.dm), custom_call_target="tpu_custom_call" | custom-call | flops 2000000000 | bytes 3000000 | tf_op jit(solution)/shard_map/kernel_grad/pallas_call | solution.py:615
  32.6 0.0 collective-permute-done.5.given_ref
  32.6 0.7 join.1
  33.2 2.0 %collective-permute-start.6 = (bf16[4,144,128]{2,1,0:T(8,128)(2,1)S(1)}, bf16[4,144,128]{2,1,0:T(8,128)(2,1)S(1)}, u32[]{:S(2)}, u32[]{:S(2)}) collective-permute-start(bf16[4,144,128]{2,1,0:T(8,128)(2,1)S(1)} %get-tuple-element.77), channel_id=1, source_target_pairs={{0,1},{1,0},{16,17},{17,16},{2,3},{3,2},{18,19},{19,18},{4,5},{5,4... | collective-permute-start | bytes 442376 | tf_op jit(solution)/shard_map/ppermute | solution.py:473
  35.2 1.5 %collective-permute-start.7 = (bf16[4,144,128]{2,1,0:T(8,128)(2,1)S(1)}, bf16[4,144,128]{2,1,0:T(8,128)(2,1)S(1)}, u32[]{:S(2)}, u32[]{:S(2)}) collective-permute-start(bf16[4,144,128]{2,1,0:T(8,128)(2,1)S(1)} %get-tuple-element.78), channel_id=1, source_target_pairs={{0,16},{1,17},{16,0},{17,1},{2,18},{3,19},{18,2},{19,3},{4,20},{5,... | collective-permute-start | bytes 442376 | tf_op jit(solution)/shard_map/ppermute | solution.py:473
  36.7 0.1 collective-permute-start.8
  36.8 6.0 %backward.1 = (bf16[192,512]{1,0:T(8,128)(2,1)}, f32[384,512]{1,0:T(8,128)S(1)}, bf16[384,512]{1,0:T(8,128)(2,1)S(1)}, bf16[384,512]{1,0:T(8,128)(2,1)S(1)}) custom-call(s32[3]{0:T(128)S(1)} %pad_add_fusion.device_ref.refs_0_, bf16[192,512]{1,0:T(8,128)(2,1)S(1)} %get-tuple-element.52.q_ref.refs_1_, ...), custom_call_target="tpu_custom_call" | custom-call | flops 6000000000 | bytes 10000000 | tf_op jit(solution)/shard_map/backward/pallas_call | solution.py:640
  42.8 0.0 collective-permute-done.6
  42.8 0.0 collective-permute-done.7
  42.8 1.3 %collective-permute-done.8 = bf16[4,144,128]{2,1,0:T(8,128)(2,1)S(1)} collective-permute-done((bf16[4,144,128]{2,1,0:T(8,128)(2,1)S(1)}, bf16[4,144,128]{2,1,0:T(8,128)(2,1)S(1)}, u32[]{:S(2)}, u32[]{:S(2)}) %collective-permute-start.8) | collective-permute-done | bytes 147488 | tf_op jit(solution)/shard_map/ppermute | solution.py:473
  44.1 0.1 add_convert_fusion.2
  44.2 4.6 %collective-permute-start.9 = (bf16[4,144,128]{2,1,0:T(8,128)(2,1)S(1)}, bf16[4,144,128]{2,1,0:T(8,128)(2,1)S(1)}, u32[]{:S(2)}, u32[]{:S(2)}) collective-permute-start(bf16[4,144,128]{2,1,0:T(8,128)(2,1)S(1)} %add_convert_fusion.2), channel_id=1, source_target_pairs={{0,2},{2,0},{4,6},{6,4},{1,3},{3,1},{5,7},{7,5},{8,10},{10,8},{12,... | collective-permute-start | bytes 442376 | tf_op jit(solution)/shard_map/ppermute | solution.py:479
  48.8 0.4 collective-permute-start.11
  49.1 3.1 %collective-permute-done.9 = bf16[4,144,128]{2,1,0:T(8,128)(2,1)S(1)} collective-permute-done((bf16[4,144,128]{2,1,0:T(8,128)(2,1)S(1)}, bf16[4,144,128]{2,1,0:T(8,128)(2,1)S(1)}, u32[]{:S(2)}, u32[]{:S(2)}) %collective-permute-start.9) | collective-permute-done | bytes 147488 | tf_op jit(solution)/shard_map/ppermute | solution.py:479
  52.2 4.2 %collective-permute-start.10 = (bf16[4,144,128]{2,1,0:T(8,128)(2,1)S(1)}, bf16[4,144,128]{2,1,0:T(8,128)(2,1)S(1)}, u32[]{:S(2)}, u32[]{:S(2)}) collective-permute-start(bf16[4,144,128]{2,1,0:T(8,128)(2,1)S(1)} %add_convert_fusion.1), channel_id=1, source_target_pairs={{0,4},{2,6},{4,0},{6,2},{1,5},{3,7},{5,1},{7,3},{8,12},{10,14},{12... | collective-permute-start | bytes 442376 | tf_op jit(solution)/shard_map/ppermute | solution.py:479
  56.5 5.4 %collective-permute-done.10 = bf16[4,144,128]{2,1,0:T(8,128)(2,1)S(1)} collective-permute-done((bf16[4,144,128]{2,1,0:T(8,128)(2,1)S(1)}, bf16[4,144,128]{2,1,0:T(8,128)(2,1)S(1)}, u32[]{:S(2)}, u32[]{:S(2)}) %collective-permute-start.10) | collective-permute-done | bytes 147488 | tf_op jit(solution)/shard_map/ppermute | solution.py:479
  61.9 0.0 collective-permute-done.11.swapped_ref.refs_1_
  61.9 0.7 relay.1
  62.6 1.3 %collective-permute-start.19 = (bf16[384,512]{1,0:T(8,128)(2,1)S(1)}, bf16[384,512]{1,0:T(8,128)(2,1)S(1)}, u32[]{:S(2)}, u32[]{:S(2)}) collective-permute-start(bf16[384,512]{1,0:T(8,128)(2,1)S(1)} %relay.1), channel_id=1, source_target_pairs={{2,0},{3,1},{4,2},{5,3},{6,4},{7,5},{10,8},{11,9},{12,10},{13,11},... | collective-permute-start | bytes 1179656 | tf_op jit(solution)/shard_map/ppermute | solution.py:34
  63.9 2.3 %collective-permute-start.17 = (bf16[4,144,128]{2,1,0:T(8,128)(2,1)S(1)}, bf16[4,144,128]{2,1,0:T(8,128)(2,1)S(1)}, u32[]{:S(2)}, u32[]{:S(2)}) collective-permute-start(bf16[4,144,128]{2,1,0:T(8,128)(2,1)S(1)} %add_convert_fusion.refs_0_), channel_id=1, source_target_pairs={{0,17},{1,16},{16,1},{17,0},{2,19},{3,18},{18,3},{19,2},{4,21},{5,... | collective-permute-start | bytes 442376 | tf_op jit(solution)/shard_map/ppermute | solution.py:473
  66.2 0.5 collective-permute-start.15
  66.7 0.8 collective-permute-start.13
  67.5 0.0 collective-permute-start.12
  67.5 1.3 %unpack_early.1.refs_8_ = f32[512,1024]{1,0:T(8,128)} custom-call(s32[3]{0:T(128)S(1)} %pad_add_fusion.device_ref.refs_0_, bf16[4,144,128]{2,1,0:T(8,128)(2,1)S(1)} %add_convert_fusion.refs_0_), custom_call_target="tpu_custom_call" | custom-call | flops 1000000000 | bytes 3000000 | tf_op jit(solution)/shard_map/unpack_early/pallas_call | solution.py:704
  68.7 2.8 %collective-permute-done.17.refs_3_ = bf16[4,144,128]{2,1,0:T(8,128)(2,1)S(1)} collective-permute-done((bf16[4,144,128]{2,1,0:T(8,128)(2,1)S(1)}, bf16[4,144,128]{2,1,0:T(8,128)(2,1)S(1)}, u32[]{:S(2)}, u32[]{:S(2)}) %collective-permute-start.17) | collective-permute-done | bytes 147488 | tf_op jit(solution)/shard_map/ppermute | solution.py:473
  71.5 0.0 collective-permute-start.18
  71.5 1.7 %collective-permute-done.15.refs_2_ = bf16[4,144,128]{2,1,0:T(8,128)(2,1)S(1)} collective-permute-done((bf16[4,144,128]{2,1,0:T(8,128)(2,1)S(1)}, bf16[4,144,128]{2,1,0:T(8,128)(2,1)S(1)}, u32[]{:S(2)}, u32[]{:S(2)}) %collective-permute-start.15) | collective-permute-done | bytes 147488 | tf_op jit(solution)/shard_map/ppermute | solution.py:473
  73.2 0.0 collective-permute-start.16
  73.2 0.0 collective-permute-done.13.refs_1_
  73.2 0.5 collective-permute-start.14
  73.8 0.9 %collective-permute-done.19.refs_0_ = bf16[384,512]{1,0:T(8,128)(2,1)S(1)} collective-permute-done((bf16[384,512]{1,0:T(8,128)(2,1)S(1)}, bf16[384,512]{1,0:T(8,128)(2,1)S(1)}, u32[]{:S(2)}, u32[]{:S(2)}) %collective-permute-start.19) | collective-permute-done | bytes 393248 | tf_op jit(solution)/shard_map/ppermute | solution.py:34
  74.7 1.4 %merge.1 = (bf16[192,512]{1,0:T(8,128)(2,1)}, bf16[192,512]{1,0:T(8,128)(2,1)}) custom-call(s32[3]{0:T(128)S(1)} %pad_add_fusion.device_ref.refs_0_, bf16[384,512]{1,0:T(8,128)(2,1)S(1)} %collective-permute-done.19.refs_0_, bf16[384,512]{1,0:T(8,128)(2,1)S(1)} %collective-permute-done.11.swapped_ref.refs_1_, f32[384,512]{1,0:T(8,128)S(1)} %get-tuple-element.87.refs_2_), custom_call_target="tpu_custom_call" | custom-call | flops 16000000000 | bytes 10000000 | tf_op jit(solution)/shard_map/merge/pallas_call | solution.py:681
  76.1 0.0 collective-permute-done.12.refs_4_
  76.1 0.0 collective-permute-done.18.refs_7_
  76.1 0.0 collective-permute-done.16.refs_6_
  76.1 0.0 collective-permute-done.14.refs_5_
  76.1 1.9 %unpack_late.1 = (f32[512,1024]{1,0:T(8,128)}, f32[31,1024]{1,0:T(8,128)}) custom-call(s32[3]{0:T(128)S(1)} %pad_add_fusion.device_ref.refs_0_, bf16[4,144,128]{2,1,0:T(8,128)(2,1)S(1)} %add_convert_fusion.refs_0_, bf16[4,144,128]{2,1,0:T(8,128)(2,1)S(1)} %collective-permute-done.13.refs_1_, ...), custom_call_target="tpu_custom_call", output_to_operand_aliasing={{0}: (9, {})} | custom-call | tf_op jit(solution)/shard_map/unpack_late/pallas_call | solution.py:717
  (3 shorter events, 0.1 us)
Async XLA Ops:
  2.1 15.3 %collective-permute-start.1 = (bf16[384,512]{1,0:T(8,128)(2,1)S(1)}, bf16[384,512]{1,0:T(8,128)(2,1)S(1)}, u32[]{:S(2)}, u32[]{:S(2)}) collective-permute-start(bf16[384,512]{1,0:T(8,128)(2,1)S(1)} %get-tuple-element.53.refs_0_.refs_3_.refs_2_), channel_id=1, source_target_pairs={{0,2},{1,3},{2,4},{3,5},{4,6},{5,7},{8,10},{9,11},{10,12},{11,13},... | collective-permute-start | bytes 1179656 | tf_op jit(solution)/shard_map/ppermute | solution.py:34
  7.0 12.9 %collective-permute-start = (bf16[224,512]{1,0:T(8,128)(2,1)S(1)}, bf16[224,512]{1,0:T(8,128)(2,1)S(1)}, u32[]{:S(2)}, u32[]{:S(2)}) collective-permute-start(bf16[224,512]{1,0:T(8,128)(2,1)S(1)} %get-tuple-element.54), channel_id=1, source_target_pairs={{0,1},{1,2},{2,3},{3,4},{4,5},{5,6},{6,7},{8,9},{9,10},{10,11},{11... | collective-permute-start | bytes 688136 | tf_op jit(solution)/shard_map/ppermute | solution.py:34
  10.5 9.4 %collective-permute-start.3 = (bf16[160,512]{1,0:T(8,128)(2,1)S(1)}, bf16[160,512]{1,0:T(8,128)(2,1)S(1)}, u32[]{:S(2)}, u32[]{:S(2)}) collective-permute-start(bf16[160,512]{1,0:T(8,128)(2,1)S(1)} %get-tuple-element.57), channel_id=1, source_target_pairs={{1,0},{2,1},{3,2},{4,3},{5,4},{6,5},{7,6},{9,8},{10,9},{11,10},{12... | collective-permute-start | bytes 491528 | tf_op jit(solution)/shard_map/ppermute | solution.py:34
  11.8 9.6 %collective-permute-start.2 = (bf16[64,512]{1,0:T(8,128)(2,1)S(1)}, bf16[64,512]{1,0:T(8,128)(2,1)S(1)}, u32[]{:S(2)}, u32[]{:S(2)}) collective-permute-start(bf16[64,512]{1,0:T(8,128)(2,1)S(1)} %get-tuple-element.55), channel_id=1, source_target_pairs={{0,3},{1,4},{2,5},{3,6},{4,7},{8,11},{9,12},{10,13},{11,14},{12,15... | collective-permute-start | bytes 196616 | tf_op jit(solution)/shard_map/ppermute | solution.py:34
  17.4 6.3 %collective-permute-start.4 = (bf16[192,512]{1,0:T(8,128)(2,1)S(1)}, bf16[192,512]{1,0:T(8,128)(2,1)S(1)}, u32[]{:S(2)}, u32[]{:S(2)}) collective-permute-start(bf16[192,512]{1,0:T(8,128)(2,1)S(1)} %choose.1), channel_id=1, source_target_pairs={{0,1},{1,0},{2,3},{3,2},{4,5},{5,4},{6,7},{7,6},{8,9},{9,8},{10,11... | collective-permute-start | bytes 589832 | tf_op jit(solution)/shard_map/ppermute | solution.py:537
  30.6 2.0 %collective-permute-start.5 = (bf16[16,128,128]{2,1,0:T(8,128)(2,1)S(1)}, bf16[16,128,128]{2,1,0:T(8,128)(2,1)S(1)}, u32[]{:S(2)}, u32[]{:S(2)}) collective-permute-start(bf16[16,128,128]{2,1,0:T(8,128)(2,1)S(1)} %get-tuple-element.65), channel_id=1, source_target_pairs={{0,8},{8,0},{1,9},{9,1},{2,10},{10,2},{3,11},{11,3},{4,12},{12,4},... | collective-permute-start | bytes 1572872 | tf_op jit(solution)/shard_map/ppermute | solution.py:486
  33.2 9.5 %collective-permute-start.6 = (bf16[4,144,128]{2,1,0:T(8,128)(2,1)S(1)}, bf16[4,144,128]{2,1,0:T(8,128)(2,1)S(1)}, u32[]{:S(2)}, u32[]{:S(2)}) collective-permute-start(bf16[4,144,128]{2,1,0:T(8,128)(2,1)S(1)} %get-tuple-element.77), channel_id=1, source_target_pairs={{0,1},{1,0},{16,17},{17,16},{2,3},{3,2},{18,19},{19,18},{4,5},{5,4... | collective-permute-start | bytes 442376 | tf_op jit(solution)/shard_map/ppermute | solution.py:473
  35.2 7.6 %collective-permute-start.7 = (bf16[4,144,128]{2,1,0:T(8,128)(2,1)S(1)}, bf16[4,144,128]{2,1,0:T(8,128)(2,1)S(1)}, u32[]{:S(2)}, u32[]{:S(2)}) collective-permute-start(bf16[4,144,128]{2,1,0:T(8,128)(2,1)S(1)} %get-tuple-element.78), channel_id=1, source_target_pairs={{0,16},{1,17},{16,0},{17,1},{2,18},{3,19},{18,2},{19,3},{4,20},{5,... | collective-permute-start | bytes 442376 | tf_op jit(solution)/shard_map/ppermute | solution.py:473
  36.7 7.4 %collective-permute-start.8 = (bf16[4,144,128]{2,1,0:T(8,128)(2,1)S(1)}, bf16[4,144,128]{2,1,0:T(8,128)(2,1)S(1)}, u32[]{:S(2)}, u32[]{:S(2)}) collective-permute-start(bf16[4,144,128]{2,1,0:T(8,128)(2,1)S(1)} %get-tuple-element.79), channel_id=1, source_target_pairs={{0,17},{1,16},{16,1},{17,0},{2,19},{3,18},{18,3},{19,2},{4,21},{5,... | collective-permute-start | bytes 442376 | tf_op jit(solution)/shard_map/ppermute | solution.py:473
  44.2 8.0 %collective-permute-start.9 = (bf16[4,144,128]{2,1,0:T(8,128)(2,1)S(1)}, bf16[4,144,128]{2,1,0:T(8,128)(2,1)S(1)}, u32[]{:S(2)}, u32[]{:S(2)}) collective-permute-start(bf16[4,144,128]{2,1,0:T(8,128)(2,1)S(1)} %add_convert_fusion.2), channel_id=1, source_target_pairs={{0,2},{2,0},{4,6},{6,4},{1,3},{3,1},{5,7},{7,5},{8,10},{10,8},{12,... | collective-permute-start | bytes 442376 | tf_op jit(solution)/shard_map/ppermute | solution.py:479
  48.8 13.1 %collective-permute-start.11 = (bf16[384,512]{1,0:T(8,128)(2,1)S(1)}, bf16[384,512]{1,0:T(8,128)(2,1)S(1)}, u32[]{:S(2)}, u32[]{:S(2)}) collective-permute-start(bf16[384,512]{1,0:T(8,128)(2,1)S(1)} %get-tuple-element.83), channel_id=1, source_target_pairs={{0,1},{1,0},{2,3},{3,2},{4,5},{5,4},{6,7},{7,6},{8,9},{9,8},{10,11... | collective-permute-start | bytes 1179656 | tf_op jit(solution)/shard_map/ppermute | solution.py:663
  52.2 9.6 %collective-permute-start.10 = (bf16[4,144,128]{2,1,0:T(8,128)(2,1)S(1)}, bf16[4,144,128]{2,1,0:T(8,128)(2,1)S(1)}, u32[]{:S(2)}, u32[]{:S(2)}) collective-permute-start(bf16[4,144,128]{2,1,0:T(8,128)(2,1)S(1)} %add_convert_fusion.1), channel_id=1, source_target_pairs={{0,4},{2,6},{4,0},{6,2},{1,5},{3,7},{5,1},{7,3},{8,12},{10,14},{12... | collective-permute-start | bytes 442376 | tf_op jit(solution)/shard_map/ppermute | solution.py:479
  62.6 12.1 %collective-permute-start.19 = (bf16[384,512]{1,0:T(8,128)(2,1)S(1)}, bf16[384,512]{1,0:T(8,128)(2,1)S(1)}, u32[]{:S(2)}, u32[]{:S(2)}) collective-permute-start(bf16[384,512]{1,0:T(8,128)(2,1)S(1)} %relay.1), channel_id=1, source_target_pairs={{2,0},{3,1},{4,2},{5,3},{6,4},{7,5},{10,8},{11,9},{12,10},{13,11},... | collective-permute-start | bytes 1179656 | tf_op jit(solution)/shard_map/ppermute | solution.py:34
  63.9 7.6 %collective-permute-start.17 = (bf16[4,144,128]{2,1,0:T(8,128)(2,1)S(1)}, bf16[4,144,128]{2,1,0:T(8,128)(2,1)S(1)}, u32[]{:S(2)}, u32[]{:S(2)}) collective-permute-start(bf16[4,144,128]{2,1,0:T(8,128)(2,1)S(1)} %add_convert_fusion.refs_0_), channel_id=1, source_target_pairs={{0,17},{1,16},{16,1},{17,0},{2,19},{3,18},{18,3},{19,2},{4,21},{5,... | collective-permute-start | bytes 442376 | tf_op jit(solution)/shard_map/ppermute | solution.py:473
  66.2 7.1 %collective-permute-start.15 = (bf16[4,144,128]{2,1,0:T(8,128)(2,1)S(1)}, bf16[4,144,128]{2,1,0:T(8,128)(2,1)S(1)}, u32[]{:S(2)}, u32[]{:S(2)}) collective-permute-start(bf16[4,144,128]{2,1,0:T(8,128)(2,1)S(1)} %add_convert_fusion.refs_0_), channel_id=1, source_target_pairs={{0,16},{1,17},{16,0},{17,1},{2,18},{3,19},{18,2},{19,3},{4,20},{5,... | collective-permute-start | bytes 442376 | tf_op jit(solution)/shard_map/ppermute | solution.py:473
  66.7 6.6 %collective-permute-start.13 = (bf16[4,144,128]{2,1,0:T(8,128)(2,1)S(1)}, bf16[4,144,128]{2,1,0:T(8,128)(2,1)S(1)}, u32[]{:S(2)}, u32[]{:S(2)}) collective-permute-start(bf16[4,144,128]{2,1,0:T(8,128)(2,1)S(1)} %add_convert_fusion.refs_0_), channel_id=1, source_target_pairs={{0,1},{1,0},{16,17},{17,16},{2,3},{3,2},{18,19},{19,18},{4,5},{5,4... | collective-permute-start | bytes 442376 | tf_op jit(solution)/shard_map/ppermute | solution.py:473
  67.5 8.6 %collective-permute-start.12 = (bf16[4,144,128]{2,1,0:T(8,128)(2,1)S(1)}, bf16[4,144,128]{2,1,0:T(8,128)(2,1)S(1)}, u32[]{:S(2)}, u32[]{:S(2)}) collective-permute-start(bf16[4,144,128]{2,1,0:T(8,128)(2,1)S(1)} %add_convert_fusion.refs_0_), channel_id=1, source_target_pairs={{0,8},{8,0},{1,9},{9,1},{2,10},{10,2},{3,11},{11,3},{4,12},{12,4},... | collective-permute-start | bytes 442376 | tf_op jit(solution)/shard_map/ppermute | solution.py:486
  71.5 4.5 %collective-permute-start.18 = (bf16[4,144,128]{2,1,0:T(8,128)(2,1)S(1)}, bf16[4,144,128]{2,1,0:T(8,128)(2,1)S(1)}, u32[]{:S(2)}, u32[]{:S(2)}) collective-permute-start(bf16[4,144,128]{2,1,0:T(8,128)(2,1)S(1)} %collective-permute-done.17.refs_3_), channel_id=1, source_target_pairs={{0,8},{8,0},{1,9},{9,1},{2,10},{10,2},{3,11},{11,3},{4,12},{12,4},... | collective-permute-start | bytes 442376 | tf_op jit(solution)/shard_map/ppermute | solution.py:486
  73.2 2.8 %collective-permute-start.16 = (bf16[4,144,128]{2,1,0:T(8,128)(2,1)S(1)}, bf16[4,144,128]{2,1,0:T(8,128)(2,1)S(1)}, u32[]{:S(2)}, u32[]{:S(2)}) collective-permute-start(bf16[4,144,128]{2,1,0:T(8,128)(2,1)S(1)} %collective-permute-done.15.refs_2_), channel_id=1, source_target_pairs={{0,8},{8,0},{1,9},{9,1},{2,10},{10,2},{3,11},{11,3},{4,12},{12,4},... | collective-permute-start | bytes 442376 | tf_op jit(solution)/shard_map/ppermute | solution.py:486
  73.2 2.8 %collective-permute-start.14 = (bf16[4,144,128]{2,1,0:T(8,128)(2,1)S(1)}, bf16[4,144,128]{2,1,0:T(8,128)(2,1)S(1)}, u32[]{:S(2)}, u32[]{:S(2)}) collective-permute-start(bf16[4,144,128]{2,1,0:T(8,128)(2,1)S(1)} %collective-permute-done.13.refs_1_), channel_id=1, source_target_pairs={{0,8},{8,0},{1,9},{9,1},{2,10},{10,2},{3,11},{11,3},{4,12},{12,4},... | collective-permute-start | bytes 442376 | tf_op jit(solution)/shard_map/ppermute | solution.py:486

commit v14 on v13

--- a/solution.py
+++ b/solution.py
@@ -13,6 +13,7 @@
 CTX_MAX = 3
 LANES = 128
 SUBLANES = 8
+CHUNK = 32
 NEGATIVE = -1e30
 RUN_AXES = ("z", "y")
 PLANE_AXES = ("x", "y")
@@ -117,7 +118,7 @@
     return places + [(ref, 0, ref, rows) for ref in further_refs]
 
 
-def score_block(b, place, start, span, qx, kx, bias, weights_ref):
+def score_block(b, place, start, span, qx, kx, bias, held, weights_ref):
     pairs = qx.shape[1] // LANES
     block = LANES
     keys = span + block
@@ -132,14 +133,20 @@
     for pair in range(pairs):
         columns = slice(pair * LANES, (pair + 1) * LANES)
         qs = stack_heads(qx[b * block : (b + 1) * block, columns])
-        scores = dot(qs, kx[b * block : b * block + keys, columns], NT)
-        hidden_pairs = bias[...]
-        scores = scores + jnp.concatenate([hidden_pairs, hidden_pairs], axis=0)
-        row_max = jnp.max(scores, axis=1, keepdims=True)
-        weights = jnp.exp(scores - row_max)
-        row_sum = jnp.sum(weights, axis=1, keepdims=True)
-        weights_ref[place * pairs + pair] = (weights * (1.0 / row_sum)).astype(jnp.bfloat16)
-        log_sum = row_max + jnp.log(row_sum)
+        slot = pair % 2
+        held[slot] = dot(qs, kx[b * block : b * block + keys, columns], NT)
+        log_sum = []
+        for first in range(0, 2 * block, CHUNK):
+            at = first % block
+            scores = held[slot, first : first + CHUNK] + bias[at : at + CHUNK]
+            row_max = jnp.max(scores, axis=1, keepdims=True)
+            weights = jnp.exp(scores - row_max)
+            row_sum = jnp.sum(weights, axis=1, keepdims=True)
+            weights_ref[place * pairs + pair, first : first + CHUNK] = (
+                weights * (1.0 / row_sum)
+            ).astype(jnp.bfloat16)
+            log_sum.append(row_max + jnp.log(row_sum))
+        log_sum = jnp.concatenate(log_sum, axis=0)
         log_sums = jnp.where(lane_id == 2 * pair, log_sum[:block], log_sums)
         log_sums = jnp.where(lane_id == 2 * pair + 1, log_sum[block:], log_sums)
     return log_sums
@@ -148,7 +155,7 @@
 def scores_kernel(context, rows, edge, blocks, device_ref, q_ref, *refs):
     own_refs = refs[: 1 + context]
     keys_ref = own_refs[1]
-    edge_ref, weights_ref, lse_ref, qx, kx, lx, bias = refs[1 + context :]
+    edge_ref, weights_ref, lse_ref, qx, kx, lx, bias, held = refs[1 + context :]
     span = context * rows
     scale = 1.0 / math.sqrt(HEAD_DIM)
     start = device_ref[0] * rows - edge
@@ -164,7 +171,7 @@
         qx[edge + rows :] = edge_ref[2 * edge : 3 * edge] * scale
     for place, b in enumerate(blocks):
         lx[place * LANES : (place + 1) * LANES] = score_block(
-            b, place, start, span, qx, kx, bias, weights_ref
+            b, place, start, span, qx, kx, bias, held, weights_ref
         )
     lse_ref[...] = jnp.transpose(lx[...])[: lse_ref.shape[0]]
 
@@ -398,7 +405,7 @@
     att_ref, late_ref, early_ref, dhid_ref, w_ref = refs[2 + tiles : 7 + tiles]
     dq_ref, own_ref = refs[7 + tiles : 9 + tiles]
     message_refs = refs[9 + tiles : 9 + tiles + context]
-    datt, bias, lse_ref = refs[9 + tiles + context :]
+    datt, bias, lse_ref, scores, dprobs, probs, dscores = refs[9 + tiles + context :]
 
     att = q_ref.shape[1]
     heads = att // HEAD_DIM
@@ -437,13 +444,19 @@
         for offset, (k_ref, k_at, v_ref, v_at) in enumerate(places):
             kp = k_ref[k_at : k_at + rows, columns]
             vp = v_ref[v_at : v_at + rows, columns]
-            hidden_pairs = jnp.concatenate([bias[offset], bias[offset]], axis=1)
-            probs = jnp.exp(dot(kp, qs, NT) + hidden_pairs - log_sum)
-            dprobs = dot(vp, ds, NT)
-            dscores = (probs * (dprobs - delta)).astype(jnp.bfloat16)
-            dvalue = dot(probs.astype(jnp.bfloat16), ds, NN)
-            dkey = dot(dscores, qs, NN)
-            dquery += dot(dscores, kp, TN)
+            slot = offset % 2
+            scores[slot] = dot(kp, qs, NT)
+            dprobs[slot] = dot(vp, ds, NT)
+            for first in range(0, rows, CHUNK):
+                part = slice(first, first + CHUNK)
+                hidden_pairs = jnp.concatenate([bias[offset, part], bias[offset, part]], axis=1)
+                chance = jnp.exp(scores[slot, part] + hidden_pairs - log_sum)
+                dscore = chance * (dprobs[slot, part] - delta)
+                probs[slot, part] = chance.astype(jnp.bfloat16)
+                dscores[slot, part] = dscore.astype(jnp.bfloat16)
+            dvalue = dot(probs[slot], ds, NN)
+            dkey = dot(dscores[slot], qs, NN)
+            dquery += dot(dscores[slot], kp, TN)
             target = message_refs[offset - 1] if offset else own_ref
             target[:rows, columns] = dkey.astype(target.dtype)
             target[rows:, columns] = dvalue.astype(target.dtype)
@@ -452,20 +465,24 @@
 
 def relay_kernel(device_ref, swapped_ref, message_ref, out_ref):
     odd = lax.rem(device_ref[0], 2).astype(jnp.float32)
-    swapped = swapped_ref[...].astype(jnp.float32) * odd
-    out_ref[...] = (message_ref[...].astype(jnp.float32) + swapped).astype(jnp.bfloat16)
+    for first in range(0, out_ref.shape[0], CHUNK):
+        part = slice(first, first + CHUNK)
+        total = message_ref[part].astype(jnp.float32) + swapped_ref[part].astype(jnp.float32) * odd
+        out_ref[part] = total.astype(jnp.bfloat16)
 
 
 def merge_kernel(device_ref, *refs):
     *message_refs, swapped_ref, own_ref, dk_ref, dv_ref = refs
     rows = dk_ref.shape[0]
     even = 1.0 - lax.rem(device_ref[0], 2).astype(jnp.float32)
-    total = swapped_ref[...].astype(jnp.float32) * even
-    for message_ref in message_refs:
-        total += message_ref[...].astype(jnp.float32)
-    total = (total + own_ref[...]).astype(jnp.bfloat16)
-    dk_ref[...] = total[:rows]
-    dv_ref[...] = total[rows:]
+    for first in range(0, 2 * rows, CHUNK):
+        part = slice(first, first + CHUNK)
+        total = own_ref[part] + swapped_ref[part].astype(jnp.float32) * even
+        for message_ref in message_refs:
+            total += message_ref[part].astype(jnp.float32)
+        target = dk_ref if first < rows else dv_ref
+        at = first % rows
+        target[at : at + CHUNK] = total.astype(jnp.bfloat16)
 
 
 def from_peer(x, mask):
@@ -565,6 +582,7 @@
                 pltpu.VMEM((key_rows, att), bf16),
                 pltpu.VMEM((len(blocks) * LANES, LANES), f32),
                 pltpu.VMEM((LANES, key_span), f32),
+                pltpu.VMEM((2, 2 * LANES, key_span), f32),
             ],
             compiler_params=params,
             cost_estimate=cost(5 * 10**9, 10**7),
@@ -650,6 +668,10 @@
             pltpu.VMEM((rows, att), bf16),
             pltpu.VMEM((context + 1, rows, rows), f32),
             pltpu.VMEM((heads, rows), f32),
+            pltpu.VMEM((2, rows, 2 * rows), f32),
+            pltpu.VMEM((2, rows, 2 * rows), f32),
+            pltpu.VMEM((2, rows, 2 * rows), bf16),
+            pltpu.VMEM((2, rows, 2 * rows), bf16),
         ],
         compiler_params=params,
         cost_estimate=cost(6 * 10**9, 10**7),

time: 78.2 us -> 79.9 us (1.022)
  Pallas kernels: 24.9 us -> 27.1 us
  waiting for transfers between devices: 16.2 us -> 14.9 us
  starting transfers between devices: 35.8 us -> 36.6 us
    pallas_call x2, Pallas kernels: 2.85 us -> 4.9 us  [score(): pl.pallas_call(functools.partial(scores_kernel, context, rows, edge, bloc...]
    ppermute x1, waiting for transfers between devices: 0.92 us -> 0.01 us  [per_device(): values = lax.ppermute(values, 'y', [(0, 1), (1, 0)])]
  transfers between devices with their start and end apart: 20 -> 20, of which waited for: 7 -> 6; matrix products, arithmetic and copies ran while one was open for 0% -> 0% of each run, Pallas kernels for 17% -> 20%
where the time goes in v14:
time: 79.9 us; the launch traced here: 79.6 us
  starting transfers between devices  36.6 us (46%)
  Pallas kernels  27.1 us (34%)
  waiting for transfers between devices  14.9 us (19%)
    ppermute x5, starting transfers between devices, shifted(): lax.ppermute(x, RUN_AXES, [(i, i + by) for i in devices if i + by in devi...  16.5 us
    ppermute x2, starting transfers between devices, summed_along(): other = lax.ppermute(x, axis, [(i, i ^ step) for i in range(size)])  8.28 us
    ppermute x2, waiting for transfers between devices, summed_along(): other = lax.ppermute(x, axis, [(i, i ^ step) for i in range(size)])  7.84 us
    ppermute x6, starting transfers between devices, from_peer(): return lax.ppermute(x, PLANE_AXES, [(i, i ^ mask) for i in devices])  7.79 us
    pallas_call x1, Pallas kernels, per_device(): pl.pallas_call(functools.partial(forward_kernel, context, rows, edge, tap...  6.92 us
    pallas_call x1, Pallas kernels, per_device(): pl.pallas_call(functools.partial(backward_kernel, context, rows), out_sha...  6.11 us
    ppermute x6, waiting for transfers between devices, from_peer(): return lax.ppermute(x, PLANE_AXES, [(i, i ^ mask) for i in devices])  6.06 us
    pallas_call x2, Pallas kernels, score(): pl.pallas_call(functools.partial(scores_kernel, context, rows, edge, bloc...  4.9 us
  transfers between devices with their start and end apart: 20, of which 6 were waited for; matrix products, arithmetic and copies ran while one was open for 0% of the time, Pallas kernels for 20%

profile of v14, /device:TPU:0, one launch (start us, length us, event | category | flops | bytes accessed | tf_op | source)
XLA Modules:
  0.0 79.6 jit_solution(12487433222855211410)
XLA Ops:
  0.6 1.4 %pack.1 = (bf16[384,512]{1,0:T(8,128)(2,1)S(1)}, bf16[224,512]{1,0:T(8,128)(2,1)S(1)}, bf16[192,512]{1,0:T(8,128)(2,1)S(1)}, bf16[192,512]{1,0:T(8,128)(2,1)S(1)...) custom-call(bf16[192,512]{1,0:T(8,128)(2,1)} %bitcast.13, bf16[192,512]{1,0:T(8,128)(2,1)} %bitcast.14, ...), custom_call_target="tpu_custom_call" | custom-call | tf_op jit(solution)/shard_map/pack/pallas_call | solution.py:526
  2.1 5.0 %collective-permute-start.1 = (bf16[384,512]{1,0:T(8,128)(2,1)S(1)}, bf16[384,512]{1,0:T(8,128)(2,1)S(1)}, u32[]{:S(2)}, u32[]{:S(2)}) collective-permute-start(bf16[384,512]{1,0:T(8,128)(2,1)S(1)} %get-tuple-element.53.refs_0_.refs_3_.refs_2_), channel_id=1, source_target_pairs={{0,2},{1,3},{2,4},{3,5},{4,6},{5,7},{8,10},{9,11},{10,12},{11,13},... | collective-permute-start | bytes 1179656 | tf_op jit(solution)/shard_map/ppermute | solution.py:35
  7.0 3.4 %collective-permute-start = (bf16[224,512]{1,0:T(8,128)(2,1)S(1)}, bf16[224,512]{1,0:T(8,128)(2,1)S(1)}, u32[]{:S(2)}, u32[]{:S(2)}) collective-permute-start(bf16[224,512]{1,0:T(8,128)(2,1)S(1)} %get-tuple-element.54), channel_id=1, source_target_pairs={{0,1},{1,2},{2,3},{3,4},{4,5},{5,6},{6,7},{8,9},{9,10},{10,11},{11... | collective-permute-start | bytes 688136 | tf_op jit(solution)/shard_map/ppermute | solution.py:35
  10.5 1.3 %collective-permute-start.3 = (bf16[160,512]{1,0:T(8,128)(2,1)S(1)}, bf16[160,512]{1,0:T(8,128)(2,1)S(1)}, u32[]{:S(2)}, u32[]{:S(2)}) collective-permute-start(bf16[160,512]{1,0:T(8,128)(2,1)S(1)} %get-tuple-element.57), channel_id=1, source_target_pairs={{1,0},{2,1},{3,2},{4,3},{5,4},{6,5},{7,6},{9,8},{10,9},{11,10},{12... | collective-permute-start | bytes 491528 | tf_op jit(solution)/shard_map/ppermute | solution.py:35
  11.8 5.5 %collective-permute-start.2 = (bf16[64,512]{1,0:T(8,128)(2,1)S(1)}, bf16[64,512]{1,0:T(8,128)(2,1)S(1)}, u32[]{:S(2)}, u32[]{:S(2)}) collective-permute-start(bf16[64,512]{1,0:T(8,128)(2,1)S(1)} %get-tuple-element.55), channel_id=1, source_target_pairs={{0,3},{1,4},{2,5},{3,6},{4,7},{8,11},{9,12},{10,13},{11,14},{12,15... | collective-permute-start | bytes 196616 | tf_op jit(solution)/shard_map/ppermute | solution.py:35
  17.3 0.1 pad_add_fusion.device_ref.refs_0_
  17.4 0.0 collective-permute-done.1.refs_2_.odd_ref.refs_6_.refs_5_
  17.4 2.5 %collective-permute-start.4 = (bf16[192,512]{1,0:T(8,128)(2,1)S(1)}, bf16[192,512]{1,0:T(8,128)(2,1)S(1)}, u32[]{:S(2)}, u32[]{:S(2)}) collective-permute-start(bf16[192,512]{1,0:T(8,128)(2,1)S(1)} %choose.1), channel_id=1, source_target_pairs={{0,1},{1,0},{2,3},{3,2},{4,5},{5,4},{6,7},{7,6},{8,9},{9,8},{10,11... | collective-permute-start | bytes 589832 | tf_op jit(solution)/shard_map/ppermute | solution.py:554
  19.9 0.0 collective-permute-done.3.refs_3_.refs_8_
  19.9 0.0 collective-permute-done.refs_1_.refs_4_.refs_3_
  19.9 2.4 %scores.3 = (bf16[4,256,512]{2,1,0:T(8,128)(2,1)S(1)}, f32[8,128]{1,0:T(8,128)S(1)}) custom-call(s32[3]{0:T(128)S(1)} %pad_add_fusion.device_ref.refs_0_, bf16[192,512]{1,0:T(8,128)(2,1)S(1)} %get-tuple-element.52.q_ref.refs_1_, bf16[384,512]{1,0:T(8,128)(2,1)S(1)} %get-tuple-element.53.refs_0_.refs_3_.refs_2_, ...), custom_call_target="tpu_custom_call" | custom-call | flops 5000000000 | bytes 10000000 | tf_op jit(solution)/shard_map/scores/pallas_call | solution.py:572
  22.4 0.0 collective-permute-done.2.refs_3_.refs_7_
  22.4 2.5 %scores.2 = (bf16[4,256,512]{2,1,0:T(8,128)(2,1)S(1)}, f32[8,128]{1,0:T(8,128)S(1)}) custom-call(s32[3]{0:T(128)S(1)} %pad_add_fusion.device_ref.refs_0_, bf16[192,512]{1,0:T(8,128)(2,1)S(1)} %get-tuple-element.52.q_ref.refs_1_, bf16[384,512]{1,0:T(8,128)(2,1)S(1)} %get-tuple-element.53.refs_0_.refs_3_.refs_2_, ...), custom_call_target="tpu_custom_call" | custom-call | flops 5000000000 | bytes 10000000 | tf_op jit(solution)/shard_map/scores/pallas_call | solution.py:572
  24.8 0.0 collective-permute-done.4.refs_5_.refs_4_
  24.8 6.9 %forward.1 = (bf16[192,1024]{1,0:T(8,128)(2,1)}, bf16[192,512]{1,0:T(8,128)(2,1)S(1)}, bf16[192,1024]{1,0:T(8,128)(2,1)S(1)}, bf16[16,128,128]{2,1,0:T(8,128)(2,...) custom-call(s32[3]{0:T(128)S(1)} %pad_add_fusion.device_ref.refs_0_,, ...), custom_call_target="tpu_custom_call" | custom-call | flops 8000000000 | bytes 10000000 | tf_op jit(solution)/shard_map/forward/pallas_call | solution.py:594
  31.7 0.1 collective-permute-start.5
  31.8 1.9 %kernel_grad.1.rows_ref = bf16[16,16,128]{2,1,0:T(8,128)(2,1)S(1)} custom-call(f32[8,256,128]{2,1,0:T(8,128)S(1)} %get-tuple-element.66.hid, f32[8,232,128]{2,1,0:T(8,128)S(1)} %get-tuple-element.67.dm), custom_call_target="tpu_custom_call" | custom-call | flops 2000000000 | bytes 3000000 | tf_op jit(solution)/shard_map/kernel_grad/pallas_call | solution.py:633
  33.7 0.0 collective-permute-done.5.given_ref
  33.7 0.7 join.1
  34.4 2.7 %collective-permute-start.6 = (bf16[4,144,128]{2,1,0:T(8,128)(2,1)S(1)}, bf16[4,144,128]{2,1,0:T(8,128)(2,1)S(1)}, u32[]{:S(2)}, u32[]{:S(2)}) collective-permute-start(bf16[4,144,128]{2,1,0:T(8,128)(2,1)S(1)} %get-tuple-element.77), channel_id=1, source_target_pairs={{0,1},{1,0},{16,17},{17,16},{2,3},{3,2},{18,19},{19,18},{4,5},{5,4... | collective-permute-start | bytes 442376 | tf_op jit(solution)/shard_map/ppermute | solution.py:490
  37.1 1.5 %collective-permute-start.7 = (bf16[4,144,128]{2,1,0:T(8,128)(2,1)S(1)}, bf16[4,144,128]{2,1,0:T(8,128)(2,1)S(1)}, u32[]{:S(2)}, u32[]{:S(2)}) collective-permute-start(bf16[4,144,128]{2,1,0:T(8,128)(2,1)S(1)} %get-tuple-element.78), channel_id=1, source_target_pairs={{0,16},{1,17},{16,0},{17,1},{2,18},{3,19},{18,2},{19,3},{4,20},{5,... | collective-permute-start | bytes 442376 | tf_op jit(solution)/shard_map/ppermute | solution.py:490
  38.6 0.1 collective-permute-start.8
  38.6 6.1 %backward.1 = (bf16[192,512]{1,0:T(8,128)(2,1)}, f32[384,512]{1,0:T(8,128)S(1)}, bf16[384,512]{1,0:T(8,128)(2,1)S(1)}, bf16[384,512]{1,0:T(8,128)(2,1)S(1)}) custom-call(s32[3]{0:T(128)S(1)} %pad_add_fusion.device_ref.refs_0_, bf16[192,512]{1,0:T(8,128)(2,1)S(1)} %get-tuple-element.52.q_ref.refs_1_, ...), custom_call_target="tpu_custom_call" | custom-call | flops 6000000000 | bytes 10000000 | tf_op jit(solution)/shard_map/backward/pallas_call | solution.py:658
  44.7 0.0 collective-permute-done.6
  44.7 0.0 collective-permute-done.7
  44.7 1.3 %collective-permute-done.8 = bf16[4,144,128]{2,1,0:T(8,128)(2,1)S(1)} collective-permute-done((bf16[4,144,128]{2,1,0:T(8,128)(2,1)S(1)}, bf16[4,144,128]{2,1,0:T(8,128)(2,1)S(1)}, u32[]{:S(2)}, u32[]{:S(2)}) %collective-permute-start.8) | collective-permute-done | bytes 147488 | tf_op jit(solution)/shard_map/ppermute | solution.py:490
  46.0 0.1 add_convert_fusion.2
  46.1 3.7 %collective-permute-start.9 = (bf16[4,144,128]{2,1,0:T(8,128)(2,1)S(1)}, bf16[4,144,128]{2,1,0:T(8,128)(2,1)S(1)}, u32[]{:S(2)}, u32[]{:S(2)}) collective-permute-start(bf16[4,144,128]{2,1,0:T(8,128)(2,1)S(1)} %add_convert_fusion.2), channel_id=1, source_target_pairs={{0,2},{2,0},{4,6},{6,4},{1,3},{3,1},{5,7},{7,5},{8,10},{10,8},{12,... | collective-permute-start | bytes 442376 | tf_op jit(solution)/shard_map/ppermute | solution.py:496
  49.8 1.0 %collective-permute-start.11 = (bf16[384,512]{1,0:T(8,128)(2,1)S(1)}, bf16[384,512]{1,0:T(8,128)(2,1)S(1)}, u32[]{:S(2)}, u32[]{:S(2)}) collective-permute-start(bf16[384,512]{1,0:T(8,128)(2,1)S(1)} %get-tuple-element.83), channel_id=1, source_target_pairs={{0,1},{1,0},{2,3},{3,2},{4,5},{5,4},{6,7},{7,6},{8,9},{9,8},{10,11... | collective-permute-start | bytes 1179656 | tf_op jit(solution)/shard_map/ppermute | solution.py:685
  50.8 2.4 %collective-permute-done.9 = bf16[4,144,128]{2,1,0:T(8,128)(2,1)S(1)} collective-permute-done((bf16[4,144,128]{2,1,0:T(8,128)(2,1)S(1)}, bf16[4,144,128]{2,1,0:T(8,128)(2,1)S(1)}, u32[]{:S(2)}, u32[]{:S(2)}) %collective-permute-start.9) | collective-permute-done | bytes 147488 | tf_op jit(solution)/shard_map/ppermute | solution.py:496
  53.3 4.6 %collective-permute-start.10 = (bf16[4,144,128]{2,1,0:T(8,128)(2,1)S(1)}, bf16[4,144,128]{2,1,0:T(8,128)(2,1)S(1)}, u32[]{:S(2)}, u32[]{:S(2)}) collective-permute-start(bf16[4,144,128]{2,1,0:T(8,128)(2,1)S(1)} %add_convert_fusion.1), channel_id=1, source_target_pairs={{0,4},{2,6},{4,0},{6,2},{1,5},{3,7},{5,1},{7,3},{8,12},{10,14},{12... | collective-permute-start | bytes 442376 | tf_op jit(solution)/shard_map/ppermute | solution.py:496
  57.8 5.4 %collective-permute-done.10 = bf16[4,144,128]{2,1,0:T(8,128)(2,1)S(1)} collective-permute-done((bf16[4,144,128]{2,1,0:T(8,128)(2,1)S(1)}, bf16[4,144,128]{2,1,0:T(8,128)(2,1)S(1)}, u32[]{:S(2)}, u32[]{:S(2)}) %collective-permute-start.10) | collective-permute-done | bytes 147488 | tf_op jit(solution)/shard_map/ppermute | solution.py:496
  63.3 0.0 collective-permute-done.11.swapped_ref.refs_1_
  63.3 0.7 relay.1
  64.0 1.3 %collective-permute-start.19 = (bf16[384,512]{1,0:T(8,128)(2,1)S(1)}, bf16[384,512]{1,0:T(8,128)(2,1)S(1)}, u32[]{:S(2)}, u32[]{:S(2)}) collective-permute-start(bf16[384,512]{1,0:T(8,128)(2,1)S(1)} %relay.1), channel_id=1, source_target_pairs={{2,0},{3,1},{4,2},{5,3},{6,4},{7,5},{10,8},{11,9},{12,10},{13,11},... | collective-permute-start | bytes 1179656 | tf_op jit(solution)/shard_map/ppermute | solution.py:35
  65.3 2.3 %collective-permute-start.17 = (bf16[4,144,128]{2,1,0:T(8,128)(2,1)S(1)}, bf16[4,144,128]{2,1,0:T(8,128)(2,1)S(1)}, u32[]{:S(2)}, u32[]{:S(2)}) collective-permute-start(bf16[4,144,128]{2,1,0:T(8,128)(2,1)S(1)} %add_convert_fusion.refs_0_), channel_id=1, source_target_pairs={{0,17},{1,16},{16,1},{17,0},{2,19},{3,18},{18,3},{19,2},{4,21},{5,... | collective-permute-start | bytes 442376 | tf_op jit(solution)/shard_map/ppermute | solution.py:490
  67.5 0.5 collective-permute-start.15
  68.1 0.8 collective-permute-start.13
  68.8 0.0 collective-permute-start.12
  68.8 1.3 %unpack_early.1.refs_8_ = f32[512,1024]{1,0:T(8,128)} custom-call(s32[3]{0:T(128)S(1)} %pad_add_fusion.device_ref.refs_0_, bf16[4,144,128]{2,1,0:T(8,128)(2,1)S(1)} %add_convert_fusion.refs_0_), custom_call_target="tpu_custom_call" | custom-call | flops 1000000000 | bytes 3000000 | tf_op jit(solution)/shard_map/unpack_early/pallas_call | solution.py:726
  70.1 2.9 %collective-permute-done.17.refs_3_ = bf16[4,144,128]{2,1,0:T(8,128)(2,1)S(1)} collective-permute-done((bf16[4,144,128]{2,1,0:T(8,128)(2,1)S(1)}, bf16[4,144,128]{2,1,0:T(8,128)(2,1)S(1)}, u32[]{:S(2)}, u32[]{:S(2)}) %collective-permute-start.17) | collective-permute-done | bytes 147488 | tf_op jit(solution)/shard_map/ppermute | solution.py:490
  73.0 0.0 collective-permute-start.18
  73.0 1.9 %collective-permute-done.15.refs_2_ = bf16[4,144,128]{2,1,0:T(8,128)(2,1)S(1)} collective-permute-done((bf16[4,144,128]{2,1,0:T(8,128)(2,1)S(1)}, bf16[4,144,128]{2,1,0:T(8,128)(2,1)S(1)}, u32[]{:S(2)}, u32[]{:S(2)}) %collective-permute-start.15) | collective-permute-done | bytes 147488 | tf_op jit(solution)/shard_map/ppermute | solution.py:490
  74.9 0.0 collective-permute-start.16
  74.9 0.0 collective-permute-done.13.refs_1_
  74.9 0.5 collective-permute-start.14
  75.4 0.9 %collective-permute-done.19.refs_0_ = bf16[384,512]{1,0:T(8,128)(2,1)S(1)} collective-permute-done((bf16[384,512]{1,0:T(8,128)(2,1)S(1)}, bf16[384,512]{1,0:T(8,128)(2,1)S(1)}, u32[]{:S(2)}, u32[]{:S(2)}) %collective-permute-start.19) | collective-permute-done | bytes 393248 | tf_op jit(solution)/shard_map/ppermute | solution.py:35
  76.3 1.4 %merge.1 = (bf16[192,512]{1,0:T(8,128)(2,1)}, bf16[192,512]{1,0:T(8,128)(2,1)}) custom-call(s32[3]{0:T(128)S(1)} %pad_add_fusion.device_ref.refs_0_, bf16[384,512]{1,0:T(8,128)(2,1)S(1)} %collective-permute-done.19.refs_0_, bf16[384,512]{1,0:T(8,128)(2,1)S(1)} %collective-permute-done.11.swapped_ref.refs_1_, f32[384,512]{1,0:T(8,128)S(1)} %get-tuple-element.87.refs_2_), custom_call_target="tpu_custom_call" | custom-call | flops 16000000000 | bytes 10000000 | tf_op jit(solution)/shard_map/merge/pallas_call | solution.py:703
  77.7 0.0 collective-permute-done.12.refs_4_
  77.7 0.0 collective-permute-done.18.refs_7_
  77.7 0.0 collective-permute-done.16.refs_6_
  77.7 0.0 collective-permute-done.14.refs_5_
  77.7 1.9 %unpack_late.1 = (f32[512,1024]{1,0:T(8,128)}, f32[31,1024]{1,0:T(8,128)}) custom-call(s32[3]{0:T(128)S(1)} %pad_add_fusion.device_ref.refs_0_, bf16[4,144,128]{2,1,0:T(8,128)(2,1)S(1)} %add_convert_fusion.refs_0_, bf16[4,144,128]{2,1,0:T(8,128)(2,1)S(1)} %collective-permute-done.13.refs_1_, ...), custom_call_target="tpu_custom_call", output_to_operand_aliasing={{0}: (9, {})} | custom-call | tf_op jit(solution)/shard_map/unpack_late/pallas_call | solution.py:739
  (3 shorter events, 0.1 us)
Async XLA Ops:
  2.1 15.3 %collective-permute-start.1 = (bf16[384,512]{1,0:T(8,128)(2,1)S(1)}, bf16[384,512]{1,0:T(8,128)(2,1)S(1)}, u32[]{:S(2)}, u32[]{:S(2)}) collective-permute-start(bf16[384,512]{1,0:T(8,128)(2,1)S(1)} %get-tuple-element.53.refs_0_.refs_3_.refs_2_), channel_id=1, source_target_pairs={{0,2},{1,3},{2,4},{3,5},{4,6},{5,7},{8,10},{9,11},{10,12},{11,13},... | collective-permute-start | bytes 1179656 | tf_op jit(solution)/shard_map/ppermute | solution.py:35
  7.0 12.9 %collective-permute-start = (bf16[224,512]{1,0:T(8,128)(2,1)S(1)}, bf16[224,512]{1,0:T(8,128)(2,1)S(1)}, u32[]{:S(2)}, u32[]{:S(2)}) collective-permute-start(bf16[224,512]{1,0:T(8,128)(2,1)S(1)} %get-tuple-element.54), channel_id=1, source_target_pairs={{0,1},{1,2},{2,3},{3,4},{4,5},{5,6},{6,7},{8,9},{9,10},{10,11},{11... | collective-permute-start | bytes 688136 | tf_op jit(solution)/shard_map/ppermute | solution.py:35
  10.5 9.4 %collective-permute-start.3 = (bf16[160,512]{1,0:T(8,128)(2,1)S(1)}, bf16[160,512]{1,0:T(8,128)(2,1)S(1)}, u32[]{:S(2)}, u32[]{:S(2)}) collective-permute-start(bf16[160,512]{1,0:T(8,128)(2,1)S(1)} %get-tuple-element.57), channel_id=1, source_target_pairs={{1,0},{2,1},{3,2},{4,3},{5,4},{6,5},{7,6},{9,8},{10,9},{11,10},{12... | collective-permute-start | bytes 491528 | tf_op jit(solution)/shard_map/ppermute | solution.py:35
  11.8 10.6 %collective-permute-start.2 = (bf16[64,512]{1,0:T(8,128)(2,1)S(1)}, bf16[64,512]{1,0:T(8,128)(2,1)S(1)}, u32[]{:S(2)}, u32[]{:S(2)}) collective-permute-start(bf16[64,512]{1,0:T(8,128)(2,1)S(1)} %get-tuple-element.55), channel_id=1, source_target_pairs={{0,3},{1,4},{2,5},{3,6},{4,7},{8,11},{9,12},{10,13},{11,14},{12,15... | collective-permute-start | bytes 196616 | tf_op jit(solution)/shard_map/ppermute | solution.py:35
  17.4 7.4 %collective-permute-start.4 = (bf16[192,512]{1,0:T(8,128)(2,1)S(1)}, bf16[192,512]{1,0:T(8,128)(2,1)S(1)}, u32[]{:S(2)}, u32[]{:S(2)}) collective-permute-start(bf16[192,512]{1,0:T(8,128)(2,1)S(1)} %choose.1), channel_id=1, source_target_pairs={{0,1},{1,0},{2,3},{3,2},{4,5},{5,4},{6,7},{7,6},{8,9},{9,8},{10,11... | collective-permute-start | bytes 589832 | tf_op jit(solution)/shard_map/ppermute | solution.py:554
  31.7 2.0 %collective-permute-start.5 = (bf16[16,128,128]{2,1,0:T(8,128)(2,1)S(1)}, bf16[16,128,128]{2,1,0:T(8,128)(2,1)S(1)}, u32[]{:S(2)}, u32[]{:S(2)}) collective-permute-start(bf16[16,128,128]{2,1,0:T(8,128)(2,1)S(1)} %get-tuple-element.65), channel_id=1, source_target_pairs={{0,8},{8,0},{1,9},{9,1},{2,10},{10,2},{3,11},{11,3},{4,12},{12,4},... | collective-permute-start | bytes 1572872 | tf_op jit(solution)/shard_map/ppermute | solution.py:503
  34.4 10.3 %collective-permute-start.6 = (bf16[4,144,128]{2,1,0:T(8,128)(2,1)S(1)}, bf16[4,144,128]{2,1,0:T(8,128)(2,1)S(1)}, u32[]{:S(2)}, u32[]{:S(2)}) collective-permute-start(bf16[4,144,128]{2,1,0:T(8,128)(2,1)S(1)} %get-tuple-element.77), channel_id=1, source_target_pairs={{0,1},{1,0},{16,17},{17,16},{2,3},{3,2},{18,19},{19,18},{4,5},{5,4... | collective-permute-start | bytes 442376 | tf_op jit(solution)/shard_map/ppermute | solution.py:490
  37.1 7.7 %collective-permute-start.7 = (bf16[4,144,128]{2,1,0:T(8,128)(2,1)S(1)}, bf16[4,144,128]{2,1,0:T(8,128)(2,1)S(1)}, u32[]{:S(2)}, u32[]{:S(2)}) collective-permute-start(bf16[4,144,128]{2,1,0:T(8,128)(2,1)S(1)} %get-tuple-element.78), channel_id=1, source_target_pairs={{0,16},{1,17},{16,0},{17,1},{2,18},{3,19},{18,2},{19,3},{4,20},{5,... | collective-permute-start | bytes 442376 | tf_op jit(solution)/shard_map/ppermute | solution.py:490
  38.6 7.4 %collective-permute-start.8 = (bf16[4,144,128]{2,1,0:T(8,128)(2,1)S(1)}, bf16[4,144,128]{2,1,0:T(8,128)(2,1)S(1)}, u32[]{:S(2)}, u32[]{:S(2)}) collective-permute-start(bf16[4,144,128]{2,1,0:T(8,128)(2,1)S(1)} %get-tuple-element.79), channel_id=1, source_target_pairs={{0,17},{1,16},{16,1},{17,0},{2,19},{3,18},{18,3},{19,2},{4,21},{5,... | collective-permute-start | bytes 442376 | tf_op jit(solution)/shard_map/ppermute | solution.py:490
  46.1 7.1 %collective-permute-start.9 = (bf16[4,144,128]{2,1,0:T(8,128)(2,1)S(1)}, bf16[4,144,128]{2,1,0:T(8,128)(2,1)S(1)}, u32[]{:S(2)}, u32[]{:S(2)}) collective-permute-start(bf16[4,144,128]{2,1,0:T(8,128)(2,1)S(1)} %add_convert_fusion.2), channel_id=1, source_target_pairs={{0,2},{2,0},{4,6},{6,4},{1,3},{3,1},{5,7},{7,5},{8,10},{10,8},{12,... | collective-permute-start | bytes 442376 | tf_op jit(solution)/shard_map/ppermute | solution.py:496
  49.8 13.5 %collective-permute-start.11 = (bf16[384,512]{1,0:T(8,128)(2,1)S(1)}, bf16[384,512]{1,0:T(8,128)(2,1)S(1)}, u32[]{:S(2)}, u32[]{:S(2)}) collective-permute-start(bf16[384,512]{1,0:T(8,128)(2,1)S(1)} %get-tuple-element.83), channel_id=1, source_target_pairs={{0,1},{1,0},{2,3},{3,2},{4,5},{5,4},{6,7},{7,6},{8,9},{9,8},{10,11... | collective-permute-start | bytes 1179656 | tf_op jit(solution)/shard_map/ppermute | solution.py:685
  53.3 10.0 %collective-permute-start.10 = (bf16[4,144,128]{2,1,0:T(8,128)(2,1)S(1)}, bf16[4,144,128]{2,1,0:T(8,128)(2,1)S(1)}, u32[]{:S(2)}, u32[]{:S(2)}) collective-permute-start(bf16[4,144,128]{2,1,0:T(8,128)(2,1)S(1)} %add_convert_fusion.1), channel_id=1, source_target_pairs={{0,4},{2,6},{4,0},{6,2},{1,5},{3,7},{5,1},{7,3},{8,12},{10,14},{12... | collective-permute-start | bytes 442376 | tf_op jit(solution)/shard_map/ppermute | solution.py:496
  64.0 12.4 %collective-permute-start.19 = (bf16[384,512]{1,0:T(8,128)(2,1)S(1)}, bf16[384,512]{1,0:T(8,128)(2,1)S(1)}, u32[]{:S(2)}, u32[]{:S(2)}) collective-permute-start(bf16[384,512]{1,0:T(8,128)(2,1)S(1)} %relay.1), channel_id=1, source_target_pairs={{2,0},{3,1},{4,2},{5,3},{6,4},{7,5},{10,8},{11,9},{12,10},{13,11},... | collective-permute-start | bytes 1179656 | tf_op jit(solution)/shard_map/ppermute | solution.py:35
  65.3 7.8 %collective-permute-start.17 = (bf16[4,144,128]{2,1,0:T(8,128)(2,1)S(1)}, bf16[4,144,128]{2,1,0:T(8,128)(2,1)S(1)}, u32[]{:S(2)}, u32[]{:S(2)}) collective-permute-start(bf16[4,144,128]{2,1,0:T(8,128)(2,1)S(1)} %add_convert_fusion.refs_0_), channel_id=1, source_target_pairs={{0,17},{1,16},{16,1},{17,0},{2,19},{3,18},{18,3},{19,2},{4,21},{5,... | collective-permute-start | bytes 442376 | tf_op jit(solution)/shard_map/ppermute | solution.py:490
  67.5 7.4 %collective-permute-start.15 = (bf16[4,144,128]{2,1,0:T(8,128)(2,1)S(1)}, bf16[4,144,128]{2,1,0:T(8,128)(2,1)S(1)}, u32[]{:S(2)}, u32[]{:S(2)}) collective-permute-start(bf16[4,144,128]{2,1,0:T(8,128)(2,1)S(1)} %add_convert_fusion.refs_0_), channel_id=1, source_target_pairs={{0,16},{1,17},{16,0},{17,1},{2,18},{3,19},{18,2},{19,3},{4,20},{5,... | collective-permute-start | bytes 442376 | tf_op jit(solution)/shard_map/ppermute | solution.py:490
  68.1 6.8 %collective-permute-start.13 = (bf16[4,144,128]{2,1,0:T(8,128)(2,1)S(1)}, bf16[4,144,128]{2,1,0:T(8,128)(2,1)S(1)}, u32[]{:S(2)}, u32[]{:S(2)}) collective-permute-start(bf16[4,144,128]{2,1,0:T(8,128)(2,1)S(1)} %add_convert_fusion.refs_0_), channel_id=1, source_target_pairs={{0,1},{1,0},{16,17},{17,16},{2,3},{3,2},{18,19},{19,18},{4,5},{5,4... | collective-permute-start | bytes 442376 | tf_op jit(solution)/shard_map/ppermute | solution.py:490
  68.8 8.9 %collective-permute-start.12 = (bf16[4,144,128]{2,1,0:T(8,128)(2,1)S(1)}, bf16[4,144,128]{2,1,0:T(8,128)(2,1)S(1)}, u32[]{:S(2)}, u32[]{:S(2)}) collective-permute-start(bf16[4,144,128]{2,1,0:T(8,128)(2,1)S(1)} %add_convert_fusion.refs_0_), channel_id=1, source_target_pairs={{0,8},{8,0},{1,9},{9,1},{2,10},{10,2},{3,11},{11,3},{4,12},{12,4},... | collective-permute-start | bytes 442376 | tf_op jit(solution)/shard_map/ppermute | solution.py:503
  73.0 4.7 %collective-permute-start.18 = (bf16[4,144,128]{2,1,0:T(8,128)(2,1)S(1)}, bf16[4,144,128]{2,1,0:T(8,128)(2,1)S(1)}, u32[]{:S(2)}, u32[]{:S(2)}) collective-permute-start(bf16[4,144,128]{2,1,0:T(8,128)(2,1)S(1)} %collective-permute-done.17.refs_3_), channel_id=1, source_target_pairs={{0,8},{8,0},{1,9},{9,1},{2,10},{10,2},{3,11},{11,3},{4,12},{12,4},... | collective-permute-start | bytes 442376 | tf_op jit(solution)/shard_map/ppermute | solution.py:503
  74.9 2.8 %collective-permute-start.16 = (bf16[4,144,128]{2,1,0:T(8,128)(2,1)S(1)}, bf16[4,144,128]{2,1,0:T(8,128)(2,1)S(1)}, u32[]{:S(2)}, u32[]{:S(2)}) collective-permute-start(bf16[4,144,128]{2,1,0:T(8,128)(2,1)S(1)} %collective-permute-done.15.refs_2_), channel_id=1, source_target_pairs={{0,8},{8,0},{1,9},{9,1},{2,10},{10,2},{3,11},{11,3},{4,12},{12,4},... | collective-permute-start | bytes 442376 | tf_op jit(solution)/shard_map/ppermute | solution.py:503
  74.9 2.8 %collective-permute-start.14 = (bf16[4,144,128]{2,1,0:T(8,128)(2,1)S(1)}, bf16[4,144,128]{2,1,0:T(8,128)(2,1)S(1)}, u32[]{:S(2)}, u32[]{:S(2)}) collective-permute-start(bf16[4,144,128]{2,1,0:T(8,128)(2,1)S(1)} %collective-permute-done.13.refs_1_), channel_id=1, source_target_pairs={{0,8},{8,0},{1,9},{9,1},{2,10},{10,2},{3,11},{11,3},{4,12},{12,4},... | collective-permute-start | bytes 442376 | tf_op jit(solution)/shard_map/ppermute | solution.py:503

commit v15 on v13

--- a/solution.py
+++ b/solution.py
@@ -40,6 +40,16 @@
 
 def cost(flops, data):
     return pl.CostEstimate(flops=flops, bytes_accessed=data, transcendentals=0)
+
+
+def located(kernel, split):
+    def run(*refs):
+        device = lax.axis_index("z") * 2 + lax.axis_index("y")
+        core = lax.axis_index("core") if split else 0
+        spot = lax.axis_index("x") * 2 + lax.axis_index("y") if split else 0
+        return kernel((device, core, spot), *refs)
+
+    return run
 
 
 def head_masks():
@@ -490,7 +500,6 @@
     bf16, f32 = jnp.bfloat16, jnp.float32
     query, key, value, cot = queries[0], key_in[0], value_in[0], cotangent[0]
     runs = lax.axis_size(RUN_AXES)
-    device = lax.axis_index(RUN_AXES).astype(jnp.int32)
     rows, att = query.shape
     width = out_weight.shape[1]
     heads = att // HEAD_DIM
@@ -502,9 +511,13 @@
     key_rows = query_rows + context * rows
     chunks = width // LANES
     vmem = pl.BlockSpec(memory_space=pltpu.VMEM)
-    smem = pl.BlockSpec(memory_space=pltpu.SMEM)
     hbm = pl.BlockSpec(memory_space=pltpu.HBM)
     params = pltpu.CompilerParams(vmem_limit_bytes=VMEM_LIMIT)
+
+    pieces = att // 32
+    layers = lax.axis_size("z")
+    split = pieces == layers * lax.axis_size(PLANE_AXES) and layers & (layers - 1) == 0
+    plane = lax.axis_size(PLANE_AXES)
 
     own, keys, values, packed_query, far, near = pl.pallas_call(
         functools.partial(pack_kernel, edge),
@@ -527,38 +540,31 @@
     near = shifted(near, -1)
     if further:
         values = pl.pallas_call(
-            choose_kernel,
+            located(choose_kernel, split),
             out_shape=jax.ShapeDtypeStruct((rows, att), bf16),
-            in_specs=[smem, vmem, vmem],
+            in_specs=[vmem, vmem],
             out_specs=vmem,
             compiler_params=params,
             name="choose",
-        )(device[None], values, further[0])
+        )(values, further[0])
         values = lax.ppermute(values, "y", [(0, 1), (1, 0)])
     else:
         values = shifted(values, 1)
     tiles = [own, keys, values, *further]
     far = shifted(far, context + 1)
 
-    pieces = att // 32
-    layers = lax.axis_size("z")
-    split = pieces == layers * lax.axis_size(PLANE_AXES) and layers & (layers - 1) == 0
-    core = lax.axis_index("core").astype(jnp.int32) if split else jnp.int32(0)
-    plane = lax.axis_size(PLANE_AXES)
-    spot = lax.axis_index(PLANE_AXES).astype(jnp.int32) if split else jnp.int32(0)
-    place = jnp.stack([device, core, spot])
     blocks = query_rows // LANES
     pairs = att // LANES
     key_span = context * rows + LANES
 
     def score(blocks, edge_rows):
         return pl.pallas_call(
-            functools.partial(scores_kernel, context, rows, edge, blocks),
+            located(functools.partial(scores_kernel, context, rows, edge, blocks), split),
             out_shape=(
                 jax.ShapeDtypeStruct((len(blocks) * pairs, 2 * LANES, key_span), bf16),
                 jax.ShapeDtypeStruct((heads, len(blocks) * LANES), f32),
             ),
-            in_specs=[smem] + [vmem] * (3 + context),
+            in_specs=[vmem] * (3 + context),
             out_specs=(vmem,) * 2,
             scratch_shapes=[
                 pltpu.VMEM((query_rows, att), bf16),
@@ -569,12 +575,12 @@
             compiler_params=params,
             cost_estimate=cost(5 * 10**9, 10**7),
             name="scores",
-        )(place, packed_query, own, keys, *further, edge_rows)
+        )(packed_query, own, keys, *further, edge_rows)
 
     early, early_sums = score(list(range(1, blocks)), near)
     late, late_sums = score([0], far)
     out_frames, attended, dhidden, keep, give, hidden, dmixed, held_weight = pl.pallas_call(
-        functools.partial(forward_kernel, context, rows, edge, taps),
+        located(functools.partial(forward_kernel, context, rows, edge, taps), split),
         out_shape=(
             jax.ShapeDtypeStruct((rows, width), bf16),
             jax.ShapeDtypeStruct((rows, att), bf16),
@@ -586,7 +592,7 @@
             jax.ShapeDtypeStruct((chunks, rows + edge + 8, LANES), f32),
             jax.ShapeDtypeStruct((att, width), bf16),
         ),
-        in_specs=[smem] + [vmem] * (6 + context) + [hbm] * 3,
+        in_specs=[vmem] * (6 + context) + [hbm] * 3,
         out_specs=(hbm,) + (vmem,) * 7,
         scratch_shapes=[
             pltpu.VMEM((key_rows, att), bf16),
@@ -602,7 +608,6 @@
         cost_estimate=cost(8 * 10**9, 10**7),
         name="forward",
     )(
-        place,
         late,
         early,
         *tiles,
@@ -628,23 +633,23 @@
 
     if split:
         slabs = pl.pallas_call(
-            join_kernel,
+            located(join_kernel, split),
             out_shape=(jax.ShapeDtypeStruct((layers, 18 * chunks, LANES), bf16),) * plane,
-            in_specs=[smem] + [vmem] * 3,
+            in_specs=[vmem] * 3,
             out_specs=(vmem,) * plane,
             compiler_params=params,
             name="join",
-        )(place, keep, other_core(give), kernel_rows)
+        )(keep, other_core(give), kernel_rows)
         *slabs, dhidden = lax.optimization_barrier((*slabs, dhidden))
         slabs = [slabs[0]] + [from_peer(slabs[mask], mask) for mask in range(1, plane)]
     query_grad, own_grads, *messages = pl.pallas_call(
-        functools.partial(backward_kernel, context, rows),
+        located(functools.partial(backward_kernel, context, rows), split),
         out_shape=(
             jax.ShapeDtypeStruct((rows, att), bf16),
             jax.ShapeDtypeStruct((2 * rows, att), f32),
         )
         + (jax.ShapeDtypeStruct((2 * rows, att), bf16),) * context,
-        in_specs=[smem] + [vmem] * (8 + context),
+        in_specs=[vmem] * (8 + context),
         out_specs=(vmem,) * (2 + context),
         scratch_shapes=[
             pltpu.VMEM((rows, att), bf16),
@@ -654,7 +659,7 @@
         compiler_params=params,
         cost_estimate=cost(6 * 10**9, 10**7),
         name="backward",
-    )(place, packed_query, *tiles, attended, late_sums, early_sums, dhidden, held_weight)
+    )(packed_query, *tiles, attended, late_sums, early_sums, dhidden, held_weight)
     if split:
         mine = sum(slab.astype(f32) for slab in slabs).astype(bf16)
         mine, *messages = lax.optimization_barrier((mine, *messages))
@@ -662,14 +667,14 @@
     if context > 1:
         swapped = lax.ppermute(messages.pop(1), "y", [(0, 1), (1, 0)])
         messages[2] = pl.pallas_call(
-            relay_kernel,
+            located(relay_kernel, split),
             out_shape=jax.ShapeDtypeStruct((2 * rows, att), bf16),
-            in_specs=[smem] + [vmem] * 2,
+            in_specs=[vmem] * 2,
             out_specs=vmem,
             compiler_params=params,
             cost_estimate=cost(25 * 10**9, 10**7),
             name="relay",
-        )(place, swapped, messages[2])
+        )(swapped, messages[2])
     else:
         swapped = jnp.zeros((2 * rows, att), bf16)
     if split:
@@ -679,14 +684,14 @@
     if split:
         near_slabs = [mine] + [from_peer(mine, mask) for mask in range(1, plane)]
     key_grad, value_grad = pl.pallas_call(
-        merge_kernel,
+        located(merge_kernel, split),
         out_shape=(jax.ShapeDtypeStruct((rows, att), bf16),) * 2,
-        in_specs=[smem] + [vmem] * (2 + len(messages)),
+        in_specs=[vmem] * (2 + len(messages)),
         out_specs=(vmem,) * 2,
         compiler_params=params,
         cost_estimate=cost(16 * 10**9, 10**7),
         name="merge",
-    )(place, *messages, swapped, own_grads)
+    )(*messages, swapped, own_grads)
     if split:
         far_slabs = [other_core(slab) for slab in near_slabs]
         far_slabs, key_grad, value_grad = lax.optimization_barrier(
@@ -702,9 +707,9 @@
         return pltpu.VMEM((count, att // 2 // plane, width), f32)
 
     weight_total = pl.pallas_call(
-        unpack_early_kernel,
+        located(unpack_early_kernel, split),
         out_shape=jax.ShapeDtypeStruct((att, width), f32),
-        in_specs=[smem] + [vmem] * len(EARLY_SLABS),
+        in_specs=[vmem] * len(EARLY_SLABS),
         out_specs=hbm,
         scratch_shapes=[
             slab_scratch(len(EARLY_SLABS)),
@@ -713,14 +718,14 @@
         compiler_params=params,
         cost_estimate=cost(10**9, 3 * 10**6),
         name="unpack_early",
-    )(place, *[near_slabs[slab] for slab in EARLY_SLABS])
+    )(*[near_slabs[slab] for slab in EARLY_SLABS])
     weight_total, kernel_total = pl.pallas_call(
-        unpack_late_kernel,
+        located(unpack_late_kernel, split),
         out_shape=(
             jax.ShapeDtypeStruct((att, width), f32),
             jax.ShapeDtypeStruct((taps, width), f32),
         ),
-        in_specs=[smem] + [vmem] * (2 * plane) + [hbm],
+        in_specs=[vmem] * (2 * plane) + [hbm],
         out_specs=(hbm, hbm),
         scratch_shapes=[
             slab_scratch(len(LATE_SLABS)),
@@ -731,10 +736,10 @@
             pltpu.SemaphoreType.DMA((plane,)),
             pltpu.SemaphoreType.DMA,
         ],
-        input_output_aliases={1 + 2 * plane: 0},
+        input_output_aliases={2 * plane: 0},
         compiler_params=params,
         name="unpack_late",
-    )(place, *near_slabs, *far_slabs, weight_total)
+    )(*near_slabs, *far_slabs, weight_total)
     return (
         out_frames[None],
         query_grad[None],

time: 78.2 us -> 75.9 us (0.971)
  Pallas kernels: 24.9 us -> 20.4 us
  waiting for transfers between devices: 16.2 us -> 18.4 us
    pallas_call x10, Pallas kernels: 21.6 us -> 17.1 us  [the longest x1 6.69 us: per_device(): pl.pallas_call(located(functools.partial(forward_kernel, context, rows, e...]
    ppermute x6, waiting for transfers between devices: 5.84 us -> 6.92 us  [from_peer(): return lax.ppermute(x, PLANE_AXES, [(i, i ^ mask) for i in devices])]
    ppermute x1, waiting for transfers between devices: 0.92 us -> 1.99 us  [per_device(): values = lax.ppermute(values, 'y', [(0, 1), (1, 0)])]
  transfers between devices with their start and end apart: 20 -> 20, of which waited for: 7 -> 7; matrix products, arithmetic and copies ran while one was open for 0% -> 0% of each run, Pallas kernels for 17% -> 14%
where the time goes in v15:
time: 75.9 us; the launch traced here: 75.6 us
  starting transfers between devices  35.9 us (47%)
  Pallas kernels  20.4 us (27%)
  waiting for transfers between devices  18.4 us (24%)
  between operations  0.78 us (1%)
    ppermute x5, starting transfers between devices, shifted(): lax.ppermute(x, RUN_AXES, [(i, i + by) for i in devices if i + by in devi...  16.5 us
    ppermute x2, starting transfers between devices, summed_along(): other = lax.ppermute(x, axis, [(i, i ^ step) for i in range(size)])  8.86 us
    ppermute x2, waiting for transfers between devices, summed_along(): other = lax.ppermute(x, axis, [(i, i ^ step) for i in range(size)])  8.46 us
    ppermute x6, starting transfers between devices, from_peer(): return lax.ppermute(x, PLANE_AXES, [(i, i ^ mask) for i in devices])  7.11 us
    ppermute x6, waiting for transfers between devices, from_peer(): return lax.ppermute(x, PLANE_AXES, [(i, i ^ mask) for i in devices])  6.92 us
    pallas_call x1, Pallas kernels, per_device(): pl.pallas_call(located(functools.partial(forward_kernel, context, rows, e...  6.69 us
    pallas_call x1, Pallas kernels, per_device(): pl.pallas_call(located(functools.partial(backward_kernel, context, rows),...  5.44 us
    ppermute x1, starting transfers between devices, per_device(): values = lax.ppermute(values, 'y', [(0, 1), (1, 0)])  2.48 us
  transfers between devices with their start and end apart: 20, of which 7 were waited for; matrix products, arithmetic and copies ran while one was open for 0% of the time, Pallas kernels for 14%

profile of v15, /device:TPU:0, one launch (start us, length us, event | category | flops | bytes accessed | tf_op | source)
XLA Modules:
  0.0 75.6 jit_solution(16035488926161921169)
XLA Ops:
  0.6 1.4 %pack.1 = (bf16[384,512]{1,0:T(8,128)(2,1)S(1)}, bf16[224,512]{1,0:T(8,128)(2,1)S(1)}, bf16[192,512]{1,0:T(8,128)(2,1)S(1)}, bf16[192,512]{1,0:T(8,128)(2,1)S(1)...) custom-call(bf16[192,512]{1,0:T(8,128)(2,1)} %bitcast.10, bf16[192,512]{1,0:T(8,128)(2,1)} %bitcast.11, ...), custom_call_target="tpu_custom_call" | custom-call | tf_op jit(solution)/shard_map/pack/pallas_call | solution.py:522
  2.1 5.0 %collective-permute-start.1 = (bf16[384,512]{1,0:T(8,128)(2,1)S(1)}, bf16[384,512]{1,0:T(8,128)(2,1)S(1)}, u32[]{:S(2)}, u32[]{:S(2)}) collective-permute-start(bf16[384,512]{1,0:T(8,128)(2,1)S(1)} %get-tuple-element.53.refs_1_.refs_2_), channel_id=1, source_target_pairs={{0,2},{1,3},{2,4},{3,5},{4,6},{5,7},{8,10},{9,11},{10,12},{11,13},... | collective-permute-start | bytes 1179656 | tf_op jit(solution)/shard_map/ppermute | solution.py:34
  7.0 3.4 %collective-permute-start = (bf16[224,512]{1,0:T(8,128)(2,1)S(1)}, bf16[224,512]{1,0:T(8,128)(2,1)S(1)}, u32[]{:S(2)}, u32[]{:S(2)}) collective-permute-start(bf16[224,512]{1,0:T(8,128)(2,1)S(1)} %get-tuple-element.54), channel_id=1, source_target_pairs={{0,1},{1,2},{2,3},{3,4},{4,5},{5,6},{6,7},{8,9},{9,10},{10,11},{11... | collective-permute-start | bytes 688136 | tf_op jit(solution)/shard_map/ppermute | solution.py:34
  10.5 1.3 %collective-permute-start.3 = (bf16[160,512]{1,0:T(8,128)(2,1)S(1)}, bf16[160,512]{1,0:T(8,128)(2,1)S(1)}, u32[]{:S(2)}, u32[]{:S(2)}) collective-permute-start(bf16[160,512]{1,0:T(8,128)(2,1)S(1)} %get-tuple-element.57), channel_id=1, source_target_pairs={{1,0},{2,1},{3,2},{4,3},{5,4},{6,5},{7,6},{9,8},{10,9},{11,10},{12... | collective-permute-start | bytes 491528 | tf_op jit(solution)/shard_map/ppermute | solution.py:34
  11.8 5.5 %collective-permute-start.2 = (bf16[64,512]{1,0:T(8,128)(2,1)S(1)}, bf16[64,512]{1,0:T(8,128)(2,1)S(1)}, u32[]{:S(2)}, u32[]{:S(2)}) collective-permute-start(bf16[64,512]{1,0:T(8,128)(2,1)S(1)} %get-tuple-element.55), channel_id=1, source_target_pairs={{0,3},{1,4},{2,5},{3,6},{4,7},{8,11},{9,12},{10,13},{11,14},{12,15... | collective-permute-start | bytes 196616 | tf_op jit(solution)/shard_map/ppermute | solution.py:34
  17.3 0.0 collective-permute-done.1.refs_3_.refs_1_.refs_5_.refs_4_
  17.4 2.5 %collective-permute-start.4 = (bf16[192,512]{1,0:T(8,128)(2,1)S(1)}, bf16[192,512]{1,0:T(8,128)(2,1)S(1)}, u32[]{:S(2)}, u32[]{:S(2)}) collective-permute-start(bf16[192,512]{1,0:T(8,128)(2,1)S(1)} %choose.1), channel_id=1, source_target_pairs={{0,1},{1,0},{2,3},{3,2},{4,5},{5,4},{6,7},{7,6},{8,9},{9,8},{10,11... | collective-permute-start | bytes 589832 | tf_op jit(solution)/shard_map/ppermute | solution.py:550
  19.8 0.0 collective-permute-done.3.refs_4_.refs_7_
  19.8 0.0 collective-permute-done.refs_2_.refs_3_
  19.9 0.9 %scores.3 = (bf16[4,256,512]{2,1,0:T(8,128)(2,1)S(1)}, f32[8,128]{1,0:T(8,128)S(1)}) custom-call(bf16[192,512]{1,0:T(8,128)(2,1)S(1)} %get-tuple-element.52.refs_0_, bf16[384,512]{1,0:T(8,128)(2,1)S(1)} %get-tuple-element.53.refs_1_.refs_2_, bf16[224,512]{1,0:T(8,128)(2,1)S(1)} %collective-permute-done.refs_2_.refs_3_, ...), custom_call_target="tpu_custom_call" | custom-call | flops 5000000000 | bytes 10000000 | tf_op jit(solution)/shard_map/scores/pallas_call | solution.py:561
  20.7 0.0 collective-permute-done.2.refs_4_.refs_6_
  20.7 0.9 %scores.2 = (bf16[4,256,512]{2,1,0:T(8,128)(2,1)S(1)}, f32[8,128]{1,0:T(8,128)S(1)}) custom-call(bf16[192,512]{1,0:T(8,128)(2,1)S(1)} %get-tuple-element.52.refs_0_, bf16[384,512]{1,0:T(8,128)(2,1)S(1)} %get-tuple-element.53.refs_1_.refs_2_, bf16[224,512]{1,0:T(8,128)(2,1)S(1)} %collective-permute-done.refs_2_.refs_3_, ...), custom_call_target="tpu_custom_call" | custom-call | flops 5000000000 | bytes 10000000 | tf_op jit(solution)/shard_map/scores/pallas_call | solution.py:561
  21.6 2.0 %collective-permute-done.4.refs_4_.refs_3_ = bf16[192,512]{1,0:T(8,128)(2,1)S(1)} collective-permute-done((bf16[192,512]{1,0:T(8,128)(2,1)S(1)}, bf16[192,512]{1,0:T(8,128)(2,1)S(1)}, u32[]{:S(2)}, u32[]{:S(2)}) %collective-permute-start.4) | collective-permute-done | bytes 196640 | tf_op jit(solution)/shard_map/ppermute | solution.py:550
  23.6 6.7 %forward.1 = (bf16[192,1024]{1,0:T(8,128)(2,1)}, bf16[192,512]{1,0:T(8,128)(2,1)S(1)}, bf16[192,1024]{1,0:T(8,128)(2,1)S(1)}, bf16[16,128,128]{2,1,0:T(8,128)(2,...) custom-call(bf16[4,256,512]{2,1,0:T(8,128)(2,1)S(1)} %get-tuple-elem, ...), custom_call_target="tpu_custom_call" | custom-call | flops 8000000000 | bytes 10000000 | tf_op jit(solution)/shard_map/forward/pallas_call | solution.py:582
  30.3 0.1 collective-permute-start.5
  30.4 1.9 %kernel_grad.1.refs_2_ = bf16[16,16,128]{2,1,0:T(8,128)(2,1)S(1)} custom-call(f32[8,256,128]{2,1,0:T(8,128)S(1)} %get-tuple-element.66.hid, f32[8,232,128]{2,1,0:T(8,128)S(1)} %get-tuple-element.67.dm), custom_call_target="tpu_custom_call" | custom-call | flops 2000000000 | bytes 3000000 | tf_op jit(solution)/shard_map/kernel_grad/pallas_call | solution.py:620
  32.3 0.0 collective-permute-done.5.refs_1_
  32.3 0.1 join.1
  32.4 2.0 %collective-permute-start.6 = (bf16[4,144,128]{2,1,0:T(8,128)(2,1)S(1)}, bf16[4,144,128]{2,1,0:T(8,128)(2,1)S(1)}, u32[]{:S(2)}, u32[]{:S(2)}) collective-permute-start(bf16[4,144,128]{2,1,0:T(8,128)(2,1)S(1)} %get-tuple-element.77), channel_id=1, source_target_pairs={{0,1},{1,0},{16,17},{17,16},{2,3},{3,2},{18,19},{19,18},{4,5},{5,4... | collective-permute-start | bytes 442376 | tf_op jit(solution)/shard_map/ppermute | solution.py:483
  34.4 1.5 %collective-permute-start.7 = (bf16[4,144,128]{2,1,0:T(8,128)(2,1)S(1)}, bf16[4,144,128]{2,1,0:T(8,128)(2,1)S(1)}, u32[]{:S(2)}, u32[]{:S(2)}) collective-permute-start(bf16[4,144,128]{2,1,0:T(8,128)(2,1)S(1)} %get-tuple-element.78), channel_id=1, source_target_pairs={{0,16},{1,17},{16,0},{17,1},{2,18},{3,19},{18,2},{19,3},{4,20},{5,... | collective-permute-start | bytes 442376 | tf_op jit(solution)/shard_map/ppermute | solution.py:483
  35.9 0.1 collective-permute-start.8
  36.0 5.4 %backward.1 = (bf16[192,512]{1,0:T(8,128)(2,1)}, f32[384,512]{1,0:T(8,128)S(1)}, bf16[384,512]{1,0:T(8,128)(2,1)S(1)}, bf16[384,512]{1,0:T(8,128)(2,1)S(1)}) custom-call(bf16[192,512]{1,0:T(8,128)(2,1)S(1)} %get-tuple-element.52.refs_0_, bf16[384,512]{1,0:T(8,128)(2,1)S(1)} %get-tuple-element.53.refs_1_.refs_2_, ...), custom_call_target="tpu_custom_call" | custom-call | flops 6000000000 | bytes 10000000 | tf_op jit(solution)/shard_map/backward/pallas_call | solution.py:645
  41.4 0.0 collective-permute-done.6
  41.4 0.0 collective-permute-done.7
  41.4 1.9 %collective-permute-done.8 = bf16[4,144,128]{2,1,0:T(8,128)(2,1)S(1)} collective-permute-done((bf16[4,144,128]{2,1,0:T(8,128)(2,1)S(1)}, bf16[4,144,128]{2,1,0:T(8,128)(2,1)S(1)}, u32[]{:S(2)}, u32[]{:S(2)}) %collective-permute-start.8) | collective-permute-done | bytes 147488 | tf_op jit(solution)/shard_map/ppermute | solution.py:483
  43.3 0.1 add_convert_fusion.2
  43.4 4.6 %collective-permute-start.9 = (bf16[4,144,128]{2,1,0:T(8,128)(2,1)S(1)}, bf16[4,144,128]{2,1,0:T(8,128)(2,1)S(1)}, u32[]{:S(2)}, u32[]{:S(2)}) collective-permute-start(bf16[4,144,128]{2,1,0:T(8,128)(2,1)S(1)} %add_convert_fusion.2), channel_id=1, source_target_pairs={{0,2},{2,0},{4,6},{6,4},{1,3},{3,1},{5,7},{7,5},{8,10},{10,8},{12,... | collective-permute-start | bytes 442376 | tf_op jit(solution)/shard_map/ppermute | solution.py:489
  48.0 0.4 collective-permute-start.11
  48.4 3.1 %collective-permute-done.9 = bf16[4,144,128]{2,1,0:T(8,128)(2,1)S(1)} collective-permute-done((bf16[4,144,128]{2,1,0:T(8,128)(2,1)S(1)}, bf16[4,144,128]{2,1,0:T(8,128)(2,1)S(1)}, u32[]{:S(2)}, u32[]{:S(2)}) %collective-permute-start.9) | collective-permute-done | bytes 147488 | tf_op jit(solution)/shard_map/ppermute | solution.py:489
  51.5 4.2 %collective-permute-start.10 = (bf16[4,144,128]{2,1,0:T(8,128)(2,1)S(1)}, bf16[4,144,128]{2,1,0:T(8,128)(2,1)S(1)}, u32[]{:S(2)}, u32[]{:S(2)}) collective-permute-start(bf16[4,144,128]{2,1,0:T(8,128)(2,1)S(1)} %add_convert_fusion.1), channel_id=1, source_target_pairs={{0,4},{2,6},{4,0},{6,2},{1,5},{3,7},{5,1},{7,3},{8,12},{10,14},{12... | collective-permute-start | bytes 442376 | tf_op jit(solution)/shard_map/ppermute | solution.py:489
  55.7 5.4 %collective-permute-done.10 = bf16[4,144,128]{2,1,0:T(8,128)(2,1)S(1)} collective-permute-done((bf16[4,144,128]{2,1,0:T(8,128)(2,1)S(1)}, bf16[4,144,128]{2,1,0:T(8,128)(2,1)S(1)}, u32[]{:S(2)}, u32[]{:S(2)}) %collective-permute-start.10) | collective-permute-done | bytes 147488 | tf_op jit(solution)/shard_map/ppermute | solution.py:489
  61.2 0.0 collective-permute-done.11.refs_0_.refs_1_
  61.2 0.1 relay.1
  61.3 1.3 %collective-permute-start.19 = (bf16[384,512]{1,0:T(8,128)(2,1)S(1)}, bf16[384,512]{1,0:T(8,128)(2,1)S(1)}, u32[]{:S(2)}, u32[]{:S(2)}) collective-permute-start(bf16[384,512]{1,0:T(8,128)(2,1)S(1)} %relay.1), channel_id=1, source_target_pairs={{2,0},{3,1},{4,2},{5,3},{6,4},{7,5},{10,8},{11,9},{12,10},{13,11},... | collective-permute-start | bytes 1179656 | tf_op jit(solution)/shard_map/ppermute | solution.py:34
  62.6 2.3 %collective-permute-start.17 = (bf16[4,144,128]{2,1,0:T(8,128)(2,1)S(1)}, bf16[4,144,128]{2,1,0:T(8,128)(2,1)S(1)}, u32[]{:S(2)}, u32[]{:S(2)}) collective-permute-start(bf16[4,144,128]{2,1,0:T(8,128)(2,1)S(1)} %add_convert_fusion.refs_0_), channel_id=1, source_target_pairs={{0,17},{1,16},{16,1},{17,0},{2,19},{3,18},{18,3},{19,2},{4,21},{5,... | collective-permute-start | bytes 442376 | tf_op jit(solution)/shard_map/ppermute | solution.py:483
  64.9 0.5 collective-permute-start.15
  65.4 0.8 %collective-permute-start.13 = (bf16[4,144,128]{2,1,0:T(8,128)(2,1)S(1)}, bf16[4,144,128]{2,1,0:T(8,128)(2,1)S(1)}, u32[]{:S(2)}, u32[]{:S(2)}) collective-permute-start(bf16[4,144,128]{2,1,0:T(8,128)(2,1)S(1)} %add_convert_fusion.refs_0_), channel_id=1, source_target_pairs={{0,1},{1,0},{16,17},{17,16},{2,3},{3,2},{18,19},{19,18},{4,5},{5,4... | collective-permute-start | bytes 442376 | tf_op jit(solution)/shard_map/ppermute | solution.py:483
  66.2 0.0 collective-permute-start.12
  66.2 0.7 unpack_early.1.refs_8_
  66.9 3.3 %collective-permute-done.17.refs_3_ = bf16[4,144,128]{2,1,0:T(8,128)(2,1)S(1)} collective-permute-done((bf16[4,144,128]{2,1,0:T(8,128)(2,1)S(1)}, bf16[4,144,128]{2,1,0:T(8,128)(2,1)S(1)}, u32[]{:S(2)}, u32[]{:S(2)}) %collective-permute-start.17) | collective-permute-done | bytes 147488 | tf_op jit(solution)/shard_map/ppermute | solution.py:483
  70.2 0.0 collective-permute-start.18
  70.2 1.7 %collective-permute-done.15.refs_2_ = bf16[4,144,128]{2,1,0:T(8,128)(2,1)S(1)} collective-permute-done((bf16[4,144,128]{2,1,0:T(8,128)(2,1)S(1)}, bf16[4,144,128]{2,1,0:T(8,128)(2,1)S(1)}, u32[]{:S(2)}, u32[]{:S(2)}) %collective-permute-start.15) | collective-permute-done | bytes 147488 | tf_op jit(solution)/shard_map/ppermute | solution.py:483
  72.0 0.0 collective-permute-start.16
  72.0 0.0 collective-permute-done.13.refs_1_
  72.0 0.5 collective-permute-start.14
  72.5 0.9 %collective-permute-done.19.refs_0_ = bf16[384,512]{1,0:T(8,128)(2,1)S(1)} collective-permute-done((bf16[384,512]{1,0:T(8,128)(2,1)S(1)}, bf16[384,512]{1,0:T(8,128)(2,1)S(1)}, u32[]{:S(2)}, u32[]{:S(2)}) %collective-permute-start.19) | collective-permute-done | bytes 393248 | tf_op jit(solution)/shard_map/ppermute | solution.py:34
  73.4 0.8 %merge.1 = (bf16[192,512]{1,0:T(8,128)(2,1)}, bf16[192,512]{1,0:T(8,128)(2,1)}) custom-call(bf16[384,512]{1,0:T(8,128)(2,1)S(1)} %collective-permute-done.19.refs_0_, bf16[384,512]{1,0:T(8,128)(2,1)S(1)} %collective-permute-done.11.refs_0_.refs_1_, f32[384,512]{1,0:T(8,128)S(1)} %get-tuple-element.87.refs_2_), custom_call_target="tpu_custom_call" | custom-call | flops 16000000000 | bytes 10000000 | tf_op jit(solution)/shard_map/merge/pallas_call | solution.py:686
  74.3 0.0 collective-permute-done.12.refs_4_
  74.3 0.0 collective-permute-done.18.refs_7_
  74.3 0.0 collective-permute-done.16.refs_6_
  74.3 0.0 collective-permute-done.14.refs_5_
  74.3 1.4 %unpack_late.1 = (f32[512,1024]{1,0:T(8,128)}, f32[31,1024]{1,0:T(8,128)}) custom-call(bf16[4,144,128]{2,1,0:T(8,128)(2,1)S(1)} %add_convert_fusion.refs_0_, bf16[4,144,128]{2,1,0:T(8,128)(2,1)S(1)} %collective-permute-done.13.refs_1_, bf16[4,144,128]{2,1,0:T(8,128)(2,1)S(1)} %collective-permute-done.15.refs_2_, ...), custom_call_target="tpu_custom_call", output_to_operand_aliasing={{0}: (8, {})} | custom-call | tf_op jit(solution)/shard_map/unpack_late/pallas_call | solution.py:722
  (3 shorter events, 0.1 us)
Async XLA Ops:
  2.1 15.2 %collective-permute-start.1 = (bf16[384,512]{1,0:T(8,128)(2,1)S(1)}, bf16[384,512]{1,0:T(8,128)(2,1)S(1)}, u32[]{:S(2)}, u32[]{:S(2)}) collective-permute-start(bf16[384,512]{1,0:T(8,128)(2,1)S(1)} %get-tuple-element.53.refs_1_.refs_2_), channel_id=1, source_target_pairs={{0,2},{1,3},{2,4},{3,5},{4,6},{5,7},{8,10},{9,11},{10,12},{11,13},... | collective-permute-start | bytes 1179656 | tf_op jit(solution)/shard_map/ppermute | solution.py:34
  7.0 12.8 %collective-permute-start = (bf16[224,512]{1,0:T(8,128)(2,1)S(1)}, bf16[224,512]{1,0:T(8,128)(2,1)S(1)}, u32[]{:S(2)}, u32[]{:S(2)}) collective-permute-start(bf16[224,512]{1,0:T(8,128)(2,1)S(1)} %get-tuple-element.54), channel_id=1, source_target_pairs={{0,1},{1,2},{2,3},{3,4},{4,5},{5,6},{6,7},{8,9},{9,10},{10,11},{11... | collective-permute-start | bytes 688136 | tf_op jit(solution)/shard_map/ppermute | solution.py:34
  10.5 9.4 %collective-permute-start.3 = (bf16[160,512]{1,0:T(8,128)(2,1)S(1)}, bf16[160,512]{1,0:T(8,128)(2,1)S(1)}, u32[]{:S(2)}, u32[]{:S(2)}) collective-permute-start(bf16[160,512]{1,0:T(8,128)(2,1)S(1)} %get-tuple-element.57), channel_id=1, source_target_pairs={{1,0},{2,1},{3,2},{4,3},{5,4},{6,5},{7,6},{9,8},{10,9},{11,10},{12... | collective-permute-start | bytes 491528 | tf_op jit(solution)/shard_map/ppermute | solution.py:34
  11.8 9.0 %collective-permute-start.2 = (bf16[64,512]{1,0:T(8,128)(2,1)S(1)}, bf16[64,512]{1,0:T(8,128)(2,1)S(1)}, u32[]{:S(2)}, u32[]{:S(2)}) collective-permute-start(bf16[64,512]{1,0:T(8,128)(2,1)S(1)} %get-tuple-element.55), channel_id=1, source_target_pairs={{0,3},{1,4},{2,5},{3,6},{4,7},{8,11},{9,12},{10,13},{11,14},{12,15... | collective-permute-start | bytes 196616 | tf_op jit(solution)/shard_map/ppermute | solution.py:34
  17.4 6.3 %collective-permute-start.4 = (bf16[192,512]{1,0:T(8,128)(2,1)S(1)}, bf16[192,512]{1,0:T(8,128)(2,1)S(1)}, u32[]{:S(2)}, u32[]{:S(2)}) collective-permute-start(bf16[192,512]{1,0:T(8,128)(2,1)S(1)} %choose.1), channel_id=1, source_target_pairs={{0,1},{1,0},{2,3},{3,2},{4,5},{5,4},{6,7},{7,6},{8,9},{9,8},{10,11... | collective-permute-start | bytes 589832 | tf_op jit(solution)/shard_map/ppermute | solution.py:550
  30.3 2.0 %collective-permute-start.5 = (bf16[16,128,128]{2,1,0:T(8,128)(2,1)S(1)}, bf16[16,128,128]{2,1,0:T(8,128)(2,1)S(1)}, u32[]{:S(2)}, u32[]{:S(2)}) collective-permute-start(bf16[16,128,128]{2,1,0:T(8,128)(2,1)S(1)} %get-tuple-element.65), channel_id=1, source_target_pairs={{0,8},{8,0},{1,9},{9,1},{2,10},{10,2},{3,11},{11,3},{4,12},{12,4},... | collective-permute-start | bytes 1572872 | tf_op jit(solution)/shard_map/ppermute | solution.py:496
  32.4 9.0 %collective-permute-start.6 = (bf16[4,144,128]{2,1,0:T(8,128)(2,1)S(1)}, bf16[4,144,128]{2,1,0:T(8,128)(2,1)S(1)}, u32[]{:S(2)}, u32[]{:S(2)}) collective-permute-start(bf16[4,144,128]{2,1,0:T(8,128)(2,1)S(1)} %get-tuple-element.77), channel_id=1, source_target_pairs={{0,1},{1,0},{16,17},{17,16},{2,3},{3,2},{18,19},{19,18},{4,5},{5,4... | collective-permute-start | bytes 442376 | tf_op jit(solution)/shard_map/ppermute | solution.py:483
  34.4 7.0 %collective-permute-start.7 = (bf16[4,144,128]{2,1,0:T(8,128)(2,1)S(1)}, bf16[4,144,128]{2,1,0:T(8,128)(2,1)S(1)}, u32[]{:S(2)}, u32[]{:S(2)}) collective-permute-start(bf16[4,144,128]{2,1,0:T(8,128)(2,1)S(1)} %get-tuple-element.78), channel_id=1, source_target_pairs={{0,16},{1,17},{16,0},{17,1},{2,18},{3,19},{18,2},{19,3},{4,20},{5,... | collective-permute-start | bytes 442376 | tf_op jit(solution)/shard_map/ppermute | solution.py:483
  35.9 7.4 %collective-permute-start.8 = (bf16[4,144,128]{2,1,0:T(8,128)(2,1)S(1)}, bf16[4,144,128]{2,1,0:T(8,128)(2,1)S(1)}, u32[]{:S(2)}, u32[]{:S(2)}) collective-permute-start(bf16[4,144,128]{2,1,0:T(8,128)(2,1)S(1)} %get-tuple-element.79), channel_id=1, source_target_pairs={{0,17},{1,16},{16,1},{17,0},{2,19},{3,18},{18,3},{19,2},{4,21},{5,... | collective-permute-start | bytes 442376 | tf_op jit(solution)/shard_map/ppermute | solution.py:483
  43.4 8.0 %collective-permute-start.9 = (bf16[4,144,128]{2,1,0:T(8,128)(2,1)S(1)}, bf16[4,144,128]{2,1,0:T(8,128)(2,1)S(1)}, u32[]{:S(2)}, u32[]{:S(2)}) collective-permute-start(bf16[4,144,128]{2,1,0:T(8,128)(2,1)S(1)} %add_convert_fusion.2), channel_id=1, source_target_pairs={{0,2},{2,0},{4,6},{6,4},{1,3},{3,1},{5,7},{7,5},{8,10},{10,8},{12,... | collective-permute-start | bytes 442376 | tf_op jit(solution)/shard_map/ppermute | solution.py:489
  48.0 13.1 %collective-permute-start.11 = (bf16[384,512]{1,0:T(8,128)(2,1)S(1)}, bf16[384,512]{1,0:T(8,128)(2,1)S(1)}, u32[]{:S(2)}, u32[]{:S(2)}) collective-permute-start(bf16[384,512]{1,0:T(8,128)(2,1)S(1)} %get-tuple-element.83), channel_id=1, source_target_pairs={{0,1},{1,0},{2,3},{3,2},{4,5},{5,4},{6,7},{7,6},{8,9},{9,8},{10,11... | collective-permute-start | bytes 1179656 | tf_op jit(solution)/shard_map/ppermute | solution.py:668
  51.5 9.6 %collective-permute-start.10 = (bf16[4,144,128]{2,1,0:T(8,128)(2,1)S(1)}, bf16[4,144,128]{2,1,0:T(8,128)(2,1)S(1)}, u32[]{:S(2)}, u32[]{:S(2)}) collective-permute-start(bf16[4,144,128]{2,1,0:T(8,128)(2,1)S(1)} %add_convert_fusion.1), channel_id=1, source_target_pairs={{0,4},{2,6},{4,0},{6,2},{1,5},{3,7},{5,1},{7,3},{8,12},{10,14},{12... | collective-permute-start | bytes 442376 | tf_op jit(solution)/shard_map/ppermute | solution.py:489
  61.3 12.1 %collective-permute-start.19 = (bf16[384,512]{1,0:T(8,128)(2,1)S(1)}, bf16[384,512]{1,0:T(8,128)(2,1)S(1)}, u32[]{:S(2)}, u32[]{:S(2)}) collective-permute-start(bf16[384,512]{1,0:T(8,128)(2,1)S(1)} %relay.1), channel_id=1, source_target_pairs={{2,0},{3,1},{4,2},{5,3},{6,4},{7,5},{10,8},{11,9},{12,10},{13,11},... | collective-permute-start | bytes 1179656 | tf_op jit(solution)/shard_map/ppermute | solution.py:34
  62.6 7.6 %collective-permute-start.17 = (bf16[4,144,128]{2,1,0:T(8,128)(2,1)S(1)}, bf16[4,144,128]{2,1,0:T(8,128)(2,1)S(1)}, u32[]{:S(2)}, u32[]{:S(2)}) collective-permute-start(bf16[4,144,128]{2,1,0:T(8,128)(2,1)S(1)} %add_convert_fusion.refs_0_), channel_id=1, source_target_pairs={{0,17},{1,16},{16,1},{17,0},{2,19},{3,18},{18,3},{19,2},{4,21},{5,... | collective-permute-start | bytes 442376 | tf_op jit(solution)/shard_map/ppermute | solution.py:483
  64.9 7.1 %collective-permute-start.15 = (bf16[4,144,128]{2,1,0:T(8,128)(2,1)S(1)}, bf16[4,144,128]{2,1,0:T(8,128)(2,1)S(1)}, u32[]{:S(2)}, u32[]{:S(2)}) collective-permute-start(bf16[4,144,128]{2,1,0:T(8,128)(2,1)S(1)} %add_convert_fusion.refs_0_), channel_id=1, source_target_pairs={{0,16},{1,17},{16,0},{17,1},{2,18},{3,19},{18,2},{19,3},{4,20},{5,... | collective-permute-start | bytes 442376 | tf_op jit(solution)/shard_map/ppermute | solution.py:483
  65.4 6.6 %collective-permute-start.13 = (bf16[4,144,128]{2,1,0:T(8,128)(2,1)S(1)}, bf16[4,144,128]{2,1,0:T(8,128)(2,1)S(1)}, u32[]{:S(2)}, u32[]{:S(2)}) collective-permute-start(bf16[4,144,128]{2,1,0:T(8,128)(2,1)S(1)} %add_convert_fusion.refs_0_), channel_id=1, source_target_pairs={{0,1},{1,0},{16,17},{17,16},{2,3},{3,2},{18,19},{19,18},{4,5},{5,4... | collective-permute-start | bytes 442376 | tf_op jit(solution)/shard_map/ppermute | solution.py:483
  66.2 8.1 %collective-permute-start.12 = (bf16[4,144,128]{2,1,0:T(8,128)(2,1)S(1)}, bf16[4,144,128]{2,1,0:T(8,128)(2,1)S(1)}, u32[]{:S(2)}, u32[]{:S(2)}) collective-permute-start(bf16[4,144,128]{2,1,0:T(8,128)(2,1)S(1)} %add_convert_fusion.refs_0_), channel_id=1, source_target_pairs={{0,8},{8,0},{1,9},{9,1},{2,10},{10,2},{3,11},{11,3},{4,12},{12,4},... | collective-permute-start | bytes 442376 | tf_op jit(solution)/shard_map/ppermute | solution.py:496
  70.2 4.0 %collective-permute-start.18 = (bf16[4,144,128]{2,1,0:T(8,128)(2,1)S(1)}, bf16[4,144,128]{2,1,0:T(8,128)(2,1)S(1)}, u32[]{:S(2)}, u32[]{:S(2)}) collective-permute-start(bf16[4,144,128]{2,1,0:T(8,128)(2,1)S(1)} %collective-permute-done.17.refs_3_), channel_id=1, source_target_pairs={{0,8},{8,0},{1,9},{9,1},{2,10},{10,2},{3,11},{11,3},{4,12},{12,4},... | collective-permute-start | bytes 442376 | tf_op jit(solution)/shard_map/ppermute | solution.py:496
  72.0 2.3 %collective-permute-start.16 = (bf16[4,144,128]{2,1,0:T(8,128)(2,1)S(1)}, bf16[4,144,128]{2,1,0:T(8,128)(2,1)S(1)}, u32[]{:S(2)}, u32[]{:S(2)}) collective-permute-start(bf16[4,144,128]{2,1,0:T(8,128)(2,1)S(1)} %collective-permute-done.15.refs_2_), channel_id=1, source_target_pairs={{0,8},{8,0},{1,9},{9,1},{2,10},{10,2},{3,11},{11,3},{4,12},{12,4},... | collective-permute-start | bytes 442376 | tf_op jit(solution)/shard_map/ppermute | solution.py:496
  72.0 2.3 %collective-permute-start.14 = (bf16[4,144,128]{2,1,0:T(8,128)(2,1)S(1)}, bf16[4,144,128]{2,1,0:T(8,128)(2,1)S(1)}, u32[]{:S(2)}, u32[]{:S(2)}) collective-permute-start(bf16[4,144,128]{2,1,0:T(8,128)(2,1)S(1)} %collective-permute-done.13.refs_1_), channel_id=1, source_target_pairs={{0,8},{8,0},{1,9},{9,1},{2,10},{10,2},{3,11},{11,3},{4,12},{12,4},... | collective-permute-start | bytes 442376 | tf_op jit(solution)/shard_map/ppermute | solution.py:496

commit v16 on v15

--- a/solution.py
+++ b/solution.py
@@ -273,7 +273,7 @@
             dhid_ref[first : first + part, columns] = dhidden.astype(jnp.bfloat16)
         return carry
 
-    lax.fori_loop(0, width // LANES, convolve, 0)
+    lax.fori_loop(0, width // LANES, convolve, 0, unroll=2)
     store = pltpu.make_async_copy(out_ref, out_hbm, sems.at[3])
     store.start()
 
@@ -323,7 +323,7 @@
         kp[chunk, :taps] = total
         return carry
 
-    lax.fori_loop(0, chunks, correlate, 0)
+    lax.fori_loop(0, chunks, correlate, 0, unroll=2)
     for piece in range(pieces):
         block = [kp[chunk, tap : tap + 1] for tap in (piece, pieces + piece) for chunk in range(chunks)]
         rows_ref[piece] = jnp.concatenate(block, axis=0).astype(jnp.bfloat16)

time: 75.9 us -> 75.8 us (level)
  transfers between devices with their start and end apart: 20 -> 20, of which waited for: 7 -> 8; matrix products, arithmetic and copies ran while one was open for 0% -> 0% of each run, Pallas kernels for 14% -> 14%
where the time goes in v16:
time: 75.8 us; the launch traced here: 75.5 us
  starting transfers between devices  35.9 us (47%)
  Pallas kernels  20.4 us (27%)
  waiting for transfers between devices  18.3 us (24%)
  between operations  0.78 us (1%)
    ppermute x5, starting transfers between devices, shifted(): lax.ppermute(x, RUN_AXES, [(i, i + by) for i in devices if i + by in devi...  16.5 us
    ppermute x2, starting transfers between devices, summed_along(): other = lax.ppermute(x, axis, [(i, i ^ step) for i in range(size)])  8.86 us
    ppermute x2, waiting for transfers between devices, summed_along(): other = lax.ppermute(x, axis, [(i, i ^ step) for i in range(size)])  8.4 us
    ppermute x6, starting transfers between devices, from_peer(): return lax.ppermute(x, PLANE_AXES, [(i, i ^ mask) for i in devices])  7.11 us
    ppermute x6, waiting for transfers between devices, from_peer(): return lax.ppermute(x, PLANE_AXES, [(i, i ^ mask) for i in devices])  6.88 us
    pallas_call x1, Pallas kernels, per_device(): pl.pallas_call(located(functools.partial(forward_kernel, context, rows, e...  6.67 us
    pallas_call x1, Pallas kernels, per_device(): pl.pallas_call(located(functools.partial(backward_kernel, context, rows),...  5.44 us
    ppermute x1, starting transfers between devices, per_device(): values = lax.ppermute(values, 'y', [(0, 1), (1, 0)])  2.48 us
  transfers between devices with their start and end apart: 20, of which 8 were waited for; matrix products, arithmetic and copies ran while one was open for 0% of the time, Pallas kernels for 14%

profile of v16, /device:TPU:0, one launch (start us, length us, event | category | flops | bytes accessed | tf_op | source)
XLA Modules:
  0.0 75.5 jit_solution(12545105745450085578)
XLA Ops:
  0.6 1.4 %pack.1 = (bf16[384,512]{1,0:T(8,128)(2,1)S(1)}, bf16[224,512]{1,0:T(8,128)(2,1)S(1)}, bf16[192,512]{1,0:T(8,128)(2,1)S(1)}, bf16[192,512]{1,0:T(8,128)(2,1)S(1)...) custom-call(bf16[192,512]{1,0:T(8,128)(2,1)} %bitcast.10, bf16[192,512]{1,0:T(8,128)(2,1)} %bitcast.11, ...), custom_call_target="tpu_custom_call" | custom-call | tf_op jit(solution)/shard_map/pack/pallas_call | solution.py:522
  2.1 5.0 %collective-permute-start.1 = (bf16[384,512]{1,0:T(8,128)(2,1)S(1)}, bf16[384,512]{1,0:T(8,128)(2,1)S(1)}, u32[]{:S(2)}, u32[]{:S(2)}) collective-permute-start(bf16[384,512]{1,0:T(8,128)(2,1)S(1)} %get-tuple-element.53.refs_1_.refs_2_), channel_id=1, source_target_pairs={{0,2},{1,3},{2,4},{3,5},{4,6},{5,7},{8,10},{9,11},{10,12},{11,13},... | collective-permute-start | bytes 1179656 | tf_op jit(solution)/shard_map/ppermute | solution.py:34
  7.0 3.4 %collective-permute-start = (bf16[224,512]{1,0:T(8,128)(2,1)S(1)}, bf16[224,512]{1,0:T(8,128)(2,1)S(1)}, u32[]{:S(2)}, u32[]{:S(2)}) collective-permute-start(bf16[224,512]{1,0:T(8,128)(2,1)S(1)} %get-tuple-element.54), channel_id=1, source_target_pairs={{0,1},{1,2},{2,3},{3,4},{4,5},{5,6},{6,7},{8,9},{9,10},{10,11},{11... | collective-permute-start | bytes 688136 | tf_op jit(solution)/shard_map/ppermute | solution.py:34
  10.5 1.3 %collective-permute-start.3 = (bf16[160,512]{1,0:T(8,128)(2,1)S(1)}, bf16[160,512]{1,0:T(8,128)(2,1)S(1)}, u32[]{:S(2)}, u32[]{:S(2)}) collective-permute-start(bf16[160,512]{1,0:T(8,128)(2,1)S(1)} %get-tuple-element.57), channel_id=1, source_target_pairs={{1,0},{2,1},{3,2},{4,3},{5,4},{6,5},{7,6},{9,8},{10,9},{11,10},{12... | collective-permute-start | bytes 491528 | tf_op jit(solution)/shard_map/ppermute | solution.py:34
  11.8 5.5 %collective-permute-start.2 = (bf16[64,512]{1,0:T(8,128)(2,1)S(1)}, bf16[64,512]{1,0:T(8,128)(2,1)S(1)}, u32[]{:S(2)}, u32[]{:S(2)}) collective-permute-start(bf16[64,512]{1,0:T(8,128)(2,1)S(1)} %get-tuple-element.55), channel_id=1, source_target_pairs={{0,3},{1,4},{2,5},{3,6},{4,7},{8,11},{9,12},{10,13},{11,14},{12,15... | collective-permute-start | bytes 196616 | tf_op jit(solution)/shard_map/ppermute | solution.py:34
  17.3 0.0 collective-permute-done.1.refs_3_.refs_1_.refs_5_.refs_4_
  17.4 2.5 %collective-permute-start.4 = (bf16[192,512]{1,0:T(8,128)(2,1)S(1)}, bf16[192,512]{1,0:T(8,128)(2,1)S(1)}, u32[]{:S(2)}, u32[]{:S(2)}) collective-permute-start(bf16[192,512]{1,0:T(8,128)(2,1)S(1)} %choose.1), channel_id=1, source_target_pairs={{0,1},{1,0},{2,3},{3,2},{4,5},{5,4},{6,7},{7,6},{8,9},{9,8},{10,11... | collective-permute-start | bytes 589832 | tf_op jit(solution)/shard_map/ppermute | solution.py:550
  19.8 0.0 collective-permute-done.3.refs_4_.refs_7_
  19.8 0.0 collective-permute-done.refs_2_.refs_3_
  19.9 0.9 %scores.3 = (bf16[4,256,512]{2,1,0:T(8,128)(2,1)S(1)}, f32[8,128]{1,0:T(8,128)S(1)}) custom-call(bf16[192,512]{1,0:T(8,128)(2,1)S(1)} %get-tuple-element.52.refs_0_, bf16[384,512]{1,0:T(8,128)(2,1)S(1)} %get-tuple-element.53.refs_1_.refs_2_, bf16[224,512]{1,0:T(8,128)(2,1)S(1)} %collective-permute-done.refs_2_.refs_3_, ...), custom_call_target="tpu_custom_call" | custom-call | flops 5000000000 | bytes 10000000 | tf_op jit(solution)/shard_map/scores/pallas_call | solution.py:561
  20.7 0.0 collective-permute-done.2.refs_4_.refs_6_
  20.7 0.9 %scores.2 = (bf16[4,256,512]{2,1,0:T(8,128)(2,1)S(1)}, f32[8,128]{1,0:T(8,128)S(1)}) custom-call(bf16[192,512]{1,0:T(8,128)(2,1)S(1)} %get-tuple-element.52.refs_0_, bf16[384,512]{1,0:T(8,128)(2,1)S(1)} %get-tuple-element.53.refs_1_.refs_2_, bf16[224,512]{1,0:T(8,128)(2,1)S(1)} %collective-permute-done.refs_2_.refs_3_, ...), custom_call_target="tpu_custom_call" | custom-call | flops 5000000000 | bytes 10000000 | tf_op jit(solution)/shard_map/scores/pallas_call | solution.py:561
  21.6 2.0 %collective-permute-done.4.refs_4_.refs_3_ = bf16[192,512]{1,0:T(8,128)(2,1)S(1)} collective-permute-done((bf16[192,512]{1,0:T(8,128)(2,1)S(1)}, bf16[192,512]{1,0:T(8,128)(2,1)S(1)}, u32[]{:S(2)}, u32[]{:S(2)}) %collective-permute-start.4) | collective-permute-done | bytes 196640 | tf_op jit(solution)/shard_map/ppermute | solution.py:550
  23.6 6.7 %forward.1 = (bf16[192,1024]{1,0:T(8,128)(2,1)}, bf16[192,512]{1,0:T(8,128)(2,1)S(1)}, bf16[192,1024]{1,0:T(8,128)(2,1)S(1)}, bf16[16,128,128]{2,1,0:T(8,128)(2,...) custom-call(bf16[4,256,512]{2,1,0:T(8,128)(2,1)S(1)} %get-tuple-elem, ...), custom_call_target="tpu_custom_call" | custom-call | flops 8000000000 | bytes 10000000 | tf_op jit(solution)/shard_map/forward/pallas_call | solution.py:582
  30.3 0.1 collective-permute-start.5
  30.4 1.8 %kernel_grad.1.refs_2_ = bf16[16,16,128]{2,1,0:T(8,128)(2,1)S(1)} custom-call(f32[8,256,128]{2,1,0:T(8,128)S(1)} %get-tuple-element.66.hid, f32[8,232,128]{2,1,0:T(8,128)S(1)} %get-tuple-element.67.dm), custom_call_target="tpu_custom_call" | custom-call | flops 2000000000 | bytes 3000000 | tf_op jit(solution)/shard_map/kernel_grad/pallas_call | solution.py:620
  32.2 0.1 collective-permute-done.5.refs_1_
  32.3 0.1 join.1
  32.4 2.0 %collective-permute-start.6 = (bf16[4,144,128]{2,1,0:T(8,128)(2,1)S(1)}, bf16[4,144,128]{2,1,0:T(8,128)(2,1)S(1)}, u32[]{:S(2)}, u32[]{:S(2)}) collective-permute-start(bf16[4,144,128]{2,1,0:T(8,128)(2,1)S(1)} %get-tuple-element.77), channel_id=1, source_target_pairs={{0,1},{1,0},{16,17},{17,16},{2,3},{3,2},{18,19},{19,18},{4,5},{5,4... | collective-permute-start | bytes 442376 | tf_op jit(solution)/shard_map/ppermute | solution.py:483
  34.4 1.5 %collective-permute-start.7 = (bf16[4,144,128]{2,1,0:T(8,128)(2,1)S(1)}, bf16[4,144,128]{2,1,0:T(8,128)(2,1)S(1)}, u32[]{:S(2)}, u32[]{:S(2)}) collective-permute-start(bf16[4,144,128]{2,1,0:T(8,128)(2,1)S(1)} %get-tuple-element.78), channel_id=1, source_target_pairs={{0,16},{1,17},{16,0},{17,1},{2,18},{3,19},{18,2},{19,3},{4,20},{5,... | collective-permute-start | bytes 442376 | tf_op jit(solution)/shard_map/ppermute | solution.py:483
  35.9 0.1 collective-permute-start.8
  36.0 5.4 %backward.1 = (bf16[192,512]{1,0:T(8,128)(2,1)}, f32[384,512]{1,0:T(8,128)S(1)}, bf16[384,512]{1,0:T(8,128)(2,1)S(1)}, bf16[384,512]{1,0:T(8,128)(2,1)S(1)}) custom-call(bf16[192,512]{1,0:T(8,128)(2,1)S(1)} %get-tuple-element.52.refs_0_, bf16[384,512]{1,0:T(8,128)(2,1)S(1)} %get-tuple-element.53.refs_1_.refs_2_, ...), custom_call_target="tpu_custom_call" | custom-call | flops 6000000000 | bytes 10000000 | tf_op jit(solution)/shard_map/backward/pallas_call | solution.py:645
  41.4 0.0 collective-permute-done.6
  41.4 0.0 collective-permute-done.7
  41.4 1.9 %collective-permute-done.8 = bf16[4,144,128]{2,1,0:T(8,128)(2,1)S(1)} collective-permute-done((bf16[4,144,128]{2,1,0:T(8,128)(2,1)S(1)}, bf16[4,144,128]{2,1,0:T(8,128)(2,1)S(1)}, u32[]{:S(2)}, u32[]{:S(2)}) %collective-permute-start.8) | collective-permute-done | bytes 147488 | tf_op jit(solution)/shard_map/ppermute | solution.py:483
  43.3 0.1 add_convert_fusion.2
  43.4 4.6 %collective-permute-start.9 = (bf16[4,144,128]{2,1,0:T(8,128)(2,1)S(1)}, bf16[4,144,128]{2,1,0:T(8,128)(2,1)S(1)}, u32[]{:S(2)}, u32[]{:S(2)}) collective-permute-start(bf16[4,144,128]{2,1,0:T(8,128)(2,1)S(1)} %add_convert_fusion.2), channel_id=1, source_target_pairs={{0,2},{2,0},{4,6},{6,4},{1,3},{3,1},{5,7},{7,5},{8,10},{10,8},{12,... | collective-permute-start | bytes 442376 | tf_op jit(solution)/shard_map/ppermute | solution.py:489
  48.0 0.4 collective-permute-start.11
  48.3 3.0 %collective-permute-done.9 = bf16[4,144,128]{2,1,0:T(8,128)(2,1)S(1)} collective-permute-done((bf16[4,144,128]{2,1,0:T(8,128)(2,1)S(1)}, bf16[4,144,128]{2,1,0:T(8,128)(2,1)S(1)}, u32[]{:S(2)}, u32[]{:S(2)}) %collective-permute-start.9) | collective-permute-done | bytes 147488 | tf_op jit(solution)/shard_map/ppermute | solution.py:489
  51.4 4.2 %collective-permute-start.10 = (bf16[4,144,128]{2,1,0:T(8,128)(2,1)S(1)}, bf16[4,144,128]{2,1,0:T(8,128)(2,1)S(1)}, u32[]{:S(2)}, u32[]{:S(2)}) collective-permute-start(bf16[4,144,128]{2,1,0:T(8,128)(2,1)S(1)} %add_convert_fusion.1), channel_id=1, source_target_pairs={{0,4},{2,6},{4,0},{6,2},{1,5},{3,7},{5,1},{7,3},{8,12},{10,14},{12... | collective-permute-start | bytes 442376 | tf_op jit(solution)/shard_map/ppermute | solution.py:489
  55.6 5.4 %collective-permute-done.10 = bf16[4,144,128]{2,1,0:T(8,128)(2,1)S(1)} collective-permute-done((bf16[4,144,128]{2,1,0:T(8,128)(2,1)S(1)}, bf16[4,144,128]{2,1,0:T(8,128)(2,1)S(1)}, u32[]{:S(2)}, u32[]{:S(2)}) %collective-permute-start.10) | collective-permute-done | bytes 147488 | tf_op jit(solution)/shard_map/ppermute | solution.py:489
  61.1 0.0 collective-permute-done.11.refs_0_.refs_1_
  61.1 0.1 relay.1
  61.2 1.3 %collective-permute-start.19 = (bf16[384,512]{1,0:T(8,128)(2,1)S(1)}, bf16[384,512]{1,0:T(8,128)(2,1)S(1)}, u32[]{:S(2)}, u32[]{:S(2)}) collective-permute-start(bf16[384,512]{1,0:T(8,128)(2,1)S(1)} %relay.1), channel_id=1, source_target_pairs={{2,0},{3,1},{4,2},{5,3},{6,4},{7,5},{10,8},{11,9},{12,10},{13,11},... | collective-permute-start | bytes 1179656 | tf_op jit(solution)/shard_map/ppermute | solution.py:34
  62.5 2.2 %collective-permute-start.17 = (bf16[4,144,128]{2,1,0:T(8,128)(2,1)S(1)}, bf16[4,144,128]{2,1,0:T(8,128)(2,1)S(1)}, u32[]{:S(2)}, u32[]{:S(2)}) collective-permute-start(bf16[4,144,128]{2,1,0:T(8,128)(2,1)S(1)} %add_convert_fusion.refs_0_), channel_id=1, source_target_pairs={{0,17},{1,16},{16,1},{17,0},{2,19},{3,18},{18,3},{19,2},{4,21},{5,... | collective-permute-start | bytes 442376 | tf_op jit(solution)/shard_map/ppermute | solution.py:483
  64.7 0.5 collective-permute-start.15
  65.3 0.8 %collective-permute-start.13 = (bf16[4,144,128]{2,1,0:T(8,128)(2,1)S(1)}, bf16[4,144,128]{2,1,0:T(8,128)(2,1)S(1)}, u32[]{:S(2)}, u32[]{:S(2)}) collective-permute-start(bf16[4,144,128]{2,1,0:T(8,128)(2,1)S(1)} %add_convert_fusion.refs_0_), channel_id=1, source_target_pairs={{0,1},{1,0},{16,17},{17,16},{2,3},{3,2},{18,19},{19,18},{4,5},{5,4... | collective-permute-start | bytes 442376 | tf_op jit(solution)/shard_map/ppermute | solution.py:483
  66.1 0.0 collective-permute-start.12
  66.1 0.7 unpack_early.1.refs_8_
  66.8 3.3 %collective-permute-done.17.refs_3_ = bf16[4,144,128]{2,1,0:T(8,128)(2,1)S(1)} collective-permute-done((bf16[4,144,128]{2,1,0:T(8,128)(2,1)S(1)}, bf16[4,144,128]{2,1,0:T(8,128)(2,1)S(1)}, u32[]{:S(2)}, u32[]{:S(2)}) %collective-permute-start.17) | collective-permute-done | bytes 147488 | tf_op jit(solution)/shard_map/ppermute | solution.py:483
  70.1 0.0 collective-permute-start.18
  70.1 1.7 %collective-permute-done.15.refs_2_ = bf16[4,144,128]{2,1,0:T(8,128)(2,1)S(1)} collective-permute-done((bf16[4,144,128]{2,1,0:T(8,128)(2,1)S(1)}, bf16[4,144,128]{2,1,0:T(8,128)(2,1)S(1)}, u32[]{:S(2)}, u32[]{:S(2)}) %collective-permute-start.15) | collective-permute-done | bytes 147488 | tf_op jit(solution)/shard_map/ppermute | solution.py:483
  71.8 0.0 collective-permute-start.16
  71.8 0.0 collective-permute-done.13.refs_1_
  71.8 0.5 collective-permute-start.14
  72.3 0.9 %collective-permute-done.19.refs_0_ = bf16[384,512]{1,0:T(8,128)(2,1)S(1)} collective-permute-done((bf16[384,512]{1,0:T(8,128)(2,1)S(1)}, bf16[384,512]{1,0:T(8,128)(2,1)S(1)}, u32[]{:S(2)}, u32[]{:S(2)}) %collective-permute-start.19) | collective-permute-done | bytes 393248 | tf_op jit(solution)/shard_map/ppermute | solution.py:34
  73.3 0.8 %merge.1 = (bf16[192,512]{1,0:T(8,128)(2,1)}, bf16[192,512]{1,0:T(8,128)(2,1)}) custom-call(bf16[384,512]{1,0:T(8,128)(2,1)S(1)} %collective-permute-done.19.refs_0_, bf16[384,512]{1,0:T(8,128)(2,1)S(1)} %collective-permute-done.11.refs_0_.refs_1_, f32[384,512]{1,0:T(8,128)S(1)} %get-tuple-element.87.refs_2_), custom_call_target="tpu_custom_call" | custom-call | flops 16000000000 | bytes 10000000 | tf_op jit(solution)/shard_map/merge/pallas_call | solution.py:686
  74.1 0.0 collective-permute-done.12.refs_4_
  74.1 0.0 collective-permute-done.18.refs_7_
  74.1 0.0 collective-permute-done.16.refs_6_
  74.2 0.0 collective-permute-done.14.refs_5_
  74.2 1.4 %unpack_late.1 = (f32[512,1024]{1,0:T(8,128)}, f32[31,1024]{1,0:T(8,128)}) custom-call(bf16[4,144,128]{2,1,0:T(8,128)(2,1)S(1)} %add_convert_fusion.refs_0_, bf16[4,144,128]{2,1,0:T(8,128)(2,1)S(1)} %collective-permute-done.13.refs_1_, bf16[4,144,128]{2,1,0:T(8,128)(2,1)S(1)} %collective-permute-done.15.refs_2_, ...), custom_call_target="tpu_custom_call", output_to_operand_aliasing={{0}: (8, {})} | custom-call | tf_op jit(solution)/shard_map/unpack_late/pallas_call | solution.py:722
  (3 shorter events, 0.1 us)
Async XLA Ops:
  2.1 15.2 %collective-permute-start.1 = (bf16[384,512]{1,0:T(8,128)(2,1)S(1)}, bf16[384,512]{1,0:T(8,128)(2,1)S(1)}, u32[]{:S(2)}, u32[]{:S(2)}) collective-permute-start(bf16[384,512]{1,0:T(8,128)(2,1)S(1)} %get-tuple-element.53.refs_1_.refs_2_), channel_id=1, source_target_pairs={{0,2},{1,3},{2,4},{3,5},{4,6},{5,7},{8,10},{9,11},{10,12},{11,13},... | collective-permute-start | bytes 1179656 | tf_op jit(solution)/shard_map/ppermute | solution.py:34
  7.0 12.8 %collective-permute-start = (bf16[224,512]{1,0:T(8,128)(2,1)S(1)}, bf16[224,512]{1,0:T(8,128)(2,1)S(1)}, u32[]{:S(2)}, u32[]{:S(2)}) collective-permute-start(bf16[224,512]{1,0:T(8,128)(2,1)S(1)} %get-tuple-element.54), channel_id=1, source_target_pairs={{0,1},{1,2},{2,3},{3,4},{4,5},{5,6},{6,7},{8,9},{9,10},{10,11},{11... | collective-permute-start | bytes 688136 | tf_op jit(solution)/shard_map/ppermute | solution.py:34
  10.5 9.4 %collective-permute-start.3 = (bf16[160,512]{1,0:T(8,128)(2,1)S(1)}, bf16[160,512]{1,0:T(8,128)(2,1)S(1)}, u32[]{:S(2)}, u32[]{:S(2)}) collective-permute-start(bf16[160,512]{1,0:T(8,128)(2,1)S(1)} %get-tuple-element.57), channel_id=1, source_target_pairs={{1,0},{2,1},{3,2},{4,3},{5,4},{6,5},{7,6},{9,8},{10,9},{11,10},{12... | collective-permute-start | bytes 491528 | tf_op jit(solution)/shard_map/ppermute | solution.py:34
  11.8 9.0 %collective-permute-start.2 = (bf16[64,512]{1,0:T(8,128)(2,1)S(1)}, bf16[64,512]{1,0:T(8,128)(2,1)S(1)}, u32[]{:S(2)}, u32[]{:S(2)}) collective-permute-start(bf16[64,512]{1,0:T(8,128)(2,1)S(1)} %get-tuple-element.55), channel_id=1, source_target_pairs={{0,3},{1,4},{2,5},{3,6},{4,7},{8,11},{9,12},{10,13},{11,14},{12,15... | collective-permute-start | bytes 196616 | tf_op jit(solution)/shard_map/ppermute | solution.py:34
  17.4 6.3 %collective-permute-start.4 = (bf16[192,512]{1,0:T(8,128)(2,1)S(1)}, bf16[192,512]{1,0:T(8,128)(2,1)S(1)}, u32[]{:S(2)}, u32[]{:S(2)}) collective-permute-start(bf16[192,512]{1,0:T(8,128)(2,1)S(1)} %choose.1), channel_id=1, source_target_pairs={{0,1},{1,0},{2,3},{3,2},{4,5},{5,4},{6,7},{7,6},{8,9},{9,8},{10,11... | collective-permute-start | bytes 589832 | tf_op jit(solution)/shard_map/ppermute | solution.py:550
  30.3 2.0 %collective-permute-start.5 = (bf16[16,128,128]{2,1,0:T(8,128)(2,1)S(1)}, bf16[16,128,128]{2,1,0:T(8,128)(2,1)S(1)}, u32[]{:S(2)}, u32[]{:S(2)}) collective-permute-start(bf16[16,128,128]{2,1,0:T(8,128)(2,1)S(1)} %get-tuple-element.65), channel_id=1, source_target_pairs={{0,8},{8,0},{1,9},{9,1},{2,10},{10,2},{3,11},{11,3},{4,12},{12,4},... | collective-permute-start | bytes 1572872 | tf_op jit(solution)/shard_map/ppermute | solution.py:496
  32.4 9.0 %collective-permute-start.6 = (bf16[4,144,128]{2,1,0:T(8,128)(2,1)S(1)}, bf16[4,144,128]{2,1,0:T(8,128)(2,1)S(1)}, u32[]{:S(2)}, u32[]{:S(2)}) collective-permute-start(bf16[4,144,128]{2,1,0:T(8,128)(2,1)S(1)} %get-tuple-element.77), channel_id=1, source_target_pairs={{0,1},{1,0},{16,17},{17,16},{2,3},{3,2},{18,19},{19,18},{4,5},{5,4... | collective-permute-start | bytes 442376 | tf_op jit(solution)/shard_map/ppermute | solution.py:483
  34.4 7.0 %collective-permute-start.7 = (bf16[4,144,128]{2,1,0:T(8,128)(2,1)S(1)}, bf16[4,144,128]{2,1,0:T(8,128)(2,1)S(1)}, u32[]{:S(2)}, u32[]{:S(2)}) collective-permute-start(bf16[4,144,128]{2,1,0:T(8,128)(2,1)S(1)} %get-tuple-element.78), channel_id=1, source_target_pairs={{0,16},{1,17},{16,0},{17,1},{2,18},{3,19},{18,2},{19,3},{4,20},{5,... | collective-permute-start | bytes 442376 | tf_op jit(solution)/shard_map/ppermute | solution.py:483
  35.9 7.4 %collective-permute-start.8 = (bf16[4,144,128]{2,1,0:T(8,128)(2,1)S(1)}, bf16[4,144,128]{2,1,0:T(8,128)(2,1)S(1)}, u32[]{:S(2)}, u32[]{:S(2)}) collective-permute-start(bf16[4,144,128]{2,1,0:T(8,128)(2,1)S(1)} %get-tuple-element.79), channel_id=1, source_target_pairs={{0,17},{1,16},{16,1},{17,0},{2,19},{3,18},{18,3},{19,2},{4,21},{5,... | collective-permute-start | bytes 442376 | tf_op jit(solution)/shard_map/ppermute | solution.py:483
  43.4 8.0 %collective-permute-start.9 = (bf16[4,144,128]{2,1,0:T(8,128)(2,1)S(1)}, bf16[4,144,128]{2,1,0:T(8,128)(2,1)S(1)}, u32[]{:S(2)}, u32[]{:S(2)}) collective-permute-start(bf16[4,144,128]{2,1,0:T(8,128)(2,1)S(1)} %add_convert_fusion.2), channel_id=1, source_target_pairs={{0,2},{2,0},{4,6},{6,4},{1,3},{3,1},{5,7},{7,5},{8,10},{10,8},{12,... | collective-permute-start | bytes 442376 | tf_op jit(solution)/shard_map/ppermute | solution.py:489
  48.0 13.1 %collective-permute-start.11 = (bf16[384,512]{1,0:T(8,128)(2,1)S(1)}, bf16[384,512]{1,0:T(8,128)(2,1)S(1)}, u32[]{:S(2)}, u32[]{:S(2)}) collective-permute-start(bf16[384,512]{1,0:T(8,128)(2,1)S(1)} %get-tuple-element.83), channel_id=1, source_target_pairs={{0,1},{1,0},{2,3},{3,2},{4,5},{5,4},{6,7},{7,6},{8,9},{9,8},{10,11... | collective-permute-start | bytes 1179656 | tf_op jit(solution)/shard_map/ppermute | solution.py:668
  51.4 9.6 %collective-permute-start.10 = (bf16[4,144,128]{2,1,0:T(8,128)(2,1)S(1)}, bf16[4,144,128]{2,1,0:T(8,128)(2,1)S(1)}, u32[]{:S(2)}, u32[]{:S(2)}) collective-permute-start(bf16[4,144,128]{2,1,0:T(8,128)(2,1)S(1)} %add_convert_fusion.1), channel_id=1, source_target_pairs={{0,4},{2,6},{4,0},{6,2},{1,5},{3,7},{5,1},{7,3},{8,12},{10,14},{12... | collective-permute-start | bytes 442376 | tf_op jit(solution)/shard_map/ppermute | solution.py:489
  61.2 12.1 %collective-permute-start.19 = (bf16[384,512]{1,0:T(8,128)(2,1)S(1)}, bf16[384,512]{1,0:T(8,128)(2,1)S(1)}, u32[]{:S(2)}, u32[]{:S(2)}) collective-permute-start(bf16[384,512]{1,0:T(8,128)(2,1)S(1)} %relay.1), channel_id=1, source_target_pairs={{2,0},{3,1},{4,2},{5,3},{6,4},{7,5},{10,8},{11,9},{12,10},{13,11},... | collective-permute-start | bytes 1179656 | tf_op jit(solution)/shard_map/ppermute | solution.py:34
  62.5 7.6 %collective-permute-start.17 = (bf16[4,144,128]{2,1,0:T(8,128)(2,1)S(1)}, bf16[4,144,128]{2,1,0:T(8,128)(2,1)S(1)}, u32[]{:S(2)}, u32[]{:S(2)}) collective-permute-start(bf16[4,144,128]{2,1,0:T(8,128)(2,1)S(1)} %add_convert_fusion.refs_0_), channel_id=1, source_target_pairs={{0,17},{1,16},{16,1},{17,0},{2,19},{3,18},{18,3},{19,2},{4,21},{5,... | collective-permute-start | bytes 442376 | tf_op jit(solution)/shard_map/ppermute | solution.py:483
  64.7 7.1 %collective-permute-start.15 = (bf16[4,144,128]{2,1,0:T(8,128)(2,1)S(1)}, bf16[4,144,128]{2,1,0:T(8,128)(2,1)S(1)}, u32[]{:S(2)}, u32[]{:S(2)}) collective-permute-start(bf16[4,144,128]{2,1,0:T(8,128)(2,1)S(1)} %add_convert_fusion.refs_0_), channel_id=1, source_target_pairs={{0,16},{1,17},{16,0},{17,1},{2,18},{3,19},{18,2},{19,3},{4,20},{5,... | collective-permute-start | bytes 442376 | tf_op jit(solution)/shard_map/ppermute | solution.py:483
  65.3 6.6 %collective-permute-start.13 = (bf16[4,144,128]{2,1,0:T(8,128)(2,1)S(1)}, bf16[4,144,128]{2,1,0:T(8,128)(2,1)S(1)}, u32[]{:S(2)}, u32[]{:S(2)}) collective-permute-start(bf16[4,144,128]{2,1,0:T(8,128)(2,1)S(1)} %add_convert_fusion.refs_0_), channel_id=1, source_target_pairs={{0,1},{1,0},{16,17},{17,16},{2,3},{3,2},{18,19},{19,18},{4,5},{5,4... | collective-permute-start | bytes 442376 | tf_op jit(solution)/shard_map/ppermute | solution.py:483
  66.1 8.1 %collective-permute-start.12 = (bf16[4,144,128]{2,1,0:T(8,128)(2,1)S(1)}, bf16[4,144,128]{2,1,0:T(8,128)(2,1)S(1)}, u32[]{:S(2)}, u32[]{:S(2)}) collective-permute-start(bf16[4,144,128]{2,1,0:T(8,128)(2,1)S(1)} %add_convert_fusion.refs_0_), channel_id=1, source_target_pairs={{0,8},{8,0},{1,9},{9,1},{2,10},{10,2},{3,11},{11,3},{4,12},{12,4},... | collective-permute-start | bytes 442376 | tf_op jit(solution)/shard_map/ppermute | solution.py:496
  70.1 4.0 %collective-permute-start.18 = (bf16[4,144,128]{2,1,0:T(8,128)(2,1)S(1)}, bf16[4,144,128]{2,1,0:T(8,128)(2,1)S(1)}, u32[]{:S(2)}, u32[]{:S(2)}) collective-permute-start(bf16[4,144,128]{2,1,0:T(8,128)(2,1)S(1)} %collective-permute-done.17.refs_3_), channel_id=1, source_target_pairs={{0,8},{8,0},{1,9},{9,1},{2,10},{10,2},{3,11},{11,3},{4,12},{12,4},... | collective-permute-start | bytes 442376 | tf_op jit(solution)/shard_map/ppermute | solution.py:496
  71.8 2.3 %collective-permute-start.16 = (bf16[4,144,128]{2,1,0:T(8,128)(2,1)S(1)}, bf16[4,144,128]{2,1,0:T(8,128)(2,1)S(1)}, u32[]{:S(2)}, u32[]{:S(2)}) collective-permute-start(bf16[4,144,128]{2,1,0:T(8,128)(2,1)S(1)} %collective-permute-done.15.refs_2_), channel_id=1, source_target_pairs={{0,8},{8,0},{1,9},{9,1},{2,10},{10,2},{3,11},{11,3},{4,12},{12,4},... | collective-permute-start | bytes 442376 | tf_op jit(solution)/shard_map/ppermute | solution.py:496
  71.8 2.3 %collective-permute-start.14 = (bf16[4,144,128]{2,1,0:T(8,128)(2,1)S(1)}, bf16[4,144,128]{2,1,0:T(8,128)(2,1)S(1)}, u32[]{:S(2)}, u32[]{:S(2)}) collective-permute-start(bf16[4,144,128]{2,1,0:T(8,128)(2,1)S(1)} %collective-permute-done.13.refs_1_), channel_id=1, source_target_pairs={{0,8},{8,0},{1,9},{9,1},{2,10},{10,2},{3,11},{11,3},{4,12},{12,4},... | collective-permute-start | bytes 442376 | tf_op jit(solution)/shard_map/ppermute | solution.py:496
